TPU v7x, 32 devices: a whole 2x2x4 slice. The times are simulated.
32 devices in a mesh: pair: 2 (over x), gx: 4 (over y, core), gy: 4 (over z).
Axes of the slice: x: 2, y: 2, z: 4, core: 2. Of those that a mesh axis runs over, the one named last changes fastest.
Arguments:
- sound_speed_sq: float32 [32, 32, 1024], P('gx', 'gy'), may hold values from 0.5 to 2
- wind_profile: float32 [3, 1024], replicated, may hold values from -0.6 to 0.6
- forward_field: bfloat16 [4, 4, 32, 32, 1024], P(None, None, 'gx', 'gy'), may hold values from -6 to 6
- adjoint_state: float32 [2, 4, 32, 32, 1024], P('pair', None, 'gx', 'gy'), may hold values from -0.3125 to 0.3125
- pair_counts: int32 [2], P('pair'), may hold values from 64 to 256, as said below
- source_cells: int32 [512, 3], P('pair'), may hold values from 0 to 1023, as said below
- receiver_cells: int32 [512, 3], P('pair'), may hold values from 0 to 1023, as said below
- residuals: float32 [512, 4], P('pair'), may hold values from -16 to 16
Outputs:
- kernels: float32 [4, 32, 32, 1024], P(None, 'gx', 'gy', 'pair')
- final_state: float32 [2, 4, 32, 32, 1024], P('pair', None, 'gx', 'gy')
Inputs may be any that keep to these rules, and one draw needn't show every extreme that they name: `pair_counts`: one group in every draw has exactly 256 live pairs. `source_cells`: columns are the cell along the first, second and third dimension, each within the grid. `receiver_cells`: columns are the cell along the first, second and third dimension, each within the grid; several pairs may share a cell.
All inputs are finite; a program needn't handle non-finite values.
Results may differ from a plain program's by a relative error of at most 0.00115.
Values may be sent and summed in bfloat16 or wider, within the bound.
No kernel may reach another device: no remote copies, remote signals or barrier semaphores. Data moves between devices by JAX's collectives and lax.ppermute only.
A program may use at most 128 MiB of HBM per device.

v0:
```python
import jax
import jax.numpy as jnp
from jax import lax
from jax.sharding import PartitionSpec as P

step_length = 0.25


def extended(shard, sides, width):
    for axis, dim in sides:
        size, length = (lax.axis_size(axis), shard.shape[dim])
        up = [(i, (i + 1) % size) for i in range(size - 1)]
        down = [(j, i) for i, j in up]
        last = lax.slice_in_dim(shard, length - width, length, axis=dim)
        initial = lax.slice_in_dim(shard, 0, width, axis=dim)
        before = lax.ppermute(last, axis, up)
        after = lax.ppermute(initial, axis, down)
        shard = jnp.concatenate([before, shard, after], axis=dim)
    return shard


def central(padded):
    dims = padded.ndim
    east_diff = (padded[..., 2:, 1:-1, :] - padded[..., :-2, 1:-1, :]) * 0.5
    north_diff = (padded[..., 1:-1, 2:, :] - padded[..., 1:-1, :-2, :]) * 0.5
    center = padded[..., 1:-1, 1:-1, :]
    vertical = jnp.pad(center, [(0, 0)] * (dims - 1) + [(1, 1)])
    up_diff = (vertical[..., 2:] - vertical[..., :-2]) * 0.5
    return (east_diff, north_diff, up_diff, center)


def local_flat(cells, width_x, width_y, depth):
    local_x = cells[:, 0] - lax.axis_index("gx") * width_x
    local_y = cells[:, 1] - lax.axis_index("gy") * width_y
    inside = (local_x >= 0) & (local_x < width_x) & (local_y >= 0) & (local_y < width_y)
    flat = (
        jnp.clip(local_x, 0, width_x - 1) * width_y + jnp.clip(local_y, 0, width_y - 1)
    ) * depth + cells[:, 2]
    return (flat, inside.astype(jnp.float32))


def shards(
    sound_speed_sq,
    wind_profile,
    forward_field,
    adjoint_state,
    pair_counts,
    source_cells,
    receiver_cells,
    residuals,
):
    steps_total = forward_field.shape[0]
    width_x, width_y, depth = sound_speed_sq.shape
    slots = residuals.shape[0]
    east_wind = wind_profile[0]
    north_wind = wind_profile[1]
    vertical_wind = wind_profile[2]
    live = (jnp.arange(slots, dtype=jnp.int32) < pair_counts[0]).astype(jnp.float32)
    src_flat, src_inside = local_flat(source_cells, width_x, width_y, depth)
    rcv_flat, rcv_inside = local_flat(receiver_cells, width_x, width_y, depth)
    pressure_snaps = forward_field[:, 0].reshape(steps_total, -1)
    local_samples = (
        jnp.take(pressure_snaps, src_flat, axis=1).astype(jnp.float32) * src_inside[None, :]
    )
    samples = lax.psum(local_samples, ("gx", "gy"))
    state = adjoint_state[0]
    kernel_local = jnp.zeros((4, width_x, width_y, depth), jnp.float32)
    for step in range(steps_total):
        snap = steps_total - 1 - step
        amplitude = residuals[:, snap] * samples[snap] * live * rcv_inside
        injected = (
            jnp.zeros((width_x * width_y * depth,), jnp.float32)
            .at[rcv_flat]
            .add(amplitude)
            .reshape(width_x, width_y, depth)
        )
        padded = extended(state, (("gx", 1), ("gy", 2)), 1)
        east_diff, north_diff, up_diff, center = central(padded)
        pressure = center[0]
        velocity = center[1:]
        divergence = east_diff[1] + north_diff[2] + up_diff[3]
        p_new = (
            pressure
            + step_length
            * (
                sound_speed_sq * divergence
                + east_wind * east_diff[0]
                + north_wind * north_diff[0]
                + vertical_wind * up_diff[0]
            )
            + injected
        )
        p_padded = extended(p_new, (("gx", 0), ("gy", 1)), 1)
        p_east, p_north, p_up, unused_center = central(p_padded)
        gradient = jnp.stack([p_east, p_north, p_up])
        a_new = velocity + step_length * (
            gradient
            + east_wind * east_diff[1:]
            + north_wind * north_diff[1:]
            + vertical_wind * up_diff[1:]
        )
        forward_rim = extended(forward_field[snap], (("gx", 1), ("gy", 2)), 1).astype(jnp.float32)
        f_east, f_north, f_up, unused_forward = central(forward_rim)
        pieces = [p_new * (f_east[1] + f_north[2] + f_up[3])]
        for along in (f_east, f_north, f_up):
            pieces.append(
                p_new * along[0] + a_new[0] * along[1] + a_new[1] * along[2] + a_new[2] * along[3]
            )
        increment = jnp.stack(pieces)
        kernel_local = kernel_local + increment
        state = jnp.concatenate([p_new[None], a_new], axis=0)
    kernels = lax.psum_scatter(kernel_local, "pair", scatter_dimension=3, tiled=True)
    return (kernels, state[None])


def solution(mesh):
    in_specs = (
        P("gx", "gy", None),
        P(),
        P(None, None, "gx", "gy", None),
        P("pair", None, "gx", "gy", None),
        P("pair"),
        P("pair", None),
        P("pair", None),
        P("pair", None),
    )
    out_specs = (P(None, "gx", "gy", "pair"), P("pair", None, "gx", "gy", None))
    return jax.shard_map(shards, mesh=mesh, in_specs=in_specs, out_specs=out_specs, check_vma=False)
```

profile of v0, /device:TPU:1, one launch (start us, length us, event | category | flops | bytes accessed | tf_op | source)
XLA Modules:
  0.0 326.8 jit_solution(6222700085133830216)
XLA Ops:
  9.7 2.0 collective-permute-start.5
  11.7 4.5 %collective-permute-start.4 = (bf16[4,1,8,1024]{3,2,1,0:T(8,128)(2,1)}, bf16[4,1,8,1024]{3,2,1,0:T(8,128)(2,1)}, u32[]{:S(2)}, u32[]{:S(2)}) collective-permute-start(bf16[4,1,8,1024]{3,2,1,0:T(8,128)(2,1)} %get-tuple-element.82), channel_id=1, source_target_pairs={{0,4},{4,8},{8,12},{1,5},{5,9},{9,13},{2,6},{6,10},{10,14},{3,7},{... | collective-permute-start | bytes 196616 | tf_op jit(solution)/shard_map/ppermute | solution.py:16
  17.0 3.0 collective-permute-start.1
  20.0 1.9 collective-permute-start
  27.5 13.0 %copy.11 = bf16[4,1,8,8,1024]{0,4,3,2,1:T(8,128)(2,1)} copy(bf16[4,1,8,8,1024]{4,3,2,1,0:T(8,128)(2,1)} %slice.831) | data formatting | bytes 1048576 | tf_op jit(solution)/shard_map/slice | solution.py:61
  40.5 8.7 %gather_fusion = bf16[256,4]{1,0:T(8,128)(2,1)S(1)} fusion(bf16[4,65536]{0,1:T(8,128)(2,1)} %bitcast.532, s32[1024]{0:T(1024)S(1)} %pad_clamp_fusion), kind=kCustom, calls=%fused_computation | custom fusion | bytes 5120 | tf_op jit(solution)/shard_map/jit(_take)/gather | solution.py:63
  49.3 61.3 %psum.7 = f32[4,256]{0,1:T(8,128)S(1)} all-reduce(f32[4,256]{0,1:T(8,128)S(1)} %multiply_bitcast_fusion), channel_id=1, replica_groups=mesh['pair'=2,'gx'=4,'gy'=4] {'gx','gy'}, use_global_device_ids=true, to_apply=%region_0.1 | all-reduce | flops 1024 | bytes 8192 | tf_op jit(solution)/shard_map/psum | solution.py:65
  115.7 2.2 scatter_custom_fusion
  118.6 2.2 scatter_custom_fusion.1
  121.5 2.2 scatter_custom_fusion.2
  124.5 2.8 scatter_custom_fusion.3
  128.2 4.6 %collective-permute-start.16 = (bf16[4,1,8,1024]{3,2,1,0:T(8,128)(2,1)}, bf16[4,1,8,1024]{3,2,1,0:T(8,128)(2,1)S(1)}, u32[]{:S(2)}, u32[]{:S(2)}) collective-permute-start(bf16[4,1,8,1024]{3,2,1,0:T(8,128)(2,1)} %get-tuple-element.80), channel_id=1, source_target_pairs={{0,4},{4,8},{8,12},{1,5},{5,9},{9,13},{2,6},{6,10},{10,14},{3,7},{... | collective-permute-start | bytes 196616 | tf_op jit(solution)/shard_map/ppermute | solution.py:16
  132.8 2.2 collective-permute-start.29
  136.3 3.3 %collective-permute-start.28 = (bf16[4,1,8,1024]{3,2,1,0:T(8,128)(2,1)}, bf16[4,1,8,1024]{3,2,1,0:T(8,128)(2,1)S(1)}, u32[]{:S(2)}, u32[]{:S(2)}) collective-permute-start(bf16[4,1,8,1024]{3,2,1,0:T(8,128)(2,1)} %get-tuple-element.78), channel_id=1, source_target_pairs={{0,4},{4,8},{8,12},{1,5},{5,9},{9,13},{2,6},{6,10},{10,14},{3,7},{... | collective-permute-start | bytes 196616 | tf_op jit(solution)/shard_map/ppermute | solution.py:16
  142.7 3.6 %collective-permute-start.40 = (bf16[4,1,8,1024]{3,2,1,0:T(8,128)(2,1)}, bf16[4,1,8,1024]{3,2,1,0:T(8,128)(2,1)S(1)}, u32[]{:S(2)}, u32[]{:S(2)}) collective-permute-start(bf16[4,1,8,1024]{3,2,1,0:T(8,128)(2,1)} %get-tuple-element.76), channel_id=1, source_target_pairs={{0,4},{4,8},{8,12},{1,5},{5,9},{9,13},{2,6},{6,10},{10,14},{3,7},{... | collective-permute-start | bytes 196616 | tf_op jit(solution)/shard_map/ppermute | solution.py:16
  147.9 4.0 %collective-permute-start.6 = (bf16[4,10,1,1024]{3,2,1,0:T(2,128)(2,1)S(1)}, bf16[4,10,1,1024]{3,2,1,0:T(2,128)(2,1)S(1)}, u32[]{:S(2)}, u32[]{:S(2)}) collective-permute-start(bf16[4,10,1,1024]{3,2,1,0:T(2,128)(2,1)S(1)} %get-tuple-element.74), channel_id=1, source_target_pairs={{0,1},{1,2},{2,3},{4,5},{5,6},{6,7},{8,9},{9,10},{10,11},{12,13},{... | collective-permute-start | bytes 245768 | tf_op jit(solution)/shard_map/ppermute | solution.py:16
  153.4 4.0 %collective-permute-start.18 = (bf16[4,10,1,1024]{3,2,1,0:T(2,128)(2,1)S(1)}, bf16[4,10,1,1024]{3,2,1,0:T(2,128)(2,1)S(1)}, u32[]{:S(2)}, u32[]{:S(2)}) collective-permute-start(bf16[4,10,1,1024]{3,2,1,0:T(2,128)(2,1)S(1)} %get-tuple-element.72), channel_id=1, source_target_pairs={{0,1},{1,2},{2,3},{4,5},{5,6},{6,7},{8,9},{9,10},{10,11},{12,13},{... | collective-permute-start | bytes 245768 | tf_op jit(solution)/shard_map/ppermute | solution.py:16
  159.9 4.0 %collective-permute-start.3 = (f32[4,10,1,1024]{3,2,1,0:T(1,128)S(1)}, f32[4,10,1,1024]{3,2,1,0:T(1,128)S(1)}, u32[]{:S(2)}, u32[]{:S(2)}) collective-permute-start(f32[4,10,1,1024]{3,2,1,0:T(1,128)S(1)} %get-tuple-element.47), channel_id=1, source_target_pairs={{0,1},{1,2},{2,3},{4,5},{5,6},{6,7},{8,9},{9,10},{10,11},{12,13},{... | collective-permute-start | bytes 491528 | tf_op jit(solution)/shard_map/ppermute | solution.py:16
  168.3 4.1 %collective-permute-start.30 = (bf16[4,10,1,1024]{3,2,1,0:T(2,128)(2,1)S(1)}, bf16[4,10,1,1024]{3,2,1,0:T(2,128)(2,1)S(1)}, u32[]{:S(2)}, u32[]{:S(2)}) collective-permute-start(bf16[4,10,1,1024]{3,2,1,0:T(2,128)(2,1)S(1)} %get-tuple-element.70), channel_id=1, source_target_pairs={{0,1},{1,2},{2,3},{4,5},{5,6},{6,7},{8,9},{9,10},{10,11},{12,13},{... | collective-permute-start | bytes 245768 | tf_op jit(solution)/shard_map/ppermute | solution.py:16
  173.7 1.9 fusion.39
  176.0 4.2 %collective-permute-start.9 = (f32[1,8,1024]{2,1,0:T(8,128)S(1)}, f32[1,8,1024]{2,1,0:T(8,128)S(1)}, u32[]{:S(2)}, u32[]{:S(2)}) collective-permute-start(f32[1,8,1024]{2,1,0:T(8,128)S(1)} %get-tuple-element.110), channel_id=1, source_target_pairs={{0,4},{4,8},{8,12},{1,5},{5,9},{9,13},{2,6},{6,10},{10,14},{3,7},{... | collective-permute-start | bytes 98312 | tf_op jit(solution)/shard_map/ppermute | solution.py:16
  180.2 1.9 collective-permute-start.8
  185.5 4.3 %collective-permute-start.11 = (f32[10,1,1024]{2,1,0:T(1,128)S(1)}, f32[10,1,1024]{2,1,0:T(1,128)S(1)}, u32[]{:S(2)}, u32[]{:S(2)}) collective-permute-start(f32[10,1,1024]{2,1,0:T(1,128)S(1)} %get-tuple-element.99), channel_id=1, source_target_pairs={{0,1},{1,2},{2,3},{4,5},{5,6},{6,7},{8,9},{9,10},{10,11},{12,13},{... | collective-permute-start | bytes 122888 | tf_op jit(solution)/shard_map/ppermute | solution.py:16
  191.7 2.8 collective-permute-done.10
  195.2 3.3 %collective-permute-start.13 = (f32[4,1,8,1024]{3,2,1,0:T(8,128)S(1)}, f32[4,1,8,1024]{3,2,1,0:T(8,128)S(1)}, u32[]{:S(2)}, u32[]{:S(2)}) collective-permute-start(f32[4,1,8,1024]{3,2,1,0:T(8,128)S(1)} %get-tuple-element.61), channel_id=1, source_target_pairs={{0,4},{4,8},{8,12},{1,5},{5,9},{9,13},{2,6},{6,10},{10,14},{3,7},{... | collective-permute-start | bytes 393224 | tf_op jit(solution)/shard_map/ppermute | solution.py:16
  198.6 1.9 collective-permute-start.12
  202.8 2.1 collective-permute-done.12
  205.1 1.9 collective-permute-start.15
  209.5 3.6 %collective-permute-done.14 = f32[4,10,1,1024]{3,2,1,0:T(1,128)S(1)} collective-permute-done((f32[4,10,1,1024]{3,2,1,0:T(1,128)S(1)}, f32[4,10,1,1024]{3,2,1,0:T(1,128)S(1)}, u32[]{:S(2)}, u32[]{:S(2)}) %collective-permute-start.14) | collective-permute-done | bytes 163872 | tf_op jit(solution)/shard_map/ppermute | solution.py:17
  214.5 3.4 %collective-permute-start.21 = (f32[1,8,1024]{2,1,0:T(8,128)S(1)}, f32[1,8,1024]{2,1,0:T(8,128)S(1)}, u32[]{:S(2)}, u32[]{:S(2)}) collective-permute-start(f32[1,8,1024]{2,1,0:T(8,128)S(1)} %get-tuple-element.107), channel_id=1, source_target_pairs={{0,4},{4,8},{8,12},{1,5},{5,9},{9,13},{2,6},{6,10},{10,14},{3,7},{... | collective-permute-start | bytes 98312 | tf_op jit(solution)/shard_map/ppermute | solution.py:16
  218.0 1.9 collective-permute-start.20
  220.5 2.7 collective-permute-done.20
  226.9 2.7 collective-permute-done.22
  230.3 3.3 %collective-permute-start.25 = (f32[4,1,8,1024]{3,2,1,0:T(8,128)S(1)}, f32[4,1,8,1024]{3,2,1,0:T(8,128)S(1)}, u32[]{:S(2)}, u32[]{:S(2)}) collective-permute-start(f32[4,1,8,1024]{3,2,1,0:T(8,128)S(1)} %get-tuple-element.56), channel_id=1, source_target_pairs={{0,4},{4,8},{8,12},{1,5},{5,9},{9,13},{2,6},{6,10},{10,14},{3,7},{... | collective-permute-start | bytes 393224 | tf_op jit(solution)/shard_map/ppermute | solution.py:16
  233.7 1.9 collective-permute-start.24
  236.1 3.8 %collective-permute-done.24 = f32[4,1,8,1024]{3,2,1,0:T(8,128)S(1)} collective-permute-done((f32[4,1,8,1024]{3,2,1,0:T(8,128)S(1)}, f32[4,1,8,1024]{3,2,1,0:T(8,128)S(1)}, u32[]{:S(2)}, u32[]{:S(2)}) %collective-permute-start.24) | collective-permute-done | bytes 131104 | tf_op jit(solution)/shard_map/ppermute | solution.py:17
  244.6 3.3 %collective-permute-done.26 = f32[4,10,1,1024]{3,2,1,0:T(1,128)S(1)} collective-permute-done((f32[4,10,1,1024]{3,2,1,0:T(1,128)S(1)}, f32[4,10,1,1024]{3,2,1,0:T(1,128)S(1)}, u32[]{:S(2)}, u32[]{:S(2)}) %collective-permute-start.26) | collective-permute-done | bytes 163872 | tf_op jit(solution)/shard_map/ppermute | solution.py:17
  249.4 3.2 collective-permute-start.33
  252.6 1.9 collective-permute-start.32
  254.9 3.0 collective-permute-done.32
  261.0 3.3 %collective-permute-done.34 = f32[10,1,1024]{2,1,0:T(1,128)S(1)} collective-permute-done((f32[10,1,1024]{2,1,0:T(1,128)S(1)}, f32[10,1,1024]{2,1,0:T(1,128)S(1)}, u32[]{:S(2)}, u32[]{:S(2)}) %collective-permute-start.34) | collective-permute-done | bytes 40992 | tf_op jit(solution)/shard_map/ppermute | solution.py:17
  265.0 3.3 %collective-permute-start.37 = (f32[4,1,8,1024]{3,2,1,0:T(8,128)S(1)}, f32[4,1,8,1024]{3,2,1,0:T(8,128)S(1)}, u32[]{:S(2)}, u32[]{:S(2)}) collective-permute-start(f32[4,1,8,1024]{3,2,1,0:T(8,128)S(1)} %get-tuple-element.51), channel_id=1, source_target_pairs={{0,4},{4,8},{8,12},{1,5},{5,9},{9,13},{2,6},{6,10},{10,14},{3,7},{... | collective-permute-start | bytes 393224 | tf_op jit(solution)/shard_map/ppermute | solution.py:16
  270.6 4.0 %collective-permute-done.36 = f32[4,1,8,1024]{3,2,1,0:T(8,128)S(1)} collective-permute-done((f32[4,1,8,1024]{3,2,1,0:T(8,128)S(1)}, f32[4,1,8,1024]{3,2,1,0:T(8,128)S(1)}, u32[]{:S(2)}, u32[]{:S(2)}) %collective-permute-start.36) | collective-permute-done | bytes 131104 | tf_op jit(solution)/shard_map/ppermute | solution.py:17
  278.8 3.8 %collective-permute-done.38 = f32[4,10,1,1024]{3,2,1,0:T(1,128)S(1)} collective-permute-done((f32[4,10,1,1024]{3,2,1,0:T(1,128)S(1)}, f32[4,10,1,1024]{3,2,1,0:T(1,128)S(1)}, u32[]{:S(2)}, u32[]{:S(2)}) %collective-permute-start.38) | collective-permute-done | bytes 163872 | tf_op jit(solution)/shard_map/ppermute | solution.py:17
  284.0 3.2 collective-permute-start.45
  289.5 2.9 collective-permute-done.44
  295.7 3.3 %collective-permute-done.46 = f32[10,1,1024]{2,1,0:T(1,128)S(1)} collective-permute-done((f32[10,1,1024]{2,1,0:T(1,128)S(1)}, f32[10,1,1024]{2,1,0:T(1,128)S(1)}, u32[]{:S(2)}, u32[]{:S(2)}) %collective-permute-start.46) | collective-permute-done | bytes 40992 | tf_op jit(solution)/shard_map/ppermute | solution.py:17
  302.7 17.2 %reduce-scatter.2.cloned.1.call-done = f32[4,8,8,512]{3,2,1,0:T(8,128)} async-done(((f32[4,8,8,1024]{3,2,1,0:T(8,128)}), f32[4,8,8,512]{3,2,1,0:T(8,128)}) %reduce-scatter.2.cloned.1.call-update) | async-done | bytes 524304 | tf_op jit(solution)/shard_map/reduce_scatter | solution.py:112
  (154 shorter events, 77.1 us)
Async XLA Ops:
  7.2 312.7 %reduce-scatter.2.cloned.1.call-start = ((), (), s32[]{:S(2)}) async-start(), calls=%async_computation.1 | async-start | bytes 1572864 | tf_op jit(solution)/shard_map/reduce_scatter | solution.py:112
  9.7 118.5 %collective-permute-start.5 = (bf16[4,1,8,1024]{3,2,1,0:T(8,128)(2,1)}, bf16[4,1,8,1024]{3,2,1,0:T(8,128)(2,1)}, u32[]{:S(2)}, u32[]{:S(2)}) collective-permute-start(bf16[4,1,8,1024]{3,2,1,0:T(8,128)(2,1)} %get-tuple-element.83), channel_id=1, source_target_pairs={{4,0},{8,4},{12,8},{5,1},{9,5},{13,9},{6,2},{10,6},{14,10},{7,3},{... | collective-permute-start | bytes 196616 | tf_op jit(solution)/shard_map/ppermute | solution.py:17
  11.7 121.1 %collective-permute-start.4 = (bf16[4,1,8,1024]{3,2,1,0:T(8,128)(2,1)}, bf16[4,1,8,1024]{3,2,1,0:T(8,128)(2,1)}, u32[]{:S(2)}, u32[]{:S(2)}) collective-permute-start(bf16[4,1,8,1024]{3,2,1,0:T(8,128)(2,1)} %get-tuple-element.82), channel_id=1, source_target_pairs={{0,4},{4,8},{8,12},{1,5},{5,9},{9,13},{2,6},{6,10},{10,14},{3,7},{... | collective-permute-start | bytes 196616 | tf_op jit(solution)/shard_map/ppermute | solution.py:16
  17.0 136.5 %collective-permute-start.1 = (f32[4,1,8,1024]{3,2,1,0:T(8,128)}, f32[4,1,8,1024]{3,2,1,0:T(8,128)S(1)}, u32[]{:S(2)}, u32[]{:S(2)}) collective-permute-start(f32[4,1,8,1024]{3,2,1,0:T(8,128)} %get-tuple-element.66), channel_id=1, source_target_pairs={{0,4},{4,8},{8,12},{1,5},{5,9},{9,13},{2,6},{6,10},{10,14},{3,7},{... | collective-permute-start | bytes 393224 | tf_op jit(solution)/shard_map/ppermute | solution.py:16
  20.0 137.5 %collective-permute-start = (f32[4,1,8,1024]{3,2,1,0:T(8,128)}, f32[4,1,8,1024]{3,2,1,0:T(8,128)}, u32[]{:S(2)}, u32[]{:S(2)}) collective-permute-start(f32[4,1,8,1024]{3,2,1,0:T(8,128)} %get-tuple-element.67), channel_id=1, source_target_pairs={{4,0},{8,4},{12,8},{5,1},{9,5},{13,9},{6,2},{10,6},{14,10},{7,3},{... | collective-permute-start | bytes 393224 | tf_op jit(solution)/shard_map/ppermute | solution.py:17
  22.5 113.7 %collective-permute-start.17 = (bf16[4,1,8,1024]{3,2,1,0:T(8,128)(2,1)}, bf16[4,1,8,1024]{3,2,1,0:T(8,128)(2,1)}, u32[]{:S(2)}, u32[]{:S(2)}) collective-permute-start(bf16[4,1,8,1024]{3,2,1,0:T(8,128)(2,1)} %get-tuple-element.81), channel_id=1, source_target_pairs={{4,0},{8,4},{12,8},{5,1},{9,5},{13,9},{6,2},{10,6},{14,10},{7,3},{... | collective-permute-start | bytes 196616 | tf_op jit(solution)/shard_map/ppermute | solution.py:17
  128.2 11.4 %collective-permute-start.16 = (bf16[4,1,8,1024]{3,2,1,0:T(8,128)(2,1)}, bf16[4,1,8,1024]{3,2,1,0:T(8,128)(2,1)S(1)}, u32[]{:S(2)}, u32[]{:S(2)}) collective-permute-start(bf16[4,1,8,1024]{3,2,1,0:T(8,128)(2,1)} %get-tuple-element.80), channel_id=1, source_target_pairs={{0,4},{4,8},{8,12},{1,5},{5,9},{9,13},{2,6},{6,10},{10,14},{3,7},{... | collective-permute-start | bytes 196616 | tf_op jit(solution)/shard_map/ppermute | solution.py:16
  132.8 9.8 %collective-permute-start.29 = (bf16[4,1,8,1024]{3,2,1,0:T(8,128)(2,1)}, bf16[4,1,8,1024]{3,2,1,0:T(8,128)(2,1)S(1)}, u32[]{:S(2)}, u32[]{:S(2)}) collective-permute-start(bf16[4,1,8,1024]{3,2,1,0:T(8,128)(2,1)} %get-tuple-element.79), channel_id=1, source_target_pairs={{4,0},{8,4},{12,8},{5,1},{9,5},{13,9},{6,2},{10,6},{14,10},{7,3},{... | collective-permute-start | bytes 196616 | tf_op jit(solution)/shard_map/ppermute | solution.py:17
  136.3 10.1 %collective-permute-start.28 = (bf16[4,1,8,1024]{3,2,1,0:T(8,128)(2,1)}, bf16[4,1,8,1024]{3,2,1,0:T(8,128)(2,1)S(1)}, u32[]{:S(2)}, u32[]{:S(2)}) collective-permute-start(bf16[4,1,8,1024]{3,2,1,0:T(8,128)(2,1)} %get-tuple-element.78), channel_id=1, source_target_pairs={{0,4},{4,8},{8,12},{1,5},{5,9},{9,13},{2,6},{6,10},{10,14},{3,7},{... | collective-permute-start | bytes 196616 | tf_op jit(solution)/shard_map/ppermute | solution.py:16
  139.6 8.3 %collective-permute-start.41 = (bf16[4,1,8,1024]{3,2,1,0:T(8,128)(2,1)}, bf16[4,1,8,1024]{3,2,1,0:T(8,128)(2,1)S(1)}, u32[]{:S(2)}, u32[]{:S(2)}) collective-permute-start(bf16[4,1,8,1024]{3,2,1,0:T(8,128)(2,1)} %get-tuple-element.77), channel_id=1, source_target_pairs={{4,0},{8,4},{12,8},{5,1},{9,5},{13,9},{6,2},{10,6},{14,10},{7,3},{... | collective-permute-start | bytes 196616 | tf_op jit(solution)/shard_map/ppermute | solution.py:17
  142.7 9.2 %collective-permute-start.40 = (bf16[4,1,8,1024]{3,2,1,0:T(8,128)(2,1)}, bf16[4,1,8,1024]{3,2,1,0:T(8,128)(2,1)S(1)}, u32[]{:S(2)}, u32[]{:S(2)}) collective-permute-start(bf16[4,1,8,1024]{3,2,1,0:T(8,128)(2,1)} %get-tuple-element.76), channel_id=1, source_target_pairs={{0,4},{4,8},{8,12},{1,5},{5,9},{9,13},{2,6},{6,10},{10,14},{3,7},{... | collective-permute-start | bytes 196616 | tf_op jit(solution)/shard_map/ppermute | solution.py:16
  146.3 13.6 %collective-permute-start.7 = (bf16[4,10,1,1024]{3,2,1,0:T(2,128)(2,1)S(1)}, bf16[4,10,1,1024]{3,2,1,0:T(2,128)(2,1)S(1)}, u32[]{:S(2)}, u32[]{:S(2)}) collective-permute-start(bf16[4,10,1,1024]{3,2,1,0:T(2,128)(2,1)S(1)} %get-tuple-element.75), channel_id=1, source_target_pairs={{1,0},{2,1},{3,2},{5,4},{6,5},{7,6},{9,8},{10,9},{11,10},{13,12},{... | collective-permute-start | bytes 245768 | tf_op jit(solution)/shard_map/ppermute | solution.py:17
  147.9 16.1 %collective-permute-start.6 = (bf16[4,10,1,1024]{3,2,1,0:T(2,128)(2,1)S(1)}, bf16[4,10,1,1024]{3,2,1,0:T(2,128)(2,1)S(1)}, u32[]{:S(2)}, u32[]{:S(2)}) collective-permute-start(bf16[4,10,1,1024]{3,2,1,0:T(2,128)(2,1)S(1)} %get-tuple-element.74), channel_id=1, source_target_pairs={{0,1},{1,2},{2,3},{4,5},{5,6},{6,7},{8,9},{9,10},{10,11},{12,13},{... | collective-permute-start | bytes 245768 | tf_op jit(solution)/shard_map/ppermute | solution.py:16
  151.9 24.1 %collective-permute-start.19 = (bf16[4,10,1,1024]{3,2,1,0:T(2,128)(2,1)S(1)}, bf16[4,10,1,1024]{3,2,1,0:T(2,128)(2,1)S(1)}, u32[]{:S(2)}, u32[]{:S(2)}) collective-permute-start(bf16[4,10,1,1024]{3,2,1,0:T(2,128)(2,1)S(1)} %get-tuple-element.73), channel_id=1, source_target_pairs={{1,0},{2,1},{3,2},{5,4},{6,5},{7,6},{9,8},{10,9},{11,10},{13,12},{... | collective-permute-start | bytes 245768 | tf_op jit(solution)/shard_map/ppermute | solution.py:17
  153.4 26.8 %collective-permute-start.18 = (bf16[4,10,1,1024]{3,2,1,0:T(2,128)(2,1)S(1)}, bf16[4,10,1,1024]{3,2,1,0:T(2,128)(2,1)S(1)}, u32[]{:S(2)}, u32[]{:S(2)}) collective-permute-start(bf16[4,10,1,1024]{3,2,1,0:T(2,128)(2,1)S(1)} %get-tuple-element.72), channel_id=1, source_target_pairs={{0,1},{1,2},{2,3},{4,5},{5,6},{6,7},{8,9},{9,10},{10,11},{12,13},{... | collective-permute-start | bytes 245768 | tf_op jit(solution)/shard_map/ppermute | solution.py:16
  157.4 49.6 %collective-permute-start.31 = (bf16[4,10,1,1024]{3,2,1,0:T(2,128)(2,1)S(1)}, bf16[4,10,1,1024]{3,2,1,0:T(2,128)(2,1)S(1)}, u32[]{:S(2)}, u32[]{:S(2)}) collective-permute-start(bf16[4,10,1,1024]{3,2,1,0:T(2,128)(2,1)S(1)} %get-tuple-element.71), channel_id=1, source_target_pairs={{1,0},{2,1},{3,2},{5,4},{6,5},{7,6},{9,8},{10,9},{11,10},{13,12},{... | collective-permute-start | bytes 245768 | tf_op jit(solution)/shard_map/ppermute | solution.py:17
  159.9 8.3 %collective-permute-start.3 = (f32[4,10,1,1024]{3,2,1,0:T(1,128)S(1)}, f32[4,10,1,1024]{3,2,1,0:T(1,128)S(1)}, u32[]{:S(2)}, u32[]{:S(2)}) collective-permute-start(f32[4,10,1,1024]{3,2,1,0:T(1,128)S(1)} %get-tuple-element.47), channel_id=1, source_target_pairs={{0,1},{1,2},{2,3},{4,5},{5,6},{6,7},{8,9},{9,10},{10,11},{12,13},{... | collective-permute-start | bytes 491528 | tf_op jit(solution)/shard_map/ppermute | solution.py:16
  164.0 8.5 %collective-permute-start.2 = (f32[4,10,1,1024]{3,2,1,0:T(1,128)S(1)}, f32[4,10,1,1024]{3,2,1,0:T(1,128)S(1)}, u32[]{:S(2)}, u32[]{:S(2)}) collective-permute-start(f32[4,10,1,1024]{3,2,1,0:T(1,128)S(1)} %get-tuple-element.46), channel_id=1, source_target_pairs={{1,0},{2,1},{3,2},{5,4},{6,5},{7,6},{9,8},{10,9},{11,10},{13,12},{... | collective-permute-start | bytes 491528 | tf_op jit(solution)/shard_map/ppermute | solution.py:17
  168.3 40.1 %collective-permute-start.30 = (bf16[4,10,1,1024]{3,2,1,0:T(2,128)(2,1)S(1)}, bf16[4,10,1,1024]{3,2,1,0:T(2,128)(2,1)S(1)}, u32[]{:S(2)}, u32[]{:S(2)}) collective-permute-start(bf16[4,10,1,1024]{3,2,1,0:T(2,128)(2,1)S(1)} %get-tuple-element.70), channel_id=1, source_target_pairs={{0,1},{1,2},{2,3},{4,5},{5,6},{6,7},{8,9},{9,10},{10,11},{12,13},{... | collective-permute-start | bytes 245768 | tf_op jit(solution)/shard_map/ppermute | solution.py:16
  172.4 53.8 %collective-permute-start.43 = (bf16[4,10,1,1024]{3,2,1,0:T(2,128)(2,1)S(1)}, bf16[4,10,1,1024]{3,2,1,0:T(2,128)(2,1)S(1)}, u32[]{:S(2)}, u32[]{:S(2)}) collective-permute-start(bf16[4,10,1,1024]{3,2,1,0:T(2,128)(2,1)S(1)} %get-tuple-element.69), channel_id=1, source_target_pairs={{1,0},{2,1},{3,2},{5,4},{6,5},{7,6},{9,8},{10,9},{11,10},{13,12},{... | collective-permute-start | bytes 245768 | tf_op jit(solution)/shard_map/ppermute | solution.py:17
  176.0 7.6 %collective-permute-start.9 = (f32[1,8,1024]{2,1,0:T(8,128)S(1)}, f32[1,8,1024]{2,1,0:T(8,128)S(1)}, u32[]{:S(2)}, u32[]{:S(2)}) collective-permute-start(f32[1,8,1024]{2,1,0:T(8,128)S(1)} %get-tuple-element.110), channel_id=1, source_target_pairs={{0,4},{4,8},{8,12},{1,5},{5,9},{9,13},{2,6},{6,10},{10,14},{3,7},{... | collective-permute-start | bytes 98312 | tf_op jit(solution)/shard_map/ppermute | solution.py:16
  180.2 5.2 %collective-permute-start.8 = (f32[1,8,1024]{2,1,0:T(8,128)S(1)}, f32[1,8,1024]{2,1,0:T(8,128)S(1)}, u32[]{:S(2)}, u32[]{:S(2)}) collective-permute-start(f32[1,8,1024]{2,1,0:T(8,128)S(1)} %get-tuple-element.111), channel_id=1, source_target_pairs={{4,0},{8,4},{12,8},{5,1},{9,5},{13,9},{6,2},{10,6},{14,10},{7,3},{... | collective-permute-start | bytes 98312 | tf_op jit(solution)/shard_map/ppermute | solution.py:17
  185.5 6.2 %collective-permute-start.11 = (f32[10,1,1024]{2,1,0:T(1,128)S(1)}, f32[10,1,1024]{2,1,0:T(1,128)S(1)}, u32[]{:S(2)}, u32[]{:S(2)}) collective-permute-start(f32[10,1,1024]{2,1,0:T(1,128)S(1)} %get-tuple-element.99), channel_id=1, source_target_pairs={{0,1},{1,2},{2,3},{4,5},{5,6},{6,7},{8,9},{9,10},{10,11},{12,13},{... | collective-permute-start | bytes 122888 | tf_op jit(solution)/shard_map/ppermute | solution.py:16
  189.8 4.7 %collective-permute-start.10 = (f32[10,1,1024]{2,1,0:T(1,128)S(1)}, f32[10,1,1024]{2,1,0:T(1,128)S(1)}, u32[]{:S(2)}, u32[]{:S(2)}) collective-permute-start(f32[10,1,1024]{2,1,0:T(1,128)S(1)} %get-tuple-element.98), channel_id=1, source_target_pairs={{1,0},{2,1},{3,2},{5,4},{6,5},{7,6},{9,8},{10,9},{11,10},{13,12},{... | collective-permute-start | bytes 122888 | tf_op jit(solution)/shard_map/ppermute | solution.py:17
  195.2 5.9 %collective-permute-start.13 = (f32[4,1,8,1024]{3,2,1,0:T(8,128)S(1)}, f32[4,1,8,1024]{3,2,1,0:T(8,128)S(1)}, u32[]{:S(2)}, u32[]{:S(2)}) collective-permute-start(f32[4,1,8,1024]{3,2,1,0:T(8,128)S(1)} %get-tuple-element.61), channel_id=1, source_target_pairs={{0,4},{4,8},{8,12},{1,5},{5,9},{9,13},{2,6},{6,10},{10,14},{3,7},{... | collective-permute-start | bytes 393224 | tf_op jit(solution)/shard_map/ppermute | solution.py:16
  198.6 6.3 %collective-permute-start.12 = (f32[4,1,8,1024]{3,2,1,0:T(8,128)S(1)}, f32[4,1,8,1024]{3,2,1,0:T(8,128)S(1)}, u32[]{:S(2)}, u32[]{:S(2)}) collective-permute-start(f32[4,1,8,1024]{3,2,1,0:T(8,128)S(1)} %get-tuple-element.62), channel_id=1, source_target_pairs={{4,0},{8,4},{12,8},{5,1},{9,5},{13,9},{6,2},{10,6},{14,10},{7,3},{... | collective-permute-start | bytes 393224 | tf_op jit(solution)/shard_map/ppermute | solution.py:17
  201.1 25.1 %collective-permute-start.42 = (bf16[4,10,1,1024]{3,2,1,0:T(2,128)(2,1)S(1)}, bf16[4,10,1,1024]{3,2,1,0:T(2,128)(2,1)S(1)}, u32[]{:S(2)}, u32[]{:S(2)}) collective-permute-start(bf16[4,10,1,1024]{3,2,1,0:T(2,128)(2,1)S(1)} %get-tuple-element.68), channel_id=1, source_target_pairs={{0,1},{1,2},{2,3},{4,5},{5,6},{6,7},{8,9},{9,10},{10,11},{12,13},{... | collective-permute-start | bytes 245768 | tf_op jit(solution)/shard_map/ppermute | solution.py:16
  205.1 4.4 %collective-permute-start.15 = (f32[4,10,1,1024]{3,2,1,0:T(1,128)S(1)}, f32[4,10,1,1024]{3,2,1,0:T(1,128)S(1)}, u32[]{:S(2)}, u32[]{:S(2)}) collective-permute-start(f32[4,10,1,1024]{3,2,1,0:T(1,128)S(1)} %get-tuple-element.43), channel_id=1, source_target_pairs={{0,1},{1,2},{2,3},{4,5},{5,6},{6,7},{8,9},{9,10},{10,11},{12,13},{... | collective-permute-start | bytes 491528 | tf_op jit(solution)/shard_map/ppermute | solution.py:16
  207.0 6.1 %collective-permute-start.14 = (f32[4,10,1,1024]{3,2,1,0:T(1,128)S(1)}, f32[4,10,1,1024]{3,2,1,0:T(1,128)S(1)}, u32[]{:S(2)}, u32[]{:S(2)}) collective-permute-start(f32[4,10,1,1024]{3,2,1,0:T(1,128)S(1)} %get-tuple-element.42), channel_id=1, source_target_pairs={{1,0},{2,1},{3,2},{5,4},{6,5},{7,6},{9,8},{10,9},{11,10},{13,12},{... | collective-permute-start | bytes 491528 | tf_op jit(solution)/shard_map/ppermute | solution.py:17
  214.5 6.0 %collective-permute-start.21 = (f32[1,8,1024]{2,1,0:T(8,128)S(1)}, f32[1,8,1024]{2,1,0:T(8,128)S(1)}, u32[]{:S(2)}, u32[]{:S(2)}) collective-permute-start(f32[1,8,1024]{2,1,0:T(8,128)S(1)} %get-tuple-element.107), channel_id=1, source_target_pairs={{0,4},{4,8},{8,12},{1,5},{5,9},{9,13},{2,6},{6,10},{10,14},{3,7},{... | collective-permute-start | bytes 98312 | tf_op jit(solution)/shard_map/ppermute | solution.py:16
  218.0 5.2 %collective-permute-start.20 = (f32[1,8,1024]{2,1,0:T(8,128)S(1)}, f32[1,8,1024]{2,1,0:T(8,128)S(1)}, u32[]{:S(2)}, u32[]{:S(2)}) collective-permute-start(f32[1,8,1024]{2,1,0:T(8,128)S(1)} %get-tuple-element.108), channel_id=1, source_target_pairs={{4,0},{8,4},{12,8},{5,1},{9,5},{13,9},{6,2},{10,6},{14,10},{7,3},{... | collective-permute-start | bytes 98312 | tf_op jit(solution)/shard_map/ppermute | solution.py:17
  223.2 3.7 %collective-permute-start.23 = (f32[10,1,1024]{2,1,0:T(1,128)S(1)}, f32[10,1,1024]{2,1,0:T(1,128)S(1)}, u32[]{:S(2)}, u32[]{:S(2)}) collective-permute-start(f32[10,1,1024]{2,1,0:T(1,128)S(1)} %get-tuple-element.95), channel_id=1, source_target_pairs={{0,1},{1,2},{2,3},{4,5},{5,6},{6,7},{8,9},{9,10},{10,11},{12,13},{... | collective-permute-start | bytes 122888 | tf_op jit(solution)/shard_map/ppermute | solution.py:16
  224.9 4.7 %collective-permute-start.22 = (f32[10,1,1024]{2,1,0:T(1,128)S(1)}, f32[10,1,1024]{2,1,0:T(1,128)S(1)}, u32[]{:S(2)}, u32[]{:S(2)}) collective-permute-start(f32[10,1,1024]{2,1,0:T(1,128)S(1)} %get-tuple-element.94), channel_id=1, source_target_pairs={{1,0},{2,1},{3,2},{5,4},{6,5},{7,6},{9,8},{10,9},{11,10},{13,12},{... | collective-permute-start | bytes 122888 | tf_op jit(solution)/shard_map/ppermute | solution.py:17
  230.3 5.8 %collective-permute-start.25 = (f32[4,1,8,1024]{3,2,1,0:T(8,128)S(1)}, f32[4,1,8,1024]{3,2,1,0:T(8,128)S(1)}, u32[]{:S(2)}, u32[]{:S(2)}) collective-permute-start(f32[4,1,8,1024]{3,2,1,0:T(8,128)S(1)} %get-tuple-element.56), channel_id=1, source_target_pairs={{0,4},{4,8},{8,12},{1,5},{5,9},{9,13},{2,6},{6,10},{10,14},{3,7},{... | collective-permute-start | bytes 393224 | tf_op jit(solution)/shard_map/ppermute | solution.py:16
  233.7 6.3 %collective-permute-start.24 = (f32[4,1,8,1024]{3,2,1,0:T(8,128)S(1)}, f32[4,1,8,1024]{3,2,1,0:T(8,128)S(1)}, u32[]{:S(2)}, u32[]{:S(2)}) collective-permute-start(f32[4,1,8,1024]{3,2,1,0:T(8,128)S(1)} %get-tuple-element.57), channel_id=1, source_target_pairs={{4,0},{8,4},{12,8},{5,1},{9,5},{13,9},{6,2},{10,6},{14,10},{7,3},{... | collective-permute-start | bytes 393224 | tf_op jit(solution)/shard_map/ppermute | solution.py:17
  240.2 4.4 %collective-permute-start.27 = (f32[4,10,1,1024]{3,2,1,0:T(1,128)S(1)}, f32[4,10,1,1024]{3,2,1,0:T(1,128)S(1)}, u32[]{:S(2)}, u32[]{:S(2)}) collective-permute-start(f32[4,10,1,1024]{3,2,1,0:T(1,128)S(1)} %get-tuple-element.39), channel_id=1, source_target_pairs={{0,1},{1,2},{2,3},{4,5},{5,6},{6,7},{8,9},{9,10},{10,11},{12,13},{... | collective-permute-start | bytes 491528 | tf_op jit(solution)/shard_map/ppermute | solution.py:16
  241.8 6.1 %collective-permute-start.26 = (f32[4,10,1,1024]{3,2,1,0:T(1,128)S(1)}, f32[4,10,1,1024]{3,2,1,0:T(1,128)S(1)}, u32[]{:S(2)}, u32[]{:S(2)}) collective-permute-start(f32[4,10,1,1024]{3,2,1,0:T(1,128)S(1)} %get-tuple-element.38), channel_id=1, source_target_pairs={{1,0},{2,1},{3,2},{5,4},{6,5},{7,6},{9,8},{10,9},{11,10},{13,12},{... | collective-permute-start | bytes 491528 | tf_op jit(solution)/shard_map/ppermute | solution.py:17
  249.4 5.5 %collective-permute-start.33 = (f32[1,8,1024]{2,1,0:T(8,128)S(1)}, f32[1,8,1024]{2,1,0:T(8,128)S(1)}, u32[]{:S(2)}, u32[]{:S(2)}) collective-permute-start(f32[1,8,1024]{2,1,0:T(8,128)S(1)} %get-tuple-element.104), channel_id=1, source_target_pairs={{0,4},{4,8},{8,12},{1,5},{5,9},{9,13},{2,6},{6,10},{10,14},{3,7},{... | collective-permute-start | bytes 98312 | tf_op jit(solution)/shard_map/ppermute | solution.py:16
  252.6 5.2 %collective-permute-start.32 = (f32[1,8,1024]{2,1,0:T(8,128)S(1)}, f32[1,8,1024]{2,1,0:T(8,128)S(1)}, u32[]{:S(2)}, u32[]{:S(2)}) collective-permute-start(f32[1,8,1024]{2,1,0:T(8,128)S(1)} %get-tuple-element.105), channel_id=1, source_target_pairs={{4,0},{8,4},{12,8},{5,1},{9,5},{13,9},{6,2},{10,6},{14,10},{7,3},{... | collective-permute-start | bytes 98312 | tf_op jit(solution)/shard_map/ppermute | solution.py:17
  259.5 4.7 %collective-permute-start.34 = (f32[10,1,1024]{2,1,0:T(1,128)S(1)}, f32[10,1,1024]{2,1,0:T(1,128)S(1)}, u32[]{:S(2)}, u32[]{:S(2)}) collective-permute-start(f32[10,1,1024]{2,1,0:T(1,128)S(1)} %get-tuple-element.90), channel_id=1, source_target_pairs={{1,0},{2,1},{3,2},{5,4},{6,5},{7,6},{9,8},{10,9},{11,10},{13,12},{... | collective-permute-start | bytes 122888 | tf_op jit(solution)/shard_map/ppermute | solution.py:17
  265.0 5.6 %collective-permute-start.37 = (f32[4,1,8,1024]{3,2,1,0:T(8,128)S(1)}, f32[4,1,8,1024]{3,2,1,0:T(8,128)S(1)}, u32[]{:S(2)}, u32[]{:S(2)}) collective-permute-start(f32[4,1,8,1024]{3,2,1,0:T(8,128)S(1)} %get-tuple-element.51), channel_id=1, source_target_pairs={{0,4},{4,8},{8,12},{1,5},{5,9},{9,13},{2,6},{6,10},{10,14},{3,7},{... | collective-permute-start | bytes 393224 | tf_op jit(solution)/shard_map/ppermute | solution.py:16
  268.4 6.3 %collective-permute-start.36 = (f32[4,1,8,1024]{3,2,1,0:T(8,128)S(1)}, f32[4,1,8,1024]{3,2,1,0:T(8,128)S(1)}, u32[]{:S(2)}, u32[]{:S(2)}) collective-permute-start(f32[4,1,8,1024]{3,2,1,0:T(8,128)S(1)} %get-tuple-element.52), channel_id=1, source_target_pairs={{4,0},{8,4},{12,8},{5,1},{9,5},{13,9},{6,2},{10,6},{14,10},{7,3},{... | collective-permute-start | bytes 393224 | tf_op jit(solution)/shard_map/ppermute | solution.py:17
  274.9 3.9 %collective-permute-start.39 = (f32[4,10,1,1024]{3,2,1,0:T(1,128)S(1)}, f32[4,10,1,1024]{3,2,1,0:T(1,128)S(1)}, u32[]{:S(2)}, u32[]{:S(2)}) collective-permute-start(f32[4,10,1,1024]{3,2,1,0:T(1,128)S(1)} %get-tuple-element.35), channel_id=1, source_target_pairs={{0,1},{1,2},{2,3},{4,5},{5,6},{6,7},{8,9},{9,10},{10,11},{12,13},{... | collective-permute-start | bytes 491528 | tf_op jit(solution)/shard_map/ppermute | solution.py:16
  276.5 6.1 %collective-permute-start.38 = (f32[4,10,1,1024]{3,2,1,0:T(1,128)S(1)}, f32[4,10,1,1024]{3,2,1,0:T(1,128)S(1)}, u32[]{:S(2)}, u32[]{:S(2)}) collective-permute-start(f32[4,10,1,1024]{3,2,1,0:T(1,128)S(1)} %get-tuple-element.34), channel_id=1, source_target_pairs={{1,0},{2,1},{3,2},{5,4},{6,5},{7,6},{9,8},{10,9},{11,10},{13,12},{... | collective-permute-start | bytes 491528 | tf_op jit(solution)/shard_map/ppermute | solution.py:17
  284.0 5.5 %collective-permute-start.45 = (f32[1,8,1024]{2,1,0:T(8,128)S(1)}, f32[1,8,1024]{2,1,0:T(8,128)S(1)}, u32[]{:S(2)}, u32[]{:S(2)}) collective-permute-start(f32[1,8,1024]{2,1,0:T(8,128)S(1)} %get-tuple-element.101), channel_id=1, source_target_pairs={{0,4},{4,8},{8,12},{1,5},{5,9},{9,13},{2,6},{6,10},{10,14},{3,7},{... | collective-permute-start | bytes 98312 | tf_op jit(solution)/shard_map/ppermute | solution.py:16
  287.3 5.2 %collective-permute-start.44 = (f32[1,8,1024]{2,1,0:T(8,128)S(1)}, f32[1,8,1024]{2,1,0:T(8,128)S(1)}, u32[]{:S(2)}, u32[]{:S(2)}) collective-permute-start(f32[1,8,1024]{2,1,0:T(8,128)S(1)} %get-tuple-element.102), channel_id=1, source_target_pairs={{4,0},{8,4},{12,8},{5,1},{9,5},{13,9},{6,2},{10,6},{14,10},{7,3},{... | collective-permute-start | bytes 98312 | tf_op jit(solution)/shard_map/ppermute | solution.py:17
  292.5 3.1 collective-permute-start.47
  294.2 4.7 %collective-permute-start.46 = (f32[10,1,1024]{2,1,0:T(1,128)S(1)}, f32[10,1,1024]{2,1,0:T(1,128)S(1)}, u32[]{:S(2)}, u32[]{:S(2)}) collective-permute-start(f32[10,1,1024]{2,1,0:T(1,128)S(1)} %get-tuple-element.86), channel_id=1, source_target_pairs={{1,0},{2,1},{3,2},{5,4},{6,5},{7,6},{9,8},{10,9},{11,10},{13,12},{... | collective-permute-start | bytes 122888 | tf_op jit(solution)/shard_map/ppermute | solution.py:17
  (9 other events, 95.9 us)
Sparse Core Ops, SparseCore 0:
  301.7 18.1 reduce-scatter.1
where the time goes:
time: 330 us; the launch traced here: 327 us
  starting transfers between devices  115 us (35%)
  waiting for transfers between devices  61.7 us (19%)
  blocking collectives  61.3 us (19%)
  other arithmetic  39.5 us (12%)
  local copies, waits for them, and re-layouts  33.9 us (10%)
  between operations  15.8 us (5%)
    ppermute x24, starting transfers between devices, extended(): before = lax.ppermute(last, axis, up)  75.2 us
    psum x1, blocking collectives, shards(): samples = lax.psum(local_samples, ('gx', 'gy'))  61.3 us
    ppermute x24, waiting for transfers between devices, extended(): after = lax.ppermute(initial, axis, down)  43.2 us
    ppermute x24, starting transfers between devices, extended(): after = lax.ppermute(initial, axis, down)  39.3 us
    reduce_scatter x1, waiting for transfers between devices, shards(): lax.psum_scatter(kernel_local, 'pair', scatter_dimension=3, tiled=True)  17.2 us
    slice x2, local copies, waits for them, and re-layouts, shards(): pressure_snaps = forward_field[:, 0].reshape(steps_total, -1)  14.9 us
    scatter-add x4, other arithmetic, shards(): injected = jnp.zeros((width_x * width_y * depth,), jnp.float32).at[rcv_fl...  9.22 us
    gather x1, local copies, waits for them, and re-layouts, shards(): jnp.take(pressure_snaps, src_flat, axis=1).astype(jnp.float32)  8.65 us
  transfers between devices with their start and end apart: 49, of which 17 were waited for; matrix products, arithmetic and copies ran while one was open for 19% of the time, Pallas kernels for 0%

commit v1 on v0

v1 whole, which is shorter than its diff:
```python
import jax
import jax.numpy as jnp
from jax import lax
from jax.experimental import pallas as pl
from jax.experimental.pallas import tpu as pltpu
from jax.sharding import PartitionSpec as P

step_length = 0.25
SCALE = 0.5 * step_length
HALO = 4
PER_ROUND = 2
LANES = 128
ROWS = 8
VMEM = pltpu.VMEM
CORNER = [(i, j) for i in range(1, HALO) for j in range(1, HALO) if i + j <= HALO]
BF = jnp.bfloat16
F32 = jnp.float32


def swap_pairs(size, odd):
    partner = [((i - odd) ^ 1) + odd for i in range(size)]
    return [(i, j if 0 <= j < size else i) for i, j in enumerate(partner)]


def swapped(x, axis, odd):
    return lax.ppermute(x, axis, swap_pairs(lax.axis_size(axis), odd))


def diagonal(x, odd_x, odd_y):
    size_x, size_y = lax.axis_size("gx"), lax.axis_size("gy")
    pairs = [
        (i * size_y + j, k * size_y + m)
        for i, k in swap_pairs(size_x, odd_x)
        for j, m in swap_pairs(size_y, odd_y)
    ]
    return lax.ppermute(x, ("gx", "gy"), pairs)


def summed(x):
    for axis in ("gx", "gy"):
        size = lax.axis_size(axis)
        terms = [x]
        for k in range(1, size):
            terms.append(lax.ppermute(x, axis, [(i, (i + k) % size) for i in range(size)]))
        x = sum(terms)
    return x


def call(kernel, outs, scratch=(), cost=10_000_000, specs=None, grid=()):
    def run(*args):
        return pl.pallas_call(
            kernel,
            out_shape=outs,
            grid=grid,
            in_specs=specs or [pl.BlockSpec(memory_space=VMEM)] * len(args),
            out_specs=jax.tree.map(lambda _: pl.BlockSpec(memory_space=VMEM), outs),
            scratch_shapes=list(scratch),
            compiler_params=pltpu.CompilerParams(vmem_limit_bytes=48 * 2**20),
            cost_estimate=pl.CostEstimate(flops=cost, bytes_accessed=1_000_000, transcendentals=0),
        )(*args)

    return run


def struct(shape, dtype):
    return jax.ShapeDtypeStruct(shape, dtype)


class Place:
    def __init__(self):
        self.index = {}
        self.size = {}
        for axis in ("gx", "gy"):
            self.index[axis] = lax.axis_index(axis)
            self.size[axis] = lax.axis_size(axis)

    def plus(self, axis, odd):
        return lax.rem(self.index[axis], 2) == odd

    def has(self, axis, odd):
        i = self.index[axis]
        if not odd:
            return None
        return jnp.logical_and(i > 0, i < self.size[axis] - 1)


def column_rows(y, n):
    start = y * ROWS
    if not isinstance(start, int):
        start = pl.multiple_of(start, ROWS)
    return pl.ds(start, n * ROWS)


def pack_edges(place, load, fields, width_x, width_y, z_out, x_out, c_out):
    for odd in (0, 1):
        y0 = jnp.where(place.plus("gy", odd), width_y - HALO, 0)
        x0 = jnp.where(place.plus("gx", odd), width_x - HALO, 0)
        for f in range(fields):
            for x in range(width_x):
                z_out[odd][f, x] = load(f, x, y0, HALO).astype(BF)
            for j in range(HALO):
                x_out[odd][f, j] = load(f, x0 + j, 0, width_y).astype(BF)
    for odd_x in (0, 1):
        plus_x = place.plus("gx", odd_x)
        for odd_y in (0, 1):
            plus_y = place.plus("gy", odd_y)
            out = c_out[2 * odd_x + odd_y]
            for f in range(fields):
                for k in range(0, len(CORNER), 2):
                    two = []
                    for i, j in CORNER[k : k + 2]:
                        x = jnp.where(plus_x, width_x - i, i - 1)
                        y = jnp.where(plus_y, width_y - j, j - 1)
                        two.append(load(f, x, y, 1))
                    out[f, k * ROWS : (k + 2) * ROWS] = jnp.concatenate(two, axis=0).astype(BF)


def place_edges(place, store, fields, width_x, width_y, z_in, x_in, c_in):
    def masked(value, *conditions):
        value = value.astype(F32)
        for condition in conditions:
            if condition is not None:
                value = jnp.where(condition, value, 0.0)
        return value

    for odd in (0, 1):
        y0 = jnp.where(place.plus("gy", odd), width_y + HALO, 0)
        x0 = jnp.where(place.plus("gx", odd), width_x + HALO, 0)
        for f in range(fields):
            for x in range(width_x):
                store(f, HALO + x, y0, HALO, masked(z_in[odd][f, x], place.has("gy", odd)))
            for j in range(HALO):
                store(f, x0 + j, HALO, width_y, masked(x_in[odd][f, j], place.has("gx", odd)))
    for odd_x in (0, 1):
        plus_x = place.plus("gx", odd_x)
        for odd_y in (0, 1):
            plus_y = place.plus("gy", odd_y)
            got = c_in[2 * odd_x + odd_y]
            for f in range(fields):
                for k in range(0, len(CORNER), 2):
                    two = masked(
                        got[f, k * ROWS : (k + 2) * ROWS],
                        place.has("gx", odd_x),
                        place.has("gy", odd_y),
                    )
                    for n, (i, j) in enumerate(CORNER[k : k + 2]):
                        x = jnp.where(plus_x, HALO + width_x - 1 + i, HALO - i)
                        y = jnp.where(plus_y, HALO + width_y - 1 + j, HALO - j)
                        store(f, x, y, 1, two[n * ROWS : (n + 1) * ROWS])


class Altitude:
    def __init__(self):
        lane = lax.broadcasted_iota(jnp.int32, (ROWS, LANES), 1)
        row = lax.broadcasted_iota(jnp.int32, (ROWS, LANES), 0)
        self.last_lane = lane == LANES - 1
        self.first_lane = lane == 0
        self.last_row = row == ROWS - 1
        self.first_row = row == 0

    def __call__(self, v):
        up = pltpu.roll(v, LANES - 1, 1)
        carried = jnp.where(self.last_row, 0.0, pltpu.roll(up, ROWS - 1, 0))
        up = jnp.where(self.last_lane, carried, up)
        down = pltpu.roll(v, 1, 1)
        carried = jnp.where(self.first_row, 0.0, pltpu.roll(down, 1, 0))
        down = jnp.where(self.first_lane, carried, down)
        return up - down


def over_diamond(radius, width_x, width_y, row):
    if radius >= 0:

        def own(i, carry):
            row(HALO + i, HALO - radius, width_y + 2 * radius)
            return carry

        lax.fori_loop(0, width_x, own, 0)
    for d in range(1, radius + 1):
        rest = radius - d
        row(HALO - d, HALO - rest, width_y + 2 * rest)
        row(HALO + width_x - 1 + d, HALO - rest, width_y + 2 * rest)


def advance(place, altitude, old, new, speed, wind, inject, carry_dz, radius, width_x, width_y):
    east, north, vertical = wind

    def at(ref, x, y):
        return ref[x, column_rows(y, 1), :]

    def clear(fields, reach):
        length = width_y + 2 * reach
        sides = (("gx", 0, 0), ("gx", 1, 1), ("gy", 0, 0), ("gy", 1, 1))
        for axis, high, _ in sides:
            edge = place.index[axis] == (place.size[axis] - 1 if high else 0)

            @pl.when(edge)
            def _():
                for f in fields:
                    if axis == "gx":
                        for d in range(1, reach + 1):
                            x = HALO + width_x - 1 + d if high else HALO - d
                            new[f, x, column_rows(HALO - reach, length), :] = jnp.zeros(
                                (length * ROWS, LANES), F32
                            )
                    else:
                        y = HALO + width_y if high else HALO - reach
                        for x in range(HALO - reach, HALO + width_x + reach):
                            new[f, x, column_rows(y, reach), :] = jnp.zeros(
                                (reach * ROWS, LANES), F32
                            )

    p, ax, ay, az = (old.at[f] for f in range(4))

    def p_row(x, y0, n):
        ps = [at(p, x, y0 + k - 1) for k in range(n + 2)]
        ays = [at(ay, x, y0 + k - 1) for k in range(n + 2)]
        for k in range(n):
            y = y0 + k
            up = altitude(at(az, x, y))
            carry_dz[x, column_rows(y, 1), :] = up
            div = (at(ax, x + 1, y) - at(ax, x - 1, y)) + (ays[k + 2] - ays[k]) + up
            value = (
                at(speed, x, y) * div
                + east * (at(p, x + 1, y) - at(p, x - 1, y))
                + north * (ps[k + 2] - ps[k])
                + vertical * altitude(ps[k + 1])
            )
            new[0, x, column_rows(y, 1), :] = ps[k + 1] + value + inject(x, y)

    over_diamond(radius, width_x, width_y, p_row)
    if radius:
        clear((0,), radius)
    pn = new.at[0]

    def a_row(x, y0, n):
        ps = [at(pn, x, y0 + k - 1) for k in range(n + 2)]
        for f, a in ((1, ax), (2, ay), (3, az)):
            vs = [at(a, x, y0 + k - 1) for k in range(n + 2)]
            for k in range(n):
                y = y0 + k
                if f == 1:
                    grad = at(pn, x + 1, y) - at(pn, x - 1, y)
                elif f == 2:
                    grad = ps[k + 2] - ps[k]
                else:
                    grad = altitude(ps[k + 1])
                up = carry_dz[x, column_rows(y, 1), :] if f == 3 else altitude(vs[k + 1])
                value = (
                    SCALE * grad
                    + east * (at(a, x + 1, y) - at(a, x - 1, y))
                    + north * (vs[k + 2] - vs[k])
                    + vertical * up
                )
                new[f, x, column_rows(y, 1), :] = vs[k + 1] + value

    over_diamond(radius - 1, width_x, width_y, a_row)
    if radius > 1:
        clear((1, 2, 3), radius - 1)


def add_increment(altitude, state, forward, total, width_x, width_y):
    wide = width_y + 2

    def column(f, x, y):
        start = (x * wide + y) * ROWS
        return forward[f, pl.ds(pl.multiple_of(start, ROWS), ROWS), :]

    def row(i, carry):
        for k in range(width_y):
            p, ax, ay, az = (state(f, i, k) for f in range(4))
            dx = [column(f, i + 2, k + 1) - column(f, i, k + 1) for f in range(4)]
            dy = [column(f, i + 1, k + 2) - column(f, i + 1, k) for f in range(4)]
            dz = [altitude(column(f, i + 1, k + 1)) for f in range(4)]
            rows = column_rows(k, 1)
            total[0, i, rows, :] += p * (dx[1] + dy[2] + dz[3])
            for n, d in ((1, dx), (2, dy), (3, dz)):
                total[n, i, rows, :] += p * d[0] + ax * d[1] + ay * d[2] + az * d[3]
        return carry

    lax.fori_loop(0, width_x, row, 0)


def halo_structs(fields, width_x, width_y):
    faces_z = [struct((fields, width_x, HALO * ROWS, LANES), BF)] * 2
    faces_x = [struct((fields, HALO, width_y * ROWS, LANES), BF)] * 2
    corners = [struct((fields, len(CORNER) * ROWS, LANES), BF)] * 4
    return faces_z + faces_x + corners


def exchanged(edges):
    z, x, c = edges[:2], edges[2:4], edges[4:]
    z = [swapped(z[odd], "gy", odd) for odd in (0, 1)]
    c = [diagonal(c[2 * i + j], i, j) for i in (0, 1) for j in (0, 1)]
    x = [swapped(x[odd], "gx", odd) for odd in (0, 1)]
    return z + x + c


def shards(
    sound_speed_sq,
    wind_profile,
    forward_field,
    adjoint_state,
    pair_counts,
    source_cells,
    receiver_cells,
    residuals,
):
    steps_total = forward_field.shape[0]
    width_x, width_y, depth = sound_speed_sq.shape
    slots = residuals.shape[0]
    ext_x, ext_y = width_x + 2 * HALO, width_y + 2 * HALO
    blocks = depth // LANES
    assert blocks == ROWS and steps_total == 2 * PER_ROUND
    tile = (width_x, width_y * ROWS, LANES)
    ext = (ext_x, ext_y * ROWS, LANES)

    def pack_kernel(state, speed, cols, speed_cols, *outs):
        place = Place()
        for x in range(width_x):
            for b in range(blocks):
                at = pl.ds(b, width_y, stride=ROWS)
                here = slice(b * LANES, (b + 1) * LANES)
                for f in range(4):
                    cols[f, x, at, :] = state[0, f, x, :, here]
                speed_cols[x, at, :] = speed[x, :, here] * SCALE

        def load(f, x, y, n):
            ref = cols.at[f] if f < 4 else speed_cols
            return ref[x, column_rows(y, n), :]

        pack_edges(place, load, 5, width_x, width_y, outs[:2], outs[2:4], outs[4:])

    packed = call(
        pack_kernel,
        [struct((4,) + tile, F32), struct(tile, F32)] + halo_structs(5, width_x, width_y),
    )(adjoint_state, sound_speed_sq)
    cols, speed_cols, edges = packed[0], packed[1], packed[2:]
    first_halo = exchanged(edges)

    forward_edges = []
    for axis, dim in (("gy", 3), ("gx", 2)):
        for odd in (0, 1):
            plus = lax.rem(lax.axis_index(axis), 2) == odd
            start = jnp.where(plus, forward_field.shape[dim] - 1, 0)
            edge = lax.dynamic_slice_in_dim(forward_field, start, 1, axis=dim)
            forward_edges.append(swapped(jnp.squeeze(edge, dim), axis, odd))

    def sample_kernel(source, pressure, out):
        local_x = source[:, 0:1] - lax.axis_index("gx") * width_x
        local_y = source[:, 1:2] - lax.axis_index("gy") * width_y
        inside = (local_x >= 0) & (local_x < width_x) & (local_y >= 0) & (local_y < width_y)
        where = jnp.where(inside, local_x * width_y + local_y, -1)
        cells = width_x * width_y
        chosen = lax.broadcasted_iota(jnp.int32, (slots, cells), 1) == where
        chosen = jnp.where(chosen, 1.0, 0.0).astype(BF)
        level = lax.broadcasted_iota(jnp.int32, (slots, depth), 1) == source[:, 2:3]
        lane = lax.broadcasted_iota(jnp.int32, (slots, LANES), 1)
        result = jnp.zeros((slots, LANES), F32)
        for t in range(steps_total):
            columns = jnp.dot(
                chosen, pressure[t, 0].reshape(cells, depth), preferred_element_type=F32
            )
            picked = jnp.sum(jnp.where(level, columns, 0.0), axis=1, keepdims=True)
            result = jnp.where(lane == t, picked, result)
        out[...] = result.T[:ROWS]

    samples = call(
        sample_kernel,
        struct((ROWS, slots), F32),
        specs=[
            pl.BlockSpec(memory_space=VMEM),
            pl.BlockSpec((steps_total, 1, width_x, width_y, depth), lambda i: (0, 0, 0, 0, 0)),
        ],
        grid=(1,),
    )(source_cells, forward_field)
    samples = summed(samples)

    def inject_kernel(counts, receiver, receiver_rows, misfit, sample, out):
        local_x = receiver_rows[0:1] - (lax.axis_index("gx") * width_x - HALO)
        local_y = receiver_rows[1:2] - (lax.axis_index("gy") * width_y - HALO)
        inside = (local_x >= 0) & (local_x < ext_x) & (local_y >= 0) & (local_y < ext_y)
        live = lax.broadcasted_iota(jnp.int32, (1, slots), 1) < counts[0]
        where = jnp.where(inside & live, local_x * ext_y + local_y, -1)
        cells = ext_x * ext_y
        chosen = lax.broadcasted_iota(jnp.int32, (cells, slots), 0) == where
        level = lax.broadcasted_iota(jnp.int32, (slots, depth), 1) == receiver[:, 2:3]
        level = jnp.where(level, 1.0, 0.0).astype(BF)
        for t in range(steps_total):
            amplitude = misfit[t : t + 1] * sample[t : t + 1]
            head = amplitude.astype(BF).astype(F32)
            result = jnp.zeros((cells, depth), F32)
            for part in (head, amplitude - head):
                spread = jnp.where(chosen, part, 0.0).astype(BF)
                result += jnp.dot(spread, level, preferred_element_type=F32)
            for g in range(cells // ROWS):
                for b in range(blocks):
                    out[t, pl.ds(g * ROWS * ROWS + b, ROWS, stride=ROWS), :] = result[
                        g * ROWS : (g + 1) * ROWS, b * LANES : (b + 1) * LANES
                    ]

    injected = call(
        inject_kernel,
        struct((steps_total, ext_x * ext_y * ROWS, LANES), F32),
        specs=[pl.BlockSpec(memory_space=pltpu.SMEM)] + [pl.BlockSpec(memory_space=VMEM)] * 4,
    )(pair_counts, receiver_cells, receiver_cells.T, residuals.T, samples)

    wind = wind_profile.reshape(3, ROWS, LANES) * SCALE

    def run_round(place, number, wind, inject, buffers, speed, carry_dz, after):
        altitude = Altitude()
        winds = tuple(wind[i] for i in range(3))
        for s in range(PER_ROUND):
            step = number * PER_ROUND + s
            snap = steps_total - 1 - step
            old, new = buffers[s % 2], buffers[(s + 1) % 2]

            def injected_at(x, y):
                start = (x * ext_y + y) * ROWS
                if not isinstance(start, int):
                    start = pl.multiple_of(start, ROWS)
                return inject[snap, pl.ds(start, ROWS), :]

            radius = 2 * (PER_ROUND - 1 - s) + 1
            advance(
                place, altitude, old, new, speed, winds, injected_at, carry_dz, radius, width_x, width_y
            )
            after(altitude, s, snap, new)

    def own(ref, f, x, y, n):
        return ref[f, HALO + x, column_rows(HALO + y, n), :]

    def fill(place, buffer, speed, cols, speed_cols, halo):
        def store(f, x, y, n, value):
            ref = buffer.at[f] if f < 4 else speed
            ref[x, column_rows(y, n), :] = value

        for f in range(4):
            for x in range(width_x):
                store(f, HALO + x, HALO, width_y, cols[f, x])
        fields = 4
        if speed_cols is not None:
            fields = 5
            for x in range(width_x):
                store(4, HALO + x, HALO, width_y, speed_cols[x])
        place_edges(place, store, fields, width_x, width_y, halo[:2], halo[2:4], halo[4:])

    halos = 8

    def first_kernel(wind, inject, cols, speed_cols, *refs):
        halo, refs = refs[:halos], refs[halos:]
        early, late, speed, edges = refs[0], refs[1], refs[2], refs[3 : 3 + halos]
        here, there, carry_dz = refs[3 + halos :]
        place = Place()
        fill(place, here, speed, cols, speed_cols, halo)

        def after(altitude, s, snap, state):
            out = (early, late)[s]
            for f in range(4):
                for x in range(width_x):
                    out[f, x] = own(state, f, x, 0, width_y)

        run_round(place, 0, wind, inject, (here, there), speed, carry_dz, after)

        def load(f, x, y, n):
            return own(here, f, x, y, n)

        pack_edges(place, load, 4, width_x, width_y, edges[:2], edges[2:4], edges[4:])

    first = call(
        first_kernel,
        [struct((4,) + tile, F32)] * 2 + [struct(ext, F32)] + halo_structs(4, width_x, width_y),
        scratch=[VMEM((4,) + ext, F32)] * 2 + [VMEM(ext, F32)],
    )(wind, injected, cols, speed_cols, *first_halo)
    early, late, speed_ext, edges = first[0], first[1], first[2], first[3:]
    second_halo = exchanged(edges)

    rim = (width_x + 2) * (width_y + 2) * ROWS
    wide = width_y + 2

    def early_kernel(early, late, forward, *refs):
        edges, (total, kept), (columns,) = refs[:4], refs[4:6], refs[6:]
        place = Place()
        altitude = Altitude()

        def spread(snap, target):
            for f in range(4):
                for x in range(width_x):
                    for b in range(blocks):
                        target[f, pl.ds(((x + 1) * wide + 1) * ROWS + b, width_y, stride=ROWS), :] = (
                            forward[snap, f, x, :, b * LANES : (b + 1) * LANES].astype(F32)
                        )
                for odd in (0, 1):
                    y = jnp.where(place.plus("gy", odd), width_y + 1, 0)
                    x = jnp.where(place.plus("gx", odd), width_x + 1, 0)
                    for b in range(blocks):
                        here = slice(b * LANES, (b + 1) * LANES)
                        value = edges[odd][snap, f, :, here].astype(F32)
                        if odd:
                            value = jnp.where(place.has("gy", odd), value, 0.0)
                        target[f, pl.ds((wide + y) * ROWS + b, width_x, stride=wide * ROWS), :] = value
                        value = edges[2 + odd][snap, f, :, here].astype(F32)
                        if odd:
                            value = jnp.where(place.has("gx", odd), value, 0.0)
                        target[f, pl.ds((x * wide + 1) * ROWS + b, width_y, stride=ROWS), :] = value

        total[...] = jnp.zeros_like(total)
        for s, state in ((0, early), (1, late)):
            spread(steps_total - 1 - s, columns)
            add_increment(
                altitude,
                lambda f, x, y: state[f, x, column_rows(y, 1), :],
                columns,
                total,
                width_x,
                width_y,
            )
        for s in range(PER_ROUND):
            spread(steps_total - 1 - PER_ROUND - s, kept.at[s])

    total, kept = call(
        early_kernel,
        [struct((4,) + tile, F32), struct((PER_ROUND, 4, rim, LANES), F32)],
        scratch=[VMEM((4, rim, LANES), F32)],
    )(early, late, forward_field, *forward_edges)

    half = depth // 2

    def second_kernel(wind, inject, cols, speed, total, kept, *refs):
        halo, refs = refs[:halos], refs[halos:]
        final, mine, other = refs[:3]
        here, there, carry_dz, sums = refs[3:]
        place = Place()
        fill(place, here, None, cols, None, halo)
        sums[...] = total[...]

        def after(altitude, s, snap, state):
            add_increment(
                altitude,
                lambda f, x, y: own(state, f, x, y, 1),
                kept.at[s],
                sums,
                width_x,
                width_y,
            )

        run_round(place, 1, wind, inject, (here, there), speed, carry_dz, after)
        me = lax.axis_index("pair")
        for f in range(4):
            for x in range(width_x):
                for b in range(blocks):
                    final[0, f, x, :, b * LANES : (b + 1) * LANES] = here[
                        f, HALO + x, pl.ds(HALO * ROWS + b, width_y, stride=ROWS), :
                    ]
                for b in range(blocks // 2):
                    for ref, part in ((mine, me), (other, 1 - me)):
                        ref[f, x, :, b * LANES : (b + 1) * LANES] = 0.5 * sums[
                            f, x, pl.ds(part * (blocks // 2) + b, width_y, stride=ROWS), :
                        ]

    kernel_half = struct((4, width_x, width_y, half), F32)
    final, mine, other = call(
        second_kernel,
        [struct(adjoint_state.shape, F32), kernel_half, kernel_half],
        scratch=[VMEM((4,) + ext, F32)] * 2 + [VMEM(ext, F32), VMEM((4,) + tile, F32)],
    )(wind, injected, late, speed_ext, total, kept, *second_halo)
    received = lax.ppermute(other, "pair", [(0, 1), (1, 0)])
    return (mine + received, final)


def solution(mesh):
    assert mesh.shape["pair"] == 2 and mesh.shape["gx"] % 2 == 0 and mesh.shape["gy"] % 2 == 0
    in_specs = (
        P("gx", "gy", None),
        P(),
        P(None, None, "gx", "gy", None),
        P("pair", None, "gx", "gy", None),
        P("pair"),
        P("pair", None),
        P("pair", None),
        P("pair", None),
    )
    out_specs = (P(None, "gx", "gy", "pair"), P("pair", None, "gx", "gy", None))
    return jax.shard_map(shards, mesh=mesh, in_specs=in_specs, out_specs=out_specs, check_vma=False)
```

time: 330 us -> 117 us (0.35)
  starting transfers between devices: 115 us -> 40.2 us
  blocking collectives: 61.3 us -> 0 us
  other arithmetic: 39.5 us -> 2.33 us
  waiting for transfers between devices: 61.7 us -> 25 us
  Pallas kernels: 0 us -> 31 us
  local copies, waits for them, and re-layouts: 33.9 us -> 15 us
  between operations: 15.8 us -> 1.54 us
    ppermute x48 -> x27, starting transfers between devices: 115 us -> 40.2 us  [the longest x12 17.8 us: swapped(): return lax.ppermute(x, axis, swap_pairs(lax.axis_size(axis), odd))]
    psum x1 -> x0, blocking collectives: 61.3 us -> none  [shards(): samples = lax.psum(local_samples, ('gx', 'gy'))]
    pallas_call x0 -> x6, Pallas kernels: none -> 31 us  [run(): pl.pallas_call(kernel, out_shape=outs, grid=grid, in_specs=specs or [pl.B...]
    slice x14 -> x0, local copies, waits for them, and re-layouts: 20.1 us -> none  [the longest x2 14.9 us: shards(): pressure_snaps = forward_field[:, 0].reshape(steps_total, -1)]
    ppermute x48 -> x27, waiting for transfers between devices: 44.4 us -> 25 us  [the longest x1 10.4 us: shards(): received = lax.ppermute(other, 'pair', [(0, 1), (1, 0)])]
    reduce_scatter x1 -> x0, waiting for transfers between devices: 17.2 us -> none  [shards(): lax.psum_scatter(kernel_local, 'pair', scatter_dimension=3, tiled=True)]
    unnamed x16 -> x33, local copies, waits for them, and re-layouts: 0.04 us -> 11.8 us
    mul x17 -> x0, other arithmetic: 11.5 us -> none  [the longest x8 5.83 us: central(): east_diff = (padded[..., 2:, 1:-1, :] - padded[..., :-2, 1:-1, :]) * 0.5]
  transfers between devices with their start and end apart: 49 -> 27, of which waited for: 17 -> 7; matrix products, arithmetic and copies ran while one was open for 19% -> 7% of each run, Pallas kernels for 0% -> 15%
where the time goes in v1:
time: 117 us; the launch traced here: 115 us
  starting transfers between devices  40.2 us (34%)
  Pallas kernels  31 us (26%)
  waiting for transfers between devices  25 us (21%)
  local copies, waits for them, and re-layouts  15 us (13%)
  other arithmetic  2.33 us (2%)
  between operations  1.54 us (1%)
    pallas_call x6, Pallas kernels, run(): pl.pallas_call(kernel, out_shape=outs, grid=grid, in_specs=specs or [pl.B...  31 us
    ppermute x12, starting transfers between devices, swapped(): return lax.ppermute(x, axis, swap_pairs(lax.axis_size(axis), odd))  17.8 us
    ppermute x8, starting transfers between devices, diagonal(): return lax.ppermute(x, ('gx', 'gy'), pairs)  12.6 us
    unnamed x33, local copies, waits for them, and re-layouts  11.8 us
    ppermute x1, waiting for transfers between devices, shards(): received = lax.ppermute(other, 'pair', [(0, 1), (1, 0)])  10.4 us
    ppermute x6, starting transfers between devices, summed(): lax.ppermute(x, axis, [(i, (i + k) % size) for i in range(size)])  8.5 us
    ppermute x6, waiting for transfers between devices, summed(): lax.ppermute(x, axis, [(i, (i + k) % size) for i in range(size)])  8.18 us
    ppermute x8, waiting for transfers between devices, diagonal(): return lax.ppermute(x, ('gx', 'gy'), pairs)  6.4 us
  transfers between devices with their start and end apart: 27, of which 7 were waited for; matrix products, arithmetic and copies ran while one was open for 7% of the time, Pallas kernels for 15%

profile of v1, /device:TPU:1, one launch (start us, length us, event | category | flops | bytes accessed | tf_op | source)
XLA Modules:
  0.0 115.0 jit_solution(15396932186783683441)
XLA Ops:
  0.6 0.8 copy.12.source
  1.5 1.6 %copy-done.1 = bf16[4,4,8,8,1024]{4,3,2,1,0:T(8,128)(2,1)S(1)} copy-done((bf16[4,4,8,8,1024]{4,3,2,1,0:T(8,128)(2,1)S(1)}, bf16[4,4,8,8,1024]{4,3,2,1,0:T(8,128)(2,1)}, u32[]{:S(2)}) %copy-start.1) | copy-done | bytes 2097176
  3.1 1.0 shard_map.95
  4.2 2.7 %collective-permute-start.1 = (f32[8,256]{1,0:T(8,128)S(1)}, f32[8,256]{1,0:T(8,128)S(1)}, u32[]{:S(2)}, u32[]{:S(2)}) collective-permute-start(f32[8,256]{1,0:T(8,128)S(1)} %shard_map.95), channel_id=1, source_target_pairs={{0,8},{4,12},{8,0},{12,4},{1,9},{5,13},{9,1},{13,5},{2,10},{6,14},... | collective-permute-start | bytes 24584 | tf_op jit(solution)/shard_map/ppermute | solution.py:44
  6.9 1.3 %collective-permute-start = (f32[8,256]{1,0:T(8,128)S(1)}, f32[8,256]{1,0:T(8,128)S(1)}, u32[]{:S(2)}, u32[]{:S(2)}) collective-permute-start(f32[8,256]{1,0:T(8,128)S(1)} %shard_map.95), channel_id=1, source_target_pairs={{0,4},{4,8},{8,12},{12,0},{1,5},{5,9},{9,13},{13,1},{2,6},{6,10},{... | collective-permute-start | bytes 24584 | tf_op jit(solution)/shard_map/ppermute | solution.py:44
  8.2 1.2 %copy-done.3 = f32[1,4,8,8,1024]{4,3,2,1,0:T(8,128)S(1)} copy-done((f32[1,4,8,8,1024]{4,3,2,1,0:T(8,128)S(1)}, f32[1,4,8,8,1024]{4,3,2,1,0:T(8,128)}, u32[]{:S(2)}) %copy-start.3) | copy-done | bytes 1048600
  9.4 0.9 copy-done.5
  10.4 1.2 %shard_map.97 = (f32[4,8,64,128]{3,2,1,0:T(8,128)S(1)}, f32[8,64,128]{2,1,0:T(8,128)S(1)}, bf16[5,8,32,128]{3,2,1,0:T(8,128)(2,1)}, bf16[5,8,32,128]{3,2,1,0:T(8...) custom-call(f32[1,4,8,8,1024]{4,3,2,1,0:T(8,128)S(1)} %copy-done.3, ...), custom_call_target="tpu_custom_call" | custom-call | flops 10000000 | bytes 1000000 | tf_op jit(solution)/shard_map/pallas_call | solution.py:51
  11.6 1.0 copy-done.4
  12.6 1.3 %collective-permute-start.6 = (bf16[5,8,32,128]{3,2,1,0:T(8,128)(2,1)}, bf16[5,8,32,128]{3,2,1,0:T(8,128)(2,1)S(1)}, u32[]{:S(2)}, u32[]{:S(2)}) collective-permute-start(bf16[5,8,32,128]{3,2,1,0:T(8,128)(2,1)} %get-tuple-element.30), channel_id=1, source_target_pairs={{0,1},{1,0},{2,3},{3,2},{4,5},{5,4},{6,7},{7,6},{8,9},{9,8},{10,11... | collective-permute-start | bytes 983048 | tf_op jit(solution)/shard_map/ppermute | solution.py:26
  13.9 1.6 %collective-permute-start.7 = (bf16[5,8,32,128]{3,2,1,0:T(8,128)(2,1)}, bf16[5,8,32,128]{3,2,1,0:T(8,128)(2,1)S(1)}, u32[]{:S(2)}, u32[]{:S(2)}) collective-permute-start(bf16[5,8,32,128]{3,2,1,0:T(8,128)(2,1)} %get-tuple-element.31), channel_id=1, source_target_pairs={{0,0},{1,2},{2,1},{3,3},{4,4},{5,6},{6,5},{7,7},{8,8},{9,10},{10,9... | collective-permute-start | bytes 983048 | tf_op jit(solution)/shard_map/ppermute | solution.py:26
  15.5 2.2 %collective-permute-start.5 = (f32[8,256]{1,0:T(8,128)S(1)}, f32[8,256]{1,0:T(8,128)S(1)}, u32[]{:S(2)}, u32[]{:S(2)}) collective-permute-start(f32[8,256]{1,0:T(8,128)S(1)} %add_add_fusion.1), channel_id=1, source_target_pairs={{0,3},{1,0},{2,1},{3,2},{4,7},{5,4},{6,5},{7,6},{8,11},{9,8},{10,9... | collective-permute-start | bytes 24584 | tf_op jit(solution)/shard_map/ppermute | solution.py:44
  17.7 1.9 %collective-permute-start.4 = (f32[8,256]{1,0:T(8,128)S(1)}, f32[8,256]{1,0:T(8,128)S(1)}, u32[]{:S(2)}, u32[]{:S(2)}) collective-permute-start(f32[8,256]{1,0:T(8,128)S(1)} %add_add_fusion.1), channel_id=1, source_target_pairs={{0,2},{1,3},{2,0},{3,1},{4,6},{5,7},{6,4},{7,5},{8,10},{9,11},{10,... | collective-permute-start | bytes 24584 | tf_op jit(solution)/shard_map/ppermute | solution.py:44
  19.6 2.4 %collective-permute-done.5 = f32[8,256]{1,0:T(8,128)S(1)} collective-permute-done((f32[8,256]{1,0:T(8,128)S(1)}, f32[8,256]{1,0:T(8,128)S(1)}, u32[]{:S(2)}, u32[]{:S(2)}) %collective-permute-start.5) | collective-permute-done | bytes 8224 | tf_op jit(solution)/shard_map/ppermute | solution.py:44
  22.0 0.4 collective-permute-start.11
  22.4 4.0 %collective-permute-done.4 = f32[8,256]{1,0:T(8,128)S(1)} collective-permute-done((f32[8,256]{1,0:T(8,128)S(1)}, f32[8,256]{1,0:T(8,128)S(1)}, u32[]{:S(2)}, u32[]{:S(2)}) %collective-permute-start.4) | collective-permute-done | bytes 8224 | tf_op jit(solution)/shard_map/ppermute | solution.py:44
  26.7 2.2 %constant_dynamic-slice_fusion = (bf16[4,4,8,1,1024]{4,3,2,1,0:T(2,128)(2,1)}, bf16[4,4,8,1,1024]{4,3,2,1,0:T(2,128)(2,1)}) fusion(bf16[4,4,8,8,1024]{4,3,2,1,0:T(8,128)(2,1)S(1)} %copy-done.2, s32[]{:T(128)S(6)} %select_n.18, s32[]{:T(128)S(6)} %select_n.17), kind=kLoop, calls=%fused_computation.8 | loop fusion | bytes 1048584 | tf_op jit(solution)/shard_map/dynamic_slice | solution.py:346
  28.9 1.8 %collective-permute-done.3 = f32[8,256]{1,0:T(8,128)S(1)} collective-permute-done((f32[8,256]{1,0:T(8,128)S(1)}, f32[8,256]{1,0:T(8,128)S(1)}, u32[]{:S(2)}, u32[]{:S(2)}) %collective-permute-start.3) | collective-permute-done | bytes 8224 | tf_op jit(solution)/shard_map/ppermute | solution.py:44
  30.7 0.6 copy-done.13
  31.3 0.6 collective-permute-start.12
  31.9 3.7 %collective-permute-start.13 = (bf16[5,48,128]{2,1,0:T(8,128)(2,1)}, bf16[5,48,128]{2,1,0:T(8,128)(2,1)S(1)}, u32[]{:S(2)}, u32[]{:S(2)}) collective-permute-start(bf16[5,48,128]{2,1,0:T(8,128)(2,1)} %get-tuple-element.37), channel_id=1, source_target_pairs={{0,0},{1,2},{2,1},{3,3},{4,8},{5,10},{6,9},{7,11},{8,4},{9,6},{10,... | collective-permute-start | bytes 184328 | tf_op jit(solution)/shard_map/ppermute | solution.py:36
  35.7 0.9 dynamic-slice_bitcast_fusion
  36.6 1.8 %copy.23 = bf16[4,4,8,1,1024]{4,2,1,0,3:T(8,128)(2,1)} copy(bf16[4,4,8,1,1024]{4,3,2,1,0:T(2,128)(2,1)} %get-tuple-element.57) | data formatting | bytes 524288
  38.4 2.6 %collective-permute-start.17 = (bf16[4,4,8,1024]{3,2,1,0:T(8,128)(2,1)}, bf16[4,4,8,1024]{3,2,1,0:T(8,128)(2,1)S(1)}, u32[]{:S(2)}, u32[]{:S(2)}) collective-permute-start(bf16[4,4,8,1024]{3,2,1,0:T(8,128)(2,1)} %get-tuple-element.54), channel_id=1, source_target_pairs={{0,0},{4,8},{8,4},{12,12},{1,1},{5,9},{9,5},{13,13},{2,2},{6,10},{... | collective-permute-start | bytes 786440 | tf_op jit(solution)/shard_map/ppermute | solution.py:26
  41.0 0.6 copy-done.6
  41.7 1.6 %collective-permute-start.14 = (bf16[4,4,8,1024]{3,2,1,0:T(8,128)(2,1)}, bf16[4,4,8,1024]{3,2,1,0:T(8,128)(2,1)S(1)}, u32[]{:S(2)}, u32[]{:S(2)}) collective-permute-start(bf16[4,4,8,1024]{3,2,1,0:T(8,128)(2,1)} %bitcast.15), channel_id=1, source_target_pairs={{0,1},{1,0},{2,3},{3,2},{4,5},{5,4},{6,7},{7,6},{8,9},{9,8},{10,11... | collective-permute-start | bytes 786440 | tf_op jit(solution)/shard_map/ppermute | solution.py:26
  43.3 2.9 %collective-permute-start.9 = (bf16[5,4,64,128]{3,2,1,0:T(8,128)(2,1)}, bf16[5,4,64,128]{3,2,1,0:T(8,128)(2,1)S(1)}, u32[]{:S(2)}, u32[]{:S(2)}) collective-permute-start(bf16[5,4,64,128]{3,2,1,0:T(8,128)(2,1)} %copy-done.10), channel_id=1, source_target_pairs={{0,0},{4,8},{8,4},{12,12},{1,1},{5,9},{9,5},{13,13},{2,2},{6,10},{... | collective-permute-start | bytes 983048 | tf_op jit(solution)/shard_map/ppermute | solution.py:26
  46.2 0.7 multiply_bitcast_fusion
  47.7 1.1 copy.22
  48.9 0.7 collective-permute-start.15
  49.6 0.7 add_add_fusion.sample
  50.3 1.6 %shard_map.96.inject = f32[4,2048,128]{2,1,0:T(8,128)S(1)} custom-call(s32[1]{0:T(128)S(6)} %copy.25.counts, s32[256,3]{1,0:T(8,128)S(1)} %copy.13.receiver, s32[3,256]{1,0:T(4,128)S(1)} %bitcast.19, f32[4,256]{1,0:T(4,128)S(1)} %bitcast.20, f32[8,256]{1,0:T(8,128)S(1)} %add_add_fusion.sample), custom_call_target="tpu_custom_call" | custom-call | flops 10000000 | bytes 1000000 | tf_op jit(solution)/shard_map/pallas_call | solution.py:51
  51.9 1.9 %copy-done = f32[4,2048,128]{2,1,0:T(8,128)} copy-done((f32[4,2048,128]{2,1,0:T(8,128)}, f32[4,2048,128]{2,1,0:T(8,128)S(1)}, u32[]{:S(2)}) %copy-start) | copy-done | bytes 4194328
  53.9 8.1 %shard_map.98 = (f32[4,8,64,128]{3,2,1,0:T(8,128)S(1)}, f32[4,8,64,128]{3,2,1,0:T(8,128)S(1)}, f32[16,128,128]{2,1,0:T(8,128)S(1)}, bf16[4,8,32,128]{3,2,1,0:T(8...) custom-call(f32[3,8,128]{2,1,0:T(8,128)S(1)} %bitcast.17, ...), custom_call_target="tpu_custom_call" | custom-call | flops 10000000 | bytes 1000000 | tf_op jit(solution)/shard_map/pallas_call | solution.py:51
  62.0 2.4 %collective-permute-start.18 = (bf16[4,8,32,128]{3,2,1,0:T(8,128)(2,1)S(1)}, bf16[4,8,32,128]{3,2,1,0:T(8,128)(2,1)S(1)}, u32[]{:S(2)}, u32[]{:S(2)}) collective-permute-start(bf16[4,8,32,128]{3,2,1,0:T(8,128)(2,1)S(1)} %get-tuple-element.43), channel_id=1, source_target_pairs={{0,1},{1,0},{2,3},{3,2},{4,5},{5,4},{6,7},{7,6},{8,9},{9,8},{10,11... | collective-permute-start | bytes 786440 | tf_op jit(solution)/shard_map/ppermute | solution.py:26
  64.4 0.7 collective-permute-start.19
  65.0 0.6 collective-permute-start.20
  65.7 3.4 %collective-permute-start.21 = (bf16[4,4,64,128]{3,2,1,0:T(8,128)(2,1)S(1)}, bf16[4,4,64,128]{3,2,1,0:T(8,128)(2,1)S(1)}, u32[]{:S(2)}, u32[]{:S(2)}) collective-permute-start(bf16[4,4,64,128]{3,2,1,0:T(8,128)(2,1)S(1)} %get-tuple-element.46), channel_id=1, source_target_pairs={{0,0},{4,8},{8,4},{12,12},{1,1},{5,9},{9,5},{13,13},{2,2},{6,10},{... | collective-permute-start | bytes 786440 | tf_op jit(solution)/shard_map/ppermute | solution.py:26
  69.2 3.5 %collective-permute-done.22.refs_4_ = bf16[4,48,128]{2,1,0:T(8,128)(2,1)S(1)} collective-permute-done((bf16[4,48,128]{2,1,0:T(8,128)(2,1)S(1)}, bf16[4,48,128]{2,1,0:T(8,128)(2,1)S(1)}, u32[]{:S(2)}, u32[]{:S(2)}) %collective-permute-start.22) | collective-permute-done | bytes 49184 | tf_op jit(solution)/shard_map/ppermute | solution.py:36
  72.8 1.1 collective-permute-done.23.refs_5_
  73.9 4.3 %collective-permute-start.24 = (bf16[4,48,128]{2,1,0:T(8,128)(2,1)S(1)}, bf16[4,48,128]{2,1,0:T(8,128)(2,1)S(1)}, u32[]{:S(2)}, u32[]{:S(2)}) collective-permute-start(bf16[4,48,128]{2,1,0:T(8,128)(2,1)S(1)} %get-tuple-element.49), channel_id=1, source_target_pairs={{0,1},{1,0},{2,3},{3,2},{4,9},{5,8},{6,11},{7,10},{8,5},{9,4},{10,... | collective-permute-start | bytes 147464 | tf_op jit(solution)/shard_map/ppermute | solution.py:36
  78.2 1.8 %collective-permute-done.24.refs_6_ = bf16[4,48,128]{2,1,0:T(8,128)(2,1)S(1)} collective-permute-done((bf16[4,48,128]{2,1,0:T(8,128)(2,1)S(1)}, bf16[4,48,128]{2,1,0:T(8,128)(2,1)S(1)}, u32[]{:S(2)}, u32[]{:S(2)}) %collective-permute-start.24) | collective-permute-done | bytes 49184 | tf_op jit(solution)/shard_map/ppermute | solution.py:36
  80.0 3.4 %collective-permute-start.25 = (bf16[4,48,128]{2,1,0:T(8,128)(2,1)S(1)}, bf16[4,48,128]{2,1,0:T(8,128)(2,1)S(1)}, u32[]{:S(2)}, u32[]{:S(2)}) collective-permute-start(bf16[4,48,128]{2,1,0:T(8,128)(2,1)S(1)} %get-tuple-element.50), channel_id=1, source_target_pairs={{0,0},{1,2},{2,1},{3,3},{4,8},{5,10},{6,9},{7,11},{8,4},{9,6},{10,... | collective-permute-start | bytes 147464 | tf_op jit(solution)/shard_map/ppermute | solution.py:36
  83.5 6.7 %shard_map.99 = (f32[4,8,64,128]{3,2,1,0:T(8,128)S(1)}, f32[2,4,800,128]{3,2,1,0:T(8,128)}) custom-call(f32[4,8,64,128]{3,2,1,0:T(8,128)S(1)} %get-tuple-element.40.early, f32[4,8,64,128]{3,2,1,0:T(8,128)S(1)} %get-tuple-element.38.late.cols, bf16[4,4,8,8,1024]{4,3,2,1,0:T(8,128)(2,1)} %forward.1, ...), custom_call_target="tpu_custom_call" | custom-call | flops 10000000 | bytes 1000000 | tf_op jit(solution)/shard_map/pallas_call | solution.py:51
  90.2 12.3 %shard_map.100 = (f32[1,4,8,8,1024]{4,3,2,1,0:T(8,128)}, f32[4,8,8,512]{3,2,1,0:T(8,128)S(1)}, f32[4,8,8,512]{3,2,1,0:T(8,128)S(1)}) custom-call(f32[3,8,128]{2,1,0:T(8,128)S(1)} %bitcast.18, f32[4,2048,128]{2,1,0:T(8,128)} %copy-done, f32[4,8,64,128]{3,2,1,0:T(8,128)S(1)} %get-tuple-element.38.late.cols, f32[16,128,128]{2,1,0:T(8,128)S(1)} %get-tuple-element.39.speed, ...), custom_call_target="tpu_custom_call" | custom-call | flops 10000000 | bytes 1000000 | tf_op jit(solution)/shard_map/pallas_call | solution.py:51
  102.5 1.2 %collective-permute-start.26 = (f32[4,8,8,512]{3,2,1,0:T(8,128)S(1)}, f32[4,8,8,512]{3,2,1,0:T(8,128)S(1)}, u32[]{:S(2)}, u32[]{:S(2)}) collective-permute-start(f32[4,8,8,512]{3,2,1,0:T(8,128)S(1)} %get-tuple-element.52), channel_id=1, source_target_pairs={{0,16},{16,0},{1,17},{17,1},{2,18},{18,2},{3,19},{19,3},{4,20},{20... | collective-permute-start | bytes 1572872 | tf_op jit(solution)/shard_map/ppermute | solution.py:567
  103.7 10.4 %collective-permute-done.26 = f32[4,8,8,512]{3,2,1,0:T(8,128)S(1)} collective-permute-done((f32[4,8,8,512]{3,2,1,0:T(8,128)S(1)}, f32[4,8,8,512]{3,2,1,0:T(8,128)S(1)}, u32[]{:S(2)}, u32[]{:S(2)}) %collective-permute-start.26) | collective-permute-done | bytes 524320 | tf_op jit(solution)/shard_map/ppermute | solution.py:567
  114.1 0.9 add.31
  (51 shorter events, 0.8 us)
Async XLA Ops:
  1.5 1.6 %copy-start.1 = (bf16[4,4,8,8,1024]{4,3,2,1,0:T(8,128)(2,1)S(1)}, bf16[4,4,8,8,1024]{4,3,2,1,0:T(8,128)(2,1)}, u32[]{:S(2)}) copy-start(bf16[4,4,8,8,1024]{4,3,2,1,0:T(8,128)(2,1)} %forward.1) | copy-start | bytes 6291460
  3.0 23.6 %copy-start.2 = (bf16[4,4,8,8,1024]{4,3,2,1,0:T(8,128)(2,1)S(1)}, bf16[4,4,8,8,1024]{4,3,2,1,0:T(8,128)(2,1)}, u32[]{:S(2)}) copy-start(bf16[4,4,8,8,1024]{4,3,2,1,0:T(8,128)(2,1)} %forward.1) | copy-start | bytes 6291460
  4.1 11.4 %collective-permute-start.2 = (f32[8,256]{1,0:T(8,128)S(1)}, f32[8,256]{1,0:T(8,128)S(1)}, u32[]{:S(2)}, u32[]{:S(2)}) collective-permute-start(f32[8,256]{1,0:T(8,128)S(1)} %shard_map.95), channel_id=1, source_target_pairs={{0,12},{4,0},{8,4},{12,8},{1,13},{5,1},{9,5},{13,9},{2,14},{6,2},{... | collective-permute-start | bytes 24584 | tf_op jit(solution)/shard_map/ppermute | solution.py:44
  4.2 11.3 %collective-permute-start.1 = (f32[8,256]{1,0:T(8,128)S(1)}, f32[8,256]{1,0:T(8,128)S(1)}, u32[]{:S(2)}, u32[]{:S(2)}) collective-permute-start(f32[8,256]{1,0:T(8,128)S(1)} %shard_map.95), channel_id=1, source_target_pairs={{0,8},{4,12},{8,0},{12,4},{1,9},{5,13},{9,1},{13,5},{2,10},{6,14},... | collective-permute-start | bytes 24584 | tf_op jit(solution)/shard_map/ppermute | solution.py:44
  6.9 8.6 %collective-permute-start = (f32[8,256]{1,0:T(8,128)S(1)}, f32[8,256]{1,0:T(8,128)S(1)}, u32[]{:S(2)}, u32[]{:S(2)}) collective-permute-start(f32[8,256]{1,0:T(8,128)S(1)} %shard_map.95), channel_id=1, source_target_pairs={{0,4},{4,8},{8,12},{12,0},{1,5},{5,9},{9,13},{13,1},{2,6},{6,10},{... | collective-permute-start | bytes 24584 | tf_op jit(solution)/shard_map/ppermute | solution.py:44
  8.2 1.2 %copy-start.3 = (f32[1,4,8,8,1024]{4,3,2,1,0:T(8,128)S(1)}, f32[1,4,8,8,1024]{4,3,2,1,0:T(8,128)}, u32[]{:S(2)}) copy-start(f32[1,4,8,8,1024]{4,3,2,1,0:T(8,128)} %state.1) | copy-start | bytes 3145732
  9.4 0.9 copy-start.5
  11.6 1.0 copy-start.4
  12.6 7.1 %copy-start.10 = (bf16[5,4,64,128]{3,2,1,0:T(8,128)(2,1)}, bf16[5,4,64,128]{3,2,1,0:T(8,128)(2,1)S(1)}, u32[]{:S(2)}) copy-start(bf16[5,4,64,128]{3,2,1,0:T(8,128)(2,1)S(1)} %get-tuple-element.33) | copy-start | bytes 983044
  12.6 7.1 %copy-start.11 = (bf16[5,4,64,128]{3,2,1,0:T(8,128)(2,1)}, bf16[5,4,64,128]{3,2,1,0:T(8,128)(2,1)S(1)}, u32[]{:S(2)}) copy-start(bf16[5,4,64,128]{3,2,1,0:T(8,128)(2,1)S(1)} %get-tuple-element.32) | copy-start | bytes 983044
  12.6 35.0 %copy-start.8 = (s32[256,3]{0,1:T(4,128)S(1)}, s32[256,3]{0,1:T(4,128)}, u32[]{:S(2)}) copy-start(s32[256,3]{0,1:T(4,128)} %param.14) | copy-start | bytes 9220
  12.6 29.1 %collective-permute-start.6 = (bf16[5,8,32,128]{3,2,1,0:T(8,128)(2,1)}, bf16[5,8,32,128]{3,2,1,0:T(8,128)(2,1)S(1)}, u32[]{:S(2)}, u32[]{:S(2)}) collective-permute-start(bf16[5,8,32,128]{3,2,1,0:T(8,128)(2,1)} %get-tuple-element.30), channel_id=1, source_target_pairs={{0,1},{1,0},{2,3},{3,2},{4,5},{5,4},{6,7},{7,6},{8,9},{9,8},{10,11... | collective-permute-start | bytes 983048 | tf_op jit(solution)/shard_map/ppermute | solution.py:26
  13.9 29.5 %collective-permute-start.7 = (bf16[5,8,32,128]{3,2,1,0:T(8,128)(2,1)}, bf16[5,8,32,128]{3,2,1,0:T(8,128)(2,1)S(1)}, u32[]{:S(2)}, u32[]{:S(2)}) collective-permute-start(bf16[5,8,32,128]{3,2,1,0:T(8,128)(2,1)} %get-tuple-element.31), channel_id=1, source_target_pairs={{0,0},{1,2},{2,1},{3,3},{4,4},{5,6},{6,5},{7,7},{8,8},{9,10},{10,9... | collective-permute-start | bytes 983048 | tf_op jit(solution)/shard_map/ppermute | solution.py:26
  15.5 6.5 %collective-permute-start.5 = (f32[8,256]{1,0:T(8,128)S(1)}, f32[8,256]{1,0:T(8,128)S(1)}, u32[]{:S(2)}, u32[]{:S(2)}) collective-permute-start(f32[8,256]{1,0:T(8,128)S(1)} %add_add_fusion.1), channel_id=1, source_target_pairs={{0,3},{1,0},{2,1},{3,2},{4,7},{5,4},{6,5},{7,6},{8,11},{9,8},{10,9... | collective-permute-start | bytes 24584 | tf_op jit(solution)/shard_map/ppermute | solution.py:44
  17.7 8.7 %collective-permute-start.4 = (f32[8,256]{1,0:T(8,128)S(1)}, f32[8,256]{1,0:T(8,128)S(1)}, u32[]{:S(2)}, u32[]{:S(2)}) collective-permute-start(f32[8,256]{1,0:T(8,128)S(1)} %add_add_fusion.1), channel_id=1, source_target_pairs={{0,2},{1,3},{2,0},{3,1},{4,6},{5,7},{6,4},{7,5},{8,10},{9,11},{10,... | collective-permute-start | bytes 24584 | tf_op jit(solution)/shard_map/ppermute | solution.py:44
  19.6 12.3 %collective-permute-start.10 = (bf16[5,48,128]{2,1,0:T(8,128)(2,1)S(1)}, bf16[5,48,128]{2,1,0:T(8,128)(2,1)S(1)}, u32[]{:S(2)}, u32[]{:S(2)}) collective-permute-start(bf16[5,48,128]{2,1,0:T(8,128)(2,1)S(1)} %get-tuple-element.34), channel_id=1, source_target_pairs={{0,5},{1,4},{2,7},{3,6},{4,1},{5,0},{6,3},{7,2},{8,13},{9,12},{10,... | collective-permute-start | bytes 184328 | tf_op jit(solution)/shard_map/ppermute | solution.py:36
  22.0 28.2 %copy-start.9 = (f32[256,4]{0,1:T(4,128)S(1)}, f32[256,4]{0,1:T(4,128)}, u32[]{:S(2)}) copy-start(f32[256,4]{0,1:T(4,128)} %param.15) | copy-start | bytes 12292
  22.0 13.6 %collective-permute-start.11 = (bf16[5,48,128]{2,1,0:T(8,128)(2,1)S(1)}, bf16[5,48,128]{2,1,0:T(8,128)(2,1)S(1)}, u32[]{:S(2)}, u32[]{:S(2)}) collective-permute-start(bf16[5,48,128]{2,1,0:T(8,128)(2,1)S(1)} %get-tuple-element.35), channel_id=1, source_target_pairs={{0,4},{1,6},{2,5},{3,7},{4,0},{5,2},{6,1},{7,3},{8,12},{9,14},{10,... | collective-permute-start | bytes 184328 | tf_op jit(solution)/shard_map/ppermute | solution.py:36
  26.4 4.3 %copy-start.12 = (f32[8,256]{1,0:T(8,128)}, f32[8,256]{1,0:T(8,128)S(1)}, u32[]{:S(2)}) copy-start(f32[8,256]{1,0:T(8,128)S(1)} %collective-permute-done.4) | copy-start | bytes 24580
  26.4 4.3 %collective-permute-start.3 = (f32[8,256]{1,0:T(8,128)S(1)}, f32[8,256]{1,0:T(8,128)S(1)}, u32[]{:S(2)}, u32[]{:S(2)}) collective-permute-start(f32[8,256]{1,0:T(8,128)S(1)} %add_add_fusion.1), channel_id=1, source_target_pairs={{0,1},{1,2},{2,3},{3,0},{4,5},{5,6},{6,7},{7,4},{8,9},{9,10},{10,1... | collective-permute-start | bytes 24584 | tf_op jit(solution)/shard_map/ppermute | solution.py:44
  30.7 0.6 copy-start.13
  31.3 7.1 %collective-permute-start.12 = (bf16[5,48,128]{2,1,0:T(8,128)(2,1)}, bf16[5,48,128]{2,1,0:T(8,128)(2,1)S(1)}, u32[]{:S(2)}, u32[]{:S(2)}) collective-permute-start(bf16[5,48,128]{2,1,0:T(8,128)(2,1)} %get-tuple-element.36), channel_id=1, source_target_pairs={{0,1},{1,0},{2,3},{3,2},{4,9},{5,8},{6,11},{7,10},{8,5},{9,4},{10,... | collective-permute-start | bytes 184328 | tf_op jit(solution)/shard_map/ppermute | solution.py:36
  31.9 9.1 %collective-permute-start.13 = (bf16[5,48,128]{2,1,0:T(8,128)(2,1)}, bf16[5,48,128]{2,1,0:T(8,128)(2,1)S(1)}, u32[]{:S(2)}, u32[]{:S(2)}) collective-permute-start(bf16[5,48,128]{2,1,0:T(8,128)(2,1)} %get-tuple-element.37), channel_id=1, source_target_pairs={{0,0},{1,2},{2,1},{3,3},{4,8},{5,10},{6,9},{7,11},{8,4},{9,6},{10,... | collective-permute-start | bytes 184328 | tf_op jit(solution)/shard_map/ppermute | solution.py:36
  35.7 13.2 %collective-permute-start.8 = (bf16[5,4,64,128]{3,2,1,0:T(8,128)(2,1)}, bf16[5,4,64,128]{3,2,1,0:T(8,128)(2,1)S(1)}, u32[]{:S(2)}, u32[]{:S(2)}) collective-permute-start(bf16[5,4,64,128]{3,2,1,0:T(8,128)(2,1)} %copy-done.11), channel_id=1, source_target_pairs={{0,4},{4,0},{8,12},{12,8},{1,5},{5,1},{9,13},{13,9},{2,6},{6,2},{1... | collective-permute-start | bytes 983048 | tf_op jit(solution)/shard_map/ppermute | solution.py:26
  38.4 25.9 %collective-permute-start.17 = (bf16[4,4,8,1024]{3,2,1,0:T(8,128)(2,1)}, bf16[4,4,8,1024]{3,2,1,0:T(8,128)(2,1)S(1)}, u32[]{:S(2)}, u32[]{:S(2)}) collective-permute-start(bf16[4,4,8,1024]{3,2,1,0:T(8,128)(2,1)} %get-tuple-element.54), channel_id=1, source_target_pairs={{0,0},{4,8},{8,4},{12,12},{1,1},{5,9},{9,5},{13,13},{2,2},{6,10},{... | collective-permute-start | bytes 786440 | tf_op jit(solution)/shard_map/ppermute | solution.py:26
  41.0 0.6 copy-start.6
  41.7 23.4 %collective-permute-start.16 = (bf16[4,4,8,1024]{3,2,1,0:T(8,128)(2,1)}, bf16[4,4,8,1024]{3,2,1,0:T(8,128)(2,1)S(1)}, u32[]{:S(2)}, u32[]{:S(2)}) collective-permute-start(bf16[4,4,8,1024]{3,2,1,0:T(8,128)(2,1)} %get-tuple-element.55), channel_id=1, source_target_pairs={{0,4},{4,0},{8,12},{12,8},{1,5},{5,1},{9,13},{13,9},{2,6},{6,2},{1... | collective-permute-start | bytes 786440 | tf_op jit(solution)/shard_map/ppermute | solution.py:26
  41.7 24.0 %collective-permute-start.14 = (bf16[4,4,8,1024]{3,2,1,0:T(8,128)(2,1)}, bf16[4,4,8,1024]{3,2,1,0:T(8,128)(2,1)S(1)}, u32[]{:S(2)}, u32[]{:S(2)}) collective-permute-start(bf16[4,4,8,1024]{3,2,1,0:T(8,128)(2,1)} %bitcast.15), channel_id=1, source_target_pairs={{0,1},{1,0},{2,3},{3,2},{4,5},{5,4},{6,7},{7,6},{8,9},{9,8},{10,11... | collective-permute-start | bytes 786440 | tf_op jit(solution)/shard_map/ppermute | solution.py:26
  43.3 10.6 %collective-permute-start.9 = (bf16[5,4,64,128]{3,2,1,0:T(8,128)(2,1)}, bf16[5,4,64,128]{3,2,1,0:T(8,128)(2,1)S(1)}, u32[]{:S(2)}, u32[]{:S(2)}) collective-permute-start(bf16[5,4,64,128]{3,2,1,0:T(8,128)(2,1)} %copy-done.10), channel_id=1, source_target_pairs={{0,0},{4,8},{8,4},{12,12},{1,1},{5,9},{9,5},{13,13},{2,2},{6,10},{... | collective-permute-start | bytes 983048 | tf_op jit(solution)/shard_map/ppermute | solution.py:26
  48.9 20.3 %collective-permute-start.15 = (bf16[4,4,8,1024]{3,2,1,0:T(8,128)(2,1)S(1)}, bf16[4,4,8,1024]{3,2,1,0:T(8,128)(2,1)S(1)}, u32[]{:S(2)}, u32[]{:S(2)}) collective-permute-start(bf16[4,4,8,1024]{3,2,1,0:T(8,128)(2,1)S(1)} %bitcast.21), channel_id=1, source_target_pairs={{0,0},{1,2},{2,1},{3,3},{4,4},{5,6},{6,5},{7,7},{8,8},{9,10},{10,9... | collective-permute-start | bytes 786440 | tf_op jit(solution)/shard_map/ppermute | solution.py:26
  50.3 3.6 %copy-start.7 = (bf16[5,48,128]{2,1,0:T(8,128)(2,1)S(1)}, bf16[5,48,128]{2,1,0:T(8,128)(2,1)}, u32[]{:S(2)}) copy-start(bf16[5,48,128]{2,1,0:T(8,128)(2,1)} %copy-done.6) | copy-start | bytes 184324
  51.9 2.0 %copy-start = (f32[4,2048,128]{2,1,0:T(8,128)}, f32[4,2048,128]{2,1,0:T(8,128)S(1)}, u32[]{:S(2)}) copy-start(f32[4,2048,128]{2,1,0:T(8,128)S(1)} %shard_map.96.inject) | copy-start | bytes 12582916
  62.0 28.2 %collective-permute-start.18 = (bf16[4,8,32,128]{3,2,1,0:T(8,128)(2,1)S(1)}, bf16[4,8,32,128]{3,2,1,0:T(8,128)(2,1)S(1)}, u32[]{:S(2)}, u32[]{:S(2)}) collective-permute-start(bf16[4,8,32,128]{3,2,1,0:T(8,128)(2,1)S(1)} %get-tuple-element.43), channel_id=1, source_target_pairs={{0,1},{1,0},{2,3},{3,2},{4,5},{5,4},{6,7},{7,6},{8,9},{9,8},{10,11... | collective-permute-start | bytes 786440 | tf_op jit(solution)/shard_map/ppermute | solution.py:26
  64.4 25.9 %collective-permute-start.19 = (bf16[4,8,32,128]{3,2,1,0:T(8,128)(2,1)S(1)}, bf16[4,8,32,128]{3,2,1,0:T(8,128)(2,1)S(1)}, u32[]{:S(2)}, u32[]{:S(2)}) collective-permute-start(bf16[4,8,32,128]{3,2,1,0:T(8,128)(2,1)S(1)} %get-tuple-element.44), channel_id=1, source_target_pairs={{0,0},{1,2},{2,1},{3,3},{4,4},{5,6},{6,5},{7,7},{8,8},{9,10},{10,9... | collective-permute-start | bytes 786440 | tf_op jit(solution)/shard_map/ppermute | solution.py:26
  65.0 25.2 %collective-permute-start.20 = (bf16[4,4,64,128]{3,2,1,0:T(8,128)(2,1)S(1)}, bf16[4,4,64,128]{3,2,1,0:T(8,128)(2,1)S(1)}, u32[]{:S(2)}, u32[]{:S(2)}) collective-permute-start(bf16[4,4,64,128]{3,2,1,0:T(8,128)(2,1)S(1)} %get-tuple-element.45), channel_id=1, source_target_pairs={{0,4},{4,0},{8,12},{12,8},{1,5},{5,1},{9,13},{13,9},{2,6},{6,2},{1... | collective-permute-start | bytes 786440 | tf_op jit(solution)/shard_map/ppermute | solution.py:26
  65.7 24.6 %collective-permute-start.21 = (bf16[4,4,64,128]{3,2,1,0:T(8,128)(2,1)S(1)}, bf16[4,4,64,128]{3,2,1,0:T(8,128)(2,1)S(1)}, u32[]{:S(2)}, u32[]{:S(2)}) collective-permute-start(bf16[4,4,64,128]{3,2,1,0:T(8,128)(2,1)S(1)} %get-tuple-element.46), channel_id=1, source_target_pairs={{0,0},{4,8},{8,4},{12,12},{1,1},{5,9},{9,5},{13,13},{2,2},{6,10},{... | collective-permute-start | bytes 786440 | tf_op jit(solution)/shard_map/ppermute | solution.py:26
  69.1 3.6 %collective-permute-start.22 = (bf16[4,48,128]{2,1,0:T(8,128)(2,1)S(1)}, bf16[4,48,128]{2,1,0:T(8,128)(2,1)S(1)}, u32[]{:S(2)}, u32[]{:S(2)}) collective-permute-start(bf16[4,48,128]{2,1,0:T(8,128)(2,1)S(1)} %get-tuple-element.47), channel_id=1, source_target_pairs={{0,5},{1,4},{2,7},{3,6},{4,1},{5,0},{6,3},{7,2},{8,13},{9,12},{10,... | collective-permute-start | bytes 147464 | tf_op jit(solution)/shard_map/ppermute | solution.py:36
  72.7 1.2 %collective-permute-start.23 = (bf16[4,48,128]{2,1,0:T(8,128)(2,1)S(1)}, bf16[4,48,128]{2,1,0:T(8,128)(2,1)S(1)}, u32[]{:S(2)}, u32[]{:S(2)}) collective-permute-start(bf16[4,48,128]{2,1,0:T(8,128)(2,1)S(1)} %get-tuple-element.48), channel_id=1, source_target_pairs={{0,4},{1,6},{2,5},{3,7},{4,0},{5,2},{6,1},{7,3},{8,12},{9,14},{10,... | collective-permute-start | bytes 147464 | tf_op jit(solution)/shard_map/ppermute | solution.py:36
  73.9 6.1 %collective-permute-start.24 = (bf16[4,48,128]{2,1,0:T(8,128)(2,1)S(1)}, bf16[4,48,128]{2,1,0:T(8,128)(2,1)S(1)}, u32[]{:S(2)}, u32[]{:S(2)}) collective-permute-start(bf16[4,48,128]{2,1,0:T(8,128)(2,1)S(1)} %get-tuple-element.49), channel_id=1, source_target_pairs={{0,1},{1,0},{2,3},{3,2},{4,9},{5,8},{6,11},{7,10},{8,5},{9,4},{10,... | collective-permute-start | bytes 147464 | tf_op jit(solution)/shard_map/ppermute | solution.py:36
  80.0 10.2 %collective-permute-start.25 = (bf16[4,48,128]{2,1,0:T(8,128)(2,1)S(1)}, bf16[4,48,128]{2,1,0:T(8,128)(2,1)S(1)}, u32[]{:S(2)}, u32[]{:S(2)}) collective-permute-start(bf16[4,48,128]{2,1,0:T(8,128)(2,1)S(1)} %get-tuple-element.50), channel_id=1, source_target_pairs={{0,0},{1,2},{2,1},{3,3},{4,8},{5,10},{6,9},{7,11},{8,4},{9,6},{10,... | collective-permute-start | bytes 147464 | tf_op jit(solution)/shard_map/ppermute | solution.py:36
  102.5 11.6 %collective-permute-start.26 = (f32[4,8,8,512]{3,2,1,0:T(8,128)S(1)}, f32[4,8,8,512]{3,2,1,0:T(8,128)S(1)}, u32[]{:S(2)}, u32[]{:S(2)}) collective-permute-start(f32[4,8,8,512]{3,2,1,0:T(8,128)S(1)} %get-tuple-element.52), channel_id=1, source_target_pairs={{0,16},{16,0},{1,17},{17,1},{2,18},{18,2},{3,19},{19,3},{4,20},{20... | collective-permute-start | bytes 1572872 | tf_op jit(solution)/shard_map/ppermute | solution.py:567

commit v2 on v1

--- a/solution.py
+++ b/solution.py
@@ -26,27 +26,23 @@
     return lax.ppermute(x, axis, swap_pairs(lax.axis_size(axis), odd))
 
 
-def diagonal(x, odd_x, odd_y):
-    size_x, size_y = lax.axis_size("gx"), lax.axis_size("gy")
-    pairs = [
-        (i * size_y + j, k * size_y + m)
-        for i, k in swap_pairs(size_x, odd_x)
-        for j, m in swap_pairs(size_y, odd_y)
-    ]
-    return lax.ppermute(x, ("gx", "gy"), pairs)
-
-
 def summed(x):
     for axis in ("gx", "gy"):
         size = lax.axis_size(axis)
-        terms = [x]
-        for k in range(1, size):
-            terms.append(lax.ppermute(x, axis, [(i, (i + k) % size) for i in range(size)]))
-        x = sum(terms)
+        if size & (size - 1):
+            terms = [x]
+            for k in range(1, size):
+                terms.append(lax.ppermute(x, axis, [(i, (i + k) % size) for i in range(size)]))
+            x = sum(terms)
+            continue
+        k = 1
+        while k < size:
+            x = x + lax.ppermute(x, axis, [(i, i ^ k) for i in range(size)])
+            k *= 2
     return x
 
 
-def call(kernel, outs, scratch=(), cost=10_000_000, specs=None, grid=()):
+def call(kernel, outs, scratch=(), micros=1.0, specs=None, grid=(), limit=16):
     def run(*args):
         return pl.pallas_call(
             kernel,
@@ -55,8 +51,10 @@
             in_specs=specs or [pl.BlockSpec(memory_space=VMEM)] * len(args),
             out_specs=jax.tree.map(lambda _: pl.BlockSpec(memory_space=VMEM), outs),
             scratch_shapes=list(scratch),
-            compiler_params=pltpu.CompilerParams(vmem_limit_bytes=48 * 2**20),
-            cost_estimate=pl.CostEstimate(flops=cost, bytes_accessed=1_000_000, transcendentals=0),
+            compiler_params=pltpu.CompilerParams(vmem_limit_bytes=limit * 2**20),
+            cost_estimate=pl.CostEstimate(
+                flops=int(1.1e9 * micros), bytes_accessed=100_000, transcendentals=0
+            ),
         )(*args)
 
     return run
@@ -91,28 +89,28 @@
     return pl.ds(start, n * ROWS)
 
 
-def pack_edges(place, load, fields, width_x, width_y, z_out, x_out, c_out):
+def pack_faces(place, load, fields, width_x, width_y, z_out, x_out):
     for odd in (0, 1):
         y0 = jnp.where(place.plus("gy", odd), width_y - HALO, 0)
         x0 = jnp.where(place.plus("gx", odd), width_x - HALO, 0)
         for f in range(fields):
             for x in range(width_x):
-                z_out[odd][f, x] = load(f, x, y0, HALO).astype(BF)
+                value = load(f, x, y0, HALO).reshape(HALO, ROWS, LANES)
+                z_out[odd][f, x] = value.astype(BF)
             for j in range(HALO):
                 x_out[odd][f, j] = load(f, x0 + j, 0, width_y).astype(BF)
+
+
+def pack_corners(place, fields, width_x, z_in, c_out):
     for odd_x in (0, 1):
         plus_x = place.plus("gx", odd_x)
         for odd_y in (0, 1):
             plus_y = place.plus("gy", odd_y)
-            out = c_out[2 * odd_x + odd_y]
             for f in range(fields):
-                for k in range(0, len(CORNER), 2):
-                    two = []
-                    for i, j in CORNER[k : k + 2]:
-                        x = jnp.where(plus_x, width_x - i, i - 1)
-                        y = jnp.where(plus_y, width_y - j, j - 1)
-                        two.append(load(f, x, y, 1))
-                    out[f, k * ROWS : (k + 2) * ROWS] = jnp.concatenate(two, axis=0).astype(BF)
+                for k, (i, j) in enumerate(CORNER):
+                    x = jnp.where(plus_x, width_x - i, i - 1)
+                    y = jnp.where(plus_y, j - 1, HALO - j)
+                    c_out[odd_x][f, odd_y, k] = z_in[odd_y][f, x, y]
 
 
 def place_edges(place, store, fields, width_x, width_y, z_in, x_in, c_in):
@@ -128,25 +126,22 @@
         x0 = jnp.where(place.plus("gx", odd), width_x + HALO, 0)
         for f in range(fields):
             for x in range(width_x):
-                store(f, HALO + x, y0, HALO, masked(z_in[odd][f, x], place.has("gy", odd)))
+                value = masked(z_in[odd][f, x], place.has("gy", odd))
+                store(f, HALO + x, y0, HALO, value.reshape(HALO * ROWS, LANES))
             for j in range(HALO):
                 store(f, x0 + j, HALO, width_y, masked(x_in[odd][f, j], place.has("gx", odd)))
     for odd_x in (0, 1):
         plus_x = place.plus("gx", odd_x)
         for odd_y in (0, 1):
             plus_y = place.plus("gy", odd_y)
-            got = c_in[2 * odd_x + odd_y]
             for f in range(fields):
-                for k in range(0, len(CORNER), 2):
-                    two = masked(
-                        got[f, k * ROWS : (k + 2) * ROWS],
-                        place.has("gx", odd_x),
-                        place.has("gy", odd_y),
+                for k, (i, j) in enumerate(CORNER):
+                    value = masked(
+                        c_in[odd_x][f, odd_y, k], place.has("gx", odd_x), place.has("gy", odd_y)
                     )
-                    for n, (i, j) in enumerate(CORNER[k : k + 2]):
-                        x = jnp.where(plus_x, HALO + width_x - 1 + i, HALO - i)
-                        y = jnp.where(plus_y, HALO + width_y - 1 + j, HALO - j)
-                        store(f, x, y, 1, two[n * ROWS : (n + 1) * ROWS])
+                    x = jnp.where(plus_x, HALO + width_x - 1 + i, HALO - i)
+                    y = jnp.where(plus_y, HALO + width_y - 1 + j, HALO - j)
+                    store(f, x, y, 1, value)
 
 
 class Altitude:
@@ -260,40 +255,30 @@
 
 
 def add_increment(altitude, state, forward, total, width_x, width_y):
-    wide = width_y + 2
-
-    def column(f, x, y):
-        start = (x * wide + y) * ROWS
-        return forward[f, pl.ds(pl.multiple_of(start, ROWS), ROWS), :]
-
-    def row(i, carry):
+    def row(i):
         for k in range(width_y):
             p, ax, ay, az = (state(f, i, k) for f in range(4))
-            dx = [column(f, i + 2, k + 1) - column(f, i, k + 1) for f in range(4)]
-            dy = [column(f, i + 1, k + 2) - column(f, i + 1, k) for f in range(4)]
-            dz = [altitude(column(f, i + 1, k + 1)) for f in range(4)]
+            dx = [forward(f, i + 1, k) - forward(f, i - 1, k) for f in range(4)]
+            dy = [forward(f, i, k + 1) - forward(f, i, k - 1) for f in range(4)]
+            dz = [altitude(forward(f, i, k)) for f in range(4)]
             rows = column_rows(k, 1)
             total[0, i, rows, :] += p * (dx[1] + dy[2] + dz[3])
             for n, d in ((1, dx), (2, dy), (3, dz)):
                 total[n, i, rows, :] += p * d[0] + ax * d[1] + ay * d[2] + az * d[3]
+
+    def inner(i, carry):
+        row(i)
         return carry
 
-    lax.fori_loop(0, width_x, row, 0)
-
-
-def halo_structs(fields, width_x, width_y):
-    faces_z = [struct((fields, width_x, HALO * ROWS, LANES), BF)] * 2
+    row(0)
+    lax.fori_loop(1, width_x - 1, inner, 0)
+    row(width_x - 1)
+
+
+def face_structs(fields, width_x, width_y):
+    faces_z = [struct((fields, width_x, HALO, ROWS, LANES), BF)] * 2
     faces_x = [struct((fields, HALO, width_y * ROWS, LANES), BF)] * 2
-    corners = [struct((fields, len(CORNER) * ROWS, LANES), BF)] * 4
-    return faces_z + faces_x + corners
-
-
-def exchanged(edges):
-    z, x, c = edges[:2], edges[2:4], edges[4:]
-    z = [swapped(z[odd], "gy", odd) for odd in (0, 1)]
-    c = [diagonal(c[2 * i + j], i, j) for i in (0, 1) for j in (0, 1)]
-    x = [swapped(x[odd], "gx", odd) for odd in (0, 1)]
-    return z + x + c
+    return faces_z + faces_x
 
 
 def shards(
@@ -311,9 +296,21 @@
     slots = residuals.shape[0]
     ext_x, ext_y = width_x + 2 * HALO, width_y + 2 * HALO
     blocks = depth // LANES
-    assert blocks == ROWS and steps_total == 2 * PER_ROUND
+    assert blocks == ROWS and steps_total == 2 * PER_ROUND and slots % LANES == 0
     tile = (width_x, width_y * ROWS, LANES)
     ext = (ext_x, ext_y * ROWS, LANES)
+
+    def exchanged(faces, fields):
+        z = [swapped(faces[odd], "gy", odd) for odd in (0, 1)]
+        x = [swapped(faces[2 + odd], "gx", odd) for odd in (0, 1)]
+
+        def corner_kernel(z_even, z_odd, *outs):
+            pack_corners(Place(), fields, width_x, (z_even, z_odd), outs)
+
+        shape = (fields, 2, len(CORNER), ROWS, LANES)
+        corners = call(corner_kernel, [struct(shape, BF)] * 2, micros=0.7, limit=8)(*z)
+        corners = [swapped(corners[odd], "gx", odd) for odd in (0, 1)]
+        return z + x + corners
 
     def pack_kernel(state, speed, cols, speed_cols, *outs):
         place = Place()
@@ -329,41 +326,37 @@
             ref = cols.at[f] if f < 4 else speed_cols
             return ref[x, column_rows(y, n), :]
 
-        pack_edges(place, load, 5, width_x, width_y, outs[:2], outs[2:4], outs[4:])
+        pack_faces(place, load, 5, width_x, width_y, outs[:2], outs[2:])
 
     packed = call(
         pack_kernel,
-        [struct((4,) + tile, F32), struct(tile, F32)] + halo_structs(5, width_x, width_y),
+        [struct((4,) + tile, F32), struct(tile, F32)] + face_structs(5, width_x, width_y),
+        micros=1.2,
     )(adjoint_state, sound_speed_sq)
-    cols, speed_cols, edges = packed[0], packed[1], packed[2:]
-    first_halo = exchanged(edges)
-
-    forward_edges = []
-    for axis, dim in (("gy", 3), ("gx", 2)):
-        for odd in (0, 1):
-            plus = lax.rem(lax.axis_index(axis), 2) == odd
-            start = jnp.where(plus, forward_field.shape[dim] - 1, 0)
-            edge = lax.dynamic_slice_in_dim(forward_field, start, 1, axis=dim)
-            forward_edges.append(swapped(jnp.squeeze(edge, dim), axis, odd))
+    cols, speed_cols = packed[:2]
+    first_halo = exchanged(packed[2:], 5)
 
     def sample_kernel(source, pressure, out):
-        local_x = source[:, 0:1] - lax.axis_index("gx") * width_x
-        local_y = source[:, 1:2] - lax.axis_index("gy") * width_y
+        local_x = source[0:1] - lax.axis_index("gx") * width_x
+        local_y = source[1:2] - lax.axis_index("gy") * width_y
         inside = (local_x >= 0) & (local_x < width_x) & (local_y >= 0) & (local_y < width_y)
         where = jnp.where(inside, local_x * width_y + local_y, -1)
         cells = width_x * width_y
-        chosen = lax.broadcasted_iota(jnp.int32, (slots, cells), 1) == where
+        chosen = lax.broadcasted_iota(jnp.int32, (cells, slots), 0) == where
         chosen = jnp.where(chosen, 1.0, 0.0).astype(BF)
-        level = lax.broadcasted_iota(jnp.int32, (slots, depth), 1) == source[:, 2:3]
-        lane = lax.broadcasted_iota(jnp.int32, (slots, LANES), 1)
-        result = jnp.zeros((slots, LANES), F32)
+        level = lax.broadcasted_iota(jnp.int32, (depth, slots), 0) == source[2:3]
+        row = lax.broadcasted_iota(jnp.int32, (ROWS, slots), 0)
+        result = jnp.zeros((ROWS, slots), F32)
         for t in range(steps_total):
-            columns = jnp.dot(
-                chosen, pressure[t, 0].reshape(cells, depth), preferred_element_type=F32
+            columns = lax.dot_general(
+                pressure[t, 0].reshape(cells, depth),
+                chosen,
+                (((0,), (0,)), ((), ())),
+                preferred_element_type=F32,
             )
-            picked = jnp.sum(jnp.where(level, columns, 0.0), axis=1, keepdims=True)
-            result = jnp.where(lane == t, picked, result)
-        out[...] = result.T[:ROWS]
+            picked = jnp.sum(jnp.where(level, columns, 0.0), axis=0, keepdims=True)
+            result = jnp.where(row == t, picked, result)
+        out[...] = result
 
     samples = call(
         sample_kernel,
@@ -373,18 +366,20 @@
             pl.BlockSpec((steps_total, 1, width_x, width_y, depth), lambda i: (0, 0, 0, 0, 0)),
         ],
         grid=(1,),
-    )(source_cells, forward_field)
+        micros=1.2,
+        limit=12,
+    )(source_cells.T, forward_field)
     samples = summed(samples)
 
-    def inject_kernel(counts, receiver, receiver_rows, misfit, sample, out):
-        local_x = receiver_rows[0:1] - (lax.axis_index("gx") * width_x - HALO)
-        local_y = receiver_rows[1:2] - (lax.axis_index("gy") * width_y - HALO)
+    def inject_kernel(counts, receiver, misfit, sample, out):
+        local_x = receiver[0:1] - (lax.axis_index("gx") * width_x - HALO)
+        local_y = receiver[1:2] - (lax.axis_index("gy") * width_y - HALO)
         inside = (local_x >= 0) & (local_x < ext_x) & (local_y >= 0) & (local_y < ext_y)
         live = lax.broadcasted_iota(jnp.int32, (1, slots), 1) < counts[0]
         where = jnp.where(inside & live, local_x * ext_y + local_y, -1)
         cells = ext_x * ext_y
         chosen = lax.broadcasted_iota(jnp.int32, (cells, slots), 0) == where
-        level = lax.broadcasted_iota(jnp.int32, (slots, depth), 1) == receiver[:, 2:3]
+        level = lax.broadcasted_iota(jnp.int32, (depth, slots), 0) == receiver[2:3]
         level = jnp.where(level, 1.0, 0.0).astype(BF)
         for t in range(steps_total):
             amplitude = misfit[t : t + 1] * sample[t : t + 1]
@@ -392,7 +387,9 @@
             result = jnp.zeros((cells, depth), F32)
             for part in (head, amplitude - head):
                 spread = jnp.where(chosen, part, 0.0).astype(BF)
-                result += jnp.dot(spread, level, preferred_element_type=F32)
+                result += lax.dot_general(
+                    spread, level, (((1,), (1,)), ((), ())), preferred_element_type=F32
+                )
             for g in range(cells // ROWS):
                 for b in range(blocks):
                     out[t, pl.ds(g * ROWS * ROWS + b, ROWS, stride=ROWS), :] = result[
@@ -402,14 +399,80 @@
     injected = call(
         inject_kernel,
         struct((steps_total, ext_x * ext_y * ROWS, LANES), F32),
-        specs=[pl.BlockSpec(memory_space=pltpu.SMEM)] + [pl.BlockSpec(memory_space=VMEM)] * 4,
-    )(pair_counts, receiver_cells, receiver_cells.T, residuals.T, samples)
-
-    wind = wind_profile.reshape(3, ROWS, LANES) * SCALE
+        specs=[pl.BlockSpec(memory_space=pltpu.SMEM)] + [pl.BlockSpec(memory_space=VMEM)] * 3,
+        micros=1.8,
+    )(pair_counts, receiver_cells.T, residuals.T, samples)
+
+    def forward_kernel(forward, early, late, *edges):
+        place = Place()
+
+        def one(n, carry):
+            t, f = n // 4, lax.rem(n, 4)
+            for ref, snap in ((late, t), (early, t + PER_ROUND)):
+                number = snap * 4 + f
+                for x in range(width_x):
+                    for b in range(blocks):
+                        ref[n, x, pl.ds(b, width_y, stride=ROWS), :] = forward[
+                            snap, f, x, :, b * LANES : (b + 1) * LANES
+                        ].astype(F32)
+                for odd in (0, 1):
+                    y = jnp.where(place.plus("gy", odd), width_y - 1, 0)
+                    x = jnp.where(place.plus("gx", odd), width_x - 1, 0)
+                    edges[2 + odd][number] = ref[n, x].astype(BF)
+                    edges[odd][number] = ref[n, :, column_rows(y, 1), :].reshape(
+                        width_x * ROWS, LANES
+                    ).astype(BF)
+            return carry
+
+        lax.fori_loop(0, 4 * PER_ROUND, one, 0)
+
+    forward_struct = struct((4 * PER_ROUND,) + tile, F32)
+    edge_structs = [struct((4 * steps_total, n * ROWS, LANES), BF) for n in (width_x, width_y)]
+    made = call(
+        forward_kernel,
+        [forward_struct] * 2 + [edge_structs[0]] * 2 + [edge_structs[1]] * 2,
+        micros=2.0,
+    )(forward_field)
+    forward_early, forward_late = made[:2]
+    rim = [swapped(made[2 + odd], "gy", odd) for odd in (0, 1)]
+    rim += [swapped(made[4 + odd], "gx", odd) for odd in (0, 1)]
+
+    rim_scratch = [
+        VMEM((2, 4 * PER_ROUND, width_x * ROWS, LANES), F32),
+        VMEM((2, 4 * PER_ROUND, width_y * ROWS, LANES), F32),
+    ]
+
+    def forward_of(place, columns, first, rim, rim_y, rim_x):
+        for odd in (0, 1):
+            for axis, source, target in (("gy", rim[odd], rim_y), ("gx", rim[2 + odd], rim_x)):
+                side = jnp.where(place.plus(axis, odd), 1, 0)
+                for n in range(4 * PER_ROUND):
+                    value = source[4 * first + n].astype(F32)
+                    if odd:
+                        value = jnp.where(place.has(axis, odd), value, 0.0)
+                    target[side, n] = value
+
+        def reader(snap):
+            base = 4 * (snap - first)
+
+            def column(f, x, y):
+                if isinstance(x, int) and x in (-1, width_x):
+                    return rim_x[int(x > 0), base + f, column_rows(y, 1), :]
+                if y in (-1, width_y):
+                    rows = x * ROWS if isinstance(x, int) else pl.multiple_of(x * ROWS, ROWS)
+                    return rim_y[int(y > 0), base + f, pl.ds(rows, ROWS), :]
+                return columns[base + f, x, column_rows(y, 1), :]
+
+            return column
+
+        return reader
 
     def run_round(place, number, wind, inject, buffers, speed, carry_dz, after):
         altitude = Altitude()
-        winds = tuple(wind[i] for i in range(3))
+        winds = []
+        for i in range(3):
+            rows = [wind[i : i + 1, b * LANES : (b + 1) * LANES] for b in range(blocks)]
+            winds.append(jnp.concatenate(rows, axis=0) * SCALE)
         for s in range(PER_ROUND):
             step = number * PER_ROUND + s
             snap = steps_total - 1 - step
@@ -445,12 +508,12 @@
                 store(4, HALO + x, HALO, width_y, speed_cols[x])
         place_edges(place, store, fields, width_x, width_y, halo[:2], halo[2:4], halo[4:])
 
-    halos = 8
+    halos, faces = 6, 4
 
     def first_kernel(wind, inject, cols, speed_cols, *refs):
         halo, refs = refs[:halos], refs[halos:]
-        early, late, speed, edges = refs[0], refs[1], refs[2], refs[3 : 3 + halos]
-        here, there, carry_dz = refs[3 + halos :]
+        early, late, speed, edges = refs[0], refs[1], refs[2], refs[3 : 3 + faces]
+        here, there, carry_dz = refs[3 + faces :]
         place = Place()
         fill(place, here, speed, cols, speed_cols, halo)
 
@@ -465,80 +528,53 @@
         def load(f, x, y, n):
             return own(here, f, x, y, n)
 
-        pack_edges(place, load, 4, width_x, width_y, edges[:2], edges[2:4], edges[4:])
+        pack_faces(place, load, 4, width_x, width_y, edges[:2], edges[2:])
 
     first = call(
         first_kernel,
-        [struct((4,) + tile, F32)] * 2 + [struct(ext, F32)] + halo_structs(4, width_x, width_y),
+        [struct((4,) + tile, F32)] * 2 + [struct(ext, F32)] + face_structs(4, width_x, width_y),
         scratch=[VMEM((4,) + ext, F32)] * 2 + [VMEM(ext, F32)],
-    )(wind, injected, cols, speed_cols, *first_halo)
-    early, late, speed_ext, edges = first[0], first[1], first[2], first[3:]
-    second_halo = exchanged(edges)
-
-    rim = (width_x + 2) * (width_y + 2) * ROWS
-    wide = width_y + 2
-
-    def early_kernel(early, late, forward, *refs):
-        edges, (total, kept), (columns,) = refs[:4], refs[4:6], refs[6:]
-        place = Place()
+        micros=8.0,
+        limit=28,
+    )(wind_profile, injected, cols, speed_cols, *first_halo)
+    early, late, speed_ext = first[:3]
+    second_halo = exchanged(first[3:], 4)
+
+    def early_kernel(early, late, columns, *refs):
+        rim, total, rim_y, rim_x = refs[:4], refs[4], refs[5], refs[6]
         altitude = Altitude()
-
-        def spread(snap, target):
-            for f in range(4):
-                for x in range(width_x):
-                    for b in range(blocks):
-                        target[f, pl.ds(((x + 1) * wide + 1) * ROWS + b, width_y, stride=ROWS), :] = (
-                            forward[snap, f, x, :, b * LANES : (b + 1) * LANES].astype(F32)
-                        )
-                for odd in (0, 1):
-                    y = jnp.where(place.plus("gy", odd), width_y + 1, 0)
-                    x = jnp.where(place.plus("gx", odd), width_x + 1, 0)
-                    for b in range(blocks):
-                        here = slice(b * LANES, (b + 1) * LANES)
-                        value = edges[odd][snap, f, :, here].astype(F32)
-                        if odd:
-                            value = jnp.where(place.has("gy", odd), value, 0.0)
-                        target[f, pl.ds((wide + y) * ROWS + b, width_x, stride=wide * ROWS), :] = value
-                        value = edges[2 + odd][snap, f, :, here].astype(F32)
-                        if odd:
-                            value = jnp.where(place.has("gx", odd), value, 0.0)
-                        target[f, pl.ds((x * wide + 1) * ROWS + b, width_y, stride=ROWS), :] = value
-
+        reader = forward_of(Place(), columns, PER_ROUND, rim, rim_y, rim_x)
         total[...] = jnp.zeros_like(total)
         for s, state in ((0, early), (1, late)):
-            spread(steps_total - 1 - s, columns)
             add_increment(
                 altitude,
                 lambda f, x, y: state[f, x, column_rows(y, 1), :],
-                columns,
+                reader(steps_total - 1 - s),
                 total,
                 width_x,
                 width_y,
             )
-        for s in range(PER_ROUND):
-            spread(steps_total - 1 - PER_ROUND - s, kept.at[s])
-
-    total, kept = call(
-        early_kernel,
-        [struct((4,) + tile, F32), struct((PER_ROUND, 4, rim, LANES), F32)],
-        scratch=[VMEM((4, rim, LANES), F32)],
-    )(early, late, forward_field, *forward_edges)
+
+    total = call(
+        early_kernel, struct((4,) + tile, F32), scratch=rim_scratch, micros=5.0, limit=16
+    )(early, late, forward_early, *rim)
 
     half = depth // 2
 
-    def second_kernel(wind, inject, cols, speed, total, kept, *refs):
-        halo, refs = refs[:halos], refs[halos:]
+    def second_kernel(wind, inject, cols, speed, total, columns, *refs):
+        halo, rim, refs = refs[:halos], refs[halos : halos + 4], refs[halos + 4 :]
         final, mine, other = refs[:3]
-        here, there, carry_dz, sums = refs[3:]
+        here, there, carry_dz, sums, rim_y, rim_x = refs[3:]
         place = Place()
         fill(place, here, None, cols, None, halo)
+        reader = forward_of(place, columns, 0, rim, rim_y, rim_x)
         sums[...] = total[...]
 
         def after(altitude, s, snap, state):
             add_increment(
                 altitude,
                 lambda f, x, y: own(state, f, x, y, 1),
-                kept.at[s],
+                reader(snap),
                 sums,
                 width_x,
                 width_y,
@@ -562,8 +598,10 @@
     final, mine, other = call(
         second_kernel,
         [struct(adjoint_state.shape, F32), kernel_half, kernel_half],
-        scratch=[VMEM((4,) + ext, F32)] * 2 + [VMEM(ext, F32), VMEM((4,) + tile, F32)],
-    )(wind, injected, late, speed_ext, total, kept, *second_halo)
+        scratch=[VMEM((4,) + ext, F32)] * 2 + [VMEM(ext, F32), VMEM((4,) + tile, F32)] + rim_scratch,
+        micros=11.0,
+        limit=30,
+    )(wind_profile, injected, late, speed_ext, total, forward_late, *second_halo, *rim)
     received = lax.ppermute(other, "pair", [(0, 1), (1, 0)])
     return (mine + received, final)
 

time: 117 us -> 81.5 us (0.70); the launches traced: 115 us -> 81.2 us
  local copies, waits for them, and re-layouts: 15 us -> 2.34 us
  Pallas kernels: 31 us -> 20.8 us
  starting transfers between devices: 40.2 us -> 31.8 us
  other arithmetic: 2.33 us -> 0.89 us
  waiting for transfers between devices: 25 us -> 23.8 us
    ppermute x14 -> x4, starting transfers between devices: 21.1 us -> 5.75 us  [summed(): x = x + lax.ppermute(x, axis, [(i, i ^ k) for i in range(size)])]
    pallas_call x6 -> x9, Pallas kernels: 31 us -> 20.8 us  [run(): pl.pallas_call(kernel, out_shape=outs, grid=grid, in_specs=specs or [pl.B...]
    unnamed x33 -> x14, local copies, waits for them, and re-layouts: 11.8 us -> 2.34 us
    ppermute x14 -> x4, waiting for transfers between devices: 14.6 us -> 6.02 us  [summed(): x = x + lax.ppermute(x, axis, [(i, i ^ k) for i in range(size)])]
    ppermute x12 -> x16, waiting for transfers between devices: 0.03 us -> 7.26 us  [swapped(): return lax.ppermute(x, axis, swap_pairs(lax.axis_size(axis), odd))]
    ppermute x12 -> x16, starting transfers between devices: 17.8 us -> 24.8 us  [swapped(): return lax.ppermute(x, axis, swap_pairs(lax.axis_size(axis), odd))]
    dynamic_slice x1 -> x0, local copies, waits for them, and re-layouts: 2.24 us -> none  [shards(): edge = lax.dynamic_slice_in_dim(forward_field, start, 1, axis=dim)]
  transfers between devices with their start and end apart: 27 -> 21, of which waited for: 7 -> 9; matrix products, arithmetic and copies ran while one was open for 7% -> 0% of each run, Pallas kernels for 15% -> 7%
where the time goes in v2:
time: 81.5 us; the launch traced here: 81.2 us
  starting transfers between devices  31.8 us (39%)
  waiting for transfers between devices  23.8 us (29%)
  Pallas kernels  20.8 us (26%)
  local copies, waits for them, and re-layouts  2.34 us (3%)
  between operations  1.6 us (2%)
  other arithmetic  0.89 us (1%)
    ppermute x16, starting transfers between devices, swapped(): return lax.ppermute(x, axis, swap_pairs(lax.axis_size(axis), odd))  24.8 us
    pallas_call x9, Pallas kernels, run(): pl.pallas_call(kernel, out_shape=outs, grid=grid, in_specs=specs or [pl.B...  20.8 us
    ppermute x1, waiting for transfers between devices, shards(): received = lax.ppermute(other, 'pair', [(0, 1), (1, 0)])  10.5 us
    ppermute x16, waiting for transfers between devices, swapped(): return lax.ppermute(x, axis, swap_pairs(lax.axis_size(axis), odd))  7.26 us
    ppermute x4, waiting for transfers between devices, summed(): x = x + lax.ppermute(x, axis, [(i, i ^ k) for i in range(size)])  6.02 us
    ppermute x4, starting transfers between devices, summed(): x = x + lax.ppermute(x, axis, [(i, i ^ k) for i in range(size)])  5.75 us
    unnamed x14, local copies, waits for them, and re-layouts  2.34 us
  transfers between devices with their start and end apart: 21, of which 9 were waited for; matrix products, arithmetic and copies ran while one was open for 0% of the time, Pallas kernels for 7%

profile of v2, /device:TPU:1, one launch (start us, length us, event | category | flops | bytes accessed | tf_op | source)
XLA Modules:
  0.0 81.2 jit_solution(18160314404848707040)
XLA Ops:
  0.7 1.4 %copy-done.1 = f32[1,4,8,8,1024]{4,3,2,1,0:T(8,128)S(1)} copy-done((f32[1,4,8,8,1024]{4,3,2,1,0:T(8,128)S(1)}, f32[1,4,8,8,1024]{4,3,2,1,0:T(8,128)}, u32[]{:S(2)}) %copy-start.1) | copy-done | bytes 1048600
  2.0 0.9 %copy-done.2 = f32[8,8,1024]{2,1,0:T(8,128)S(1)} copy-done((f32[8,8,1024]{2,1,0:T(8,128)S(1)}, f32[8,8,1024]{2,1,0:T(8,128)}, u32[]{:S(2)}) %copy-start.2) | copy-done | bytes 262168
  3.0 0.3 shard_map.97
  3.3 2.2 %collective-permute-start.4 = (bf16[5,8,4,8,128]{4,3,2,1,0:T(8,128)(2,1)S(1)}, bf16[5,8,4,8,128]{4,3,2,1,0:T(8,128)(2,1)S(1)}, u32[]{:S(2)}, u32[]{:S(2)}) collective-permute-start(bf16[5,8,4,8,128]{4,3,2,1,0:T(8,128)(2,1)S(1)} %get-tuple-element.30), channel_id=1, source_target_pairs={{0,1},{1,0},{2,3},{3,2},{4,5},{5,4},{6,7},{7,6},{8,9},{9,8},{10,11... | collective-permute-start | bytes 983048 | tf_op jit(solution)/shard_map/ppermute | solution.py:26
  5.5 0.7 collective-permute-start.5
  6.2 1.0 %collective-permute-start.6 = (bf16[5,4,64,128]{3,2,1,0:T(8,128)(2,1)S(1)}, bf16[5,4,64,128]{3,2,1,0:T(8,128)(2,1)S(1)}, u32[]{:S(2)}, u32[]{:S(2)}) collective-permute-start(bf16[5,4,64,128]{3,2,1,0:T(8,128)(2,1)S(1)} %get-tuple-element.32), channel_id=1, source_target_pairs={{0,4},{4,0},{8,12},{12,8},{1,5},{5,1},{9,13},{13,9},{2,6},{6,2},{1... | collective-permute-start | bytes 983048 | tf_op jit(solution)/shard_map/ppermute | solution.py:26
  7.2 3.0 %collective-permute-start.7 = (bf16[5,4,64,128]{3,2,1,0:T(8,128)(2,1)S(1)}, bf16[5,4,64,128]{3,2,1,0:T(8,128)(2,1)S(1)}, u32[]{:S(2)}, u32[]{:S(2)}) collective-permute-start(bf16[5,4,64,128]{3,2,1,0:T(8,128)(2,1)S(1)} %get-tuple-element.33), channel_id=1, source_target_pairs={{0,0},{4,8},{8,4},{12,12},{1,1},{5,9},{9,5},{13,13},{2,2},{6,10},{... | collective-permute-start | bytes 983048 | tf_op jit(solution)/shard_map/ppermute | solution.py:26
  10.3 0.8 shard_map.95
  11.0 0.0 copy-start.5
  11.1 0.0 copy-start.6
  11.1 0.1 collective-permute-start
  11.1 1.2 %collective-permute-done = f32[8,256]{1,0:T(8,128)S(1)} collective-permute-done((f32[8,256]{1,0:T(8,128)S(1)}, f32[8,256]{1,0:T(8,128)S(1)}, u32[]{:S(2)}, u32[]{:S(2)}) %collective-permute-start) | collective-permute-done | bytes 8224 | tf_op jit(solution)/shard_map/ppermute | solution.py:40
  12.3 0.4 collective-permute-start.1
  12.7 2.3 %collective-permute-done.1 = f32[8,256]{1,0:T(8,128)S(1)} collective-permute-done((f32[8,256]{1,0:T(8,128)S(1)}, f32[8,256]{1,0:T(8,128)S(1)}, u32[]{:S(2)}, u32[]{:S(2)}) %collective-permute-start.1) | collective-permute-done | bytes 8224 | tf_op jit(solution)/shard_map/ppermute | solution.py:40
  15.0 4.1 %collective-permute-start.2 = (f32[8,256]{1,0:T(8,128)S(1)}, f32[8,256]{1,0:T(8,128)S(1)}, u32[]{:S(2)}, u32[]{:S(2)}) collective-permute-start(f32[8,256]{1,0:T(8,128)S(1)} %add.16), channel_id=1, source_target_pairs={{0,1},{1,0},{2,3},{3,2},{4,5},{5,4},{6,7},{7,6},{8,9},{9,8},{10,11... | collective-permute-start | bytes 24584 | tf_op jit(solution)/shard_map/ppermute | solution.py:40
  19.1 1.0 %collective-permute-done.2 = f32[8,256]{1,0:T(8,128)S(1)} collective-permute-done((f32[8,256]{1,0:T(8,128)S(1)}, f32[8,256]{1,0:T(8,128)S(1)}, u32[]{:S(2)}, u32[]{:S(2)}) %collective-permute-start.2) | collective-permute-done | bytes 8224 | tf_op jit(solution)/shard_map/ppermute | solution.py:40
  20.1 1.2 %collective-permute-start.3 = (f32[8,256]{1,0:T(8,128)S(1)}, f32[8,256]{1,0:T(8,128)S(1)}, u32[]{:S(2)}, u32[]{:S(2)}) collective-permute-start(f32[8,256]{1,0:T(8,128)S(1)} %add.17), channel_id=1, source_target_pairs={{0,2},{1,3},{2,0},{3,1},{4,6},{5,7},{6,4},{7,5},{8,10},{9,11},{10,... | collective-permute-start | bytes 24584 | tf_op jit(solution)/shard_map/ppermute | solution.py:40
  22.0 1.5 %collective-permute-done.3 = f32[8,256]{1,0:T(8,128)S(1)} collective-permute-done((f32[8,256]{1,0:T(8,128)S(1)}, f32[8,256]{1,0:T(8,128)S(1)}, u32[]{:S(2)}, u32[]{:S(2)}) %collective-permute-start.3) | collective-permute-done | bytes 8224 | tf_op jit(solution)/shard_map/ppermute | solution.py:40
  23.5 0.0 collective-permute-done.4.z_even.refs_0_
  23.5 0.0 collective-permute-done.5.z_odd.refs_1_
  23.5 0.1 shard_map.98
  23.6 3.6 %collective-permute-start.8 = (bf16[5,2,6,8,128]{4,3,2,1,0:T(8,128)(2,1)S(1)}, bf16[5,2,6,8,128]{4,3,2,1,0:T(8,128)(2,1)S(1)}, u32[]{:S(2)}, u32[]{:S(2)}) collective-permute-start(bf16[5,2,6,8,128]{4,3,2,1,0:T(8,128)(2,1)S(1)} %get-tuple-element.34), channel_id=1, source_target_pairs={{0,4},{4,0},{8,12},{12,8},{1,5},{5,1},{9,13},{13,9},{2,6},{6,2},{1... | collective-permute-start | bytes 368648 | tf_op jit(solution)/shard_map/ppermute | solution.py:26
  27.2 2.2 %collective-permute-start.9 = (bf16[5,2,6,8,128]{4,3,2,1,0:T(8,128)(2,1)S(1)}, bf16[5,2,6,8,128]{4,3,2,1,0:T(8,128)(2,1)S(1)}, u32[]{:S(2)}, u32[]{:S(2)}) collective-permute-start(bf16[5,2,6,8,128]{4,3,2,1,0:T(8,128)(2,1)S(1)} %get-tuple-element.35), channel_id=1, source_target_pairs={{0,0},{4,8},{8,4},{12,12},{1,1},{5,9},{9,5},{13,13},{2,2},{6,10},{... | collective-permute-start | bytes 368648 | tf_op jit(solution)/shard_map/ppermute | solution.py:26
  29.4 0.0 copy-start.3
  29.4 1.5 %shard_map.96.inject = f32[4,2048,128]{2,1,0:T(8,128)S(1)} custom-call(s32[1]{0:T(128)S(6)} %copy.10.counts, s32[3,256]{1,0:T(4,128)S(1)} %bitcast.4, f32[4,256]{1,0:T(4,128)S(1)} %bitcast.5, f32[8,256]{1,0:T(8,128)S(1)} %add.18.sample), custom_call_target="tpu_custom_call" | custom-call | flops 1980000000 | bytes 100000 | tf_op jit(solution)/shard_map/pallas_call | solution.py:47
  30.9 0.0 collective-permute-done.6.refs_2_
  31.0 2.4 %collective-permute-done.9.refs_5_ = bf16[5,2,6,8,128]{4,3,2,1,0:T(8,128)(2,1)S(1)} collective-permute-done((bf16[5,2,6,8,128]{4,3,2,1,0:T(8,128)(2,1)S(1)}, bf16[5,2,6,8,128]{4,3,2,1,0:T(8,128)(2,1)S(1)}, u32[]{:S(2)}, u32[]{:S(2)}) %collective-permute-start.9) | collective-permute-done | bytes 122912 | tf_op jit(solution)/shard_map/ppermute | solution.py:26
  33.4 5.8 %shard_map.99 = (f32[4,8,64,128]{3,2,1,0:T(8,128)S(1)}, f32[4,8,64,128]{3,2,1,0:T(8,128)S(1)}, f32[16,128,128]{2,1,0:T(8,128)S(1)}, bf16[4,8,4,8,128]{4,3,2,1,0:...) custom-call(f32[3,1024]{1,0:T(4,128)S(1)} %copy-done.3, ...), custom_call_target="tpu_custom_call" | custom-call | flops 8800000000 | bytes 100000 | tf_op jit(solution)/shard_map/pallas_call | solution.py:47
  39.1 1.8 %collective-permute-start.14 = (bf16[4,8,4,8,128]{4,3,2,1,0:T(8,128)(2,1)S(1)}, bf16[4,8,4,8,128]{4,3,2,1,0:T(8,128)(2,1)S(1)}, u32[]{:S(2)}, u32[]{:S(2)}) collective-permute-start(bf16[4,8,4,8,128]{4,3,2,1,0:T(8,128)(2,1)S(1)} %get-tuple-element.45), channel_id=1, source_target_pairs={{0,1},{1,0},{2,3},{3,2},{4,5},{5,4},{6,7},{7,6},{8,9},{9,8},{10,11... | collective-permute-start | bytes 786440 | tf_op jit(solution)/shard_map/ppermute | solution.py:26
  40.9 0.7 collective-permute-start.15
  41.6 0.8 %shard_map.100 = (f32[8,8,64,128]{3,2,1,0:T(8,128)S(1)}, f32[8,8,64,128]{3,2,1,0:T(8,128)S(1)}, bf16[16,64,128]{2,1,0:T(8,128)(2,1)S(1)}, bf16[16,64,128]{2,1,0:...) custom-call(bf16[4,4,8,8,1024]{4,3,2,1,0:T(8,128)(2,1)S(1)} %copy-done), custom_call_target="tpu_custom_call" | custom-call | flops 2200000000 | bytes 100000 | tf_op jit(solution)/shard_map/pallas_call | solution.py:47
  42.4 1.3 %collective-permute-start.10 = (bf16[16,64,128]{2,1,0:T(8,128)(2,1)S(1)}, bf16[16,64,128]{2,1,0:T(8,128)(2,1)S(1)}, u32[]{:S(2)}, u32[]{:S(2)}) collective-permute-start(bf16[16,64,128]{2,1,0:T(8,128)(2,1)S(1)} %get-tuple-element.40), channel_id=1, source_target_pairs={{0,1},{1,0},{2,3},{3,2},{4,5},{5,4},{6,7},{7,6},{8,9},{9,8},{10,11... | collective-permute-start | bytes 786440 | tf_op jit(solution)/shard_map/ppermute | solution.py:26
  43.8 0.7 collective-permute-start.11
  44.4 0.1 collective-permute-start.12
  44.5 3.1 %collective-permute-done.14.z_even.refs_0_ = bf16[4,8,4,8,128]{4,3,2,1,0:T(8,128)(2,1)S(1)} collective-permute-done((bf16[4,8,4,8,128]{4,3,2,1,0:T(8,128)(2,1)S(1)}, bf16[4,8,4,8,128]{4,3,2,1,0:T(8,128)(2,1)S(1)}, u32[]{:S(2)}, u32[]{:S(2)}) %collective-permute-start.14) | collective-permute-done | bytes 262176 | tf_op jit(solution)/shard_map/ppermute | solution.py:26
  47.6 1.9 %collective-permute-start.13 = (bf16[16,64,128]{2,1,0:T(8,128)(2,1)S(1)}, bf16[16,64,128]{2,1,0:T(8,128)(2,1)S(1)}, u32[]{:S(2)}, u32[]{:S(2)}) collective-permute-start(bf16[16,64,128]{2,1,0:T(8,128)(2,1)S(1)} %get-tuple-element.43), channel_id=1, source_target_pairs={{0,0},{4,8},{8,4},{12,12},{1,1},{5,9},{9,5},{13,13},{2,2},{6,10},{... | collective-permute-start | bytes 786440 | tf_op jit(solution)/shard_map/ppermute | solution.py:26
  49.6 0.1 collective-permute-start.16
  49.6 0.1 shard_map.102
  49.7 0.5 collective-permute-done.10.refs_0_.refs_6_
  50.2 3.1 %collective-permute-start.17 = (bf16[4,4,64,128]{3,2,1,0:T(8,128)(2,1)S(1)}, bf16[4,4,64,128]{3,2,1,0:T(8,128)(2,1)S(1)}, u32[]{:S(2)}, u32[]{:S(2)}) collective-permute-start(bf16[4,4,64,128]{3,2,1,0:T(8,128)(2,1)S(1)} %get-tuple-element.48), channel_id=1, source_target_pairs={{0,0},{4,8},{8,4},{12,12},{1,1},{5,9},{9,5},{13,13},{2,2},{6,10},{... | collective-permute-start | bytes 786440 | tf_op jit(solution)/shard_map/ppermute | solution.py:26
  53.4 0.1 collective-permute-start.18
  53.5 2.4 %collective-permute-start.19 = (bf16[4,2,6,8,128]{4,3,2,1,0:T(8,128)(2,1)S(1)}, bf16[4,2,6,8,128]{4,3,2,1,0:T(8,128)(2,1)S(1)}, u32[]{:S(2)}, u32[]{:S(2)}) collective-permute-start(bf16[4,2,6,8,128]{4,3,2,1,0:T(8,128)(2,1)S(1)} %get-tuple-element.50), channel_id=1, source_target_pairs={{0,0},{4,8},{8,4},{12,12},{1,1},{5,9},{9,5},{13,13},{2,2},{6,10},{... | collective-permute-start | bytes 294920 | tf_op jit(solution)/shard_map/ppermute | solution.py:26
  55.9 2.3 %shard_map.101.total = f32[4,8,64,128]{3,2,1,0:T(8,128)S(1)} custom-call(f32[4,8,64,128]{3,2,1,0:T(8,128)S(1)} %get-tuple-element.38.early, f32[4,8,64,128]{3,2,1,0:T(8,128)S(1)} %get-tuple-element.36.late.cols, f32[8,8,64,128]{3,2,1,0:T(8,128)S(1)} %get-tuple-element.39.columns, bf16[16,64,128]{2,1,0:T(8,128)(2,1)S(1)} %collective-permute-done.10.refs_0_.refs_6_, ...), custom_call_target="tpu_custom_call" | custom-call | flops 5500000256 | bytes 100000 | tf_op jit(solution)/shard_map/pallas_call | solution.py:47
  58.2 1.2 %collective-permute-done.19.refs_5_ = bf16[4,2,6,8,128]{4,3,2,1,0:T(8,128)(2,1)S(1)} collective-permute-done((bf16[4,2,6,8,128]{4,3,2,1,0:T(8,128)(2,1)S(1)}, bf16[4,2,6,8,128]{4,3,2,1,0:T(8,128)(2,1)S(1)}, u32[]{:S(2)}, u32[]{:S(2)}) %collective-permute-start.19) | collective-permute-done | bytes 98336 | tf_op jit(solution)/shard_map/ppermute | solution.py:26
  59.4 9.2 %shard_map.103 = (f32[1,4,8,8,1024]{4,3,2,1,0:T(8,128)}, f32[4,8,8,512]{3,2,1,0:T(8,128)S(1)}, f32[4,8,8,512]{3,2,1,0:T(8,128)S(1)}) custom-call(f32[3,1024]{1,0:T(4,128)S(1)} %copy-done.3, f32[4,2048,128]{2,1,0:T(8,128)S(1)} %shard_map.96.inject, f32[4,8,64,128]{3,2,1,0:T(8,128)S(1)} %get-tuple-element.36.late.cols, ...), custom_call_target="tpu_custom_call" | custom-call | flops 12099999744 | bytes 100000 | tf_op jit(solution)/shard_map/pallas_call | solution.py:47
  68.6 1.2 %collective-permute-start.20 = (f32[4,8,8,512]{3,2,1,0:T(8,128)S(1)}, f32[4,8,8,512]{3,2,1,0:T(8,128)S(1)}, u32[]{:S(2)}, u32[]{:S(2)}) collective-permute-start(f32[4,8,8,512]{3,2,1,0:T(8,128)S(1)} %get-tuple-element.52), channel_id=1, source_target_pairs={{0,16},{16,0},{1,17},{17,1},{2,18},{18,2},{3,19},{19,3},{4,20},{20... | collective-permute-start | bytes 1572872 | tf_op jit(solution)/shard_map/ppermute | solution.py:605
  69.8 10.5 %collective-permute-done.20 = f32[4,8,8,512]{3,2,1,0:T(8,128)S(1)} collective-permute-done((f32[4,8,8,512]{3,2,1,0:T(8,128)S(1)}, f32[4,8,8,512]{3,2,1,0:T(8,128)S(1)}, u32[]{:S(2)}, u32[]{:S(2)}) %collective-permute-start.20) | collective-permute-done | bytes 524320 | tf_op jit(solution)/shard_map/ppermute | solution.py:605
  80.3 0.9 %add.19 = f32[4,8,8,512]{3,2,1,0:T(8,128)} add(f32[4,8,8,512]{3,2,1,0:T(8,128)S(1)} %get-tuple-element.51, f32[4,8,8,512]{3,2,1,0:T(8,128)S(1)} %collective-permute-done.20) | non-fusion elementwise | flops 131072 | bytes 1572864 | tf_op jit(solution)/shard_map/add | solution.py:606
  (22 shorter events, 0.1 us)
Async XLA Ops:
  0.6 9.6 %copy-start = (bf16[4,4,8,8,1024]{4,3,2,1,0:T(8,128)(2,1)S(1)}, bf16[4,4,8,8,1024]{4,3,2,1,0:T(8,128)(2,1)}, u32[]{:S(2)}) copy-start(bf16[4,4,8,8,1024]{4,3,2,1,0:T(8,128)(2,1)} %forward.1) | copy-start | bytes 6291460
  0.6 1.4 %copy-start.1 = (f32[1,4,8,8,1024]{4,3,2,1,0:T(8,128)S(1)}, f32[1,4,8,8,1024]{4,3,2,1,0:T(8,128)}, u32[]{:S(2)}) copy-start(f32[1,4,8,8,1024]{4,3,2,1,0:T(8,128)} %state.1) | copy-start | bytes 3145732
  2.0 0.9 %copy-start.2 = (f32[8,8,1024]{2,1,0:T(8,128)S(1)}, f32[8,8,1024]{2,1,0:T(8,128)}, u32[]{:S(2)}) copy-start(f32[8,8,1024]{2,1,0:T(8,128)} %speed.1) | copy-start | bytes 786436
  3.0 7.3 %copy-start.4 = (s32[256,3]{0,1:T(4,128)S(1)}, s32[256,3]{0,1:T(4,128)}, u32[]{:S(2)}) copy-start(s32[256,3]{0,1:T(4,128)} %param.13) | copy-start | bytes 9220
  3.3 20.2 %collective-permute-start.4 = (bf16[5,8,4,8,128]{4,3,2,1,0:T(8,128)(2,1)S(1)}, bf16[5,8,4,8,128]{4,3,2,1,0:T(8,128)(2,1)S(1)}, u32[]{:S(2)}, u32[]{:S(2)}) collective-permute-start(bf16[5,8,4,8,128]{4,3,2,1,0:T(8,128)(2,1)S(1)} %get-tuple-element.30), channel_id=1, source_target_pairs={{0,1},{1,0},{2,3},{3,2},{4,5},{5,4},{6,7},{7,6},{8,9},{9,8},{10,11... | collective-permute-start | bytes 983048 | tf_op jit(solution)/shard_map/ppermute | solution.py:26
  5.5 18.0 %collective-permute-start.5 = (bf16[5,8,4,8,128]{4,3,2,1,0:T(8,128)(2,1)S(1)}, bf16[5,8,4,8,128]{4,3,2,1,0:T(8,128)(2,1)S(1)}, u32[]{:S(2)}, u32[]{:S(2)}) collective-permute-start(bf16[5,8,4,8,128]{4,3,2,1,0:T(8,128)(2,1)S(1)} %get-tuple-element.31), channel_id=1, source_target_pairs={{0,0},{1,2},{2,1},{3,3},{4,4},{5,6},{6,5},{7,7},{8,8},{9,10},{10,9... | collective-permute-start | bytes 983048 | tf_op jit(solution)/shard_map/ppermute | solution.py:26
  6.2 24.8 %collective-permute-start.6 = (bf16[5,4,64,128]{3,2,1,0:T(8,128)(2,1)S(1)}, bf16[5,4,64,128]{3,2,1,0:T(8,128)(2,1)S(1)}, u32[]{:S(2)}, u32[]{:S(2)}) collective-permute-start(bf16[5,4,64,128]{3,2,1,0:T(8,128)(2,1)S(1)} %get-tuple-element.32), channel_id=1, source_target_pairs={{0,4},{4,0},{8,12},{12,8},{1,5},{5,1},{9,13},{13,9},{2,6},{6,2},{1... | collective-permute-start | bytes 983048 | tf_op jit(solution)/shard_map/ppermute | solution.py:26
  7.2 23.7 %collective-permute-start.7 = (bf16[5,4,64,128]{3,2,1,0:T(8,128)(2,1)S(1)}, bf16[5,4,64,128]{3,2,1,0:T(8,128)(2,1)S(1)}, u32[]{:S(2)}, u32[]{:S(2)}) collective-permute-start(bf16[5,4,64,128]{3,2,1,0:T(8,128)(2,1)S(1)} %get-tuple-element.33), channel_id=1, source_target_pairs={{0,0},{4,8},{8,4},{12,12},{1,1},{5,9},{9,5},{13,13},{2,2},{6,10},{... | collective-permute-start | bytes 983048 | tf_op jit(solution)/shard_map/ppermute | solution.py:26
  11.0 18.3 %copy-start.5 = (s32[256,3]{0,1:T(4,128)S(1)}, s32[256,3]{0,1:T(4,128)}, u32[]{:S(2)}) copy-start(s32[256,3]{0,1:T(4,128)} %param.14) | copy-start | bytes 9220
  11.1 18.3 %copy-start.6 = (f32[256,4]{0,1:T(4,128)S(1)}, f32[256,4]{0,1:T(4,128)}, u32[]{:S(2)}) copy-start(f32[256,4]{0,1:T(4,128)} %param.15) | copy-start | bytes 12292
  11.1 1.2 %collective-permute-start = (f32[8,256]{1,0:T(8,128)S(1)}, f32[8,256]{1,0:T(8,128)S(1)}, u32[]{:S(2)}, u32[]{:S(2)}) collective-permute-start(f32[8,256]{1,0:T(8,128)S(1)} %shard_map.95), channel_id=1, source_target_pairs={{0,4},{4,0},{8,12},{12,8},{1,5},{5,1},{9,13},{13,9},{2,6},{6,2},{1... | collective-permute-start | bytes 24584 | tf_op jit(solution)/shard_map/ppermute | solution.py:40
  12.3 2.7 %collective-permute-start.1 = (f32[8,256]{1,0:T(8,128)S(1)}, f32[8,256]{1,0:T(8,128)S(1)}, u32[]{:S(2)}, u32[]{:S(2)}) collective-permute-start(f32[8,256]{1,0:T(8,128)S(1)} %add.15), channel_id=1, source_target_pairs={{0,8},{4,12},{8,0},{12,4},{1,9},{5,13},{9,1},{13,5},{2,10},{6,14},... | collective-permute-start | bytes 24584 | tf_op jit(solution)/shard_map/ppermute | solution.py:40
  15.0 5.1 %collective-permute-start.2 = (f32[8,256]{1,0:T(8,128)S(1)}, f32[8,256]{1,0:T(8,128)S(1)}, u32[]{:S(2)}, u32[]{:S(2)}) collective-permute-start(f32[8,256]{1,0:T(8,128)S(1)} %add.16), channel_id=1, source_target_pairs={{0,1},{1,0},{2,3},{3,2},{4,5},{5,4},{6,7},{7,6},{8,9},{9,8},{10,11... | collective-permute-start | bytes 24584 | tf_op jit(solution)/shard_map/ppermute | solution.py:40
  20.1 3.4 %collective-permute-start.3 = (f32[8,256]{1,0:T(8,128)S(1)}, f32[8,256]{1,0:T(8,128)S(1)}, u32[]{:S(2)}, u32[]{:S(2)}) collective-permute-start(f32[8,256]{1,0:T(8,128)S(1)} %add.17), channel_id=1, source_target_pairs={{0,2},{1,3},{2,0},{3,1},{4,6},{5,7},{6,4},{7,5},{8,10},{9,11},{10,... | collective-permute-start | bytes 24584 | tf_op jit(solution)/shard_map/ppermute | solution.py:40
  23.6 7.3 %collective-permute-start.8 = (bf16[5,2,6,8,128]{4,3,2,1,0:T(8,128)(2,1)S(1)}, bf16[5,2,6,8,128]{4,3,2,1,0:T(8,128)(2,1)S(1)}, u32[]{:S(2)}, u32[]{:S(2)}) collective-permute-start(bf16[5,2,6,8,128]{4,3,2,1,0:T(8,128)(2,1)S(1)} %get-tuple-element.34), channel_id=1, source_target_pairs={{0,4},{4,0},{8,12},{12,8},{1,5},{5,1},{9,13},{13,9},{2,6},{6,2},{1... | collective-permute-start | bytes 368648 | tf_op jit(solution)/shard_map/ppermute | solution.py:26
  27.2 6.2 %collective-permute-start.9 = (bf16[5,2,6,8,128]{4,3,2,1,0:T(8,128)(2,1)S(1)}, bf16[5,2,6,8,128]{4,3,2,1,0:T(8,128)(2,1)S(1)}, u32[]{:S(2)}, u32[]{:S(2)}) collective-permute-start(bf16[5,2,6,8,128]{4,3,2,1,0:T(8,128)(2,1)S(1)} %get-tuple-element.35), channel_id=1, source_target_pairs={{0,0},{4,8},{8,4},{12,12},{1,1},{5,9},{9,5},{13,13},{2,2},{6,10},{... | collective-permute-start | bytes 368648 | tf_op jit(solution)/shard_map/ppermute | solution.py:26
  29.4 4.0 %copy-start.3 = (f32[3,1024]{1,0:T(4,128)S(1)}, f32[3,1024]{1,0:T(4,128)}, u32[]{:S(2)}) copy-start(f32[3,1024]{1,0:T(4,128)} %wind.3) | copy-start | bytes 36868
  39.1 8.5 %collective-permute-start.14 = (bf16[4,8,4,8,128]{4,3,2,1,0:T(8,128)(2,1)S(1)}, bf16[4,8,4,8,128]{4,3,2,1,0:T(8,128)(2,1)S(1)}, u32[]{:S(2)}, u32[]{:S(2)}) collective-permute-start(bf16[4,8,4,8,128]{4,3,2,1,0:T(8,128)(2,1)S(1)} %get-tuple-element.45), channel_id=1, source_target_pairs={{0,1},{1,0},{2,3},{3,2},{4,5},{5,4},{6,7},{7,6},{8,9},{9,8},{10,11... | collective-permute-start | bytes 786440 | tf_op jit(solution)/shard_map/ppermute | solution.py:26
  40.9 8.6 %collective-permute-start.15 = (bf16[4,8,4,8,128]{4,3,2,1,0:T(8,128)(2,1)S(1)}, bf16[4,8,4,8,128]{4,3,2,1,0:T(8,128)(2,1)S(1)}, u32[]{:S(2)}, u32[]{:S(2)}) collective-permute-start(bf16[4,8,4,8,128]{4,3,2,1,0:T(8,128)(2,1)S(1)} %get-tuple-element.46), channel_id=1, source_target_pairs={{0,0},{1,2},{2,1},{3,3},{4,4},{5,6},{6,5},{7,7},{8,8},{9,10},{10,9... | collective-permute-start | bytes 786440 | tf_op jit(solution)/shard_map/ppermute | solution.py:26
  42.4 7.8 %collective-permute-start.10 = (bf16[16,64,128]{2,1,0:T(8,128)(2,1)S(1)}, bf16[16,64,128]{2,1,0:T(8,128)(2,1)S(1)}, u32[]{:S(2)}, u32[]{:S(2)}) collective-permute-start(bf16[16,64,128]{2,1,0:T(8,128)(2,1)S(1)} %get-tuple-element.40), channel_id=1, source_target_pairs={{0,1},{1,0},{2,3},{3,2},{4,5},{5,4},{6,7},{7,6},{8,9},{9,8},{10,11... | collective-permute-start | bytes 786440 | tf_op jit(solution)/shard_map/ppermute | solution.py:26
  43.8 9.6 %collective-permute-start.11 = (bf16[16,64,128]{2,1,0:T(8,128)(2,1)S(1)}, bf16[16,64,128]{2,1,0:T(8,128)(2,1)S(1)}, u32[]{:S(2)}, u32[]{:S(2)}) collective-permute-start(bf16[16,64,128]{2,1,0:T(8,128)(2,1)S(1)} %get-tuple-element.41), channel_id=1, source_target_pairs={{0,0},{1,2},{2,1},{3,3},{4,4},{5,6},{6,5},{7,7},{8,8},{9,10},{10,9... | collective-permute-start | bytes 786440 | tf_op jit(solution)/shard_map/ppermute | solution.py:26
  44.4 9.0 %collective-permute-start.12 = (bf16[16,64,128]{2,1,0:T(8,128)(2,1)S(1)}, bf16[16,64,128]{2,1,0:T(8,128)(2,1)S(1)}, u32[]{:S(2)}, u32[]{:S(2)}) collective-permute-start(bf16[16,64,128]{2,1,0:T(8,128)(2,1)S(1)} %get-tuple-element.42), channel_id=1, source_target_pairs={{0,4},{4,0},{8,12},{12,8},{1,5},{5,1},{9,13},{13,9},{2,6},{6,2},{1... | collective-permute-start | bytes 786440 | tf_op jit(solution)/shard_map/ppermute | solution.py:26
  47.6 8.3 %collective-permute-start.13 = (bf16[16,64,128]{2,1,0:T(8,128)(2,1)S(1)}, bf16[16,64,128]{2,1,0:T(8,128)(2,1)S(1)}, u32[]{:S(2)}, u32[]{:S(2)}) collective-permute-start(bf16[16,64,128]{2,1,0:T(8,128)(2,1)S(1)} %get-tuple-element.43), channel_id=1, source_target_pairs={{0,0},{4,8},{8,4},{12,12},{1,1},{5,9},{9,5},{13,13},{2,2},{6,10},{... | collective-permute-start | bytes 786440 | tf_op jit(solution)/shard_map/ppermute | solution.py:26
  49.6 8.6 %collective-permute-start.16 = (bf16[4,4,64,128]{3,2,1,0:T(8,128)(2,1)S(1)}, bf16[4,4,64,128]{3,2,1,0:T(8,128)(2,1)S(1)}, u32[]{:S(2)}, u32[]{:S(2)}) collective-permute-start(bf16[4,4,64,128]{3,2,1,0:T(8,128)(2,1)S(1)} %get-tuple-element.47), channel_id=1, source_target_pairs={{0,4},{4,0},{8,12},{12,8},{1,5},{5,1},{9,13},{13,9},{2,6},{6,2},{1... | collective-permute-start | bytes 786440 | tf_op jit(solution)/shard_map/ppermute | solution.py:26
  50.2 8.0 %collective-permute-start.17 = (bf16[4,4,64,128]{3,2,1,0:T(8,128)(2,1)S(1)}, bf16[4,4,64,128]{3,2,1,0:T(8,128)(2,1)S(1)}, u32[]{:S(2)}, u32[]{:S(2)}) collective-permute-start(bf16[4,4,64,128]{3,2,1,0:T(8,128)(2,1)S(1)} %get-tuple-element.48), channel_id=1, source_target_pairs={{0,0},{4,8},{8,4},{12,12},{1,1},{5,9},{9,5},{13,13},{2,2},{6,10},{... | collective-permute-start | bytes 786440 | tf_op jit(solution)/shard_map/ppermute | solution.py:26
  53.4 4.8 %collective-permute-start.18 = (bf16[4,2,6,8,128]{4,3,2,1,0:T(8,128)(2,1)S(1)}, bf16[4,2,6,8,128]{4,3,2,1,0:T(8,128)(2,1)S(1)}, u32[]{:S(2)}, u32[]{:S(2)}) collective-permute-start(bf16[4,2,6,8,128]{4,3,2,1,0:T(8,128)(2,1)S(1)} %get-tuple-element.49), channel_id=1, source_target_pairs={{0,4},{4,0},{8,12},{12,8},{1,5},{5,1},{9,13},{13,9},{2,6},{6,2},{1... | collective-permute-start | bytes 294920 | tf_op jit(solution)/shard_map/ppermute | solution.py:26
  53.5 5.9 %collective-permute-start.19 = (bf16[4,2,6,8,128]{4,3,2,1,0:T(8,128)(2,1)S(1)}, bf16[4,2,6,8,128]{4,3,2,1,0:T(8,128)(2,1)S(1)}, u32[]{:S(2)}, u32[]{:S(2)}) collective-permute-start(bf16[4,2,6,8,128]{4,3,2,1,0:T(8,128)(2,1)S(1)} %get-tuple-element.50), channel_id=1, source_target_pairs={{0,0},{4,8},{8,4},{12,12},{1,1},{5,9},{9,5},{13,13},{2,2},{6,10},{... | collective-permute-start | bytes 294920 | tf_op jit(solution)/shard_map/ppermute | solution.py:26
  68.6 11.7 %collective-permute-start.20 = (f32[4,8,8,512]{3,2,1,0:T(8,128)S(1)}, f32[4,8,8,512]{3,2,1,0:T(8,128)S(1)}, u32[]{:S(2)}, u32[]{:S(2)}) collective-permute-start(f32[4,8,8,512]{3,2,1,0:T(8,128)S(1)} %get-tuple-element.52), channel_id=1, source_target_pairs={{0,16},{16,0},{1,17},{17,1},{2,18},{18,2},{3,19},{19,3},{4,20},{20... | collective-permute-start | bytes 1572872 | tf_op jit(solution)/shard_map/ppermute | solution.py:605

commit v3 on v2

--- a/solution.py
+++ b/solution.py
@@ -98,22 +98,37 @@
                 value = load(f, x, y0, HALO).reshape(HALO, ROWS, LANES)
                 z_out[odd][f, x] = value.astype(BF)
             for j in range(HALO):
-                x_out[odd][f, j] = load(f, x0 + j, 0, width_y).astype(BF)
-
-
-def pack_corners(place, fields, width_x, z_in, c_out):
+                x_out[odd][HALO * f + j] = load(f, x0 + j, 0, width_y).astype(BF)
+
+
+def corner_blocks(fields, width_y):
+    return -(-2 * fields * len(CORNER) // width_y)
+
+
+def corner_place(fields, odd_y, f, k, width_y):
+    n = (odd_y * fields + f) * len(CORNER) + k
+    return n // width_y, pl.ds(n % width_y * ROWS, 2 * ROWS)
+
+
+def pack_corners(place, fields, width_x, width_y, z_in, outs, firsts):
     for odd_x in (0, 1):
         plus_x = place.plus("gx", odd_x)
         for odd_y in (0, 1):
             plus_y = place.plus("gy", odd_y)
             for f in range(fields):
-                for k, (i, j) in enumerate(CORNER):
-                    x = jnp.where(plus_x, width_x - i, i - 1)
-                    y = jnp.where(plus_y, j - 1, HALO - j)
-                    c_out[odd_x][f, odd_y, k] = z_in[odd_y][f, x, y]
-
-
-def place_edges(place, store, fields, width_x, width_y, z_in, x_in, c_in):
+                for k in range(0, len(CORNER), 2):
+                    two = []
+                    for i, j in CORNER[k : k + 2]:
+                        x = jnp.where(plus_x, width_x - i, i - 1)
+                        y = jnp.where(plus_y, j - 1, HALO - j)
+                        two.append(z_in[odd_y][f, x, y].astype(F32))
+                    block, rows = corner_place(fields, odd_y, f, k, width_y)
+                    outs[odd_x][firsts[odd_x] + block, rows, :] = jnp.concatenate(
+                        two, axis=0
+                    ).astype(BF)
+
+
+def place_edges(place, store, fields, width_x, width_y, z_in, x_in, c_in, firsts):
     def masked(value, *conditions):
         value = value.astype(F32)
         for condition in conditions:
@@ -129,19 +144,24 @@
                 value = masked(z_in[odd][f, x], place.has("gy", odd))
                 store(f, HALO + x, y0, HALO, value.reshape(HALO * ROWS, LANES))
             for j in range(HALO):
-                store(f, x0 + j, HALO, width_y, masked(x_in[odd][f, j], place.has("gx", odd)))
+                value = masked(x_in[odd][HALO * f + j], place.has("gx", odd))
+                store(f, x0 + j, HALO, width_y, value)
     for odd_x in (0, 1):
         plus_x = place.plus("gx", odd_x)
         for odd_y in (0, 1):
             plus_y = place.plus("gy", odd_y)
             for f in range(fields):
-                for k, (i, j) in enumerate(CORNER):
-                    value = masked(
-                        c_in[odd_x][f, odd_y, k], place.has("gx", odd_x), place.has("gy", odd_y)
+                for k in range(0, len(CORNER), 2):
+                    block, rows = corner_place(fields, odd_y, f, k, width_y)
+                    two = masked(
+                        c_in[odd_x][firsts[odd_x] + block, rows, :],
+                        place.has("gx", odd_x),
+                        place.has("gy", odd_y),
                     )
-                    x = jnp.where(plus_x, HALO + width_x - 1 + i, HALO - i)
-                    y = jnp.where(plus_y, HALO + width_y - 1 + j, HALO - j)
-                    store(f, x, y, 1, value)
+                    for n, (i, j) in enumerate(CORNER[k : k + 2]):
+                        x = jnp.where(plus_x, HALO + width_x - 1 + i, HALO - i)
+                        y = jnp.where(plus_y, HALO + width_y - 1 + j, HALO - j)
+                        store(f, x, y, 1, two[n * ROWS : (n + 1) * ROWS])
 
 
 class Altitude:
@@ -275,12 +295,6 @@
     row(width_x - 1)
 
 
-def face_structs(fields, width_x, width_y):
-    faces_z = [struct((fields, width_x, HALO, ROWS, LANES), BF)] * 2
-    faces_x = [struct((fields, HALO, width_y * ROWS, LANES), BF)] * 2
-    return faces_z + faces_x
-
-
 def shards(
     sound_speed_sq,
     wind_profile,
@@ -297,22 +311,41 @@
     ext_x, ext_y = width_x + 2 * HALO, width_y + 2 * HALO
     blocks = depth // LANES
     assert blocks == ROWS and steps_total == 2 * PER_ROUND and slots % LANES == 0
+    assert width_x == width_y and width_x % 2 == 0
     tile = (width_x, width_y * ROWS, LANES)
     ext = (ext_x, ext_y * ROWS, LANES)
-
-    def exchanged(faces, fields):
-        z = [swapped(faces[odd], "gy", odd) for odd in (0, 1)]
-        x = [swapped(faces[2 + odd], "gx", odd) for odd in (0, 1)]
-
-        def corner_kernel(z_even, z_odd, *outs):
-            pack_corners(Place(), fields, width_x, (z_even, z_odd), outs)
-
-        shape = (fields, 2, len(CORNER), ROWS, LANES)
-        corners = call(corner_kernel, [struct(shape, BF)] * 2, micros=0.7, limit=8)(*z)
-        corners = [swapped(corners[odd], "gx", odd) for odd in (0, 1)]
-        return z + x + corners
-
-    def pack_kernel(state, speed, cols, speed_cols, *outs):
+    block = (width_y * ROWS, LANES)
+    forward_fields = 4 * steps_total
+
+    def face_structs(fields, more=0):
+        z = struct((fields, width_x, HALO, ROWS, LANES), BF)
+        return [z, z, struct((HALO * fields,) + block, BF), struct((HALO * fields + more,) + block, BF)]
+
+    def second_hop(fields, z, faces, *more):
+        extra = sum(m.shape[0] for m in more)
+        corners = corner_blocks(fields, width_y)
+
+        def corner_kernel(z_even, z_odd, faces, *refs):
+            even, odd = refs[-2:]
+            even[: HALO * fields] = faces[...]
+            at = HALO * fields
+            for ref in refs[:-2]:
+                even[at : at + ref.shape[0]] = ref[...]
+                at += ref.shape[0]
+            pack_corners(Place(), fields, width_x, width_y, (z_even, z_odd), (even, odd), (at, 0))
+
+        even, odd = call(
+            corner_kernel,
+            [
+                struct((HALO * fields + extra + corners,) + block, BF),
+                struct((corners,) + block, BF),
+            ],
+            micros=0.3,
+            limit=8,
+        )(*z, faces, *more)
+        return swapped(even, "gx", 0), swapped(odd, "gx", 1)
+
+    def pack_kernel(state, speed, source, pressure, cols, speed_cols, sample, *outs):
         place = Place()
         for x in range(width_x):
             for b in range(blocks):
@@ -328,17 +361,8 @@
 
         pack_faces(place, load, 5, width_x, width_y, outs[:2], outs[2:])
 
-    packed = call(
-        pack_kernel,
-        [struct((4,) + tile, F32), struct(tile, F32)] + face_structs(5, width_x, width_y),
-        micros=1.2,
-    )(adjoint_state, sound_speed_sq)
-    cols, speed_cols = packed[:2]
-    first_halo = exchanged(packed[2:], 5)
-
-    def sample_kernel(source, pressure, out):
-        local_x = source[0:1] - lax.axis_index("gx") * width_x
-        local_y = source[1:2] - lax.axis_index("gy") * width_y
+        local_x = source[0:1] - place.index["gx"] * width_x
+        local_y = source[1:2] - place.index["gy"] * width_y
         inside = (local_x >= 0) & (local_x < width_x) & (local_y >= 0) & (local_y < width_y)
         where = jnp.where(inside, local_x * width_y + local_y, -1)
         cells = width_x * width_y
@@ -356,20 +380,54 @@
             )
             picked = jnp.sum(jnp.where(level, columns, 0.0), axis=0, keepdims=True)
             result = jnp.where(row == t, picked, result)
-        out[...] = result
-
-    samples = call(
-        sample_kernel,
-        struct((ROWS, slots), F32),
-        specs=[
-            pl.BlockSpec(memory_space=VMEM),
-            pl.BlockSpec((steps_total, 1, width_x, width_y, depth), lambda i: (0, 0, 0, 0, 0)),
-        ],
+        sample[...] = result
+
+    whole = pl.BlockSpec(memory_space=VMEM)
+    packed = call(
+        pack_kernel,
+        [struct((4,) + tile, F32), struct(tile, F32), struct((ROWS, slots), F32)] + face_structs(5),
+        specs=[whole] * 3
+        + [pl.BlockSpec((steps_total, 1, width_x, width_y, depth), lambda i: (0, 0, 0, 0, 0))],
         grid=(1,),
-        micros=1.2,
-        limit=12,
-    )(source_cells.T, forward_field)
+        micros=1.5,
+    )(adjoint_state, sound_speed_sq, source_cells.T, forward_field)
+    cols, speed_cols, samples = packed[:3]
+    z_even, z_odd, x_even, x_odd = packed[3:]
+    z_first = [swapped(z_even, "gy", 0), swapped(z_odd, "gy", 1)]
+    x_first = swapped(x_odd, "gx", 1)
     samples = summed(samples)
+
+    def forward_kernel(forward, early, late, *edges):
+        place = Place()
+
+        def one(n, carry):
+            t, f = n // 4, lax.rem(n, 4)
+            for ref, snap in ((late, t), (early, t + PER_ROUND)):
+                number = snap * 4 + f
+                for x in range(width_x):
+                    for b in range(blocks):
+                        ref[n, x, pl.ds(b, width_y, stride=ROWS), :] = forward[
+                            snap, f, x, :, b * LANES : (b + 1) * LANES
+                        ].astype(F32)
+                for odd in (0, 1):
+                    y = jnp.where(place.plus("gy", odd), width_y - 1, 0)
+                    x = jnp.where(place.plus("gx", odd), width_x - 1, 0)
+                    edges[2 + odd][number] = ref[n, x].astype(BF)
+                    edges[odd][number] = ref[n, :, column_rows(y, 1), :].reshape(block).astype(BF)
+            return carry
+
+        lax.fori_loop(0, 4 * PER_ROUND, one, 0)
+
+    made = call(
+        forward_kernel,
+        [struct((4 * PER_ROUND,) + tile, F32)] * 2 + [struct((forward_fields,) + block, BF)] * 4,
+        micros=0.9,
+    )(forward_field)
+    forward_early, forward_late, edge_z_even, edge_z_odd, edge_x_even, edge_x_odd = made
+    rim_z = [swapped(edge_z_even, "gy", 0), swapped(edge_z_odd, "gy", 1)]
+    hop_even, hop_odd = second_hop(5, z_first, x_even, edge_x_even)
+    rim_at = HALO * 5
+    corners_at = (rim_at + forward_fields, 0)
 
     def inject_kernel(counts, receiver, misfit, sample, out):
         local_x = receiver[0:1] - (lax.axis_index("gx") * width_x - HALO)
@@ -403,54 +461,20 @@
         micros=1.8,
     )(pair_counts, receiver_cells.T, residuals.T, samples)
 
-    def forward_kernel(forward, early, late, *edges):
-        place = Place()
-
-        def one(n, carry):
-            t, f = n // 4, lax.rem(n, 4)
-            for ref, snap in ((late, t), (early, t + PER_ROUND)):
-                number = snap * 4 + f
-                for x in range(width_x):
-                    for b in range(blocks):
-                        ref[n, x, pl.ds(b, width_y, stride=ROWS), :] = forward[
-                            snap, f, x, :, b * LANES : (b + 1) * LANES
-                        ].astype(F32)
-                for odd in (0, 1):
-                    y = jnp.where(place.plus("gy", odd), width_y - 1, 0)
-                    x = jnp.where(place.plus("gx", odd), width_x - 1, 0)
-                    edges[2 + odd][number] = ref[n, x].astype(BF)
-                    edges[odd][number] = ref[n, :, column_rows(y, 1), :].reshape(
-                        width_x * ROWS, LANES
-                    ).astype(BF)
-            return carry
-
-        lax.fori_loop(0, 4 * PER_ROUND, one, 0)
-
-    forward_struct = struct((4 * PER_ROUND,) + tile, F32)
-    edge_structs = [struct((4 * steps_total, n * ROWS, LANES), BF) for n in (width_x, width_y)]
-    made = call(
-        forward_kernel,
-        [forward_struct] * 2 + [edge_structs[0]] * 2 + [edge_structs[1]] * 2,
-        micros=2.0,
-    )(forward_field)
-    forward_early, forward_late = made[:2]
-    rim = [swapped(made[2 + odd], "gy", odd) for odd in (0, 1)]
-    rim += [swapped(made[4 + odd], "gx", odd) for odd in (0, 1)]
-
     rim_scratch = [
-        VMEM((2, 4 * PER_ROUND, width_x * ROWS, LANES), F32),
-        VMEM((2, 4 * PER_ROUND, width_y * ROWS, LANES), F32),
+        VMEM((2, 4 * PER_ROUND) + block, F32),
+        VMEM((2, 4 * PER_ROUND) + block, F32),
     ]
 
-    def forward_of(place, columns, first, rim, rim_y, rim_x):
-        for odd in (0, 1):
-            for axis, source, target in (("gy", rim[odd], rim_y), ("gx", rim[2 + odd], rim_x)):
-                side = jnp.where(place.plus(axis, odd), 1, 0)
-                for n in range(4 * PER_ROUND):
-                    value = source[4 * first + n].astype(F32)
-                    if odd:
-                        value = jnp.where(place.has(axis, odd), value, 0.0)
-                    target[side, n] = value
+    def forward_of(place, columns, first, rims, rim_y, rim_x):
+        for axis, odd, source, at in rims:
+            target = rim_y if axis == "gy" else rim_x
+            side = jnp.where(place.plus(axis, odd), 1, 0)
+            for n in range(4 * PER_ROUND):
+                value = source[at + 4 * first + n].astype(F32)
+                if odd:
+                    value = jnp.where(place.has(axis, odd), value, 0.0)
+                target[side, n] = value
 
         def reader(snap):
             base = 4 * (snap - first)
@@ -493,7 +517,7 @@
     def own(ref, f, x, y, n):
         return ref[f, HALO + x, column_rows(HALO + y, n), :]
 
-    def fill(place, buffer, speed, cols, speed_cols, halo):
+    def fill(place, buffer, speed, cols, speed_cols, z_in, x_in, c_in, firsts):
         def store(f, x, y, n, value):
             ref = buffer.at[f] if f < 4 else speed
             ref[x, column_rows(y, n), :] = value
@@ -506,16 +530,12 @@
             fields = 5
             for x in range(width_x):
                 store(4, HALO + x, HALO, width_y, speed_cols[x])
-        place_edges(place, store, fields, width_x, width_y, halo[:2], halo[2:4], halo[4:])
-
-    halos, faces = 6, 4
-
-    def first_kernel(wind, inject, cols, speed_cols, *refs):
-        halo, refs = refs[:halos], refs[halos:]
-        early, late, speed, edges = refs[0], refs[1], refs[2], refs[3 : 3 + faces]
-        here, there, carry_dz = refs[3 + faces :]
+        place_edges(place, store, fields, width_x, width_y, z_in, x_in, c_in, firsts)
+
+    def first_kernel(wind, inject, cols, speed_cols, edge_x, z0, z1, x1, c0, c1, *refs):
+        early, late, speed, *faces, here, there, carry_dz = refs
         place = Place()
-        fill(place, here, speed, cols, speed_cols, halo)
+        fill(place, here, speed, cols, speed_cols, (z0, z1), (c0, x1), (c0, c1), corners_at)
 
         def after(altitude, s, snap, state):
             out = (early, late)[s]
@@ -528,22 +548,35 @@
         def load(f, x, y, n):
             return own(here, f, x, y, n)
 
-        pack_faces(place, load, 4, width_x, width_y, edges[:2], edges[2:])
-
+        pack_faces(place, load, 4, width_x, width_y, faces[:2], faces[2:])
+        faces[3][HALO * 4 :] = edge_x[...]
+
+    injected, *rim_z = lax.optimization_barrier((injected, *rim_z))
     first = call(
         first_kernel,
-        [struct((4,) + tile, F32)] * 2 + [struct(ext, F32)] + face_structs(4, width_x, width_y),
+        [struct((4,) + tile, F32)] * 2 + [struct(ext, F32)] + face_structs(4, forward_fields),
         scratch=[VMEM((4,) + ext, F32)] * 2 + [VMEM(ext, F32)],
-        micros=8.0,
+        micros=6.0,
         limit=28,
-    )(wind_profile, injected, cols, speed_cols, *first_halo)
-    early, late, speed_ext = first[:3]
-    second_halo = exchanged(first[3:], 4)
-
-    def early_kernel(early, late, columns, *refs):
-        rim, total, rim_y, rim_x = refs[:4], refs[4], refs[5], refs[6]
+    )(
+        wind_profile, injected, cols, speed_cols, edge_x_odd, *z_first, x_first, hop_even, hop_odd
+    )
+    early, late, speed_ext, z_even, z_odd, x_even, x_odd = first
+    z_second = [swapped(z_even, "gy", 0), swapped(z_odd, "gy", 1)]
+    x_second = swapped(x_odd, "gx", 1)
+    again_even, again_odd = second_hop(4, z_second, x_even)
+
+    def rims(z_even, z_odd, x_even, x_odd):
+        return (
+            ("gy", 0, z_even, 0),
+            ("gy", 1, z_odd, 0),
+            ("gx", 0, x_even, rim_at),
+            ("gx", 1, x_odd, HALO * 4),
+        )
+
+    def early_kernel(early, late, columns, z0, z1, c0, x1, total, rim_y, rim_x):
         altitude = Altitude()
-        reader = forward_of(Place(), columns, PER_ROUND, rim, rim_y, rim_x)
+        reader = forward_of(Place(), columns, PER_ROUND, rims(z0, z1, c0, x1), rim_y, rim_x)
         total[...] = jnp.zeros_like(total)
         for s, state in ((0, early), (1, late)):
             add_increment(
@@ -555,19 +588,20 @@
                 width_y,
             )
 
-    total = call(
-        early_kernel, struct((4,) + tile, F32), scratch=rim_scratch, micros=5.0, limit=16
-    )(early, late, forward_early, *rim)
+    total = call(early_kernel, struct((4,) + tile, F32), scratch=rim_scratch, micros=2.3, limit=16)(
+        early, late, forward_early, *rim_z, hop_even, x_second
+    )
 
     half = depth // 2
-
-    def second_kernel(wind, inject, cols, speed, total, columns, *refs):
-        halo, rim, refs = refs[:halos], refs[halos : halos + 4], refs[halos + 4 :]
-        final, mine, other = refs[:3]
-        here, there, carry_dz, sums, rim_y, rim_x = refs[3:]
+    half_blocks = blocks // 2
+
+    def second_kernel(
+        wind, inject, cols, speed, total, columns, rz0, rz1, rx0, z0, z1, x1, c0, c1, *refs
+    ):
+        final, mine, other, scales, here, there, carry_dz, sums, rim_y, rim_x = refs
         place = Place()
-        fill(place, here, None, cols, None, halo)
-        reader = forward_of(place, columns, 0, rim, rim_y, rim_x)
+        fill(place, here, None, cols, None, (z0, z1), (c0, x1), (c0, c1), (HALO * 4, 0))
+        reader = forward_of(place, columns, 0, rims(rz0, rz1, rx0, x1), rim_y, rim_x)
         sums[...] = total[...]
 
         def after(altitude, s, snap, state):
@@ -582,28 +616,70 @@
 
         run_round(place, 1, wind, inject, (here, there), speed, carry_dz, after)
         me = lax.axis_index("pair")
+
+        def sums_at(f, x, part, b):
+            return sums[f, x, pl.ds(part * half_blocks + b, width_y, stride=ROWS), :]
+
+        for f in range(4):
+            for b in range(half_blocks):
+                here_lanes = slice(b * LANES, (b + 1) * LANES)
+                largest = jnp.abs(sums_at(f, 0, 1 - me, b))
+                for x in range(1, width_x):
+                    largest = jnp.maximum(largest, jnp.abs(sums_at(f, x, 1 - me, b)))
+                largest = jnp.maximum(jnp.max(largest, axis=0, keepdims=True), 1e-30)
+                scales[f : f + 1, here_lanes] = largest * (0.5 / 32767.0)
+                inverse = 32767.0 / largest
+                for x in range(0, width_x, 2):
+                    two = [sums_at(f, x + i, 1 - me, b) * inverse for i in (0, 1)]
+                    two = jnp.round(jnp.concatenate(two, axis=0))
+                    other[f, x // 2, :, here_lanes] = two.astype(jnp.int32).astype(jnp.int16)
         for f in range(4):
             for x in range(width_x):
                 for b in range(blocks):
                     final[0, f, x, :, b * LANES : (b + 1) * LANES] = here[
                         f, HALO + x, pl.ds(HALO * ROWS + b, width_y, stride=ROWS), :
                     ]
-                for b in range(blocks // 2):
-                    for ref, part in ((mine, me), (other, 1 - me)):
-                        ref[f, x, :, b * LANES : (b + 1) * LANES] = 0.5 * sums[
-                            f, x, pl.ds(part * (blocks // 2) + b, width_y, stride=ROWS), :
-                        ]
+                for b in range(half_blocks):
+                    mine[f, x, :, b * LANES : (b + 1) * LANES] = 0.5 * sums_at(f, x, me, b)
 
     kernel_half = struct((4, width_x, width_y, half), F32)
-    final, mine, other = call(
+    final, mine, other, scales = call(
         second_kernel,
-        [struct(adjoint_state.shape, F32), kernel_half, kernel_half],
+        [
+            struct(adjoint_state.shape, F32),
+            kernel_half,
+            struct((4, width_x // 2, 2 * width_y, half), jnp.int16),
+            struct((4, half), F32),
+        ],
         scratch=[VMEM((4,) + ext, F32)] * 2 + [VMEM(ext, F32), VMEM((4,) + tile, F32)] + rim_scratch,
-        micros=11.0,
+        micros=9.0,
         limit=30,
-    )(wind_profile, injected, late, speed_ext, total, forward_late, *second_halo, *rim)
-    received = lax.ppermute(other, "pair", [(0, 1), (1, 0)])
-    return (mine + received, final)
+    )(
+        wind_profile,
+        injected,
+        late,
+        speed_ext,
+        total,
+        forward_late,
+        *rim_z,
+        hop_even,
+        *z_second,
+        x_second,
+        again_even,
+        again_odd,
+    )
+    across = [(0, 1), (1, 0)]
+    other, scales = lax.ppermute(other, "pair", across), lax.ppermute(scales, "pair", across)
+
+    def sum_kernel(mine, other, scales, out):
+        for f in range(4):
+            for x in range(0, width_x, 2):
+                two = other[f, x // 2].astype(jnp.int32).astype(F32) * scales[f : f + 1]
+                for i in (0, 1):
+                    out[f, x + i] = mine[f, x + i] + two[i * width_y : (i + 1) * width_y]
+
+    kernels = call(sum_kernel, kernel_half, micros=0.8, limit=8)(mine, other, scales)
+    return (kernels, final)
 
 
 def solution(mesh):

time: 81.5 us -> 84.4 us (1.036); the launches traced: 81.2 us -> 82.8 us
  waiting for transfers between devices: 23.8 us -> 20.9 us
  starting transfers between devices: 31.8 us -> 34 us
  local copies, waits for them, and re-layouts: 2.34 us -> 4.46 us
  Pallas kernels: 20.8 us -> 22 us
  other arithmetic: 0.89 us -> 0.01 us
    ppermute x1 -> x2, waiting for transfers between devices: 10.5 us -> 4.88 us  [the longest x1 4.88 us: shards(): lax.ppermute(scales, 'pair', across)]
    ppermute x16 -> x12, waiting for transfers between devices: 7.26 us -> 10.7 us  [swapped(): return lax.ppermute(x, axis, swap_pairs(lax.axis_size(axis), odd))]
    ppermute x16 -> x12, starting transfers between devices: 24.8 us -> 27.6 us  [swapped(): return lax.ppermute(x, axis, swap_pairs(lax.axis_size(axis), odd))]
    unnamed x14 -> x16, local copies, waits for them, and re-layouts: 2.34 us -> 4.46 us
    pallas_call x9, Pallas kernels: 20.8 us -> 22 us  [run(): pl.pallas_call(kernel, out_shape=outs, grid=grid, in_specs=specs or [pl.B...]
    add x1 -> x0, other arithmetic: 0.88 us -> none  [shards(): return (mine + received, final)]
  transfers between devices with their start and end apart: 21 -> 18, of which waited for: 9 -> 9; matrix products, arithmetic and copies ran while one was open for 0% -> 0% of each run, Pallas kernels for 7% -> 6%
where the time goes in v3:
time: 84.4 us; the launch traced here: 82.8 us
  starting transfers between devices  34 us (40%)
  Pallas kernels  22 us (26%)
  waiting for transfers between devices  20.9 us (25%)
  local copies, waits for them, and re-layouts  4.46 us (5%)
  between operations  1.49 us (2%)
    ppermute x12, starting transfers between devices, swapped(): return lax.ppermute(x, axis, swap_pairs(lax.axis_size(axis), odd))  27.6 us
    pallas_call x9, Pallas kernels, run(): pl.pallas_call(kernel, out_shape=outs, grid=grid, in_specs=specs or [pl.B...  22 us
    ppermute x12, waiting for transfers between devices, swapped(): return lax.ppermute(x, axis, swap_pairs(lax.axis_size(axis), odd))  10.7 us
    ppermute x4, waiting for transfers between devices, summed(): x = x + lax.ppermute(x, axis, [(i, i ^ k) for i in range(size)])  5.32 us
    ppermute x4, starting transfers between devices, summed(): x = x + lax.ppermute(x, axis, [(i, i ^ k) for i in range(size)])  4.91 us
    ppermute x1, waiting for transfers between devices, shards(): lax.ppermute(scales, 'pair', across)  4.88 us
    unnamed x16, local copies, waits for them, and re-layouts  4.46 us
  transfers between devices with their start and end apart: 18, of which 9 were waited for; matrix products, arithmetic and copies ran while one was open for 0% of the time, Pallas kernels for 6%

profile of v3, /device:TPU:1, one launch (start us, length us, event | category | flops | bytes accessed | tf_op | source)
XLA Modules:
  0.0 82.8 jit_solution(4166724210690295457)
XLA Ops:
  0.6 1.6 %copy-done = bf16[4,4,8,8,1024]{4,3,2,1,0:T(8,128)(2,1)S(1)} copy-done((bf16[4,4,8,8,1024]{4,3,2,1,0:T(8,128)(2,1)S(1)}, bf16[4,4,8,8,1024]{4,3,2,1,0:T(8,128)(2,1)}, u32[]{:S(2)}) %copy-start) | copy-done | bytes 2097176
  2.2 1.2 %copy-done.2 = f32[1,4,8,8,1024]{4,3,2,1,0:T(8,128)S(1)} copy-done((f32[1,4,8,8,1024]{4,3,2,1,0:T(8,128)S(1)}, f32[1,4,8,8,1024]{4,3,2,1,0:T(8,128)}, u32[]{:S(2)}) %copy-start.2) | copy-done | bytes 1048600
  3.5 0.9 %copy-done.3 = f32[8,8,1024]{2,1,0:T(8,128)S(1)} copy-done((f32[8,8,1024]{2,1,0:T(8,128)S(1)}, f32[8,8,1024]{2,1,0:T(8,128)}, u32[]{:S(2)}) %copy-start.3) | copy-done | bytes 262168
  4.4 0.7 copy-done.5
  5.1 1.1 %shard_map.95 = (f32[4,8,64,128]{3,2,1,0:T(8,128)S(1)}, f32[8,64,128]{2,1,0:T(8,128)S(1)}, f32[8,256]{1,0:T(8,128)S(1)}, bf16[5,8,4,8,128]{4,3,2,1,0:T(8,128)(2,...) custom-call(f32[1,4,8,8,1024]{4,3,2,1,0:T(8,128)S(1)} %copy-done.2, ...), custom_call_target="tpu_custom_call" | custom-call | flops 1650000000 | bytes 100000 | tf_op jit(solution)/shard_map/pallas_call | solution.py:47
  6.1 2.2 %collective-permute-start.6 = (bf16[5,8,4,8,128]{4,3,2,1,0:T(8,128)(2,1)S(1)}, bf16[5,8,4,8,128]{4,3,2,1,0:T(8,128)(2,1)S(1)}, u32[]{:S(2)}, u32[]{:S(2)}) collective-permute-start(bf16[5,8,4,8,128]{4,3,2,1,0:T(8,128)(2,1)S(1)} %get-tuple-element.40), channel_id=1, source_target_pairs={{0,1},{1,0},{2,3},{3,2},{4,5},{5,4},{6,7},{7,6},{8,9},{9,8},{10,11... | collective-permute-start | bytes 983048 | tf_op jit(solution)/shard_map/ppermute | solution.py:26
  8.3 0.8 collective-permute-start.7
  9.2 0.8 shard_map.97
  10.0 5.8 %collective-permute-done.6.z_even.z0 = bf16[5,8,4,8,128]{4,3,2,1,0:T(8,128)(2,1)S(1)} collective-permute-done((bf16[5,8,4,8,128]{4,3,2,1,0:T(8,128)(2,1)S(1)}, bf16[5,8,4,8,128]{4,3,2,1,0:T(8,128)(2,1)S(1)}, u32[]{:S(2)}, u32[]{:S(2)}) %collective-permute-start.6) | collective-permute-done | bytes 327712 | tf_op jit(solution)/shard_map/ppermute | solution.py:26
  15.8 0.0 collective-permute-done.7.z_odd.z1
  15.8 0.1 shard_map.98
  15.9 1.3 %collective-permute-start.9 = (bf16[44,64,128]{2,1,0:T(8,128)(2,1)S(1)}, bf16[44,64,128]{2,1,0:T(8,128)(2,1)S(1)}, u32[]{:S(2)}, u32[]{:S(2)}) collective-permute-start(bf16[44,64,128]{2,1,0:T(8,128)(2,1)S(1)} %get-tuple-element.45), channel_id=1, source_target_pairs={{0,4},{4,0},{8,12},{12,8},{1,5},{5,1},{9,13},{13,9},{2,6},{6,2},{1... | collective-permute-start | bytes 2162696 | tf_op jit(solution)/shard_map/ppermute | solution.py:26
  17.2 3.2 %collective-permute-start.8 = (bf16[20,64,128]{2,1,0:T(8,128)(2,1)S(1)}, bf16[20,64,128]{2,1,0:T(8,128)(2,1)S(1)}, u32[]{:S(2)}, u32[]{:S(2)}) collective-permute-start(bf16[20,64,128]{2,1,0:T(8,128)(2,1)S(1)} %get-tuple-element.42), channel_id=1, source_target_pairs={{0,0},{4,8},{8,4},{12,12},{1,1},{5,9},{9,5},{13,13},{2,2},{6,10},{... | collective-permute-start | bytes 983048 | tf_op jit(solution)/shard_map/ppermute | solution.py:26
  20.4 4.5 %collective-permute-start.4 = (bf16[16,64,128]{2,1,0:T(8,128)(2,1)S(1)}, bf16[16,64,128]{2,1,0:T(8,128)(2,1)S(1)}, u32[]{:S(2)}, u32[]{:S(2)}) collective-permute-start(bf16[16,64,128]{2,1,0:T(8,128)(2,1)S(1)} %get-tuple-element.34), channel_id=1, source_target_pairs={{0,1},{1,0},{2,3},{3,2},{4,5},{5,4},{6,7},{7,6},{8,9},{9,8},{10,11... | collective-permute-start | bytes 786440 | tf_op jit(solution)/shard_map/ppermute | solution.py:26
  24.9 0.7 collective-permute-start.5
  25.6 0.1 collective-permute-start
  25.7 1.2 %collective-permute-done = f32[8,256]{1,0:T(8,128)S(1)} collective-permute-done((f32[8,256]{1,0:T(8,128)S(1)}, f32[8,256]{1,0:T(8,128)S(1)}, u32[]{:S(2)}, u32[]{:S(2)}) %collective-permute-start) | collective-permute-done | bytes 8224 | tf_op jit(solution)/shard_map/ppermute | solution.py:40
  26.8 0.6 collective-permute-start.1
  27.5 1.9 %collective-permute-done.1 = f32[8,256]{1,0:T(8,128)S(1)} collective-permute-done((f32[8,256]{1,0:T(8,128)S(1)}, f32[8,256]{1,0:T(8,128)S(1)}, u32[]{:S(2)}, u32[]{:S(2)}) %collective-permute-start.1) | collective-permute-done | bytes 8224 | tf_op jit(solution)/shard_map/ppermute | solution.py:40
  29.3 2.7 %collective-permute-start.2 = (f32[8,256]{1,0:T(8,128)S(1)}, f32[8,256]{1,0:T(8,128)S(1)}, u32[]{:S(2)}, u32[]{:S(2)}) collective-permute-start(f32[8,256]{1,0:T(8,128)S(1)} %add.13), channel_id=1, source_target_pairs={{0,1},{1,0},{2,3},{3,2},{4,5},{5,4},{6,7},{7,6},{8,9},{9,8},{10,11... | collective-permute-start | bytes 24584 | tf_op jit(solution)/shard_map/ppermute | solution.py:40
  32.0 1.0 %collective-permute-done.2 = f32[8,256]{1,0:T(8,128)S(1)} collective-permute-done((f32[8,256]{1,0:T(8,128)S(1)}, f32[8,256]{1,0:T(8,128)S(1)}, u32[]{:S(2)}, u32[]{:S(2)}) %collective-permute-start.2) | collective-permute-done | bytes 8224 | tf_op jit(solution)/shard_map/ppermute | solution.py:40
  33.1 1.5 %collective-permute-start.3 = (f32[8,256]{1,0:T(8,128)S(1)}, f32[8,256]{1,0:T(8,128)S(1)}, u32[]{:S(2)}, u32[]{:S(2)}) collective-permute-start(f32[8,256]{1,0:T(8,128)S(1)} %add.14), channel_id=1, source_target_pairs={{0,2},{1,3},{2,0},{3,1},{4,6},{5,7},{6,4},{7,5},{8,10},{9,11},{10,... | collective-permute-start | bytes 24584 | tf_op jit(solution)/shard_map/ppermute | solution.py:40
  35.2 1.3 %collective-permute-done.3 = f32[8,256]{1,0:T(8,128)S(1)} collective-permute-done((f32[8,256]{1,0:T(8,128)S(1)}, f32[8,256]{1,0:T(8,128)S(1)}, u32[]{:S(2)}, u32[]{:S(2)}) %collective-permute-start.3) | collective-permute-done | bytes 8224 | tf_op jit(solution)/shard_map/ppermute | solution.py:40
  36.5 5.9 %collective-permute-start.10 = (bf16[8,64,128]{2,1,0:T(8,128)(2,1)S(1)}, bf16[8,64,128]{2,1,0:T(8,128)(2,1)S(1)}, u32[]{:S(2)}, u32[]{:S(2)}) collective-permute-start(bf16[8,64,128]{2,1,0:T(8,128)(2,1)S(1)} %get-tuple-element.46), channel_id=1, source_target_pairs={{0,0},{4,8},{8,4},{12,12},{1,1},{5,9},{9,5},{13,13},{2,2},{6,10},{... | collective-permute-start | bytes 393224 | tf_op jit(solution)/shard_map/ppermute | solution.py:26
  42.5 0.0 copy-start.4
  42.5 1.5 %shard_map.96.inject = f32[4,2048,128]{2,1,0:T(8,128)S(1)} custom-call(s32[1]{0:T(128)S(6)} %copy.10.counts, s32[3,256]{1,0:T(4,128)S(1)} %bitcast.4, f32[4,256]{1,0:T(4,128)S(1)} %bitcast.5, f32[8,256]{1,0:T(8,128)S(1)} %add.15.sample), custom_call_target="tpu_custom_call" | custom-call | flops 1980000000 | bytes 100000 | tf_op jit(solution)/shard_map/pallas_call | solution.py:47
  44.0 0.0 collective-permute-done.4.z0.rz0
  44.0 0.0 collective-permute-done.5.z1.rz1
  44.0 0.0 collective-permute-done.8.x1
  44.0 1.0 %collective-permute-done.10.c1 = bf16[8,64,128]{2,1,0:T(8,128)(2,1)S(1)} collective-permute-done((bf16[8,64,128]{2,1,0:T(8,128)(2,1)S(1)}, bf16[8,64,128]{2,1,0:T(8,128)(2,1)S(1)}, u32[]{:S(2)}, u32[]{:S(2)}) %collective-permute-start.10) | collective-permute-done | bytes 131104 | tf_op jit(solution)/shard_map/ppermute | solution.py:26
  45.1 0.0 collective-permute-done.9.c0.rx0
  45.1 5.8 %shard_map.99 = (f32[4,8,64,128]{3,2,1,0:T(8,128)S(1)}, f32[4,8,64,128]{3,2,1,0:T(8,128)S(1)}, f32[16,128,128]{2,1,0:T(8,128)S(1)}, bf16[4,8,4,8,128]{4,3,2,1,0:...) custom-call(f32[3,1024]{1,0:T(4,128)S(1)} %copy-done.4, ...), custom_call_target="tpu_custom_call" | custom-call | flops 6600000000 | bytes 100000 | tf_op jit(solution)/shard_map/pallas_call | solution.py:47
  50.9 3.6 %collective-permute-start.11 = (bf16[32,64,128]{2,1,0:T(8,128)(2,1)S(1)}, bf16[32,64,128]{2,1,0:T(8,128)(2,1)S(1)}, u32[]{:S(2)}, u32[]{:S(2)}) collective-permute-start(bf16[32,64,128]{2,1,0:T(8,128)(2,1)S(1)} %get-tuple-element.53), channel_id=1, source_target_pairs={{0,0},{4,8},{8,4},{12,12},{1,1},{5,9},{9,5},{13,13},{2,2},{6,10},{... | collective-permute-start | bytes 1572872 | tf_op jit(solution)/shard_map/ppermute | solution.py:26
  54.5 1.8 %collective-permute-start.12 = (bf16[4,8,4,8,128]{4,3,2,1,0:T(8,128)(2,1)S(1)}, bf16[4,8,4,8,128]{4,3,2,1,0:T(8,128)(2,1)S(1)}, u32[]{:S(2)}, u32[]{:S(2)}) collective-permute-start(bf16[4,8,4,8,128]{4,3,2,1,0:T(8,128)(2,1)S(1)} %get-tuple-element.55), channel_id=1, source_target_pairs={{0,1},{1,0},{2,3},{3,2},{4,5},{5,4},{6,7},{7,6},{8,9},{9,8},{10,11... | collective-permute-start | bytes 786440 | tf_op jit(solution)/shard_map/ppermute | solution.py:26
  56.3 0.7 collective-permute-start.13
  57.0 3.1 %collective-permute-done.12.z_even.z0 = bf16[4,8,4,8,128]{4,3,2,1,0:T(8,128)(2,1)S(1)} collective-permute-done((bf16[4,8,4,8,128]{4,3,2,1,0:T(8,128)(2,1)S(1)}, bf16[4,8,4,8,128]{4,3,2,1,0:T(8,128)(2,1)S(1)}, u32[]{:S(2)}, u32[]{:S(2)}) %collective-permute-start.12) | collective-permute-done | bytes 262176 | tf_op jit(solution)/shard_map/ppermute | solution.py:26
  60.1 0.0 collective-permute-done.13.z_odd.z1
  60.1 0.1 shard_map.101
  60.2 0.1 collective-permute-start.14
  60.2 2.8 %collective-permute-start.15 = (bf16[6,64,128]{2,1,0:T(8,128)(2,1)S(1)}, bf16[6,64,128]{2,1,0:T(8,128)(2,1)S(1)}, u32[]{:S(2)}, u32[]{:S(2)}) collective-permute-start(bf16[6,64,128]{2,1,0:T(8,128)(2,1)S(1)} %get-tuple-element.59), channel_id=1, source_target_pairs={{0,0},{4,8},{8,4},{12,12},{1,1},{5,9},{9,5},{13,13},{2,2},{6,10},{... | collective-permute-start | bytes 294920 | tf_op jit(solution)/shard_map/ppermute | solution.py:26
  63.1 2.4 %shard_map.100.total = f32[4,8,64,128]{3,2,1,0:T(8,128)S(1)} custom-call(f32[4,8,64,128]{3,2,1,0:T(8,128)S(1)} %get-tuple-element.49.early, f32[4,8,64,128]{3,2,1,0:T(8,128)S(1)} %get-tuple-element.47.late.cols, f32[8,8,64,128]{3,2,1,0:T(8,128)S(1)} %get-tuple-element.50.columns, bf16[16,64,128]{2,1,0:T(8,128)(2,1)S(1)} %collective-permute-done.4.z0.rz0, ...), custom_call_target="tpu_custom_call" | custom-call | flops 2529999872 | bytes 100000 | tf_op jit(solution)/shard_map/pallas_call | solution.py:47
  65.5 0.7 collective-permute-done.15.c1
  66.2 0.0 collective-permute-done.14.c0
  66.2 9.4 %shard_map.102 = (f32[1,4,8,8,1024]{4,3,2,1,0:T(8,128)}, f32[4,8,8,512]{3,2,1,0:T(8,128)S(1)}, s16[4,4,16,512]{3,2,1,0:T(8,128)(2,1)S(1)}, f32[4,512]{1,0:T(4,128)S(1)}) custom-call(f32[3,1024]{1,0:T(4,128)S(1)} %copy-done.4, f32[4,2048,128]{2,1,0:T(8,128)S(1)} %shard_map.96.inject, f32[4,8,64,128]{3,2,1,0:T(8,128)S(1)} %get-tuple-element.47.late.cols, ...), custom_call_target="tpu_custom_call" | custom-call | flops 9900000256 | bytes 100000 | tf_op jit(solution)/shard_map/pallas_call | solution.py:47
  75.5 1.2 %collective-permute-start.16 = (s16[4,4,16,512]{3,2,1,0:T(8,128)(2,1)S(1)}, s16[4,4,16,512]{3,2,1,0:T(8,128)(2,1)S(1)}, u32[]{:S(2)}, u32[]{:S(2)}) collective-permute-start(s16[4,4,16,512]{3,2,1,0:T(8,128)(2,1)S(1)} %get-tuple-element.61), channel_id=1, source_target_pairs={{0,16},{16,0},{1,17},{17,1},{2,18},{18,2},{3,19},{19,3},{4,20},{20... | collective-permute-start | bytes 786440 | tf_op jit(solution)/shard_map/ppermute | solution.py:672
  76.7 0.3 collective-permute-start.17
  77.0 4.9 %collective-permute-done.17.scales = f32[4,512]{1,0:T(4,128)S(1)} collective-permute-done((f32[4,512]{1,0:T(4,128)S(1)}, f32[4,512]{1,0:T(4,128)S(1)}, u32[]{:S(2)}, u32[]{:S(2)}) %collective-permute-start.17) | collective-permute-done | bytes 8224 | tf_op jit(solution)/shard_map/ppermute | solution.py:672
  81.9 0.9 %shard_map.103 = f32[4,8,8,512]{3,2,1,0:T(8,128)} custom-call(f32[4,8,8,512]{3,2,1,0:T(8,128)S(1)} %get-tuple-element.60.mine, s16[4,4,16,512]{3,2,1,0:T(8,128)(2,1)S(1)} %collective-permute-done.16.other, f32[4,512]{1,0:T(4,128)S(1)} %collective-permute-done.17.scales), custom_call_target="tpu_custom_call" | custom-call | flops 880000000 | bytes 100000 | tf_op jit(solution)/shard_map/pallas_call | solution.py:47
  (17 shorter events, 0.0 us)
Async XLA Ops:
  0.6 1.6 %copy-start = (bf16[4,4,8,8,1024]{4,3,2,1,0:T(8,128)(2,1)S(1)}, bf16[4,4,8,8,1024]{4,3,2,1,0:T(8,128)(2,1)}, u32[]{:S(2)}) copy-start(bf16[4,4,8,8,1024]{4,3,2,1,0:T(8,128)(2,1)} %forward.1) | copy-start | bytes 6291460
  2.2 1.2 %copy-start.2 = (f32[1,4,8,8,1024]{4,3,2,1,0:T(8,128)S(1)}, f32[1,4,8,8,1024]{4,3,2,1,0:T(8,128)}, u32[]{:S(2)}) copy-start(f32[1,4,8,8,1024]{4,3,2,1,0:T(8,128)} %state.1) | copy-start | bytes 3145732
  3.4 0.9 %copy-start.3 = (f32[8,8,1024]{2,1,0:T(8,128)S(1)}, f32[8,8,1024]{2,1,0:T(8,128)}, u32[]{:S(2)}) copy-start(f32[8,8,1024]{2,1,0:T(8,128)} %speed.1) | copy-start | bytes 786436
  4.4 0.7 copy-start.5
  5.1 4.1 %copy-start.1 = (bf16[4,4,8,8,1024]{4,3,2,1,0:T(8,128)(2,1)S(1)}, bf16[4,4,8,8,1024]{4,3,2,1,0:T(8,128)(2,1)}, u32[]{:S(2)}) copy-start(bf16[4,4,8,8,1024]{4,3,2,1,0:T(8,128)(2,1)} %forward.1) | copy-start | bytes 6291460
  6.1 9.6 %collective-permute-start.6 = (bf16[5,8,4,8,128]{4,3,2,1,0:T(8,128)(2,1)S(1)}, bf16[5,8,4,8,128]{4,3,2,1,0:T(8,128)(2,1)S(1)}, u32[]{:S(2)}, u32[]{:S(2)}) collective-permute-start(bf16[5,8,4,8,128]{4,3,2,1,0:T(8,128)(2,1)S(1)} %get-tuple-element.40), channel_id=1, source_target_pairs={{0,1},{1,0},{2,3},{3,2},{4,5},{5,4},{6,7},{7,6},{8,9},{9,8},{10,11... | collective-permute-start | bytes 983048 | tf_op jit(solution)/shard_map/ppermute | solution.py:26
  8.3 34.1 %copy-start.6 = (s32[256,3]{0,1:T(4,128)S(1)}, s32[256,3]{0,1:T(4,128)}, u32[]{:S(2)}) copy-start(s32[256,3]{0,1:T(4,128)} %param.14) | copy-start | bytes 9220
  8.3 34.1 %copy-start.7 = (f32[256,4]{0,1:T(4,128)S(1)}, f32[256,4]{0,1:T(4,128)}, u32[]{:S(2)}) copy-start(f32[256,4]{0,1:T(4,128)} %param.15) | copy-start | bytes 12292
  8.3 7.4 %collective-permute-start.7 = (bf16[5,8,4,8,128]{4,3,2,1,0:T(8,128)(2,1)S(1)}, bf16[5,8,4,8,128]{4,3,2,1,0:T(8,128)(2,1)S(1)}, u32[]{:S(2)}, u32[]{:S(2)}) collective-permute-start(bf16[5,8,4,8,128]{4,3,2,1,0:T(8,128)(2,1)S(1)} %get-tuple-element.41), channel_id=1, source_target_pairs={{0,0},{1,2},{2,1},{3,3},{4,4},{5,6},{6,5},{7,7},{8,8},{9,10},{10,9... | collective-permute-start | bytes 983048 | tf_op jit(solution)/shard_map/ppermute | solution.py:26
  15.9 29.2 %collective-permute-start.9 = (bf16[44,64,128]{2,1,0:T(8,128)(2,1)S(1)}, bf16[44,64,128]{2,1,0:T(8,128)(2,1)S(1)}, u32[]{:S(2)}, u32[]{:S(2)}) collective-permute-start(bf16[44,64,128]{2,1,0:T(8,128)(2,1)S(1)} %get-tuple-element.45), channel_id=1, source_target_pairs={{0,4},{4,0},{8,12},{12,8},{1,5},{5,1},{9,13},{13,9},{2,6},{6,2},{1... | collective-permute-start | bytes 2162696 | tf_op jit(solution)/shard_map/ppermute | solution.py:26
  17.2 26.8 %collective-permute-start.8 = (bf16[20,64,128]{2,1,0:T(8,128)(2,1)S(1)}, bf16[20,64,128]{2,1,0:T(8,128)(2,1)S(1)}, u32[]{:S(2)}, u32[]{:S(2)}) collective-permute-start(bf16[20,64,128]{2,1,0:T(8,128)(2,1)S(1)} %get-tuple-element.42), channel_id=1, source_target_pairs={{0,0},{4,8},{8,4},{12,12},{1,1},{5,9},{9,5},{13,13},{2,2},{6,10},{... | collective-permute-start | bytes 983048 | tf_op jit(solution)/shard_map/ppermute | solution.py:26
  20.4 23.6 %collective-permute-start.4 = (bf16[16,64,128]{2,1,0:T(8,128)(2,1)S(1)}, bf16[16,64,128]{2,1,0:T(8,128)(2,1)S(1)}, u32[]{:S(2)}, u32[]{:S(2)}) collective-permute-start(bf16[16,64,128]{2,1,0:T(8,128)(2,1)S(1)} %get-tuple-element.34), channel_id=1, source_target_pairs={{0,1},{1,0},{2,3},{3,2},{4,5},{5,4},{6,7},{7,6},{8,9},{9,8},{10,11... | collective-permute-start | bytes 786440 | tf_op jit(solution)/shard_map/ppermute | solution.py:26
  24.9 19.1 %collective-permute-start.5 = (bf16[16,64,128]{2,1,0:T(8,128)(2,1)S(1)}, bf16[16,64,128]{2,1,0:T(8,128)(2,1)S(1)}, u32[]{:S(2)}, u32[]{:S(2)}) collective-permute-start(bf16[16,64,128]{2,1,0:T(8,128)(2,1)S(1)} %get-tuple-element.35), channel_id=1, source_target_pairs={{0,0},{1,2},{2,1},{3,3},{4,4},{5,6},{6,5},{7,7},{8,8},{9,10},{10,9... | collective-permute-start | bytes 786440 | tf_op jit(solution)/shard_map/ppermute | solution.py:26
  25.6 1.2 %collective-permute-start = (f32[8,256]{1,0:T(8,128)S(1)}, f32[8,256]{1,0:T(8,128)S(1)}, u32[]{:S(2)}, u32[]{:S(2)}) collective-permute-start(f32[8,256]{1,0:T(8,128)S(1)} %get-tuple-element.33), channel_id=1, source_target_pairs={{0,4},{4,0},{8,12},{12,8},{1,5},{5,1},{9,13},{13,9},{2,6},{6,2},{1... | collective-permute-start | bytes 24584 | tf_op jit(solution)/shard_map/ppermute | solution.py:40
  26.8 2.5 %collective-permute-start.1 = (f32[8,256]{1,0:T(8,128)S(1)}, f32[8,256]{1,0:T(8,128)S(1)}, u32[]{:S(2)}, u32[]{:S(2)}) collective-permute-start(f32[8,256]{1,0:T(8,128)S(1)} %add.12), channel_id=1, source_target_pairs={{0,8},{4,12},{8,0},{12,4},{1,9},{5,13},{9,1},{13,5},{2,10},{6,14},... | collective-permute-start | bytes 24584 | tf_op jit(solution)/shard_map/ppermute | solution.py:40
  29.3 3.7 %collective-permute-start.2 = (f32[8,256]{1,0:T(8,128)S(1)}, f32[8,256]{1,0:T(8,128)S(1)}, u32[]{:S(2)}, u32[]{:S(2)}) collective-permute-start(f32[8,256]{1,0:T(8,128)S(1)} %add.13), channel_id=1, source_target_pairs={{0,1},{1,0},{2,3},{3,2},{4,5},{5,4},{6,7},{7,6},{8,9},{9,8},{10,11... | collective-permute-start | bytes 24584 | tf_op jit(solution)/shard_map/ppermute | solution.py:40
  33.1 3.4 %collective-permute-start.3 = (f32[8,256]{1,0:T(8,128)S(1)}, f32[8,256]{1,0:T(8,128)S(1)}, u32[]{:S(2)}, u32[]{:S(2)}) collective-permute-start(f32[8,256]{1,0:T(8,128)S(1)} %add.14), channel_id=1, source_target_pairs={{0,2},{1,3},{2,0},{3,1},{4,6},{5,7},{6,4},{7,5},{8,10},{9,11},{10,... | collective-permute-start | bytes 24584 | tf_op jit(solution)/shard_map/ppermute | solution.py:40
  36.5 8.6 %collective-permute-start.10 = (bf16[8,64,128]{2,1,0:T(8,128)(2,1)S(1)}, bf16[8,64,128]{2,1,0:T(8,128)(2,1)S(1)}, u32[]{:S(2)}, u32[]{:S(2)}) collective-permute-start(bf16[8,64,128]{2,1,0:T(8,128)(2,1)S(1)} %get-tuple-element.46), channel_id=1, source_target_pairs={{0,0},{4,8},{8,4},{12,12},{1,1},{5,9},{9,5},{13,13},{2,2},{6,10},{... | collective-permute-start | bytes 393224 | tf_op jit(solution)/shard_map/ppermute | solution.py:26
  42.5 2.6 %copy-start.4 = (f32[3,1024]{1,0:T(4,128)S(1)}, f32[3,1024]{1,0:T(4,128)}, u32[]{:S(2)}) copy-start(f32[3,1024]{1,0:T(4,128)} %wind.3) | copy-start | bytes 36868
  50.9 12.2 %collective-permute-start.11 = (bf16[32,64,128]{2,1,0:T(8,128)(2,1)S(1)}, bf16[32,64,128]{2,1,0:T(8,128)(2,1)S(1)}, u32[]{:S(2)}, u32[]{:S(2)}) collective-permute-start(bf16[32,64,128]{2,1,0:T(8,128)(2,1)S(1)} %get-tuple-element.53), channel_id=1, source_target_pairs={{0,0},{4,8},{8,4},{12,12},{1,1},{5,9},{9,5},{13,13},{2,2},{6,10},{... | collective-permute-start | bytes 1572872 | tf_op jit(solution)/shard_map/ppermute | solution.py:26
  54.5 5.5 %collective-permute-start.12 = (bf16[4,8,4,8,128]{4,3,2,1,0:T(8,128)(2,1)S(1)}, bf16[4,8,4,8,128]{4,3,2,1,0:T(8,128)(2,1)S(1)}, u32[]{:S(2)}, u32[]{:S(2)}) collective-permute-start(bf16[4,8,4,8,128]{4,3,2,1,0:T(8,128)(2,1)S(1)} %get-tuple-element.55), channel_id=1, source_target_pairs={{0,1},{1,0},{2,3},{3,2},{4,5},{5,4},{6,7},{7,6},{8,9},{9,8},{10,11... | collective-permute-start | bytes 786440 | tf_op jit(solution)/shard_map/ppermute | solution.py:26
  56.3 3.8 %collective-permute-start.13 = (bf16[4,8,4,8,128]{4,3,2,1,0:T(8,128)(2,1)S(1)}, bf16[4,8,4,8,128]{4,3,2,1,0:T(8,128)(2,1)S(1)}, u32[]{:S(2)}, u32[]{:S(2)}) collective-permute-start(bf16[4,8,4,8,128]{4,3,2,1,0:T(8,128)(2,1)S(1)} %get-tuple-element.56), channel_id=1, source_target_pairs={{0,0},{1,2},{2,1},{3,3},{4,4},{5,6},{6,5},{7,7},{8,8},{9,10},{10,9... | collective-permute-start | bytes 786440 | tf_op jit(solution)/shard_map/ppermute | solution.py:26
  60.2 6.0 %collective-permute-start.14 = (bf16[22,64,128]{2,1,0:T(8,128)(2,1)S(1)}, bf16[22,64,128]{2,1,0:T(8,128)(2,1)S(1)}, u32[]{:S(2)}, u32[]{:S(2)}) collective-permute-start(bf16[22,64,128]{2,1,0:T(8,128)(2,1)S(1)} %get-tuple-element.58), channel_id=1, source_target_pairs={{0,4},{4,0},{8,12},{12,8},{1,5},{5,1},{9,13},{13,9},{2,6},{6,2},{1... | collective-permute-start | bytes 1081352 | tf_op jit(solution)/shard_map/ppermute | solution.py:26
  60.2 5.9 %collective-permute-start.15 = (bf16[6,64,128]{2,1,0:T(8,128)(2,1)S(1)}, bf16[6,64,128]{2,1,0:T(8,128)(2,1)S(1)}, u32[]{:S(2)}, u32[]{:S(2)}) collective-permute-start(bf16[6,64,128]{2,1,0:T(8,128)(2,1)S(1)} %get-tuple-element.59), channel_id=1, source_target_pairs={{0,0},{4,8},{8,4},{12,12},{1,1},{5,9},{9,5},{13,13},{2,2},{6,10},{... | collective-permute-start | bytes 294920 | tf_op jit(solution)/shard_map/ppermute | solution.py:26
  75.5 6.4 %collective-permute-start.16 = (s16[4,4,16,512]{3,2,1,0:T(8,128)(2,1)S(1)}, s16[4,4,16,512]{3,2,1,0:T(8,128)(2,1)S(1)}, u32[]{:S(2)}, u32[]{:S(2)}) collective-permute-start(s16[4,4,16,512]{3,2,1,0:T(8,128)(2,1)S(1)} %get-tuple-element.61), channel_id=1, source_target_pairs={{0,16},{16,0},{1,17},{17,1},{2,18},{18,2},{3,19},{19,3},{4,20},{20... | collective-permute-start | bytes 786440 | tf_op jit(solution)/shard_map/ppermute | solution.py:672
  76.7 5.1 %collective-permute-start.17 = (f32[4,512]{1,0:T(4,128)S(1)}, f32[4,512]{1,0:T(4,128)S(1)}, u32[]{:S(2)}, u32[]{:S(2)}) collective-permute-start(f32[4,512]{1,0:T(4,128)S(1)} %get-tuple-element.62), channel_id=1, source_target_pairs={{0,16},{16,0},{1,17},{17,1},{2,18},{18,2},{3,19},{19,3},{4,20},{20... | collective-permute-start | bytes 24584 | tf_op jit(solution)/shard_map/ppermute | solution.py:672

commit v4 on v3

v4 whole, which is shorter than its diff:
```python
import jax
import jax.numpy as jnp
from jax import lax
from jax.experimental import pallas as pl
from jax.experimental.pallas import tpu as pltpu
from jax.sharding import PartitionSpec as P

step_length = 0.25
SCALE = 0.5 * step_length
HALO = 4
PER_ROUND = 2
LANES = 128
ROWS = 8
VMEM = pltpu.VMEM
CORNER = [(i, j) for i in range(1, HALO) for j in range(1, HALO) if i + j <= HALO]
BF = jnp.bfloat16
F32 = jnp.float32


def swap_pairs(size, odd):
    partner = [((i - odd) ^ 1) + odd for i in range(size)]
    return [(i, j if 0 <= j < size else i) for i, j in enumerate(partner)]


def swapped(x, axis, odd):
    return lax.ppermute(x, axis, swap_pairs(lax.axis_size(axis), odd))


def diagonal(x, odd_x, odd_y):
    size_x, size_y = lax.axis_size("gx"), lax.axis_size("gy")
    pairs = [
        (i * size_y + j, k * size_y + m)
        for i, k in swap_pairs(size_x, odd_x)
        for j, m in swap_pairs(size_y, odd_y)
    ]
    return lax.ppermute(x, ("gx", "gy"), pairs)


def total_of(x, axis):
    size = lax.axis_size(axis)
    parts = [lax.ppermute(x, axis, [(i, (i + k) % size) for i in range(size)]) for k in range(1, size)]
    return sum(parts, x)


def summed(x, axis, k):
    size = lax.axis_size(axis)
    assert size & (size - 1) == 0
    while k < size:
        x = x + lax.ppermute(x, axis, [(i, i ^ k) for i in range(size)])
        k *= 2
    return x


def call(kernel, outs, scratch=(), micros=1.0, specs=None, out_specs=None, limit=16):
    def run(*args):
        return pl.pallas_call(
            kernel,
            out_shape=outs,
            in_specs=specs or [pl.BlockSpec(memory_space=VMEM)] * len(args),
            out_specs=out_specs
            or jax.tree.map(lambda _: pl.BlockSpec(memory_space=VMEM), outs),
            scratch_shapes=list(scratch),
            compiler_params=pltpu.CompilerParams(vmem_limit_bytes=limit * 2**20),
            cost_estimate=pl.CostEstimate(
                flops=int(1.1e9 * micros), bytes_accessed=100_000, transcendentals=0
            ),
        )(*args)

    return run


def struct(shape, dtype):
    return jax.ShapeDtypeStruct(shape, dtype)


class Place:
    def __init__(self):
        self.index = {}
        self.size = {}
        for axis in ("gx", "gy"):
            self.index[axis] = lax.axis_index(axis)
            self.size[axis] = lax.axis_size(axis)

    def plus(self, axis, odd):
        return lax.rem(self.index[axis], 2) == odd

    def has(self, axis, odd):
        i = self.index[axis]
        if not odd:
            return None
        return jnp.logical_and(i > 0, i < self.size[axis] - 1)


def column_rows(y, n):
    start = y * ROWS
    if not isinstance(start, int):
        start = pl.multiple_of(start, ROWS)
    return pl.ds(start, n * ROWS)


def pack_faces(place, load, fields, width_x, width_y, z_out, x_out, d_out):
    for odd in (0, 1):
        plus_y = place.plus("gy", odd)
        y0 = jnp.where(plus_y, width_y - HALO, 0)
        x0 = jnp.where(place.plus("gx", odd), width_x - HALO, 0)
        plus_x = place.plus("gx", 1)
        for f in range(fields):
            for x in range(width_x):
                value = load(f, x, y0, HALO).reshape(HALO, ROWS, LANES)
                z_out[odd][pl.ds((f * width_x + x) * HALO, HALO)] = value.astype(BF)
            for j in range(HALO):
                x_out[odd][HALO * f + j] = load(f, x0 + j, 0, width_y).astype(BF)
            for k, (i, j) in enumerate(CORNER):
                x = jnp.where(plus_x, width_x - i, i - 1)
                y = jnp.where(plus_y, width_y - j, j - 1)
                d_out[odd][f * len(CORNER) + k] = load(f, x, y, 1).astype(BF)


def corner_blocks(fields, width_y):
    return -(-2 * fields * len(CORNER) // width_y)


def corner_place(fields, odd_y, f, k, width_y):
    n = (odd_y * fields + f) * len(CORNER) + k
    return n // width_y, pl.ds(n % width_y * ROWS, 2 * ROWS)


def pack_corners(place, fields, width_x, width_y, z_in, out, first):
    plus_x = place.plus("gx", 0)
    for odd_y in (0, 1):
        plus_y = place.plus("gy", odd_y)
        for f in range(fields):
            for k in range(0, len(CORNER), 2):
                two = []
                for i, j in CORNER[k : k + 2]:
                    x = jnp.where(plus_x, width_x - i, i - 1)
                    y = jnp.where(plus_y, j - 1, HALO - j)
                    two.append(z_in[odd_y][(f * width_x + x) * HALO + y].astype(F32))
                block, rows = corner_place(fields, odd_y, f, k, width_y)
                out[first + block, rows, :] = jnp.concatenate(two, axis=0).astype(BF)


def place_edges(place, store, fields, width_x, width_y, z_in, x_in, c_in, first, d_in):
    def masked(value, *conditions):
        value = value.astype(F32)
        for condition in conditions:
            if condition is not None:
                value = jnp.where(condition, value, 0.0)
        return value

    for odd in (0, 1):
        y0 = jnp.where(place.plus("gy", odd), width_y + HALO, 0)
        x0 = jnp.where(place.plus("gx", odd), width_x + HALO, 0)
        for f in range(fields):
            for x in range(width_x):
                value = z_in[odd][pl.ds((f * width_x + x) * HALO, HALO)]
                value = masked(value, place.has("gy", odd))
                store(f, HALO + x, y0, HALO, value.reshape(HALO * ROWS, LANES))
            for j in range(HALO):
                value = masked(x_in[odd][HALO * f + j], place.has("gx", odd))
                store(f, x0 + j, HALO, width_y, value)
    for odd_x in (0, 1):
        plus_x = place.plus("gx", odd_x)
        for odd_y in (0, 1):
            plus_y = place.plus("gy", odd_y)
            for f in range(fields):
                for k in range(0, len(CORNER), 2):
                    if odd_x:
                        n = f * len(CORNER) + k
                        two = [d_in[odd_y][n], d_in[odd_y][n + 1]]
                    else:
                        block, rows = corner_place(fields, odd_y, f, k, width_y)
                        two = c_in[first + block, rows, :].astype(F32)
                        two = [two[:ROWS], two[ROWS:]]
                    for value, (i, j) in zip(two, CORNER[k : k + 2]):
                        x = jnp.where(plus_x, HALO + width_x - 1 + i, HALO - i)
                        y = jnp.where(plus_y, HALO + width_y - 1 + j, HALO - j)
                        value = masked(value, place.has("gx", odd_x), place.has("gy", odd_y))
                        store(f, x, y, 1, value)


class Altitude:
    def __init__(self):
        lane = lax.broadcasted_iota(jnp.int32, (ROWS, LANES), 1)
        row = lax.broadcasted_iota(jnp.int32, (ROWS, LANES), 0)
        self.last_lane = lane == LANES - 1
        self.first_lane = lane == 0
        self.last_row = row == ROWS - 1
        self.first_row = row == 0

    def __call__(self, v):
        up = pltpu.roll(v, LANES - 1, 1)
        carried = jnp.where(self.last_row, 0.0, pltpu.roll(up, ROWS - 1, 0))
        up = jnp.where(self.last_lane, carried, up)
        down = pltpu.roll(v, 1, 1)
        carried = jnp.where(self.first_row, 0.0, pltpu.roll(down, 1, 0))
        down = jnp.where(self.first_lane, carried, down)
        return up - down


def over_diamond(radius, width_x, width_y, row, sides):
    def own(i, carry):
        row(HALO + i, HALO - radius, width_y + 2 * radius, None)
        return carry

    lax.fori_loop(0, width_x, own, 0)
    for d in range(1, radius + 1):
        rest = radius - d
        row(HALO - d, HALO - rest, width_y + 2 * rest, sides[0])
        row(HALO + width_x - 1 + d, HALO - rest, width_y + 2 * rest, sides[1])


def advance(place, altitude, old, new, state_dz, wind, inject, radius, first, width_x, width_y):
    east, north, vertical = wind
    speed, dz_az, dz_p = state_dz
    sides = {
        axis: [
            jnp.where(place.index[axis] == edge, 0.0, 1.0) for edge in (0, place.size[axis] - 1)
        ]
        for axis in ("gx", "gy")
    }

    def at(ref, x, y):
        return ref[x, column_rows(y, 1), :]

    def inside(value, kept, y):
        if y < HALO or y >= HALO + width_y:
            side = sides["gy"][int(y > HALO)]
            kept = side if kept is None else kept * side
        return value if kept is None else value * kept

    p, ax, ay, az = (old.at[f] for f in range(4))

    def p_row(x, y0, n, kept):
        ps = [at(p, x, y0 + k - 1) for k in range(n + 2)]
        ays = [at(ay, x, y0 + k - 1) for k in range(n + 2)]
        for k in range(n):
            y = y0 + k
            up = altitude(at(az, x, y))
            dz_az[x, column_rows(y, 1), :] = up
            up_p = altitude(ps[k + 1]) if first else at(dz_p, x, y)
            div = (at(ax, x + 1, y) - at(ax, x - 1, y)) + (ays[k + 2] - ays[k]) + up
            value = (
                at(speed, x, y) * div
                + east * (at(p, x + 1, y) - at(p, x - 1, y))
                + north * (ps[k + 2] - ps[k])
                + vertical * up_p
            )
            value = ps[k + 1] + value + inject(x, y)
            new[0, x, column_rows(y, 1), :] = inside(value, kept, y)

    over_diamond(radius, width_x, width_y, p_row, sides["gx"])
    pn = new.at[0]

    def a_row(x, y0, n, kept):
        ps = [at(pn, x, y0 + k - 1) for k in range(n + 2)]
        for f, a in ((1, ax), (2, ay), (3, az)):
            vs = [at(a, x, y0 + k - 1) for k in range(n + 2)]
            for k in range(n):
                y = y0 + k
                if f == 1:
                    grad = at(pn, x + 1, y) - at(pn, x - 1, y)
                elif f == 2:
                    grad = ps[k + 2] - ps[k]
                else:
                    grad = altitude(ps[k + 1])
                    if radius > 1:
                        dz_p[x, column_rows(y, 1), :] = grad
                up = at(dz_az, x, y) if f == 3 else altitude(vs[k + 1])
                value = (
                    SCALE * grad
                    + east * (at(a, x + 1, y) - at(a, x - 1, y))
                    + north * (vs[k + 2] - vs[k])
                    + vertical * up
                )
                new[f, x, column_rows(y, 1), :] = inside(vs[k + 1] + value, kept, y)

    over_diamond(radius - 1, width_x, width_y, a_row, sides["gx"])


def add_increment(state, forward, forward_dz, total, width_x, width_y):
    def row(i):
        for k in range(width_y):
            p, ax, ay, az = (state(f, i, k) for f in range(4))
            dx = [forward(f, i + 1, k) - forward(f, i - 1, k) for f in range(4)]
            dy = [forward(f, i, k + 1) - forward(f, i, k - 1) for f in range(4)]
            dz = [forward_dz(f, i, k) for f in range(4)]
            rows = column_rows(k, 1)
            total[0, i, rows, :] += p * (dx[1] + dy[2] + dz[3])
            for n, d in ((1, dx), (2, dy), (3, dz)):
                total[n, i, rows, :] += p * d[0] + ax * d[1] + ay * d[2] + az * d[3]

    def inner(i, carry):
        row(i)
        return carry

    row(0)
    lax.fori_loop(1, width_x - 1, inner, 0)
    row(width_x - 1)


def shards(
    sound_speed_sq,
    wind_profile,
    forward_field,
    adjoint_state,
    pair_counts,
    source_cells,
    receiver_cells,
    residuals,
):
    steps_total = forward_field.shape[0]
    width_x, width_y, depth = sound_speed_sq.shape
    slots = residuals.shape[0]
    ext_x, ext_y = width_x + 2 * HALO, width_y + 2 * HALO
    blocks = depth // LANES
    assert blocks == ROWS and steps_total == 2 * PER_ROUND and slots % (2 * LANES) == 0 and slots <= 8 * LANES
    assert width_x == width_y and width_x % 2 == 0
    tile = (width_x, width_y * ROWS, LANES)
    ext = (ext_x, ext_y * ROWS, LANES)
    block = (width_y * ROWS, LANES)
    forward_fields = 4 * steps_total

    def face_structs(fields, more=0):
        z = struct((HALO * width_x * fields + more // 2 * width_x, ROWS, LANES), BF)
        x = [struct((HALO * fields + more,) + block, BF)] * 2
        d = struct((len(CORNER) * fields, ROWS, LANES), BF)
        return [z, z, *x, d, d]

    def first_hop(faces):
        z_even, z_odd, _, x_odd, d_even, d_odd = faces
        z = [swapped(z_even, "gy", 0), swapped(z_odd, "gy", 1)]
        return z, swapped(x_odd, "gx", 1), [diagonal(d_even, 1, 0), diagonal(d_odd, 1, 1)]

    def second_hop(fields, z, faces, *sample):
        at = faces.shape[0]
        ahead = at + len(sample)

        def corner_kernel(z_even, z_odd, faces, *refs):
            even = refs[len(sample)]
            even[:at] = faces[...]
            if sample:
                for n, lanes in enumerate(range(0, slots, 2 * LANES)):
                    two = [refs[0][:, lanes + i : lanes + i + LANES] for i in (0, LANES)]
                    rows = pl.ds(2 * ROWS * n, 2 * ROWS)
                    even[at, rows, :] = jnp.concatenate(two, axis=0).astype(BF)
                for odd, ref in ((0, z_even), (1, z_odd)):
                    for n in range(4 * PER_ROUND):
                        value = ref[pl.ds(rim_z_at + n * width_x, width_x)].reshape(block)
                        refs[2][4 * PER_ROUND * odd + n] = value
            pack_corners(Place(), fields, width_x, width_y, (z_even, z_odd), even, ahead)

        outs = [struct((ahead + corner_blocks(fields, width_y),) + block, BF)]
        if sample:
            outs.append(struct((8 * PER_ROUND,) + block, BF))
        made = call(corner_kernel, outs, micros=0.3, limit=8)(*z, faces, *sample)
        return [swapped(made[0], "gx", 0), *made[1:]]

    whole = pl.BlockSpec(memory_space=VMEM)
    remain = pl.BlockSpec(memory_space=pltpu.HBM)

    def sample_kernel(source, forward, sample, pressure, done):
        copy = pltpu.make_async_copy(forward.at[:, 0], pressure, done)
        copy.start()
        local_x = source[0:1] - lax.axis_index("gx") * width_x
        local_y = source[1:2] - lax.axis_index("gy") * width_y
        inside = (local_x >= 0) & (local_x < width_x) & (local_y >= 0) & (local_y < width_y)
        where = jnp.where(inside, local_x * width_y + local_y, -1)
        cells = width_x * width_y
        chosen = lax.broadcasted_iota(jnp.int32, (cells, slots), 0) == where
        chosen = jnp.where(chosen, 1.0, 0.0).astype(BF)
        level = lax.broadcasted_iota(jnp.int32, (depth, slots), 0) == source[2:3]
        row = lax.broadcasted_iota(jnp.int32, (ROWS, slots), 0)
        result = jnp.zeros((ROWS, slots), F32)
        copy.wait()
        for t in range(steps_total):
            columns = lax.dot_general(
                pressure[t].reshape(cells, depth),
                chosen,
                (((0,), (0,)), ((), ())),
                preferred_element_type=F32,
            )
            picked = jnp.sum(jnp.where(level, columns, 0.0), axis=0, keepdims=True)
            result = jnp.where(row == t, picked, result)
        sample[...] = result

    samples = call(
        sample_kernel,
        struct((ROWS, slots), F32),
        scratch=[VMEM((steps_total, width_x, width_y, depth), BF), pltpu.SemaphoreType.DMA],
        specs=[whole, remain],
        micros=1.5,
        limit=8,
    )(source_cells.T, forward_field)
    samples = total_of(samples, "gy")
    state, samples = lax.optimization_barrier((adjoint_state, samples))
    samples = summed(samples, "gx", 2)

    def pack_kernel(state, speed, forward, cols, speed_cols, early, late, *outs):
        place = Place()
        for x in range(width_x):
            for b in range(blocks):
                at = pl.ds(b, width_y, stride=ROWS)
                here = slice(b * LANES, (b + 1) * LANES)
                for f in range(4):
                    cols[f, x, at, :] = state[0, f, x, :, here]
                speed_cols[x, at, :] = speed[x, :, here] * SCALE

        def load(f, x, y, n):
            ref = cols.at[f] if f < 4 else speed_cols
            return ref[x, column_rows(y, n), :]

        pack_faces(place, load, 5, width_x, width_y, outs[:2], outs[2:4], outs[4:])

        mine_is_late = lax.axis_index("pair") == 0

        def one(n, carry):
            t, f = n // 4, lax.rem(n, 4)
            for is_late, ref, snap in ((True, late, t), (False, early, t + PER_ROUND)):
                number = snap * 4 + f
                for x in range(width_x):
                    for b in range(blocks):
                        ref[n, x, pl.ds(b, width_y, stride=ROWS), :] = forward[
                            snap, f, x, :, b * LANES : (b + 1) * LANES
                        ].astype(F32)
                for odd in (0, 1):
                    y = jnp.where(place.plus("gy", odd), width_y - 1, 0)
                    x = jnp.where(place.plus("gx", odd), width_x - 1, 0)
                    outs[2 + odd][rim_at + number] = ref[n, x].astype(BF)
                    value = ref[n, :, column_rows(y, 1), :].astype(BF)
                    to = rim_z_at + n * width_x

                    @pl.when(mine_is_late if is_late else jnp.logical_not(mine_is_late))
                    def _():
                        outs[odd][pl.ds(to, width_x)] = value

            return carry

        lax.fori_loop(0, 4 * PER_ROUND, one, 0)

    rim_z_at, rim_at = HALO * width_x * 5, HALO * 5
    packed = call(
        pack_kernel,
        [struct((4,) + tile, F32), struct(tile, F32)]
        + [struct((4 * PER_ROUND,) + tile, F32)] * 2
        + face_structs(5, forward_fields),
        micros=1.3,
        limit=12,
    )(state, sound_speed_sq, forward_field)
    cols, speed_cols, forward_early, forward_late = packed[:4]
    faces = packed[4:]
    z_first, x_first, d_first = first_hop(faces)
    z_first, x_first, d_first, samples = lax.optimization_barrier(
        (z_first, x_first, d_first, samples)
    )
    hop, rim_z = second_hop(5, z_first, faces[2], samples)
    rim_z = lax.ppermute(rim_z, "pair", [(0, 1), (1, 0)])

    def slope_kernel(early, late, *outs):
        altitude = Altitude()

        def one(n, carry):
            for ref, out in zip((early, late), outs):
                for x in range(width_x):
                    for y in range(width_y):
                        rows = column_rows(y, 1)
                        out[n, x, rows, :] = altitude(ref[n, x, rows, :])
            return carry

        lax.fori_loop(0, 4 * PER_ROUND, one, 0)

    slopes_early, slopes_late = call(
        slope_kernel, [struct((4 * PER_ROUND,) + tile, F32)] * 2, micros=3.3, limit=8
    )(forward_early, forward_late)

    def inject_kernel(counts, receiver, misfit, sample, message, out):
        parts = []
        for n in range(slots // (2 * LANES)):
            two = message[rim_at + forward_fields, pl.ds(2 * ROWS * n, 2 * ROWS), :].astype(F32)
            parts += [two[:ROWS], two[ROWS:]]
        samples = sample[...] + jnp.concatenate(parts, axis=1)
        local_x = receiver[0:1] - (lax.axis_index("gx") * width_x - HALO)
        local_y = receiver[1:2] - (lax.axis_index("gy") * width_y - HALO)
        inside = (local_x >= 0) & (local_x < ext_x) & (local_y >= 0) & (local_y < ext_y)
        live = lax.broadcasted_iota(jnp.int32, (1, slots), 1) < counts[0]
        where = jnp.where(inside & live, local_x * ext_y + local_y, -1)
        cells = ext_x * ext_y
        chosen = lax.broadcasted_iota(jnp.int32, (cells, slots), 0) == where
        level = lax.broadcasted_iota(jnp.int32, (depth, slots), 0) == receiver[2:3]
        level = jnp.where(level, 1.0, 0.0).astype(BF)
        for t in range(steps_total):
            amplitude = misfit[t : t + 1] * samples[t : t + 1]
            head = amplitude.astype(BF).astype(F32)
            result = jnp.zeros((cells, depth), F32)
            for part in (head, amplitude - head):
                spread = jnp.where(chosen, part, 0.0).astype(BF)
                result += lax.dot_general(
                    spread, level, (((1,), (1,)), ((), ())), preferred_element_type=F32
                )
            for g in range(cells // ROWS):
                for b in range(blocks):
                    out[t, pl.ds(g * ROWS * ROWS + b, ROWS, stride=ROWS), :] = result[
                        g * ROWS : (g + 1) * ROWS, b * LANES : (b + 1) * LANES
                    ]

    injected = call(
        inject_kernel,
        struct((steps_total, ext_x * ext_y * ROWS, LANES), F32),
        specs=[pl.BlockSpec(memory_space=pltpu.SMEM)] + [whole] * 4,
        micros=1.6,
    )(pair_counts, receiver_cells.T, residuals.T, samples, hop)

    rim_scratch = [
        VMEM((2, 4 * PER_ROUND) + block, F32),
        VMEM((2, 4 * PER_ROUND) + block, F32),
    ]

    def forward_of(place, columns, first, z_even, z_odd, z_other, x_even, x_odd, rim_y, rim_x):
        from_pair = (lax.axis_index("pair") == 0) == (first == 0)
        for odd, z, x in ((0, z_even, x_even), (1, z_odd, x_odd)):
            side_x = jnp.where(place.plus("gx", odd), 1, 0)
            side_y = jnp.where(place.plus("gy", odd), 1, 0)
            for n in range(4 * PER_ROUND):
                value = x[rim_at + 4 * first + n].astype(F32)
                if odd:
                    value = jnp.where(place.has("gx", odd), value, 0.0)
                rim_x[side_x, n] = value
                own_z = z[pl.ds(rim_z_at + n * width_x, width_x)].astype(F32).reshape(block)
                other = z_other[4 * PER_ROUND * odd + n].astype(F32)
                value = jnp.where(from_pair, own_z, other)
                if odd:
                    value = jnp.where(place.has("gy", odd), value, 0.0)
                rim_y[side_y, n] = value

        def reader(snap):
            base = 4 * (snap - first)

            def column(f, x, y):
                if isinstance(x, int) and x in (-1, width_x):
                    return rim_x[int(x > 0), base + f, column_rows(y, 1), :]
                if y in (-1, width_y):
                    rows = x * ROWS if isinstance(x, int) else pl.multiple_of(x * ROWS, ROWS)
                    return rim_y[int(y > 0), base + f, pl.ds(rows, ROWS), :]
                return columns[base + f, x, column_rows(y, 1), :]

            return column

        return reader

    def run_round(place, number, wind, inject, buffers, state_dz, after):
        altitude = Altitude()
        winds = []
        for i in range(3):
            rows = [wind[i : i + 1, b * LANES : (b + 1) * LANES] for b in range(blocks)]
            winds.append(jnp.concatenate(rows, axis=0) * SCALE)
        for s in range(PER_ROUND):
            step = number * PER_ROUND + s
            snap = steps_total - 1 - step
            old, new = buffers[s % 2], buffers[(s + 1) % 2]

            def injected_at(x, y):
                start = (x * ext_y + y) * ROWS
                if not isinstance(start, int):
                    start = pl.multiple_of(start, ROWS)
                return inject[snap, pl.ds(start, ROWS), :]

            radius = 2 * (PER_ROUND - 1 - s) + 1
            advance(
                place, altitude, old, new, state_dz, winds, injected_at, radius, s == 0, width_x, width_y
            )
            after(altitude, s, snap, new)

    def own(ref, f, x, y, n):
        return ref[f, HALO + x, column_rows(HALO + y, n), :]

    def fill(place, buffer, speed, cols, speed_cols, z_in, x_in, c_in, first, d_in):
        def store(f, x, y, n, value):
            ref = buffer.at[f] if f < 4 else speed
            ref[x, column_rows(y, n), :] = value

        for f in range(4):
            for x in range(width_x):
                store(f, HALO + x, HALO, width_y, cols[f, x])
        fields = 4
        if speed_cols is not None:
            fields = 5
            for x in range(width_x):
                store(4, HALO + x, HALO, width_y, speed_cols[x])
        place_edges(place, store, fields, width_x, width_y, z_in, x_in, c_in, first, d_in)

    def first_kernel(wind, inject, cols, speed_cols, z0, z1, x1, d0, d1, c0, *refs):
        early, late, speed, *faces, here, there, dz_az, dz_p = refs
        place = Place()
        fill(
            place, here, speed, cols, speed_cols, (z0, z1), (c0, x1), c0, rim_at + forward_fields + 1, (d0, d1)
        )

        def after(altitude, s, snap, state):
            out = (early, late)[s]
            for f in range(4):
                for x in range(width_x):
                    out[f, x] = own(state, f, x, 0, width_y)

        run_round(place, 0, wind, inject, (here, there), (speed, dz_az, dz_p), after)

        def load(f, x, y, n):
            return own(here, f, x, y, n)

        pack_faces(place, load, 4, width_x, width_y, faces[:2], faces[2:4], faces[4:])

    first = call(
        first_kernel,
        [struct((4,) + tile, F32)] * 2 + [struct(ext, F32)] + face_structs(4),
        scratch=[VMEM((4,) + ext, F32)] * 2 + [VMEM(ext, F32)] * 2,
        micros=6.0,
        limit=28,
    )(
        wind_profile, injected, cols, speed_cols, *z_first, x_first, *d_first, hop
    )
    early, late, speed_ext = first[:3]
    z_second, x_second, d_second = first_hop(first[3:])

    rim = (*z_first, rim_z, hop, x_first)

    def early_kernel(early, late, columns, slopes, z0, z1, zp, c0, x1, total, rim_y, rim_x):
        place = Place()
        reader = forward_of(place, columns, PER_ROUND, z0, z1, zp, c0, x1, rim_y, rim_x)
        total[...] = jnp.zeros_like(total)
        for s, state in ((0, early), (1, late)):
            add_increment(
                lambda f, x, y: state[f, x, column_rows(y, 1), :],
                reader(steps_total - 1 - s),
                lambda f, x, y: slopes[
                    4 * (steps_total - 1 - s - PER_ROUND) + f, x, column_rows(y, 1), :
                ],
                total,
                width_x,
                width_y,
            )

    total = call(early_kernel, struct((4,) + tile, F32), scratch=rim_scratch, micros=2.3, limit=16)(
        early, late, forward_early, slopes_early, *rim
    )
    z_second, x_second, d_second, total = lax.optimization_barrier(
        (z_second, x_second, d_second, total)
    )
    (again,) = second_hop(4, z_second, first[5])

    half = depth // 2
    half_blocks = blocks // 2

    def second_kernel(
        wind, inject, cols, speed, total, columns, slopes, *refs
    ):
        rims, (z0, z1, x1, d0, d1, c0), refs = refs[:5], refs[5:11], refs[11:]
        last, mine, other, scales, here, there, dz_az, dz_p, sums, rim_y, rim_x = refs
        place = Place()
        fill(place, here, None, cols, None, (z0, z1), (c0, x1), c0, HALO * 4, (d0, d1))
        reader = forward_of(place, columns, 0, *rims, rim_y, rim_x)
        sums[...] = total[...]

        def after(altitude, s, snap, state):
            add_increment(
                lambda f, x, y: own(state, f, x, y, 1),
                reader(snap),
                lambda f, x, y: slopes[4 * snap + f, x, column_rows(y, 1), :],
                sums,
                width_x,
                width_y,
            )

        run_round(place, 1, wind, inject, (here, there), (speed, dz_az, dz_p), after)
        me = lax.axis_index("pair")
        for f in range(4):
            for x in range(width_x):
                last[f, x] = own(here, f, x, 0, width_y)

        def sums_at(f, x, part, b):
            return sums[f, x, pl.ds(part * half_blocks + b, width_y, stride=ROWS), :]

        for f in range(4):
            for b in range(half_blocks):
                here_lanes = slice(b * LANES, (b + 1) * LANES)
                largest = jnp.abs(sums_at(f, 0, 1 - me, b))
                for x in range(1, width_x):
                    largest = jnp.maximum(largest, jnp.abs(sums_at(f, x, 1 - me, b)))
                largest = jnp.maximum(jnp.max(largest, axis=0, keepdims=True), 1e-30)
                scales[f : f + 1, here_lanes] = largest * (0.5 / 32767.0)
                inverse = 32767.0 / largest
                for x in range(0, width_x, 2):
                    two = [sums_at(f, x + i, 1 - me, b) * inverse for i in (0, 1)]
                    two = jnp.round(jnp.concatenate(two, axis=0))
                    other[f, x // 2, :, here_lanes] = two.astype(jnp.int32).astype(jnp.int16)
        for f in range(4):
            for x in range(width_x):
                mine[f, x] = sums[f, x]

    kernel_half = struct((4, width_x, width_y, half), F32)
    last, mine, other, scales = call(
        second_kernel,
        [
            struct((4,) + tile, F32),
            struct((4,) + tile, F32),
            struct((4, width_x // 2, 2 * width_y, half), jnp.int16),
            struct((4, half), F32),
        ],
        scratch=[VMEM((4,) + ext, F32)] * 2
        + [VMEM(ext, F32)] * 2
        + [VMEM((4,) + tile, F32)]
        + rim_scratch,
        micros=9.0,
        limit=30,
    )(
        wind_profile,
        injected,
        late,
        speed_ext,
        total,
        forward_late,
        slopes_late,
        *rim,
        *z_second,
        x_second,
        *d_second,
        again,
    )
    across = [(0, 1), (1, 0)]
    other, scales = lax.ppermute(other, "pair", across), lax.ppermute(scales, "pair", across)

    def final_kernel(last, sums, final, mine):
        me = lax.axis_index("pair")
        for f in range(4):
            for x in range(width_x):
                for b in range(blocks):
                    final[0, f, x, :, b * LANES : (b + 1) * LANES] = last[
                        f, x, pl.ds(b, width_y, stride=ROWS), :
                    ]
                for b in range(half_blocks):
                    mine[f, x, :, b * LANES : (b + 1) * LANES] = (
                        0.5 * sums[f, x, pl.ds(me * half_blocks + b, width_y, stride=ROWS), :]
                    )

    final, mine = call(
        final_kernel, [struct(adjoint_state.shape, F32), kernel_half], micros=1.0, limit=8
    )(last, mine)

    def sum_kernel(mine, other, scales, out):
        for f in range(4):
            for x in range(0, width_x, 2):
                two = other[f, x // 2].astype(jnp.int32).astype(F32) * scales[f : f + 1]
                for i in (0, 1):
                    out[f, x + i] = mine[f, x + i] + two[i * width_y : (i + 1) * width_y]

    kernels = call(sum_kernel, kernel_half, micros=0.8, limit=8)(mine, other, scales)
    return (kernels, final)


def solution(mesh):
    assert mesh.shape["pair"] == 2 and mesh.shape["gx"] % 2 == 0 and mesh.shape["gy"] % 2 == 0
    in_specs = (
        P("gx", "gy", None),
        P(),
        P(None, None, "gx", "gy", None),
        P("pair", None, "gx", "gy", None),
        P("pair"),
        P("pair", None),
        P("pair", None),
        P("pair", None),
    )
    out_specs = (P(None, "gx", "gy", "pair"), P("pair", None, "gx", "gy", None))
    return jax.shard_map(shards, mesh=mesh, in_specs=in_specs, out_specs=out_specs, check_vma=False)
```

time: 84.4 us -> 75.9 us (0.90)
  starting transfers between devices: 34 us -> 30.8 us
  waiting for transfers between devices: 20.9 us -> 18.1 us
  local copies, waits for them, and re-layouts: 4.46 us -> 2.3 us
    ppermute x0 -> x8, starting transfers between devices: none -> 15.6 us  [the longest x4 9.64 us: diagonal(): return lax.ppermute(x, ('gx', 'gy'), pairs)]
    ppermute x12 -> x8, starting transfers between devices: 27.6 us -> 13.6 us  [swapped(): return lax.ppermute(x, axis, swap_pairs(lax.axis_size(axis), odd))]
    ppermute x12 -> x8, waiting for transfers between devices: 10.7 us -> 1.96 us  [swapped(): return lax.ppermute(x, axis, swap_pairs(lax.axis_size(axis), odd))]
    ppermute x0 -> x8, waiting for transfers between devices: none -> 7.56 us  [the longest x3 3.85 us: total_of(): lax.ppermute(x, axis, [(i, (i + k) % size) for i in range(size)])]
    ppermute x4 -> x1, starting transfers between devices: 4.91 us -> 0.07 us  [summed(): x = x + lax.ppermute(x, axis, [(i, i ^ k) for i in range(size)])]
    unnamed x16, local copies, waits for them, and re-layouts: 4.46 us -> 2.3 us
    ppermute x4 -> x1, waiting for transfers between devices: 5.32 us -> 3.38 us  [summed(): x = x + lax.ppermute(x, axis, [(i, i ^ k) for i in range(size)])]
    pallas_call x9 -> x11, Pallas kernels: 22 us -> 22 us  [run(): pl.pallas_call(kernel, out_shape=outs, in_specs=specs or [pl.BlockSpec(me...]
  transfers between devices with their start and end apart: 18 -> 19, of which waited for: 9 -> 10; matrix products, arithmetic and copies ran while one was open for 0% -> 0% of each run, Pallas kernels for 6% -> 16%
where the time goes in v4:
time: 75.9 us; the launch traced here: 74.6 us
  starting transfers between devices  30.8 us (41%)
  Pallas kernels  22 us (29%)
  waiting for transfers between devices  18.1 us (24%)
  local copies, waits for them, and re-layouts  2.3 us (3%)
  between operations  1.5 us (2%)
    pallas_call x11, Pallas kernels, run(): pl.pallas_call(kernel, out_shape=outs, in_specs=specs or [pl.BlockSpec(me...  22 us
    ppermute x8, starting transfers between devices, swapped(): return lax.ppermute(x, axis, swap_pairs(lax.axis_size(axis), odd))  13.6 us
    ppermute x4, starting transfers between devices, diagonal(): return lax.ppermute(x, ('gx', 'gy'), pairs)  9.64 us
    ppermute x1, waiting for transfers between devices, shards(): lax.ppermute(scales, 'pair', across)  5.19 us
    ppermute x3, starting transfers between devices, total_of(): lax.ppermute(x, axis, [(i, (i + k) % size) for i in range(size)])  4.66 us
    ppermute x3, waiting for transfers between devices, total_of(): lax.ppermute(x, axis, [(i, (i + k) % size) for i in range(size)])  3.85 us
    ppermute x4, waiting for transfers between devices, diagonal(): return lax.ppermute(x, ('gx', 'gy'), pairs)  3.71 us
    ppermute x1, waiting for transfers between devices, summed(): x = x + lax.ppermute(x, axis, [(i, i ^ k) for i in range(size)])  3.38 us
  transfers between devices with their start and end apart: 19, of which 10 were waited for; matrix products, arithmetic and copies ran while one was open for 0% of the time, Pallas kernels for 16%

profile of v4, /device:TPU:1, one launch (start us, length us, event | category | flops | bytes accessed | tf_op | source)
XLA Modules:
  0.0 74.6 jit_solution(15243290759616240973)
XLA Ops:
  0.6 1.6 %copy-done = bf16[4,4,8,8,1024]{4,3,2,1,0:T(8,128)(2,1)S(1)} copy-done((bf16[4,4,8,8,1024]{4,3,2,1,0:T(8,128)(2,1)S(1)}, bf16[4,4,8,8,1024]{4,3,2,1,0:T(8,128)(2,1)}, u32[]{:S(2)}) %copy-start) | copy-done | bytes 2097176
  2.2 0.7 copy-done.5
  2.9 0.9 %shard_map.95 = f32[8,256]{1,0:T(8,128)S(1)} custom-call(s32[3,256]{1,0:T(4,128)S(1)} %bitcast.3, bf16[4,4,8,8,1024]{4,3,2,1,0:T(8,128)(2,1)S(1)} %copy-done), custom_call_target="tpu_custom_call" | custom-call | flops 1650000000 | bytes 100000 | tf_op jit(solution)/shard_map/pallas_call | solution.py:56
  3.9 4.2 %collective-permute-start.2 = (f32[8,256]{1,0:T(8,128)S(1)}, f32[8,256]{1,0:T(8,128)S(1)}, u32[]{:S(2)}, u32[]{:S(2)}) collective-permute-start(f32[8,256]{1,0:T(8,128)S(1)} %shard_map.95), channel_id=1, source_target_pairs={{0,3},{1,0},{2,1},{3,2},{4,7},{5,4},{6,5},{7,6},{8,11},{9,8},{10,9... | collective-permute-start | bytes 24584 | tf_op jit(solution)/shard_map/ppermute | solution.py:41
  8.1 0.0 collective-permute-start.1
  8.1 0.5 collective-permute-start
  8.5 0.3 collective-permute-done.2
  8.9 2.6 %collective-permute-done.1 = f32[8,256]{1,0:T(8,128)S(1)} collective-permute-done((f32[8,256]{1,0:T(8,128)S(1)}, f32[8,256]{1,0:T(8,128)S(1)}, u32[]{:S(2)}, u32[]{:S(2)}) %collective-permute-start.1) | collective-permute-done | bytes 8224 | tf_op jit(solution)/shard_map/ppermute | solution.py:41
  11.5 0.9 %collective-permute-done = f32[8,256]{1,0:T(8,128)S(1)} collective-permute-done((f32[8,256]{1,0:T(8,128)S(1)}, f32[8,256]{1,0:T(8,128)S(1)}, u32[]{:S(2)}, u32[]{:S(2)}) %collective-permute-start) | collective-permute-done | bytes 8224 | tf_op jit(solution)/shard_map/ppermute | solution.py:41
  12.4 0.0 copy-start.6
  12.4 0.0 copy-start.7
  12.4 1.3 %shard_map.96 = (f32[4,8,64,128]{3,2,1,0:T(8,128)S(1)}, f32[8,64,128]{2,1,0:T(8,128)S(1)}, f32[8,8,64,128]{3,2,1,0:T(8,128)S(1)}, f32[8,8,64,128]{3,2,1,0:T(8,12...) custom-call(f32[1,4,8,8,1024]{4,3,2,1,0:T(8,128)S(1)} %copy-done.2, ...), custom_call_target="tpu_custom_call" | custom-call | flops 1430000000 | bytes 100000 | tf_op jit(solution)/shard_map/pallas_call | solution.py:56
  13.8 5.1 %collective-permute-start.5 = (bf16[36,64,128]{2,1,0:T(8,128)(2,1)S(1)}, bf16[36,64,128]{2,1,0:T(8,128)(2,1)S(1)}, u32[]{:S(2)}, u32[]{:S(2)}) collective-permute-start(bf16[36,64,128]{2,1,0:T(8,128)(2,1)S(1)} %get-tuple-element.48), channel_id=1, source_target_pairs={{0,0},{4,8},{8,4},{12,12},{1,1},{5,9},{9,5},{13,13},{2,2},{6,10},{... | collective-permute-start | bytes 1769480 | tf_op jit(solution)/shard_map/ppermute | solution.py:26
  18.9 0.1 collective-permute-start.3
  19.0 0.7 collective-permute-start.4
  19.7 0.1 collective-permute-start.8
  19.8 2.7 %collective-permute-start.6 = (bf16[30,8,128]{2,1,0:T(8,128)(2,1)S(1)}, bf16[30,8,128]{2,1,0:T(8,128)(2,1)S(1)}, u32[]{:S(2)}, u32[]{:S(2)}) collective-permute-start(bf16[30,8,128]{2,1,0:T(8,128)(2,1)S(1)} %get-tuple-element.49), channel_id=1, source_target_pairs={{0,1},{1,0},{2,3},{3,2},{4,9},{5,8},{6,11},{7,10},{8,5},{9,4},{10,... | collective-permute-start | bytes 184328 | tf_op jit(solution)/shard_map/ppermute | solution.py:36
  22.5 3.4 %collective-permute-done.8 = f32[8,256]{1,0:T(8,128)S(1)} collective-permute-done((f32[8,256]{1,0:T(8,128)S(1)}, f32[8,256]{1,0:T(8,128)S(1)}, u32[]{:S(2)}, u32[]{:S(2)}) %collective-permute-start.8) | collective-permute-done | bytes 8224 | tf_op jit(solution)/shard_map/ppermute | solution.py:49
  25.9 2.5 %collective-permute-start.7 = (bf16[30,8,128]{2,1,0:T(8,128)(2,1)S(1)}, bf16[30,8,128]{2,1,0:T(8,128)(2,1)S(1)}, u32[]{:S(2)}, u32[]{:S(2)}) collective-permute-start(bf16[30,8,128]{2,1,0:T(8,128)(2,1)S(1)} %get-tuple-element.50), channel_id=1, source_target_pairs={{0,0},{1,2},{2,1},{3,3},{4,8},{5,10},{6,9},{7,11},{8,4},{9,6},{10,... | collective-permute-start | bytes 184328 | tf_op jit(solution)/shard_map/ppermute | solution.py:36
  28.4 0.7 collective-permute-done.6.d0
  29.1 2.4 %collective-permute-done.7.d1 = bf16[30,8,128]{2,1,0:T(8,128)(2,1)S(1)} collective-permute-done((bf16[30,8,128]{2,1,0:T(8,128)(2,1)S(1)}, bf16[30,8,128]{2,1,0:T(8,128)(2,1)S(1)}, u32[]{:S(2)}, u32[]{:S(2)}) %collective-permute-start.7) | collective-permute-done | bytes 61472 | tf_op jit(solution)/shard_map/ppermute | solution.py:36
  31.4 0.0 collective-permute-done.3.z_even.z0.refs_0_
  31.4 0.0 collective-permute-done.4.z_odd.z1.refs_1_
  31.4 0.0 collective-permute-done.5.x1.refs_4_
  31.4 0.1 shard_map.97
  31.5 0.1 collective-permute-start.9
  32.3 1.3 %collective-permute-start.15 = (bf16[16,64,128]{2,1,0:T(8,128)(2,1)S(1)}, bf16[16,64,128]{2,1,0:T(8,128)(2,1)S(1)}, u32[]{:S(2)}, u32[]{:S(2)}) collective-permute-start(bf16[16,64,128]{2,1,0:T(8,128)(2,1)S(1)} %get-tuple-element.73), channel_id=1, source_target_pairs={{0,16},{16,0},{1,17},{17,1},{2,18},{18,2},{3,19},{19,3},{4,20},{20... | collective-permute-start | bytes 786440 | tf_op jit(solution)/shard_map/ppermute | solution.py:457
  33.5 0.3 collective-permute-done.9.message.c0.refs_3_
  33.8 1.5 %shard_map.98.inject = f32[4,2048,128]{2,1,0:T(8,128)S(1)} custom-call(s32[1]{0:T(128)S(6)} %copy.10.counts, s32[3,256]{1,0:T(4,128)S(1)} %bitcast.4, f32[4,256]{1,0:T(4,128)S(1)} %bitcast.5, f32[8,256]{1,0:T(8,128)S(1)} %add.15.refs_0_.sample, bf16[45,64,128]{2,1,0:T(8,128)(2,1)S(1)} %collective-permute-done.9.message.c0.refs_3_), custom_call_target="tpu_custom_call" | custom-call | flops 1760000000 | bytes 100000 | tf_op jit(solution)/shard_map/pallas_call | solution.py:56
  35.4 5.6 %shard_map.99 = (f32[4,8,64,128]{3,2,1,0:T(8,128)S(1)}, f32[4,8,64,128]{3,2,1,0:T(8,128)S(1)}, f32[16,128,128]{2,1,0:T(8,128)S(1)}, bf16[128,8,128]{2,1,0:T(8,12...) custom-call(f32[3,1024]{1,0:T(4,128)S(1)} %copy-done.4, ...), custom_call_target="tpu_custom_call" | custom-call | flops 6600000000 | bytes 100000 | tf_op jit(solution)/shard_map/pallas_call | solution.py:56
  40.9 2.3 %collective-permute-start.10 = (bf16[128,8,128]{2,1,0:T(8,128)(2,1)S(1)}, bf16[128,8,128]{2,1,0:T(8,128)(2,1)S(1)}, u32[]{:S(2)}, u32[]{:S(2)}) collective-permute-start(bf16[128,8,128]{2,1,0:T(8,128)(2,1)S(1)} %get-tuple-element.64), channel_id=1, source_target_pairs={{0,1},{1,0},{2,3},{3,2},{4,5},{5,4},{6,7},{7,6},{8,9},{9,8},{10,11... | collective-permute-start | bytes 786440 | tf_op jit(solution)/shard_map/ppermute | solution.py:26
  43.2 0.7 collective-permute-start.11
  43.9 4.6 %collective-permute-start.12 = (bf16[16,64,128]{2,1,0:T(8,128)(2,1)S(1)}, bf16[16,64,128]{2,1,0:T(8,128)(2,1)S(1)}, u32[]{:S(2)}, u32[]{:S(2)}) collective-permute-start(bf16[16,64,128]{2,1,0:T(8,128)(2,1)S(1)} %get-tuple-element.66), channel_id=1, source_target_pairs={{0,0},{4,8},{8,4},{12,12},{1,1},{5,9},{9,5},{13,13},{2,2},{6,10},{... | collective-permute-start | bytes 786440 | tf_op jit(solution)/shard_map/ppermute | solution.py:26
  48.5 2.7 %shard_map.100 = (f32[8,8,64,128]{3,2,1,0:T(8,128)S(1)}, f32[8,8,64,128]{3,2,1,0:T(8,128)S(1)}) custom-call(f32[8,8,64,128]{3,2,1,0:T(8,128)S(1)} %get-tuple-element.70.early.columns, f32[8,8,64,128]{3,2,1,0:T(8,128)S(1)} %get-tuple-element.71.late.columns), custom_call_target="tpu_custom_call" | custom-call | flops 3630000128 | bytes 100000 | tf_op jit(solution)/shard_map/pallas_call | solution.py:56
  51.2 0.9 %collective-permute-start.13 = (bf16[24,8,128]{2,1,0:T(8,128)(2,1)S(1)}, bf16[24,8,128]{2,1,0:T(8,128)(2,1)S(1)}, u32[]{:S(2)}, u32[]{:S(2)}) collective-permute-start(bf16[24,8,128]{2,1,0:T(8,128)(2,1)S(1)} %get-tuple-element.67), channel_id=1, source_target_pairs={{0,1},{1,0},{2,3},{3,2},{4,9},{5,8},{6,11},{7,10},{8,5},{9,4},{10,... | collective-permute-start | bytes 147464 | tf_op jit(solution)/shard_map/ppermute | solution.py:36
  52.1 3.5 %collective-permute-start.14 = (bf16[24,8,128]{2,1,0:T(8,128)(2,1)S(1)}, bf16[24,8,128]{2,1,0:T(8,128)(2,1)S(1)}, u32[]{:S(2)}, u32[]{:S(2)}) collective-permute-start(bf16[24,8,128]{2,1,0:T(8,128)(2,1)S(1)} %get-tuple-element.68), channel_id=1, source_target_pairs={{0,0},{1,2},{2,1},{3,3},{4,8},{5,10},{6,9},{7,11},{8,4},{9,6},{10,... | collective-permute-start | bytes 147464 | tf_op jit(solution)/shard_map/ppermute | solution.py:36
  55.7 1.2 %shard_map.101.total = f32[4,8,64,128]{3,2,1,0:T(8,128)S(1)} custom-call(f32[4,8,64,128]{3,2,1,0:T(8,128)S(1)} %get-tuple-element.69.early, f32[4,8,64,128]{3,2,1,0:T(8,128)S(1)} %get-tuple-element.62.late.cols, f32[8,8,64,128]{3,2,1,0:T(8,128)S(1)} %get-tuple-element.70.early.columns, f32[8,8,64,128]{3,2,1,0:T(8,128)S(1)} %get-tuple-element.72.slopes, ...), custom_call_target="tpu_custom_call" | custom-call | flops 2529999872 | bytes 100000 | tf_op jit(solution)/shard_map/pallas_call | solution.py:56
  56.8 0.0 collective-permute-done.13.refs_8_
  56.8 0.7 collective-permute-done.14.refs_9_
  57.6 0.1 collective-permute-start.16
  57.6 1.7 %collective-permute-done.16.refs_10_ = bf16[22,64,128]{2,1,0:T(8,128)(2,1)S(1)} collective-permute-done((bf16[22,64,128]{2,1,0:T(8,128)(2,1)S(1)}, bf16[22,64,128]{2,1,0:T(8,128)(2,1)S(1)}, u32[]{:S(2)}, u32[]{:S(2)}) %collective-permute-start.16) | collective-permute-done | bytes 360480 | tf_op jit(solution)/shard_map/ppermute | solution.py:26
  59.3 6.5 %shard_map.103 = (f32[4,8,64,128]{3,2,1,0:T(8,128)S(1)}, f32[4,8,64,128]{3,2,1,0:T(8,128)S(1)}, s16[4,4,16,512]{3,2,1,0:T(8,128)(2,1)S(1)}, f32[4,512]{1,0:T(4,128)S(1)}) custom-call(f32[3,1024]{1,0:T(4,128)S(1)} %copy-done.4, f32[4,2048,128]{2,1,0:T(8,128)S(1)} %shard_map.98.inject, f32[4,8,64,128]{3,2,1,0:T(8,128)S(1)} %get-tuple-element.62.late.cols, ...), custom_call_target="tpu_custom_call" | custom-call | flops 9900000256 | bytes 100000 | tf_op jit(solution)/shard_map/pallas_call | solution.py:56
  65.8 1.2 %collective-permute-start.17 = (s16[4,4,16,512]{3,2,1,0:T(8,128)(2,1)S(1)}, s16[4,4,16,512]{3,2,1,0:T(8,128)(2,1)S(1)}, u32[]{:S(2)}, u32[]{:S(2)}) collective-permute-start(s16[4,4,16,512]{3,2,1,0:T(8,128)(2,1)S(1)} %get-tuple-element.85), channel_id=1, source_target_pairs={{0,16},{16,0},{1,17},{17,1},{2,18},{18,2},{3,19},{19,3},{4,20},{20... | collective-permute-start | bytes 786440 | tf_op jit(solution)/shard_map/ppermute | solution.py:728
  66.9 0.4 collective-permute-start.18
  67.3 1.3 %shard_map.104 = (f32[1,4,8,8,1024]{4,3,2,1,0:T(8,128)}, f32[4,8,8,512]{3,2,1,0:T(8,128)S(1)}) custom-call(f32[4,8,64,128]{3,2,1,0:T(8,128)S(1)} %get-tuple-element.82.last, f32[4,8,64,128]{3,2,1,0:T(8,128)S(1)} %get-tuple-element.83.sums), custom_call_target="tpu_custom_call" | custom-call | flops 1100000000 | bytes 100000 | tf_op jit(solution)/shard_map/pallas_call | solution.py:56
  68.6 5.2 %collective-permute-done.18.scales = f32[4,512]{1,0:T(4,128)S(1)} collective-permute-done((f32[4,512]{1,0:T(4,128)S(1)}, f32[4,512]{1,0:T(4,128)S(1)}, u32[]{:S(2)}, u32[]{:S(2)}) %collective-permute-start.18) | collective-permute-done | bytes 8224 | tf_op jit(solution)/shard_map/ppermute | solution.py:728
  73.8 0.0 collective-permute-done.17.other
  73.8 0.9 %shard_map.105 = f32[4,8,8,512]{3,2,1,0:T(8,128)} custom-call(f32[4,8,8,512]{3,2,1,0:T(8,128)S(1)} %get-tuple-element.84.mine, s16[4,4,16,512]{3,2,1,0:T(8,128)(2,1)S(1)} %collective-permute-done.17.other, f32[4,512]{1,0:T(4,128)S(1)} %collective-permute-done.18.scales), custom_call_target="tpu_custom_call" | custom-call | flops 880000000 | bytes 100000 | tf_op jit(solution)/shard_map/pallas_call | solution.py:56
  (19 shorter events, 0.1 us)
Async XLA Ops:
  0.6 1.6 %copy-start = (bf16[4,4,8,8,1024]{4,3,2,1,0:T(8,128)(2,1)S(1)}, bf16[4,4,8,8,1024]{4,3,2,1,0:T(8,128)(2,1)}, u32[]{:S(2)}) copy-start(bf16[4,4,8,8,1024]{4,3,2,1,0:T(8,128)(2,1)} %forward.3) | copy-start | bytes 6291460
  2.2 0.7 copy-start.5
  2.9 9.5 %copy-start.1 = (bf16[4,4,8,8,1024]{4,3,2,1,0:T(8,128)(2,1)S(1)}, bf16[4,4,8,8,1024]{4,3,2,1,0:T(8,128)(2,1)}, u32[]{:S(2)}) copy-start(bf16[4,4,8,8,1024]{4,3,2,1,0:T(8,128)(2,1)} %forward.3) | copy-start | bytes 6291460
  2.9 9.5 %copy-start.2 = (f32[1,4,8,8,1024]{4,3,2,1,0:T(8,128)S(1)}, f32[1,4,8,8,1024]{4,3,2,1,0:T(8,128)}, u32[]{:S(2)}) copy-start(f32[1,4,8,8,1024]{4,3,2,1,0:T(8,128)} %state) | copy-start | bytes 3145732
  2.9 9.5 %copy-start.3 = (f32[8,8,1024]{2,1,0:T(8,128)S(1)}, f32[8,8,1024]{2,1,0:T(8,128)}, u32[]{:S(2)}) copy-start(f32[8,8,1024]{2,1,0:T(8,128)} %speed.1) | copy-start | bytes 786436
  3.9 5.0 %collective-permute-start.2 = (f32[8,256]{1,0:T(8,128)S(1)}, f32[8,256]{1,0:T(8,128)S(1)}, u32[]{:S(2)}, u32[]{:S(2)}) collective-permute-start(f32[8,256]{1,0:T(8,128)S(1)} %shard_map.95), channel_id=1, source_target_pairs={{0,3},{1,0},{2,1},{3,2},{4,7},{5,4},{6,5},{7,6},{8,11},{9,8},{10,9... | collective-permute-start | bytes 24584 | tf_op jit(solution)/shard_map/ppermute | solution.py:41
  8.1 3.4 %collective-permute-start.1 = (f32[8,256]{1,0:T(8,128)S(1)}, f32[8,256]{1,0:T(8,128)S(1)}, u32[]{:S(2)}, u32[]{:S(2)}) collective-permute-start(f32[8,256]{1,0:T(8,128)S(1)} %shard_map.95), channel_id=1, source_target_pairs={{0,2},{1,3},{2,0},{3,1},{4,6},{5,7},{6,4},{7,5},{8,10},{9,11},{10,... | collective-permute-start | bytes 24584 | tf_op jit(solution)/shard_map/ppermute | solution.py:41
  8.1 4.3 %collective-permute-start = (f32[8,256]{1,0:T(8,128)S(1)}, f32[8,256]{1,0:T(8,128)S(1)}, u32[]{:S(2)}, u32[]{:S(2)}) collective-permute-start(f32[8,256]{1,0:T(8,128)S(1)} %shard_map.95), channel_id=1, source_target_pairs={{0,1},{1,2},{2,3},{3,0},{4,5},{5,6},{6,7},{7,4},{8,9},{9,10},{10,1... | collective-permute-start | bytes 24584 | tf_op jit(solution)/shard_map/ppermute | solution.py:41
  12.4 21.4 %copy-start.6 = (s32[256,3]{0,1:T(4,128)S(1)}, s32[256,3]{0,1:T(4,128)}, u32[]{:S(2)}) copy-start(s32[256,3]{0,1:T(4,128)} %param.14) | copy-start | bytes 9220
  12.4 21.4 %copy-start.7 = (f32[256,4]{0,1:T(4,128)S(1)}, f32[256,4]{0,1:T(4,128)}, u32[]{:S(2)}) copy-start(f32[256,4]{0,1:T(4,128)} %param.15) | copy-start | bytes 12292
  13.8 17.7 %collective-permute-start.5 = (bf16[36,64,128]{2,1,0:T(8,128)(2,1)S(1)}, bf16[36,64,128]{2,1,0:T(8,128)(2,1)S(1)}, u32[]{:S(2)}, u32[]{:S(2)}) collective-permute-start(bf16[36,64,128]{2,1,0:T(8,128)(2,1)S(1)} %get-tuple-element.48), channel_id=1, source_target_pairs={{0,0},{4,8},{8,4},{12,12},{1,1},{5,9},{9,5},{13,13},{2,2},{6,10},{... | collective-permute-start | bytes 1769480 | tf_op jit(solution)/shard_map/ppermute | solution.py:26
  18.9 12.5 %collective-permute-start.3 = (bf16[224,8,128]{2,1,0:T(8,128)(2,1)S(1)}, bf16[224,8,128]{2,1,0:T(8,128)(2,1)S(1)}, u32[]{:S(2)}, u32[]{:S(2)}) collective-permute-start(bf16[224,8,128]{2,1,0:T(8,128)(2,1)S(1)} %get-tuple-element.46), channel_id=1, source_target_pairs={{0,1},{1,0},{2,3},{3,2},{4,5},{5,4},{6,7},{7,6},{8,9},{9,8},{10,11... | collective-permute-start | bytes 1376264 | tf_op jit(solution)/shard_map/ppermute | solution.py:26
  19.0 12.4 %collective-permute-start.4 = (bf16[224,8,128]{2,1,0:T(8,128)(2,1)S(1)}, bf16[224,8,128]{2,1,0:T(8,128)(2,1)S(1)}, u32[]{:S(2)}, u32[]{:S(2)}) collective-permute-start(bf16[224,8,128]{2,1,0:T(8,128)(2,1)S(1)} %get-tuple-element.47), channel_id=1, source_target_pairs={{0,0},{1,2},{2,1},{3,3},{4,4},{5,6},{6,5},{7,7},{8,8},{9,10},{10,9... | collective-permute-start | bytes 1376264 | tf_op jit(solution)/shard_map/ppermute | solution.py:26
  19.7 6.2 %collective-permute-start.8 = (f32[8,256]{1,0:T(8,128)S(1)}, f32[8,256]{1,0:T(8,128)S(1)}, u32[]{:S(2)}, u32[]{:S(2)}) collective-permute-start(f32[8,256]{1,0:T(8,128)S(1)} %add_add_fusion), channel_id=1, source_target_pairs={{0,8},{4,12},{8,0},{12,4},{1,9},{5,13},{9,1},{13,5},{2,10},{6,14},... | collective-permute-start | bytes 24584 | tf_op jit(solution)/shard_map/ppermute | solution.py:49
  19.8 9.3 %collective-permute-start.6 = (bf16[30,8,128]{2,1,0:T(8,128)(2,1)S(1)}, bf16[30,8,128]{2,1,0:T(8,128)(2,1)S(1)}, u32[]{:S(2)}, u32[]{:S(2)}) collective-permute-start(bf16[30,8,128]{2,1,0:T(8,128)(2,1)S(1)} %get-tuple-element.49), channel_id=1, source_target_pairs={{0,1},{1,0},{2,3},{3,2},{4,9},{5,8},{6,11},{7,10},{8,5},{9,4},{10,... | collective-permute-start | bytes 184328 | tf_op jit(solution)/shard_map/ppermute | solution.py:36
  25.9 5.5 %collective-permute-start.7 = (bf16[30,8,128]{2,1,0:T(8,128)(2,1)S(1)}, bf16[30,8,128]{2,1,0:T(8,128)(2,1)S(1)}, u32[]{:S(2)}, u32[]{:S(2)}) collective-permute-start(bf16[30,8,128]{2,1,0:T(8,128)(2,1)S(1)} %get-tuple-element.50), channel_id=1, source_target_pairs={{0,0},{1,2},{2,1},{3,3},{4,8},{5,10},{6,9},{7,11},{8,4},{9,6},{10,... | collective-permute-start | bytes 184328 | tf_op jit(solution)/shard_map/ppermute | solution.py:36
  31.5 2.3 %collective-permute-start.9 = (bf16[45,64,128]{2,1,0:T(8,128)(2,1)S(1)}, bf16[45,64,128]{2,1,0:T(8,128)(2,1)S(1)}, u32[]{:S(2)}, u32[]{:S(2)}) collective-permute-start(bf16[45,64,128]{2,1,0:T(8,128)(2,1)S(1)} %get-tuple-element.56), channel_id=1, source_target_pairs={{0,4},{4,0},{8,12},{12,8},{1,5},{5,1},{9,13},{13,9},{2,6},{6,2},{1... | collective-permute-start | bytes 2211848 | tf_op jit(solution)/shard_map/ppermute | solution.py:26
  32.3 19.8 %collective-permute-start.15 = (bf16[16,64,128]{2,1,0:T(8,128)(2,1)S(1)}, bf16[16,64,128]{2,1,0:T(8,128)(2,1)S(1)}, u32[]{:S(2)}, u32[]{:S(2)}) collective-permute-start(bf16[16,64,128]{2,1,0:T(8,128)(2,1)S(1)} %get-tuple-element.73), channel_id=1, source_target_pairs={{0,16},{16,0},{1,17},{17,1},{2,18},{18,2},{3,19},{19,3},{4,20},{20... | collective-permute-start | bytes 786440 | tf_op jit(solution)/shard_map/ppermute | solution.py:457
  33.8 1.5 %copy-start.4 = (f32[3,1024]{1,0:T(4,128)S(1)}, f32[3,1024]{1,0:T(4,128)}, u32[]{:S(2)}) copy-start(f32[3,1024]{1,0:T(4,128)} %wind.3) | copy-start | bytes 36868
  40.9 16.6 %collective-permute-start.10 = (bf16[128,8,128]{2,1,0:T(8,128)(2,1)S(1)}, bf16[128,8,128]{2,1,0:T(8,128)(2,1)S(1)}, u32[]{:S(2)}, u32[]{:S(2)}) collective-permute-start(bf16[128,8,128]{2,1,0:T(8,128)(2,1)S(1)} %get-tuple-element.64), channel_id=1, source_target_pairs={{0,1},{1,0},{2,3},{3,2},{4,5},{5,4},{6,7},{7,6},{8,9},{9,8},{10,11... | collective-permute-start | bytes 786440 | tf_op jit(solution)/shard_map/ppermute | solution.py:26
  43.2 14.3 %collective-permute-start.11 = (bf16[128,8,128]{2,1,0:T(8,128)(2,1)S(1)}, bf16[128,8,128]{2,1,0:T(8,128)(2,1)S(1)}, u32[]{:S(2)}, u32[]{:S(2)}) collective-permute-start(bf16[128,8,128]{2,1,0:T(8,128)(2,1)S(1)} %get-tuple-element.65), channel_id=1, source_target_pairs={{0,0},{1,2},{2,1},{3,3},{4,4},{5,6},{6,5},{7,7},{8,8},{9,10},{10,9... | collective-permute-start | bytes 786440 | tf_op jit(solution)/shard_map/ppermute | solution.py:26
  43.9 13.6 %collective-permute-start.12 = (bf16[16,64,128]{2,1,0:T(8,128)(2,1)S(1)}, bf16[16,64,128]{2,1,0:T(8,128)(2,1)S(1)}, u32[]{:S(2)}, u32[]{:S(2)}) collective-permute-start(bf16[16,64,128]{2,1,0:T(8,128)(2,1)S(1)} %get-tuple-element.66), channel_id=1, source_target_pairs={{0,0},{4,8},{8,4},{12,12},{1,1},{5,9},{9,5},{13,13},{2,2},{6,10},{... | collective-permute-start | bytes 786440 | tf_op jit(solution)/shard_map/ppermute | solution.py:26
  51.2 5.6 %collective-permute-start.13 = (bf16[24,8,128]{2,1,0:T(8,128)(2,1)S(1)}, bf16[24,8,128]{2,1,0:T(8,128)(2,1)S(1)}, u32[]{:S(2)}, u32[]{:S(2)}) collective-permute-start(bf16[24,8,128]{2,1,0:T(8,128)(2,1)S(1)} %get-tuple-element.67), channel_id=1, source_target_pairs={{0,1},{1,0},{2,3},{3,2},{4,9},{5,8},{6,11},{7,10},{8,5},{9,4},{10,... | collective-permute-start | bytes 147464 | tf_op jit(solution)/shard_map/ppermute | solution.py:36
  52.1 5.4 %collective-permute-start.14 = (bf16[24,8,128]{2,1,0:T(8,128)(2,1)S(1)}, bf16[24,8,128]{2,1,0:T(8,128)(2,1)S(1)}, u32[]{:S(2)}, u32[]{:S(2)}) collective-permute-start(bf16[24,8,128]{2,1,0:T(8,128)(2,1)S(1)} %get-tuple-element.68), channel_id=1, source_target_pairs={{0,0},{1,2},{2,1},{3,3},{4,8},{5,10},{6,9},{7,11},{8,4},{9,6},{10,... | collective-permute-start | bytes 147464 | tf_op jit(solution)/shard_map/ppermute | solution.py:36
  57.6 1.7 %collective-permute-start.16 = (bf16[22,64,128]{2,1,0:T(8,128)(2,1)S(1)}, bf16[22,64,128]{2,1,0:T(8,128)(2,1)S(1)}, u32[]{:S(2)}, u32[]{:S(2)}) collective-permute-start(bf16[22,64,128]{2,1,0:T(8,128)(2,1)S(1)} %shard_map.102), channel_id=1, source_target_pairs={{0,4},{4,0},{8,12},{12,8},{1,5},{5,1},{9,13},{13,9},{2,6},{6,2},{1... | collective-permute-start | bytes 1081352 | tf_op jit(solution)/shard_map/ppermute | solution.py:26
  65.8 8.0 %collective-permute-start.17 = (s16[4,4,16,512]{3,2,1,0:T(8,128)(2,1)S(1)}, s16[4,4,16,512]{3,2,1,0:T(8,128)(2,1)S(1)}, u32[]{:S(2)}, u32[]{:S(2)}) collective-permute-start(s16[4,4,16,512]{3,2,1,0:T(8,128)(2,1)S(1)} %get-tuple-element.85), channel_id=1, source_target_pairs={{0,16},{16,0},{1,17},{17,1},{2,18},{18,2},{3,19},{19,3},{4,20},{20... | collective-permute-start | bytes 786440 | tf_op jit(solution)/shard_map/ppermute | solution.py:728
  66.9 6.8 %collective-permute-start.18 = (f32[4,512]{1,0:T(4,128)S(1)}, f32[4,512]{1,0:T(4,128)S(1)}, u32[]{:S(2)}, u32[]{:S(2)}) collective-permute-start(f32[4,512]{1,0:T(4,128)S(1)} %get-tuple-element.86), channel_id=1, source_target_pairs={{0,16},{16,0},{1,17},{17,1},{2,18},{18,2},{3,19},{19,3},{4,20},{20... | collective-permute-start | bytes 24584 | tf_op jit(solution)/shard_map/ppermute | solution.py:728

commit v5 on v4

--- a/solution.py
+++ b/solution.py
@@ -24,16 +24,6 @@
 
 def swapped(x, axis, odd):
     return lax.ppermute(x, axis, swap_pairs(lax.axis_size(axis), odd))
-
-
-def diagonal(x, odd_x, odd_y):
-    size_x, size_y = lax.axis_size("gx"), lax.axis_size("gy")
-    pairs = [
-        (i * size_y + j, k * size_y + m)
-        for i, k in swap_pairs(size_x, odd_x)
-        for j, m in swap_pairs(size_y, odd_y)
-    ]
-    return lax.ppermute(x, ("gx", "gy"), pairs)
 
 
 def total_of(x, axis):
@@ -98,22 +88,28 @@
     return pl.ds(start, n * ROWS)
 
 
-def pack_faces(place, load, fields, width_x, width_y, z_out, x_out, d_out):
+def face_depth(f, axis):
+    return HALO if f in (0, {"gx": 1, "gy": 2}[axis]) else HALO - 1
+
+
+def face_start(f, axis):
+    return sum(face_depth(g, axis) for g in range(f))
+
+
+def pack_faces(place, load, fields, width_x, width_y, z_out, x_out):
     for odd in (0, 1):
-        plus_y = place.plus("gy", odd)
-        y0 = jnp.where(plus_y, width_y - HALO, 0)
-        x0 = jnp.where(place.plus("gx", odd), width_x - HALO, 0)
-        plus_x = place.plus("gx", 1)
         for f in range(fields):
+            deep = face_depth(f, "gy")
+            y0 = jnp.where(place.plus("gy", odd), width_y - deep, 0)
             for x in range(width_x):
-                value = load(f, x, y0, HALO).reshape(HALO, ROWS, LANES)
-                z_out[odd][pl.ds((f * width_x + x) * HALO, HALO)] = value.astype(BF)
-            for j in range(HALO):
-                x_out[odd][HALO * f + j] = load(f, x0 + j, 0, width_y).astype(BF)
-            for k, (i, j) in enumerate(CORNER):
-                x = jnp.where(plus_x, width_x - i, i - 1)
-                y = jnp.where(plus_y, width_y - j, j - 1)
-                d_out[odd][f * len(CORNER) + k] = load(f, x, y, 1).astype(BF)
+                value = load(f, x, y0, deep).reshape(deep, ROWS, LANES)
+                at = face_start(f, "gy") * width_x + x * deep
+                z_out[odd][pl.ds(at, deep)] = value.astype(BF)
+            deep = face_depth(f, "gx")
+            x0 = jnp.where(place.plus("gx", odd), width_x - deep, 0)
+            for j in range(deep):
+                value = load(f, x0 + j, 0, width_y)
+                x_out[odd][face_start(f, "gx") + j] = value.astype(BF)
 
 
 def corner_blocks(fields, width_y):
@@ -125,8 +121,8 @@
     return n // width_y, pl.ds(n % width_y * ROWS, 2 * ROWS)
 
 
-def pack_corners(place, fields, width_x, width_y, z_in, out, first):
-    plus_x = place.plus("gx", 0)
+def pack_corners(place, fields, width_x, width_y, z_in, out, first, odd_x):
+    plus_x = place.plus("gx", odd_x)
     for odd_y in (0, 1):
         plus_y = place.plus("gy", odd_y)
         for f in range(fields):
@@ -134,13 +130,15 @@
                 two = []
                 for i, j in CORNER[k : k + 2]:
                     x = jnp.where(plus_x, width_x - i, i - 1)
-                    y = jnp.where(plus_y, j - 1, HALO - j)
-                    two.append(z_in[odd_y][(f * width_x + x) * HALO + y].astype(F32))
+                    deep = face_depth(f, "gy")
+                    y = jnp.where(plus_y, j - 1, deep - j)
+                    at = face_start(f, "gy") * width_x + x * deep + y
+                    two.append(z_in[odd_y][at].astype(F32))
                 block, rows = corner_place(fields, odd_y, f, k, width_y)
                 out[first + block, rows, :] = jnp.concatenate(two, axis=0).astype(BF)
 
 
-def place_edges(place, store, fields, width_x, width_y, z_in, x_in, c_in, first, d_in):
+def place_edges(place, store, fields, width_x, width_y, z_in, x_in, c_in, firsts):
     def masked(value, *conditions):
         value = value.astype(F32)
         for condition in conditions:
@@ -149,15 +147,17 @@
         return value
 
     for odd in (0, 1):
-        y0 = jnp.where(place.plus("gy", odd), width_y + HALO, 0)
-        x0 = jnp.where(place.plus("gx", odd), width_x + HALO, 0)
         for f in range(fields):
+            deep = face_depth(f, "gy")
+            y0 = jnp.where(place.plus("gy", odd), width_y + HALO, HALO - deep)
             for x in range(width_x):
-                value = z_in[odd][pl.ds((f * width_x + x) * HALO, HALO)]
-                value = masked(value, place.has("gy", odd))
-                store(f, HALO + x, y0, HALO, value.reshape(HALO * ROWS, LANES))
-            for j in range(HALO):
-                value = masked(x_in[odd][HALO * f + j], place.has("gx", odd))
+                at = face_start(f, "gy") * width_x + x * deep
+                value = masked(z_in[odd][pl.ds(at, deep)], place.has("gy", odd))
+                store(f, HALO + x, y0, deep, value.reshape(deep * ROWS, LANES))
+            deep = face_depth(f, "gx")
+            x0 = jnp.where(place.plus("gx", odd), width_x + HALO, HALO - deep)
+            for j in range(deep):
+                value = masked(x_in[odd][face_start(f, "gx") + j], place.has("gx", odd))
                 store(f, x0 + j, HALO, width_y, value)
     for odd_x in (0, 1):
         plus_x = place.plus("gx", odd_x)
@@ -165,13 +165,9 @@
             plus_y = place.plus("gy", odd_y)
             for f in range(fields):
                 for k in range(0, len(CORNER), 2):
-                    if odd_x:
-                        n = f * len(CORNER) + k
-                        two = [d_in[odd_y][n], d_in[odd_y][n + 1]]
-                    else:
-                        block, rows = corner_place(fields, odd_y, f, k, width_y)
-                        two = c_in[first + block, rows, :].astype(F32)
-                        two = [two[:ROWS], two[ROWS:]]
+                    block, rows = corner_place(fields, odd_y, f, k, width_y)
+                    two = c_in[odd_x][firsts[odd_x] + block, rows, :].astype(F32)
+                    two = [two[:ROWS], two[ROWS:]]
                     for value, (i, j) in zip(two, CORNER[k : k + 2]):
                         x = jnp.where(plus_x, HALO + width_x - 1 + i, HALO - i)
                         y = jnp.where(plus_y, HALO + width_y - 1 + j, HALO - j)
@@ -210,7 +206,9 @@
         row(HALO + width_x - 1 + d, HALO - rest, width_y + 2 * rest, sides[1])
 
 
-def advance(place, altitude, old, new, state_dz, wind, inject, radius, first, width_x, width_y):
+def advance(
+    place, altitude, old, new, state_dz, wind, inject, radius, own_dz, width_x, width_y
+):
     east, north, vertical = wind
     speed, dz_az, dz_p = state_dz
     sides = {
@@ -231,14 +229,19 @@
 
     p, ax, ay, az = (old.at[f] for f in range(4))
 
+    def slope(f, value, x, y, kept):
+        if own_dz is None or kept is not None or not HALO <= y < HALO + width_y:
+            return altitude(value)
+        return own_dz[f, x - HALO, column_rows(y - HALO, 1), :]
+
     def p_row(x, y0, n, kept):
         ps = [at(p, x, y0 + k - 1) for k in range(n + 2)]
         ays = [at(ay, x, y0 + k - 1) for k in range(n + 2)]
         for k in range(n):
             y = y0 + k
-            up = altitude(at(az, x, y))
+            up = slope(3, at(az, x, y), x, y, kept)
             dz_az[x, column_rows(y, 1), :] = up
-            up_p = altitude(ps[k + 1]) if first else at(dz_p, x, y)
+            up_p = at(dz_p, x, y) if own_dz is None else slope(0, ps[k + 1], x, y, kept)
             div = (at(ax, x + 1, y) - at(ax, x - 1, y)) + (ays[k + 2] - ays[k]) + up
             value = (
                 at(speed, x, y) * div
@@ -266,7 +269,7 @@
                     grad = altitude(ps[k + 1])
                     if radius > 1:
                         dz_p[x, column_rows(y, 1), :] = grad
-                up = at(dz_az, x, y) if f == 3 else altitude(vs[k + 1])
+                up = at(dz_az, x, y) if f == 3 else slope(f, vs[k + 1], x, y, kept)
                 value = (
                     SCALE * grad
                     + east * (at(a, x + 1, y) - at(a, x - 1, y))
@@ -322,39 +325,38 @@
     forward_fields = 4 * steps_total
 
     def face_structs(fields, more=0):
-        z = struct((HALO * width_x * fields + more // 2 * width_x, ROWS, LANES), BF)
-        x = [struct((HALO * fields + more,) + block, BF)] * 2
-        d = struct((len(CORNER) * fields, ROWS, LANES), BF)
-        return [z, z, *x, d, d]
+        columns = face_start(fields, "gy") + more // 2
+        z = struct((columns * width_x, ROWS, LANES), BF)
+        x = [struct((face_start(fields, "gx") + more,) + block, BF)] * 2
+        return [z, z, *x]
 
     def first_hop(faces):
-        z_even, z_odd, _, x_odd, d_even, d_odd = faces
+        z_even, z_odd, _, x_odd = faces
         z = [swapped(z_even, "gy", 0), swapped(z_odd, "gy", 1)]
-        return z, swapped(x_odd, "gx", 1), [diagonal(d_even, 1, 0), diagonal(d_odd, 1, 1)]
-
-    def second_hop(fields, z, faces, *sample):
-        at = faces.shape[0]
-        ahead = at + len(sample)
-
-        def corner_kernel(z_even, z_odd, faces, *refs):
-            even = refs[len(sample)]
-            even[:at] = faces[...]
-            if sample:
-                for n, lanes in enumerate(range(0, slots, 2 * LANES)):
-                    two = [refs[0][:, lanes + i : lanes + i + LANES] for i in (0, LANES)]
-                    rows = pl.ds(2 * ROWS * n, 2 * ROWS)
-                    even[at, rows, :] = jnp.concatenate(two, axis=0).astype(BF)
-                for odd, ref in ((0, z_even), (1, z_odd)):
+        return z, swapped(x_odd, "gx", 1)
+
+    def second_hop(fields, z, faces, first):
+        ahead = faces.shape[0]
+        corners = corner_blocks(fields, width_y)
+
+        def corner_kernel(z_even, z_odd, faces, even, odd, *rim):
+            place = Place()
+            even[:ahead] = faces[...]
+            z = (z_even, z_odd)
+            pack_corners(place, fields, width_x, width_y, z, even, ahead, 0)
+            pack_corners(place, fields, width_x, width_y, z, odd, 0, 1)
+            for out in rim:
+                for odd_y, ref in enumerate(z):
                     for n in range(4 * PER_ROUND):
                         value = ref[pl.ds(rim_z_at + n * width_x, width_x)].reshape(block)
-                        refs[2][4 * PER_ROUND * odd + n] = value
-            pack_corners(Place(), fields, width_x, width_y, (z_even, z_odd), even, ahead)
-
-        outs = [struct((ahead + corner_blocks(fields, width_y),) + block, BF)]
-        if sample:
+                        out[4 * PER_ROUND * odd_y + n] = value
+
+        outs = [struct((n + corners,) + block, BF) for n in (ahead, 0)]
+        if first:
             outs.append(struct((8 * PER_ROUND,) + block, BF))
-        made = call(corner_kernel, outs, micros=0.3, limit=8)(*z, faces, *sample)
-        return [swapped(made[0], "gx", 0), *made[1:]]
+        even, odd, *rim = call(corner_kernel, outs, micros=0.3, limit=8)(*z, faces)
+        rim = [lax.ppermute(r, "pair", [(0, 1), (1, 0)]) for r in rim]
+        return [swapped(even, "gx", 0), swapped(odd, "gx", 1), *rim]
 
     whole = pl.BlockSpec(memory_space=VMEM)
     remain = pl.BlockSpec(memory_space=pltpu.HBM)
@@ -392,9 +394,8 @@
         micros=1.5,
         limit=8,
     )(source_cells.T, forward_field)
-    samples = total_of(samples, "gy")
     state, samples = lax.optimization_barrier((adjoint_state, samples))
-    samples = summed(samples, "gx", 2)
+    samples = total_of(samples, "gx")
 
     def pack_kernel(state, speed, forward, cols, speed_cols, early, late, *outs):
         place = Place()
@@ -410,7 +411,7 @@
             ref = cols.at[f] if f < 4 else speed_cols
             return ref[x, column_rows(y, n), :]
 
-        pack_faces(place, load, 5, width_x, width_y, outs[:2], outs[2:4], outs[4:])
+        pack_faces(place, load, 5, width_x, width_y, outs[:2], outs[2:])
 
         mine_is_late = lax.axis_index("pair") == 0
 
@@ -438,7 +439,7 @@
 
         lax.fori_loop(0, 4 * PER_ROUND, one, 0)
 
-    rim_z_at, rim_at = HALO * width_x * 5, HALO * 5
+    rim_z_at, rim_at = face_start(5, "gy") * width_x, face_start(5, "gx")
     packed = call(
         pack_kernel,
         [struct((4,) + tile, F32), struct(tile, F32)]
@@ -449,14 +450,28 @@
     )(state, sound_speed_sq, forward_field)
     cols, speed_cols, forward_early, forward_late = packed[:4]
     faces = packed[4:]
-    z_first, x_first, d_first = first_hop(faces)
-    z_first, x_first, d_first, samples = lax.optimization_barrier(
-        (z_first, x_first, d_first, samples)
-    )
-    hop, rim_z = second_hop(5, z_first, faces[2], samples)
-    rim_z = lax.ppermute(rim_z, "pair", [(0, 1), (1, 0)])
-
-    def slope_kernel(early, late, *outs):
+    z_first, x_first = first_hop(faces)
+
+    def own_slopes(cols):
+        def kernel(cols, out):
+            altitude = Altitude()
+
+            def one(f, carry):
+                for x in range(width_x):
+                    for y in range(width_y):
+                        rows = column_rows(y, 1)
+                        out[f, x, rows, :] = altitude(cols[f, x, rows, :])
+                return carry
+
+            lax.fori_loop(0, 4, one, 0)
+
+        return call(kernel, struct((4,) + tile, F32), micros=0.8, limit=8)(cols)
+
+    own_dz = own_slopes(cols)
+
+    def slope_kernel(early, late, sample, *outs):
+        *outs, held = outs
+        held[...] = sample[...]
         altitude = Altitude()
 
         def one(n, carry):
@@ -469,16 +484,20 @@
 
         lax.fori_loop(0, 4 * PER_ROUND, one, 0)
 
-    slopes_early, slopes_late = call(
-        slope_kernel, [struct((4 * PER_ROUND,) + tile, F32)] * 2, micros=3.3, limit=8
-    )(forward_early, forward_late)
-
-    def inject_kernel(counts, receiver, misfit, sample, message, out):
-        parts = []
-        for n in range(slots // (2 * LANES)):
-            two = message[rim_at + forward_fields, pl.ds(2 * ROWS * n, 2 * ROWS), :].astype(F32)
-            parts += [two[:ROWS], two[ROWS:]]
-        samples = sample[...] + jnp.concatenate(parts, axis=1)
+    slopes_early, slopes_late, samples = call(
+        slope_kernel,
+        [struct((4 * PER_ROUND,) + tile, F32)] * 2 + [struct(samples.shape, F32)],
+        micros=2.7,
+        limit=8,
+    )(forward_early, forward_late, samples)
+    samples = total_of(samples, "gy")
+
+    z_first, x_first, samples, slopes_early, slopes_late, own_dz = lax.optimization_barrier(
+        (z_first, x_first, samples, slopes_early, slopes_late, own_dz)
+    )
+    hop, hop_odd, rim_z = second_hop(5, z_first, faces[2], True)
+
+    def inject_kernel(counts, receiver, misfit, samples, out):
         local_x = receiver[0:1] - (lax.axis_index("gx") * width_x - HALO)
         local_y = receiver[1:2] - (lax.axis_index("gy") * width_y - HALO)
         inside = (local_x >= 0) & (local_x < ext_x) & (local_y >= 0) & (local_y < ext_y)
@@ -506,9 +525,9 @@
     injected = call(
         inject_kernel,
         struct((steps_total, ext_x * ext_y * ROWS, LANES), F32),
-        specs=[pl.BlockSpec(memory_space=pltpu.SMEM)] + [whole] * 4,
+        specs=[pl.BlockSpec(memory_space=pltpu.SMEM)] + [whole] * 3,
         micros=1.6,
-    )(pair_counts, receiver_cells.T, residuals.T, samples, hop)
+    )(pair_counts, receiver_cells.T, residuals.T, samples)
 
     rim_scratch = [
         VMEM((2, 4 * PER_ROUND) + block, F32),
@@ -547,7 +566,7 @@
 
         return reader
 
-    def run_round(place, number, wind, inject, buffers, state_dz, after):
+    def run_round(place, number, wind, inject, buffers, state_dz, own_dz, after):
         altitude = Altitude()
         winds = []
         for i in range(3):
@@ -566,14 +585,24 @@
 
             radius = 2 * (PER_ROUND - 1 - s) + 1
             advance(
-                place, altitude, old, new, state_dz, winds, injected_at, radius, s == 0, width_x, width_y
+                place,
+                altitude,
+                old,
+                new,
+                state_dz,
+                winds,
+                injected_at,
+                radius,
+                None if s else own_dz,
+                width_x,
+                width_y,
             )
             after(altitude, s, snap, new)
 
     def own(ref, f, x, y, n):
         return ref[f, HALO + x, column_rows(HALO + y, n), :]
 
-    def fill(place, buffer, speed, cols, speed_cols, z_in, x_in, c_in, first, d_in):
+    def fill(place, buffer, speed, cols, speed_cols, z_in, x_in, c_in, firsts):
         def store(f, x, y, n, value):
             ref = buffer.at[f] if f < 4 else speed
             ref[x, column_rows(y, n), :] = value
@@ -586,14 +615,13 @@
             fields = 5
             for x in range(width_x):
                 store(4, HALO + x, HALO, width_y, speed_cols[x])
-        place_edges(place, store, fields, width_x, width_y, z_in, x_in, c_in, first, d_in)
-
-    def first_kernel(wind, inject, cols, speed_cols, z0, z1, x1, d0, d1, c0, *refs):
+        place_edges(place, store, fields, width_x, width_y, z_in, x_in, c_in, firsts)
+
+    def first_kernel(wind, inject, cols, own_dz, speed_cols, z0, z1, x1, c0, c1, *refs):
         early, late, speed, *faces, here, there, dz_az, dz_p = refs
         place = Place()
-        fill(
-            place, here, speed, cols, speed_cols, (z0, z1), (c0, x1), c0, rim_at + forward_fields + 1, (d0, d1)
-        )
+        corners_at = (rim_at + forward_fields, 0)
+        fill(place, here, speed, cols, speed_cols, (z0, z1), (c0, x1), (c0, c1), corners_at)
 
         def after(altitude, s, snap, state):
             out = (early, late)[s]
@@ -601,12 +629,12 @@
                 for x in range(width_x):
                     out[f, x] = own(state, f, x, 0, width_y)
 
-        run_round(place, 0, wind, inject, (here, there), (speed, dz_az, dz_p), after)
+        run_round(place, 0, wind, inject, (here, there), (speed, dz_az, dz_p), own_dz, after)
 
         def load(f, x, y, n):
             return own(here, f, x, y, n)
 
-        pack_faces(place, load, 4, width_x, width_y, faces[:2], faces[2:4], faces[4:])
+        pack_faces(place, load, 4, width_x, width_y, faces[:2], faces[2:])
 
     first = call(
         first_kernel,
@@ -615,10 +643,10 @@
         micros=6.0,
         limit=28,
     )(
-        wind_profile, injected, cols, speed_cols, *z_first, x_first, *d_first, hop
+        wind_profile, injected, cols, own_dz, speed_cols, *z_first, x_first, hop, hop_odd
     )
     early, late, speed_ext = first[:3]
-    z_second, x_second, d_second = first_hop(first[3:])
+    z_second, x_second = first_hop(first[3:])
 
     rim = (*z_first, rim_z, hop, x_first)
 
@@ -641,21 +669,22 @@
     total = call(early_kernel, struct((4,) + tile, F32), scratch=rim_scratch, micros=2.3, limit=16)(
         early, late, forward_early, slopes_early, *rim
     )
-    z_second, x_second, d_second, total = lax.optimization_barrier(
-        (z_second, x_second, d_second, total)
+    late_dz = own_slopes(late)
+    z_second, x_second, total, late_dz = lax.optimization_barrier(
+        (z_second, x_second, total, late_dz)
     )
-    (again,) = second_hop(4, z_second, first[5])
+    again, again_odd = second_hop(4, z_second, first[5], False)
 
     half = depth // 2
     half_blocks = blocks // 2
 
     def second_kernel(
-        wind, inject, cols, speed, total, columns, slopes, *refs
+        wind, inject, cols, own_dz, speed, total, columns, slopes, *refs
     ):
-        rims, (z0, z1, x1, d0, d1, c0), refs = refs[:5], refs[5:11], refs[11:]
+        rims, (z0, z1, x1, c0, c1), refs = refs[:5], refs[5:10], refs[10:]
         last, mine, other, scales, here, there, dz_az, dz_p, sums, rim_y, rim_x = refs
         place = Place()
-        fill(place, here, None, cols, None, (z0, z1), (c0, x1), c0, HALO * 4, (d0, d1))
+        fill(place, here, None, cols, None, (z0, z1), (c0, x1), (c0, c1), (face_start(4, "gx"), 0))
         reader = forward_of(place, columns, 0, *rims, rim_y, rim_x)
         sums[...] = total[...]
 
@@ -669,7 +698,7 @@
                 width_y,
             )
 
-        run_round(place, 1, wind, inject, (here, there), (speed, dz_az, dz_p), after)
+        run_round(place, 1, wind, inject, (here, there), (speed, dz_az, dz_p), own_dz, after)
         me = lax.axis_index("pair")
         for f in range(4):
             for x in range(width_x):
@@ -714,6 +743,7 @@
         wind_profile,
         injected,
         late,
+        late_dz,
         speed_ext,
         total,
         forward_late,
@@ -721,8 +751,8 @@
         *rim,
         *z_second,
         x_second,
-        *d_second,
         again,
+        again_odd,
     )
     across = [(0, 1), (1, 0)]
     other, scales = lax.ppermute(other, "pair", across), lax.ppermute(scales, "pair", across)

time: 75.9 us -> 68.5 us (0.903)
  waiting for transfers between devices: 18.1 us -> 8.57 us
  starting transfers between devices: 30.8 us -> 32.9 us
    ppermute x6 -> x1, starting transfers between devices: 11 us -> 1.28 us  [second_hop(): rim = [lax.ppermute(r, 'pair', [(0, 1), (1, 0)]) for r in rim]]
    ppermute x3 -> x6, starting transfers between devices: 4.66 us -> 12.8 us  [total_of(): lax.ppermute(x, axis, [(i, (i + k) % size) for i in range(size)])]
    ppermute x6 -> x1, waiting for transfers between devices: 7.1 us -> 0.01 us  [second_hop(): rim = [lax.ppermute(r, 'pair', [(0, 1), (1, 0)]) for r in rim]]
    ppermute x8 -> x10, waiting for transfers between devices: 1.96 us -> 5.82 us  [swapped(): return lax.ppermute(x, axis, swap_pairs(lax.axis_size(axis), odd))]
    ppermute x8 -> x10, starting transfers between devices: 13.6 us -> 17.3 us  [swapped(): return lax.ppermute(x, axis, swap_pairs(lax.axis_size(axis), odd))]
    ppermute x3 -> x6, waiting for transfers between devices: 3.85 us -> 0.18 us  [total_of(): lax.ppermute(x, axis, [(i, (i + k) % size) for i in range(size)])]
    ppermute x1, waiting for transfers between devices: 5.19 us -> 2.56 us  [shards(): lax.ppermute(scales, 'pair', across)]
    pallas_call x11 -> x13, Pallas kernels: 22 us -> 22.4 us  [run(): pl.pallas_call(kernel, out_shape=outs, in_specs=specs or [pl.BlockSpec(me...]
  transfers between devices with their start and end apart: 19 -> 19, of which waited for: 10 -> 4; matrix products, arithmetic and copies ran while one was open for 0% -> 0% of each run, Pallas kernels for 16% -> 21%
where the time goes in v5:
time: 68.5 us; the launch traced here: 67.8 us
  starting transfers between devices  32.9 us (48%)
  Pallas kernels  22.4 us (33%)
  waiting for transfers between devices  8.57 us (13%)
  local copies, waits for them, and re-layouts  2.29 us (3%)
  between operations  1.54 us (2%)
    pallas_call x13, Pallas kernels, run(): pl.pallas_call(kernel, out_shape=outs, in_specs=specs or [pl.BlockSpec(me...  22.4 us
    ppermute x10, starting transfers between devices, swapped(): return lax.ppermute(x, axis, swap_pairs(lax.axis_size(axis), odd))  17.3 us
    ppermute x6, starting transfers between devices, total_of(): lax.ppermute(x, axis, [(i, (i + k) % size) for i in range(size)])  12.8 us
    ppermute x10, waiting for transfers between devices, swapped(): return lax.ppermute(x, axis, swap_pairs(lax.axis_size(axis), odd))  5.82 us
    ppermute x1, waiting for transfers between devices, shards(): lax.ppermute(scales, 'pair', across)  2.56 us
    unnamed x16, local copies, waits for them, and re-layouts  2.29 us
  transfers between devices with their start and end apart: 19, of which 4 were waited for; matrix products, arithmetic and copies ran while one was open for 0% of the time, Pallas kernels for 21%

profile of v5, /device:TPU:1, one launch (start us, length us, event | category | flops | bytes accessed | tf_op | source)
XLA Modules:
  0.0 67.8 jit_solution(5542836491326209442)
XLA Ops:
  0.6 1.6 %copy-done = bf16[4,4,8,8,1024]{4,3,2,1,0:T(8,128)(2,1)S(1)} copy-done((bf16[4,4,8,8,1024]{4,3,2,1,0:T(8,128)(2,1)S(1)}, bf16[4,4,8,8,1024]{4,3,2,1,0:T(8,128)(2,1)}, u32[]{:S(2)}) %copy-start) | copy-done | bytes 2097176
  2.2 0.7 %copy-done.5 = s32[256,3]{0,1:T(4,128)S(1)} copy-done((s32[256,3]{0,1:T(4,128)S(1)}, s32[256,3]{0,1:T(4,128)}, u32[]{:S(2)}) %copy-start.5) | copy-done | bytes 3096
  2.9 0.9 %shard_map.95 = f32[8,256]{1,0:T(8,128)S(1)} custom-call(s32[3,256]{1,0:T(4,128)S(1)} %bitcast.3, bf16[4,4,8,8,1024]{4,3,2,1,0:T(8,128)(2,1)S(1)} %copy-done), custom_call_target="tpu_custom_call" | custom-call | flops 1650000000 | bytes 100000 | tf_op jit(solution)/shard_map/pallas_call | solution.py:46
  3.9 0.1 collective-permute-start.5
  4.0 2.7 %collective-permute-start.4 = (f32[8,256]{1,0:T(8,128)S(1)}, f32[8,256]{1,0:T(8,128)S(1)}, u32[]{:S(2)}, u32[]{:S(2)}) collective-permute-start(f32[8,256]{1,0:T(8,128)S(1)} %shard_map.95), channel_id=1, source_target_pairs={{0,8},{4,12},{8,0},{12,4},{1,9},{5,13},{9,1},{13,5},{2,10},{6,14},... | collective-permute-start | bytes 24584 | tf_op jit(solution)/shard_map/ppermute | solution.py:31
  6.7 1.3 %collective-permute-start.3 = (f32[8,256]{1,0:T(8,128)S(1)}, f32[8,256]{1,0:T(8,128)S(1)}, u32[]{:S(2)}, u32[]{:S(2)}) collective-permute-start(f32[8,256]{1,0:T(8,128)S(1)} %shard_map.95), channel_id=1, source_target_pairs={{0,4},{4,8},{8,12},{12,0},{1,5},{5,9},{9,13},{13,1},{2,6},{6,10},{... | collective-permute-start | bytes 24584 | tf_op jit(solution)/shard_map/ppermute | solution.py:31
  8.0 1.3 %shard_map.96 = (f32[4,8,64,128]{3,2,1,0:T(8,128)S(1)}, f32[8,64,128]{2,1,0:T(8,128)S(1)}, f32[8,8,64,128]{3,2,1,0:T(8,128)S(1)}, f32[8,8,64,128]{3,2,1,0:T(8,12...) custom-call(f32[1,4,8,8,1024]{4,3,2,1,0:T(8,128)S(1)} %copy-done.2, ...), custom_call_target="tpu_custom_call" | custom-call | flops 1430000000 | bytes 100000 | tf_op jit(solution)/shard_map/pallas_call | solution.py:46
  9.3 1.4 %collective-permute-start = (bf16[200,8,128]{2,1,0:T(8,128)(2,1)S(1)}, bf16[200,8,128]{2,1,0:T(8,128)(2,1)S(1)}, u32[]{:S(2)}, u32[]{:S(2)}) collective-permute-start(bf16[200,8,128]{2,1,0:T(8,128)(2,1)S(1)} %get-tuple-element.46), channel_id=1, source_target_pairs={{0,1},{1,0},{2,3},{3,2},{4,5},{5,4},{6,7},{7,6},{8,9},{9,8},{10,11... | collective-permute-start | bytes 1228808 | tf_op jit(solution)/shard_map/ppermute | solution.py:26
  10.6 0.7 collective-permute-start.1
  11.3 0.0 collective-permute-done.5
  11.3 2.2 %collective-permute-start.2 = (bf16[33,64,128]{2,1,0:T(8,128)(2,1)S(1)}, bf16[33,64,128]{2,1,0:T(8,128)(2,1)S(1)}, u32[]{:S(2)}, u32[]{:S(2)}) collective-permute-start(bf16[33,64,128]{2,1,0:T(8,128)(2,1)S(1)} %get-tuple-element.48), channel_id=1, source_target_pairs={{0,0},{4,8},{8,4},{12,12},{1,1},{5,9},{9,5},{13,13},{2,2},{6,10},{... | collective-permute-start | bytes 1622024 | tf_op jit(solution)/shard_map/ppermute | solution.py:26
  13.6 0.0 collective-permute-done.4
  13.6 0.0 collective-permute-done.3
  13.6 2.7 %shard_map.97 = (f32[8,8,64,128]{3,2,1,0:T(8,128)S(1)}, f32[8,8,64,128]{3,2,1,0:T(8,128)S(1)}, f32[8,256]{1,0:T(8,128)S(1)}) custom-call(f32[8,8,64,128]{3,2,1,0:T(8,128)S(1)} %get-tuple-element.49.early.columns, f32[8,8,64,128]{3,2,1,0:T(8,128)S(1)} %get-tuple-element.50.late.columns, f32[8,256]{1,0:T(8,128)S(1)} %add_add_fusion.1.sample), custom_call_target="tpu_custom_call" | custom-call | flops 2969999872 | bytes 100000 | tf_op jit(solution)/shard_map/pallas_call | solution.py:46
  16.3 2.2 %collective-permute-start.8 = (f32[8,256]{1,0:T(8,128)S(1)}, f32[8,256]{1,0:T(8,128)S(1)}, u32[]{:S(2)}, u32[]{:S(2)}) collective-permute-start(f32[8,256]{1,0:T(8,128)S(1)} %get-tuple-element.52), channel_id=1, source_target_pairs={{0,3},{1,0},{2,1},{3,2},{4,7},{5,4},{6,5},{7,6},{8,11},{9,8},{10,9... | collective-permute-start | bytes 24584 | tf_op jit(solution)/shard_map/ppermute | solution.py:31
  18.6 3.1 %collective-permute-start.7 = (f32[8,256]{1,0:T(8,128)S(1)}, f32[8,256]{1,0:T(8,128)S(1)}, u32[]{:S(2)}, u32[]{:S(2)}) collective-permute-start(f32[8,256]{1,0:T(8,128)S(1)} %get-tuple-element.52), channel_id=1, source_target_pairs={{0,2},{1,3},{2,0},{3,1},{4,6},{5,7},{6,4},{7,5},{8,10},{9,11},{10,... | collective-permute-start | bytes 24584 | tf_op jit(solution)/shard_map/ppermute | solution.py:31
  21.7 0.0 collective-permute-done.8
  21.7 3.3 %collective-permute-start.6 = (f32[8,256]{1,0:T(8,128)S(1)}, f32[8,256]{1,0:T(8,128)S(1)}, u32[]{:S(2)}, u32[]{:S(2)}) collective-permute-start(f32[8,256]{1,0:T(8,128)S(1)} %get-tuple-element.52), channel_id=1, source_target_pairs={{0,1},{1,2},{2,3},{3,0},{4,5},{5,6},{6,7},{7,4},{8,9},{9,10},{10,1... | collective-permute-start | bytes 24584 | tf_op jit(solution)/shard_map/ppermute | solution.py:31
  25.0 0.8 %shard_map.98.own_dz = f32[4,8,64,128]{3,2,1,0:T(8,128)S(1)} custom-call(f32[4,8,64,128]{3,2,1,0:T(8,128)S(1)} %get-tuple-element.55.cols), custom_call_target="tpu_custom_call" | custom-call | flops 880000000 | bytes 100000 | tf_op jit(solution)/shard_map/pallas_call | solution.py:46
  25.8 0.0 collective-permute-done.7
  25.8 0.2 collective-permute-done.6
  26.0 0.0 collective-permute-done.z_even.z0.refs_0_
  26.0 0.0 collective-permute-done.2.x1.refs_4_
  26.0 0.1 shard_map.100
  26.1 1.0 %collective-permute-start.9 = (bf16[41,64,128]{2,1,0:T(8,128)(2,1)S(1)}, bf16[41,64,128]{2,1,0:T(8,128)(2,1)S(1)}, u32[]{:S(2)}, u32[]{:S(2)}) collective-permute-start(bf16[41,64,128]{2,1,0:T(8,128)(2,1)S(1)} %get-tuple-element.63), channel_id=1, source_target_pairs={{0,4},{4,0},{8,12},{12,8},{1,5},{5,1},{9,13},{13,9},{2,6},{6,2},{1... | collective-permute-start | bytes 2015240 | tf_op jit(solution)/shard_map/ppermute | solution.py:26
  27.8 4.0 %collective-permute-start.10 = (bf16[8,64,128]{2,1,0:T(8,128)(2,1)S(1)}, bf16[8,64,128]{2,1,0:T(8,128)(2,1)S(1)}, u32[]{:S(2)}, u32[]{:S(2)}) collective-permute-start(bf16[8,64,128]{2,1,0:T(8,128)(2,1)S(1)} %get-tuple-element.64), channel_id=1, source_target_pairs={{0,0},{4,8},{8,4},{12,12},{1,1},{5,9},{9,5},{13,13},{2,2},{6,10},{... | collective-permute-start | bytes 393224 | tf_op jit(solution)/shard_map/ppermute | solution.py:26
  31.8 1.3 %collective-permute-start.14 = (bf16[16,64,128]{2,1,0:T(8,128)(2,1)S(1)}, bf16[16,64,128]{2,1,0:T(8,128)(2,1)S(1)}, u32[]{:S(2)}, u32[]{:S(2)}) collective-permute-start(bf16[16,64,128]{2,1,0:T(8,128)(2,1)S(1)} %get-tuple-element.71), channel_id=1, source_target_pairs={{0,16},{16,0},{1,17},{17,1},{2,18},{18,2},{3,19},{19,3},{4,20},{20... | collective-permute-start | bytes 786440 | tf_op jit(solution)/shard_map/ppermute | solution.py:358
  33.0 1.5 %shard_map.99.inject = f32[4,2048,128]{2,1,0:T(8,128)S(1)} custom-call(s32[1]{0:T(128)S(6)} %copy.10.counts, s32[3,256]{1,0:T(4,128)S(1)} %bitcast.4, f32[4,256]{1,0:T(4,128)S(1)} %bitcast.5, f32[8,256]{1,0:T(8,128)S(1)} %add_add_fusion.samples), custom_call_target="tpu_custom_call" | custom-call | flops 1760000000 | bytes 100000 | tf_op jit(solution)/shard_map/pallas_call | solution.py:46
  34.6 0.0 collective-permute-done.9.c0.refs_3_
  34.6 4.9 %shard_map.101 = (f32[4,8,64,128]{3,2,1,0:T(8,128)S(1)}, f32[4,8,64,128]{3,2,1,0:T(8,128)S(1)}, f32[16,128,128]{2,1,0:T(8,128)S(1)}, bf16[112,8,128]{2,1,0:T(8,1...) custom-call(f32[3,1024]{1,0:T(4,128)S(1)} %copy-done.4, ...), custom_call_target="tpu_custom_call" | custom-call | flops 6600000000 | bytes 100000 | tf_op jit(solution)/shard_map/pallas_call | solution.py:46
  39.5 1.8 %collective-permute-start.11 = (bf16[112,8,128]{2,1,0:T(8,128)(2,1)S(1)}, bf16[112,8,128]{2,1,0:T(8,128)(2,1)S(1)}, u32[]{:S(2)}, u32[]{:S(2)}) collective-permute-start(bf16[112,8,128]{2,1,0:T(8,128)(2,1)S(1)} %get-tuple-element.66), channel_id=1, source_target_pairs={{0,1},{1,0},{2,3},{3,2},{4,5},{5,4},{6,7},{7,6},{8,9},{9,8},{10,11... | collective-permute-start | bytes 688136 | tf_op jit(solution)/shard_map/ppermute | solution.py:26
  41.4 0.7 collective-permute-start.12
  42.0 2.8 %collective-permute-start.13 = (bf16[14,64,128]{2,1,0:T(8,128)(2,1)S(1)}, bf16[14,64,128]{2,1,0:T(8,128)(2,1)S(1)}, u32[]{:S(2)}, u32[]{:S(2)}) collective-permute-start(bf16[14,64,128]{2,1,0:T(8,128)(2,1)S(1)} %get-tuple-element.68), channel_id=1, source_target_pairs={{0,0},{4,8},{8,4},{12,12},{1,1},{5,9},{9,5},{13,13},{2,2},{6,10},{... | collective-permute-start | bytes 688136 | tf_op jit(solution)/shard_map/ppermute | solution.py:26
  44.8 0.8 %shard_map.103.own_dz = f32[4,8,64,128]{3,2,1,0:T(8,128)S(1)} custom-call(f32[4,8,64,128]{3,2,1,0:T(8,128)S(1)} %get-tuple-element.65.late.cols), custom_call_target="tpu_custom_call" | custom-call | flops 880000000 | bytes 100000 | tf_op jit(solution)/shard_map/pallas_call | solution.py:46
  45.6 0.0 collective-permute-done.14.zp.refs_2_
  45.6 1.1 %shard_map.102.total = f32[4,8,64,128]{3,2,1,0:T(8,128)S(1)} custom-call(f32[4,8,64,128]{3,2,1,0:T(8,128)S(1)} %get-tuple-element.69.early, f32[4,8,64,128]{3,2,1,0:T(8,128)S(1)} %get-tuple-element.65.late.cols, f32[8,8,64,128]{3,2,1,0:T(8,128)S(1)} %get-tuple-element.49.early.columns, f32[8,8,64,128]{3,2,1,0:T(8,128)S(1)} %get-tuple-element.70.slopes, ...), custom_call_target="tpu_custom_call" | custom-call | flops 2529999872 | bytes 100000 | tf_op jit(solution)/shard_map/pallas_call | solution.py:46
  46.7 0.0 collective-permute-done.12.z_odd.refs_6_
  46.7 2.6 %collective-permute-done.13.refs_7_ = bf16[14,64,128]{2,1,0:T(8,128)(2,1)S(1)} collective-permute-done((bf16[14,64,128]{2,1,0:T(8,128)(2,1)S(1)}, bf16[14,64,128]{2,1,0:T(8,128)(2,1)S(1)}, u32[]{:S(2)}, u32[]{:S(2)}) %collective-permute-start.13) | collective-permute-done | bytes 229408 | tf_op jit(solution)/shard_map/ppermute | solution.py:26
  49.4 0.1 shard_map.104
  49.4 0.1 collective-permute-start.15
  49.5 2.8 %collective-permute-start.16 = (bf16[6,64,128]{2,1,0:T(8,128)(2,1)S(1)}, bf16[6,64,128]{2,1,0:T(8,128)(2,1)S(1)}, u32[]{:S(2)}, u32[]{:S(2)}) collective-permute-start(bf16[6,64,128]{2,1,0:T(8,128)(2,1)S(1)} %get-tuple-element.81), channel_id=1, source_target_pairs={{0,0},{4,8},{8,4},{12,12},{1,1},{5,9},{9,5},{13,13},{2,2},{6,10},{... | collective-permute-start | bytes 294920 | tf_op jit(solution)/shard_map/ppermute | solution.py:26
  52.3 3.2 %collective-permute-done.16.refs_9_ = bf16[6,64,128]{2,1,0:T(8,128)(2,1)S(1)} collective-permute-done((bf16[6,64,128]{2,1,0:T(8,128)(2,1)S(1)}, bf16[6,64,128]{2,1,0:T(8,128)(2,1)S(1)}, u32[]{:S(2)}, u32[]{:S(2)}) %collective-permute-start.16) | collective-permute-done | bytes 98336 | tf_op jit(solution)/shard_map/ppermute | solution.py:26
  55.5 6.1 %shard_map.105 = (f32[4,8,64,128]{3,2,1,0:T(8,128)S(1)}, f32[4,8,64,128]{3,2,1,0:T(8,128)S(1)}, s16[4,4,16,512]{3,2,1,0:T(8,128)(2,1)S(1)}, f32[4,512]{1,0:T(4,128)S(1)}) custom-call(f32[3,1024]{1,0:T(4,128)S(1)} %copy-done.4, f32[4,2048,128]{2,1,0:T(8,128)S(1)} %shard_map.99.inject, f32[4,8,64,128]{3,2,1,0:T(8,128)S(1)} %get-tuple-element.65.late.cols, ...), custom_call_target="tpu_custom_call" | custom-call | flops 9900000256 | bytes 100000 | tf_op jit(solution)/shard_map/pallas_call | solution.py:46
  61.5 1.3 %collective-permute-start.17 = (s16[4,4,16,512]{3,2,1,0:T(8,128)(2,1)S(1)}, s16[4,4,16,512]{3,2,1,0:T(8,128)(2,1)S(1)}, u32[]{:S(2)}, u32[]{:S(2)}) collective-permute-start(s16[4,4,16,512]{3,2,1,0:T(8,128)(2,1)S(1)} %get-tuple-element.85), channel_id=1, source_target_pairs={{0,16},{16,0},{1,17},{17,1},{2,18},{18,2},{3,19},{19,3},{4,20},{20... | collective-permute-start | bytes 786440 | tf_op jit(solution)/shard_map/ppermute | solution.py:758
  62.8 0.3 collective-permute-start.18
  63.1 1.3 %shard_map.106 = (f32[1,4,8,8,1024]{4,3,2,1,0:T(8,128)}, f32[4,8,8,512]{3,2,1,0:T(8,128)S(1)}) custom-call(f32[4,8,64,128]{3,2,1,0:T(8,128)S(1)} %get-tuple-element.82.last, f32[4,8,64,128]{3,2,1,0:T(8,128)S(1)} %get-tuple-element.83.sums), custom_call_target="tpu_custom_call" | custom-call | flops 1100000000 | bytes 100000 | tf_op jit(solution)/shard_map/pallas_call | solution.py:46
  64.4 2.6 %collective-permute-done.18.scales = f32[4,512]{1,0:T(4,128)S(1)} collective-permute-done((f32[4,512]{1,0:T(4,128)S(1)}, f32[4,512]{1,0:T(4,128)S(1)}, u32[]{:S(2)}, u32[]{:S(2)}) %collective-permute-start.18) | collective-permute-done | bytes 8224 | tf_op jit(solution)/shard_map/ppermute | solution.py:758
  66.9 0.9 %shard_map.107 = f32[4,8,8,512]{3,2,1,0:T(8,128)} custom-call(f32[4,8,8,512]{3,2,1,0:T(8,128)S(1)} %get-tuple-element.84.mine, s16[4,4,16,512]{3,2,1,0:T(8,128)(2,1)S(1)} %collective-permute-done.17.other, f32[4,512]{1,0:T(4,128)S(1)} %collective-permute-done.18.scales), custom_call_target="tpu_custom_call" | custom-call | flops 880000000 | bytes 100000 | tf_op jit(solution)/shard_map/pallas_call | solution.py:46
  (21 shorter events, 0.1 us)
Async XLA Ops:
  0.6 1.6 %copy-start = (bf16[4,4,8,8,1024]{4,3,2,1,0:T(8,128)(2,1)S(1)}, bf16[4,4,8,8,1024]{4,3,2,1,0:T(8,128)(2,1)}, u32[]{:S(2)}) copy-start(bf16[4,4,8,8,1024]{4,3,2,1,0:T(8,128)(2,1)} %forward.3) | copy-start | bytes 6291460
  2.2 0.7 %copy-start.5 = (s32[256,3]{0,1:T(4,128)S(1)}, s32[256,3]{0,1:T(4,128)}, u32[]{:S(2)}) copy-start(s32[256,3]{0,1:T(4,128)} %param.13) | copy-start | bytes 9220
  2.9 5.1 %copy-start.1 = (bf16[4,4,8,8,1024]{4,3,2,1,0:T(8,128)(2,1)S(1)}, bf16[4,4,8,8,1024]{4,3,2,1,0:T(8,128)(2,1)}, u32[]{:S(2)}) copy-start(bf16[4,4,8,8,1024]{4,3,2,1,0:T(8,128)(2,1)} %forward.3) | copy-start | bytes 6291460
  2.9 5.1 %copy-start.2 = (f32[1,4,8,8,1024]{4,3,2,1,0:T(8,128)S(1)}, f32[1,4,8,8,1024]{4,3,2,1,0:T(8,128)}, u32[]{:S(2)}) copy-start(f32[1,4,8,8,1024]{4,3,2,1,0:T(8,128)} %state) | copy-start | bytes 3145732
  2.9 5.1 %copy-start.3 = (f32[8,8,1024]{2,1,0:T(8,128)S(1)}, f32[8,8,1024]{2,1,0:T(8,128)}, u32[]{:S(2)}) copy-start(f32[8,8,1024]{2,1,0:T(8,128)} %speed.1) | copy-start | bytes 786436
  3.9 7.5 %collective-permute-start.5 = (f32[8,256]{1,0:T(8,128)S(1)}, f32[8,256]{1,0:T(8,128)S(1)}, u32[]{:S(2)}, u32[]{:S(2)}) collective-permute-start(f32[8,256]{1,0:T(8,128)S(1)} %shard_map.95), channel_id=1, source_target_pairs={{0,12},{4,0},{8,4},{12,8},{1,13},{5,1},{9,5},{13,9},{2,14},{6,2},{... | collective-permute-start | bytes 24584 | tf_op jit(solution)/shard_map/ppermute | solution.py:31
  4.0 9.6 %collective-permute-start.4 = (f32[8,256]{1,0:T(8,128)S(1)}, f32[8,256]{1,0:T(8,128)S(1)}, u32[]{:S(2)}, u32[]{:S(2)}) collective-permute-start(f32[8,256]{1,0:T(8,128)S(1)} %shard_map.95), channel_id=1, source_target_pairs={{0,8},{4,12},{8,0},{12,4},{1,9},{5,13},{9,1},{13,5},{2,10},{6,14},... | collective-permute-start | bytes 24584 | tf_op jit(solution)/shard_map/ppermute | solution.py:31
  6.7 6.9 %collective-permute-start.3 = (f32[8,256]{1,0:T(8,128)S(1)}, f32[8,256]{1,0:T(8,128)S(1)}, u32[]{:S(2)}, u32[]{:S(2)}) collective-permute-start(f32[8,256]{1,0:T(8,128)S(1)} %shard_map.95), channel_id=1, source_target_pairs={{0,4},{4,8},{8,12},{12,0},{1,5},{5,9},{9,13},{13,1},{2,6},{6,10},{... | collective-permute-start | bytes 24584 | tf_op jit(solution)/shard_map/ppermute | solution.py:31
  9.3 16.7 %collective-permute-start = (bf16[200,8,128]{2,1,0:T(8,128)(2,1)S(1)}, bf16[200,8,128]{2,1,0:T(8,128)(2,1)S(1)}, u32[]{:S(2)}, u32[]{:S(2)}) collective-permute-start(bf16[200,8,128]{2,1,0:T(8,128)(2,1)S(1)} %get-tuple-element.46), channel_id=1, source_target_pairs={{0,1},{1,0},{2,3},{3,2},{4,5},{5,4},{6,7},{7,6},{8,9},{9,8},{10,11... | collective-permute-start | bytes 1228808 | tf_op jit(solution)/shard_map/ppermute | solution.py:26
  10.6 15.3 %collective-permute-start.1 = (bf16[200,8,128]{2,1,0:T(8,128)(2,1)S(1)}, bf16[200,8,128]{2,1,0:T(8,128)(2,1)S(1)}, u32[]{:S(2)}, u32[]{:S(2)}) collective-permute-start(bf16[200,8,128]{2,1,0:T(8,128)(2,1)S(1)} %get-tuple-element.47), channel_id=1, source_target_pairs={{0,0},{1,2},{2,1},{3,3},{4,4},{5,6},{6,5},{7,7},{8,8},{9,10},{10,9... | collective-permute-start | bytes 1228808 | tf_op jit(solution)/shard_map/ppermute | solution.py:26
  11.3 14.6 %collective-permute-start.2 = (bf16[33,64,128]{2,1,0:T(8,128)(2,1)S(1)}, bf16[33,64,128]{2,1,0:T(8,128)(2,1)S(1)}, u32[]{:S(2)}, u32[]{:S(2)}) collective-permute-start(bf16[33,64,128]{2,1,0:T(8,128)(2,1)S(1)} %get-tuple-element.48), channel_id=1, source_target_pairs={{0,0},{4,8},{8,4},{12,12},{1,1},{5,9},{9,5},{13,13},{2,2},{6,10},{... | collective-permute-start | bytes 1622024 | tf_op jit(solution)/shard_map/ppermute | solution.py:26
  16.3 5.3 %collective-permute-start.8 = (f32[8,256]{1,0:T(8,128)S(1)}, f32[8,256]{1,0:T(8,128)S(1)}, u32[]{:S(2)}, u32[]{:S(2)}) collective-permute-start(f32[8,256]{1,0:T(8,128)S(1)} %get-tuple-element.52), channel_id=1, source_target_pairs={{0,3},{1,0},{2,1},{3,2},{4,7},{5,4},{6,5},{7,6},{8,11},{9,8},{10,9... | collective-permute-start | bytes 24584 | tf_op jit(solution)/shard_map/ppermute | solution.py:31
  18.6 7.2 %collective-permute-start.7 = (f32[8,256]{1,0:T(8,128)S(1)}, f32[8,256]{1,0:T(8,128)S(1)}, u32[]{:S(2)}, u32[]{:S(2)}) collective-permute-start(f32[8,256]{1,0:T(8,128)S(1)} %get-tuple-element.52), channel_id=1, source_target_pairs={{0,2},{1,3},{2,0},{3,1},{4,6},{5,7},{6,4},{7,5},{8,10},{9,11},{10,... | collective-permute-start | bytes 24584 | tf_op jit(solution)/shard_map/ppermute | solution.py:31
  21.7 4.3 %collective-permute-start.6 = (f32[8,256]{1,0:T(8,128)S(1)}, f32[8,256]{1,0:T(8,128)S(1)}, u32[]{:S(2)}, u32[]{:S(2)}) collective-permute-start(f32[8,256]{1,0:T(8,128)S(1)} %get-tuple-element.52), channel_id=1, source_target_pairs={{0,1},{1,2},{2,3},{3,0},{4,5},{5,6},{6,7},{7,4},{8,9},{9,10},{10,1... | collective-permute-start | bytes 24584 | tf_op jit(solution)/shard_map/ppermute | solution.py:31
  24.9 8.1 %copy-start.6 = (s32[256,3]{0,1:T(4,128)S(1)}, s32[256,3]{0,1:T(4,128)}, u32[]{:S(2)}) copy-start(s32[256,3]{0,1:T(4,128)} %param.14) | copy-start | bytes 9220
  25.0 8.1 %copy-start.7 = (f32[256,4]{0,1:T(4,128)S(1)}, f32[256,4]{0,1:T(4,128)}, u32[]{:S(2)}) copy-start(f32[256,4]{0,1:T(4,128)} %param.15) | copy-start | bytes 12292
  26.1 8.5 %collective-permute-start.9 = (bf16[41,64,128]{2,1,0:T(8,128)(2,1)S(1)}, bf16[41,64,128]{2,1,0:T(8,128)(2,1)S(1)}, u32[]{:S(2)}, u32[]{:S(2)}) collective-permute-start(bf16[41,64,128]{2,1,0:T(8,128)(2,1)S(1)} %get-tuple-element.63), channel_id=1, source_target_pairs={{0,4},{4,0},{8,12},{12,8},{1,5},{5,1},{9,13},{13,9},{2,6},{6,2},{1... | collective-permute-start | bytes 2015240 | tf_op jit(solution)/shard_map/ppermute | solution.py:26
  27.8 6.8 %collective-permute-start.10 = (bf16[8,64,128]{2,1,0:T(8,128)(2,1)S(1)}, bf16[8,64,128]{2,1,0:T(8,128)(2,1)S(1)}, u32[]{:S(2)}, u32[]{:S(2)}) collective-permute-start(bf16[8,64,128]{2,1,0:T(8,128)(2,1)S(1)} %get-tuple-element.64), channel_id=1, source_target_pairs={{0,0},{4,8},{8,4},{12,12},{1,1},{5,9},{9,5},{13,13},{2,2},{6,10},{... | collective-permute-start | bytes 393224 | tf_op jit(solution)/shard_map/ppermute | solution.py:26
  31.8 13.8 %collective-permute-start.14 = (bf16[16,64,128]{2,1,0:T(8,128)(2,1)S(1)}, bf16[16,64,128]{2,1,0:T(8,128)(2,1)S(1)}, u32[]{:S(2)}, u32[]{:S(2)}) collective-permute-start(bf16[16,64,128]{2,1,0:T(8,128)(2,1)S(1)} %get-tuple-element.71), channel_id=1, source_target_pairs={{0,16},{16,0},{1,17},{17,1},{2,18},{18,2},{3,19},{19,3},{4,20},{20... | collective-permute-start | bytes 786440 | tf_op jit(solution)/shard_map/ppermute | solution.py:358
  33.0 1.6 %copy-start.4 = (f32[3,1024]{1,0:T(4,128)S(1)}, f32[3,1024]{1,0:T(4,128)}, u32[]{:S(2)}) copy-start(f32[3,1024]{1,0:T(4,128)} %wind.3) | copy-start | bytes 36868
  39.5 7.2 %collective-permute-start.11 = (bf16[112,8,128]{2,1,0:T(8,128)(2,1)S(1)}, bf16[112,8,128]{2,1,0:T(8,128)(2,1)S(1)}, u32[]{:S(2)}, u32[]{:S(2)}) collective-permute-start(bf16[112,8,128]{2,1,0:T(8,128)(2,1)S(1)} %get-tuple-element.66), channel_id=1, source_target_pairs={{0,1},{1,0},{2,3},{3,2},{4,5},{5,4},{6,7},{7,6},{8,9},{9,8},{10,11... | collective-permute-start | bytes 688136 | tf_op jit(solution)/shard_map/ppermute | solution.py:26
  41.4 5.4 %collective-permute-start.12 = (bf16[112,8,128]{2,1,0:T(8,128)(2,1)S(1)}, bf16[112,8,128]{2,1,0:T(8,128)(2,1)S(1)}, u32[]{:S(2)}, u32[]{:S(2)}) collective-permute-start(bf16[112,8,128]{2,1,0:T(8,128)(2,1)S(1)} %get-tuple-element.67), channel_id=1, source_target_pairs={{0,0},{1,2},{2,1},{3,3},{4,4},{5,6},{6,5},{7,7},{8,8},{9,10},{10,9... | collective-permute-start | bytes 688136 | tf_op jit(solution)/shard_map/ppermute | solution.py:26
  42.0 7.3 %collective-permute-start.13 = (bf16[14,64,128]{2,1,0:T(8,128)(2,1)S(1)}, bf16[14,64,128]{2,1,0:T(8,128)(2,1)S(1)}, u32[]{:S(2)}, u32[]{:S(2)}) collective-permute-start(bf16[14,64,128]{2,1,0:T(8,128)(2,1)S(1)} %get-tuple-element.68), channel_id=1, source_target_pairs={{0,0},{4,8},{8,4},{12,12},{1,1},{5,9},{9,5},{13,13},{2,2},{6,10},{... | collective-permute-start | bytes 688136 | tf_op jit(solution)/shard_map/ppermute | solution.py:26
  49.4 6.0 %collective-permute-start.15 = (bf16[20,64,128]{2,1,0:T(8,128)(2,1)S(1)}, bf16[20,64,128]{2,1,0:T(8,128)(2,1)S(1)}, u32[]{:S(2)}, u32[]{:S(2)}) collective-permute-start(bf16[20,64,128]{2,1,0:T(8,128)(2,1)S(1)} %get-tuple-element.80), channel_id=1, source_target_pairs={{0,4},{4,0},{8,12},{12,8},{1,5},{5,1},{9,13},{13,9},{2,6},{6,2},{1... | collective-permute-start | bytes 983048 | tf_op jit(solution)/shard_map/ppermute | solution.py:26
  49.5 5.9 %collective-permute-start.16 = (bf16[6,64,128]{2,1,0:T(8,128)(2,1)S(1)}, bf16[6,64,128]{2,1,0:T(8,128)(2,1)S(1)}, u32[]{:S(2)}, u32[]{:S(2)}) collective-permute-start(bf16[6,64,128]{2,1,0:T(8,128)(2,1)S(1)} %get-tuple-element.81), channel_id=1, source_target_pairs={{0,0},{4,8},{8,4},{12,12},{1,1},{5,9},{9,5},{13,13},{2,2},{6,10},{... | collective-permute-start | bytes 294920 | tf_op jit(solution)/shard_map/ppermute | solution.py:26
  61.5 5.4 %collective-permute-start.17 = (s16[4,4,16,512]{3,2,1,0:T(8,128)(2,1)S(1)}, s16[4,4,16,512]{3,2,1,0:T(8,128)(2,1)S(1)}, u32[]{:S(2)}, u32[]{:S(2)}) collective-permute-start(s16[4,4,16,512]{3,2,1,0:T(8,128)(2,1)S(1)} %get-tuple-element.85), channel_id=1, source_target_pairs={{0,16},{16,0},{1,17},{17,1},{2,18},{18,2},{3,19},{19,3},{4,20},{20... | collective-permute-start | bytes 786440 | tf_op jit(solution)/shard_map/ppermute | solution.py:758
  62.8 4.1 %collective-permute-start.18 = (f32[4,512]{1,0:T(4,128)S(1)}, f32[4,512]{1,0:T(4,128)S(1)}, u32[]{:S(2)}, u32[]{:S(2)}) collective-permute-start(f32[4,512]{1,0:T(4,128)S(1)} %get-tuple-element.86), channel_id=1, source_target_pairs={{0,16},{16,0},{1,17},{17,1},{2,18},{18,2},{3,19},{19,3},{4,20},{20... | collective-permute-start | bytes 24584 | tf_op jit(solution)/shard_map/ppermute | solution.py:758

commit v6 on v5

--- a/solution.py
+++ b/solution.py
@@ -230,9 +230,14 @@
     p, ax, ay, az = (old.at[f] for f in range(4))
 
     def slope(f, value, x, y, kept):
-        if own_dz is None or kept is not None or not HALO <= y < HALO + width_y:
+        if own_dz is None or kept is not None:
             return altitude(value)
-        return own_dz[f, x - HALO, column_rows(y - HALO, 1), :]
+        if HALO <= y < HALO + width_y:
+            return own_dz[0][f, x - HALO, column_rows(y - HALO, 1), :]
+        lower = jnp.where(place.plus("gy", 0), 1, 0)
+        if y < HALO:
+            return own_dz[1][lower, f, x - HALO, HALO - 1 - y]
+        return own_dz[1][1 - lower, f, x - HALO, y - HALO - width_y]
 
     def p_row(x, y0, n, kept):
         ps = [at(p, x, y0 + k - 1) for k in range(n + 2)]
@@ -257,9 +262,21 @@
 
     def a_row(x, y0, n, kept):
         ps = [at(pn, x, y0 + k - 1) for k in range(n + 2)]
+        away = radius - 1 - (HALO - y0)
         for f, a in ((1, ax), (2, ay), (3, az)):
+            if radius == 1:
+                deep = 0
+            elif f == 1:
+                deep = radius - 2 if not away else radius - 1 - away
+            elif f == 2:
+                deep = radius - 1 - away if away < radius - 1 else -1
+            else:
+                deep = radius - 2 - away
+            if deep < 0:
+                continue
+            start = HALO - deep - y0
             vs = [at(a, x, y0 + k - 1) for k in range(n + 2)]
-            for k in range(n):
+            for k in range(start, n - start):
                 y = y0 + k
                 if f == 1:
                     grad = at(pn, x + 1, y) - at(pn, x - 1, y)
@@ -469,6 +486,26 @@
 
     own_dz = own_slopes(cols)
 
+    def face_slopes(z):
+        def kernel(z_even, z_odd, out):
+            place, altitude = Place(), Altitude()
+
+            def one(x, carry):
+                for odd, ref in enumerate((z_even, z_odd)):
+                    plus = place.plus("gy", odd)
+                    for f, reach in enumerate((HALO - 1, 1, HALO - 2, HALO - 1)):
+                        deep = face_depth(f, "gy")
+                        for d in range(reach):
+                            at = face_start(f, "gy") * width_x + x * deep
+                            at += jnp.where(plus, d, deep - 1 - d)
+                            out[odd, f, x, d] = altitude(ref[at].astype(F32))
+                return carry
+
+            lax.fori_loop(0, width_x, one, 0)
+
+        out = struct((2, 4, width_x, HALO - 1, ROWS, LANES), F32)
+        return call(kernel, out, micros=0.6, limit=8)(*z)
+
     def slope_kernel(early, late, sample, *outs):
         *outs, held = outs
         held[...] = sample[...]
@@ -617,7 +654,7 @@
                 store(4, HALO + x, HALO, width_y, speed_cols[x])
         place_edges(place, store, fields, width_x, width_y, z_in, x_in, c_in, firsts)
 
-    def first_kernel(wind, inject, cols, own_dz, speed_cols, z0, z1, x1, c0, c1, *refs):
+    def first_kernel(wind, inject, cols, own_dz, face_dz, speed_cols, z0, z1, x1, c0, c1, *refs):
         early, late, speed, *faces, here, there, dz_az, dz_p = refs
         place = Place()
         corners_at = (rim_at + forward_fields, 0)
@@ -629,7 +666,7 @@
                 for x in range(width_x):
                     out[f, x] = own(state, f, x, 0, width_y)
 
-        run_round(place, 0, wind, inject, (here, there), (speed, dz_az, dz_p), own_dz, after)
+        run_round(place, 0, wind, inject, (here, there), (speed, dz_az, dz_p), (own_dz, face_dz), after)
 
         def load(f, x, y, n):
             return own(here, f, x, y, n)
@@ -643,7 +680,7 @@
         micros=6.0,
         limit=28,
     )(
-        wind_profile, injected, cols, own_dz, speed_cols, *z_first, x_first, hop, hop_odd
+        wind_profile, injected, cols, own_dz, face_slopes(z_first), speed_cols, *z_first, x_first, hop, hop_odd
     )
     early, late, speed_ext = first[:3]
     z_second, x_second = first_hop(first[3:])
@@ -679,7 +716,7 @@
     half_blocks = blocks // 2
 
     def second_kernel(
-        wind, inject, cols, own_dz, speed, total, columns, slopes, *refs
+        wind, inject, cols, own_dz, face_dz, speed, total, columns, slopes, *refs
     ):
         rims, (z0, z1, x1, c0, c1), refs = refs[:5], refs[5:10], refs[10:]
         last, mine, other, scales, here, there, dz_az, dz_p, sums, rim_y, rim_x = refs
@@ -698,7 +735,7 @@
                 width_y,
             )
 
-        run_round(place, 1, wind, inject, (here, there), (speed, dz_az, dz_p), own_dz, after)
+        run_round(place, 1, wind, inject, (here, there), (speed, dz_az, dz_p), (own_dz, face_dz), after)
         me = lax.axis_index("pair")
         for f in range(4):
             for x in range(width_x):
@@ -744,6 +781,7 @@
         injected,
         late,
         late_dz,
+        face_slopes(z_second),
         speed_ext,
         total,
         forward_late,

time: 68.5 us -> 67.2 us (0.981)
  waiting for transfers between devices: 8.57 us -> 7 us
    ppermute x10, waiting for transfers between devices: 5.82 us -> 4.28 us  [swapped(): return lax.ppermute(x, axis, swap_pairs(lax.axis_size(axis), odd))]
    pallas_call x13 -> x15, Pallas kernels: 22.4 us -> 22.6 us  [run(): pl.pallas_call(kernel, out_shape=outs, in_specs=specs or [pl.BlockSpec(me...]
  transfers between devices with their start and end apart: 19 -> 19, of which waited for: 4 -> 4; matrix products, arithmetic and copies ran while one was open for 0% -> 0% of each run, Pallas kernels for 21% -> 23%
where the time goes in v6:
time: 67.2 us; the launch traced here: 66.5 us
  starting transfers between devices  33 us (49%)
  Pallas kernels  22.6 us (34%)
  waiting for transfers between devices  7 us (10%)
  local copies, waits for them, and re-layouts  2.3 us (3%)
  between operations  1.6 us (2%)
    pallas_call x15, Pallas kernels, run(): pl.pallas_call(kernel, out_shape=outs, in_specs=specs or [pl.BlockSpec(me...  22.6 us
    ppermute x10, starting transfers between devices, swapped(): return lax.ppermute(x, axis, swap_pairs(lax.axis_size(axis), odd))  17.4 us
    ppermute x6, starting transfers between devices, total_of(): lax.ppermute(x, axis, [(i, (i + k) % size) for i in range(size)])  12.8 us
    ppermute x10, waiting for transfers between devices, swapped(): return lax.ppermute(x, axis, swap_pairs(lax.axis_size(axis), odd))  4.28 us
    ppermute x1, waiting for transfers between devices, shards(): lax.ppermute(scales, 'pair', across)  2.56 us
    unnamed x16, local copies, waits for them, and re-layouts  2.3 us
  transfers between devices with their start and end apart: 19, of which 4 were waited for; matrix products, arithmetic and copies ran while one was open for 0% of the time, Pallas kernels for 23%

profile of v6, /device:TPU:1, one launch (start us, length us, event | category | flops | bytes accessed | tf_op | source)
XLA Modules:
  0.0 66.5 jit_solution(9394290078063944784)
XLA Ops:
  0.6 1.6 %copy-done = bf16[4,4,8,8,1024]{4,3,2,1,0:T(8,128)(2,1)S(1)} copy-done((bf16[4,4,8,8,1024]{4,3,2,1,0:T(8,128)(2,1)S(1)}, bf16[4,4,8,8,1024]{4,3,2,1,0:T(8,128)(2,1)}, u32[]{:S(2)}) %copy-start) | copy-done | bytes 2097176
  2.2 0.7 %copy-done.5 = s32[256,3]{0,1:T(4,128)S(1)} copy-done((s32[256,3]{0,1:T(4,128)S(1)}, s32[256,3]{0,1:T(4,128)}, u32[]{:S(2)}) %copy-start.5) | copy-done | bytes 3096
  2.9 0.9 %shard_map.95 = f32[8,256]{1,0:T(8,128)S(1)} custom-call(s32[3,256]{1,0:T(4,128)S(1)} %bitcast.3, bf16[4,4,8,8,1024]{4,3,2,1,0:T(8,128)(2,1)S(1)} %copy-done), custom_call_target="tpu_custom_call" | custom-call | flops 1650000000 | bytes 100000 | tf_op jit(solution)/shard_map/pallas_call | solution.py:46
  3.9 0.1 collective-permute-start.5
  4.0 2.7 %collective-permute-start.4 = (f32[8,256]{1,0:T(8,128)S(1)}, f32[8,256]{1,0:T(8,128)S(1)}, u32[]{:S(2)}, u32[]{:S(2)}) collective-permute-start(f32[8,256]{1,0:T(8,128)S(1)} %shard_map.95), channel_id=1, source_target_pairs={{0,8},{4,12},{8,0},{12,4},{1,9},{5,13},{9,1},{13,5},{2,10},{6,14},... | collective-permute-start | bytes 24584 | tf_op jit(solution)/shard_map/ppermute | solution.py:31
  6.7 1.3 %collective-permute-start.3 = (f32[8,256]{1,0:T(8,128)S(1)}, f32[8,256]{1,0:T(8,128)S(1)}, u32[]{:S(2)}, u32[]{:S(2)}) collective-permute-start(f32[8,256]{1,0:T(8,128)S(1)} %shard_map.95), channel_id=1, source_target_pairs={{0,4},{4,8},{8,12},{12,0},{1,5},{5,9},{9,13},{13,1},{2,6},{6,10},{... | collective-permute-start | bytes 24584 | tf_op jit(solution)/shard_map/ppermute | solution.py:31
  8.0 1.3 %shard_map.96 = (f32[4,8,64,128]{3,2,1,0:T(8,128)S(1)}, f32[8,64,128]{2,1,0:T(8,128)S(1)}, f32[8,8,64,128]{3,2,1,0:T(8,128)S(1)}, f32[8,8,64,128]{3,2,1,0:T(8,12...) custom-call(f32[1,4,8,8,1024]{4,3,2,1,0:T(8,128)S(1)} %copy-done.2, ...), custom_call_target="tpu_custom_call" | custom-call | flops 1430000000 | bytes 100000 | tf_op jit(solution)/shard_map/pallas_call | solution.py:46
  9.3 1.4 %collective-permute-start = (bf16[200,8,128]{2,1,0:T(8,128)(2,1)S(1)}, bf16[200,8,128]{2,1,0:T(8,128)(2,1)S(1)}, u32[]{:S(2)}, u32[]{:S(2)}) collective-permute-start(bf16[200,8,128]{2,1,0:T(8,128)(2,1)S(1)} %get-tuple-element.46), channel_id=1, source_target_pairs={{0,1},{1,0},{2,3},{3,2},{4,5},{5,4},{6,7},{7,6},{8,9},{9,8},{10,11... | collective-permute-start | bytes 1228808 | tf_op jit(solution)/shard_map/ppermute | solution.py:26
  10.6 0.7 %collective-permute-start.1 = (bf16[200,8,128]{2,1,0:T(8,128)(2,1)S(1)}, bf16[200,8,128]{2,1,0:T(8,128)(2,1)S(1)}, u32[]{:S(2)}, u32[]{:S(2)}) collective-permute-start(bf16[200,8,128]{2,1,0:T(8,128)(2,1)S(1)} %get-tuple-element.47), channel_id=1, source_target_pairs={{0,0},{1,2},{2,1},{3,3},{4,4},{5,6},{6,5},{7,7},{8,8},{9,10},{10,9... | collective-permute-start | bytes 1228808 | tf_op jit(solution)/shard_map/ppermute | solution.py:26
  11.3 2.2 %collective-permute-start.2 = (bf16[33,64,128]{2,1,0:T(8,128)(2,1)S(1)}, bf16[33,64,128]{2,1,0:T(8,128)(2,1)S(1)}, u32[]{:S(2)}, u32[]{:S(2)}) collective-permute-start(bf16[33,64,128]{2,1,0:T(8,128)(2,1)S(1)} %get-tuple-element.48), channel_id=1, source_target_pairs={{0,0},{4,8},{8,4},{12,12},{1,1},{5,9},{9,5},{13,13},{2,2},{6,10},{... | collective-permute-start | bytes 1622024 | tf_op jit(solution)/shard_map/ppermute | solution.py:26
  13.6 0.0 collective-permute-done.4
  13.6 2.7 %shard_map.97 = (f32[8,8,64,128]{3,2,1,0:T(8,128)S(1)}, f32[8,8,64,128]{3,2,1,0:T(8,128)S(1)}, f32[8,256]{1,0:T(8,128)S(1)}) custom-call(f32[8,8,64,128]{3,2,1,0:T(8,128)S(1)} %get-tuple-element.49.early.columns, f32[8,8,64,128]{3,2,1,0:T(8,128)S(1)} %get-tuple-element.50.late.columns, f32[8,256]{1,0:T(8,128)S(1)} %add_add_fusion.1.sample), custom_call_target="tpu_custom_call" | custom-call | flops 2969999872 | bytes 100000 | tf_op jit(solution)/shard_map/pallas_call | solution.py:46
  16.3 2.2 %collective-permute-start.8 = (f32[8,256]{1,0:T(8,128)S(1)}, f32[8,256]{1,0:T(8,128)S(1)}, u32[]{:S(2)}, u32[]{:S(2)}) collective-permute-start(f32[8,256]{1,0:T(8,128)S(1)} %get-tuple-element.52), channel_id=1, source_target_pairs={{0,3},{1,0},{2,1},{3,2},{4,7},{5,4},{6,5},{7,6},{8,11},{9,8},{10,9... | collective-permute-start | bytes 24584 | tf_op jit(solution)/shard_map/ppermute | solution.py:31
  18.6 3.1 %collective-permute-start.7 = (f32[8,256]{1,0:T(8,128)S(1)}, f32[8,256]{1,0:T(8,128)S(1)}, u32[]{:S(2)}, u32[]{:S(2)}) collective-permute-start(f32[8,256]{1,0:T(8,128)S(1)} %get-tuple-element.52), channel_id=1, source_target_pairs={{0,2},{1,3},{2,0},{3,1},{4,6},{5,7},{6,4},{7,5},{8,10},{9,11},{10,... | collective-permute-start | bytes 24584 | tf_op jit(solution)/shard_map/ppermute | solution.py:31
  21.7 3.3 %collective-permute-start.6 = (f32[8,256]{1,0:T(8,128)S(1)}, f32[8,256]{1,0:T(8,128)S(1)}, u32[]{:S(2)}, u32[]{:S(2)}) collective-permute-start(f32[8,256]{1,0:T(8,128)S(1)} %get-tuple-element.52), channel_id=1, source_target_pairs={{0,1},{1,2},{2,3},{3,0},{4,5},{5,6},{6,7},{7,4},{8,9},{9,10},{10,1... | collective-permute-start | bytes 24584 | tf_op jit(solution)/shard_map/ppermute | solution.py:31
  24.9 0.8 %shard_map.98.own_dz = f32[4,8,64,128]{3,2,1,0:T(8,128)S(1)} custom-call(f32[4,8,64,128]{3,2,1,0:T(8,128)S(1)} %get-tuple-element.55.cols), custom_call_target="tpu_custom_call" | custom-call | flops 880000000 | bytes 100000 | tf_op jit(solution)/shard_map/pallas_call | solution.py:46
  25.8 0.0 copy-start.6
  25.8 0.0 copy-start.7
  25.8 0.0 collective-permute-done.7
  25.8 0.1 collective-permute-done.6
  26.0 0.0 collective-permute-done.z_even.z0.refs_0_
  26.0 0.0 collective-permute-done.1.z_odd.z1.refs_1_
  26.0 0.1 shard_map.101
  26.1 1.0 %collective-permute-start.9 = (bf16[41,64,128]{2,1,0:T(8,128)(2,1)S(1)}, bf16[41,64,128]{2,1,0:T(8,128)(2,1)S(1)}, u32[]{:S(2)}, u32[]{:S(2)}) collective-permute-start(bf16[41,64,128]{2,1,0:T(8,128)(2,1)S(1)} %get-tuple-element.63), channel_id=1, source_target_pairs={{0,4},{4,0},{8,12},{12,8},{1,5},{5,1},{9,13},{13,9},{2,6},{6,2},{1... | collective-permute-start | bytes 2015240 | tf_op jit(solution)/shard_map/ppermute | solution.py:26
  27.8 4.0 %collective-permute-start.10 = (bf16[8,64,128]{2,1,0:T(8,128)(2,1)S(1)}, bf16[8,64,128]{2,1,0:T(8,128)(2,1)S(1)}, u32[]{:S(2)}, u32[]{:S(2)}) collective-permute-start(bf16[8,64,128]{2,1,0:T(8,128)(2,1)S(1)} %get-tuple-element.64), channel_id=1, source_target_pairs={{0,0},{4,8},{8,4},{12,12},{1,1},{5,9},{9,5},{13,13},{2,2},{6,10},{... | collective-permute-start | bytes 393224 | tf_op jit(solution)/shard_map/ppermute | solution.py:26
  31.8 1.3 %collective-permute-start.14 = (bf16[16,64,128]{2,1,0:T(8,128)(2,1)S(1)}, bf16[16,64,128]{2,1,0:T(8,128)(2,1)S(1)}, u32[]{:S(2)}, u32[]{:S(2)}) collective-permute-start(bf16[16,64,128]{2,1,0:T(8,128)(2,1)S(1)} %get-tuple-element.71), channel_id=1, source_target_pairs={{0,16},{16,0},{1,17},{17,1},{2,18},{18,2},{3,19},{19,3},{4,20},{20... | collective-permute-start | bytes 786440 | tf_op jit(solution)/shard_map/ppermute | solution.py:375
  33.0 0.8 %shard_map.100.face_dz = f32[2,4,8,3,8,128]{5,4,3,2,1,0:T(8,128)S(1)} custom-call(bf16[200,8,128]{2,1,0:T(8,128)(2,1)S(1)} %collective-permute-done.z_even.z0.refs_0_, bf16[200,8,128]{2,1,0:T(8,128)(2,1)S(1)} %collective-permute-done.1.z_odd.z1.refs_1_), custom_call_target="tpu_custom_call" | custom-call | flops 660000000 | bytes 100000 | tf_op jit(solution)/shard_map/pallas_call | solution.py:46
  33.9 0.0 copy-start.4
  33.9 1.5 %shard_map.99.inject = f32[4,2048,128]{2,1,0:T(8,128)S(1)} custom-call(s32[1]{0:T(128)S(6)} %copy.10.counts, s32[3,256]{1,0:T(4,128)S(1)} %bitcast.4, f32[4,256]{1,0:T(4,128)S(1)} %bitcast.5, f32[8,256]{1,0:T(8,128)S(1)} %add_add_fusion.samples), custom_call_target="tpu_custom_call" | custom-call | flops 1760000000 | bytes 100000 | tf_op jit(solution)/shard_map/pallas_call | solution.py:46
  35.4 0.0 collective-permute-done.10.c1
  35.4 4.2 %shard_map.102 = (f32[4,8,64,128]{3,2,1,0:T(8,128)S(1)}, f32[4,8,64,128]{3,2,1,0:T(8,128)S(1)}, f32[16,128,128]{2,1,0:T(8,128)S(1)}, bf16[112,8,128]{2,1,0:T(8,1...) custom-call(f32[3,1024]{1,0:T(4,128)S(1)} %copy-done.4, ...), custom_call_target="tpu_custom_call" | custom-call | flops 6600000000 | bytes 100000 | tf_op jit(solution)/shard_map/pallas_call | solution.py:46
  39.7 1.0 %collective-permute-start.11 = (bf16[112,8,128]{2,1,0:T(8,128)(2,1)S(1)}, bf16[112,8,128]{2,1,0:T(8,128)(2,1)S(1)}, u32[]{:S(2)}, u32[]{:S(2)}) collective-permute-start(bf16[112,8,128]{2,1,0:T(8,128)(2,1)S(1)} %get-tuple-element.66), channel_id=1, source_target_pairs={{0,1},{1,0},{2,3},{3,2},{4,5},{5,4},{6,7},{7,6},{8,9},{9,8},{10,11... | collective-permute-start | bytes 688136 | tf_op jit(solution)/shard_map/ppermute | solution.py:26
  40.7 0.7 collective-permute-start.12
  41.4 3.2 %collective-permute-start.13 = (bf16[14,64,128]{2,1,0:T(8,128)(2,1)S(1)}, bf16[14,64,128]{2,1,0:T(8,128)(2,1)S(1)}, u32[]{:S(2)}, u32[]{:S(2)}) collective-permute-start(bf16[14,64,128]{2,1,0:T(8,128)(2,1)S(1)} %get-tuple-element.68), channel_id=1, source_target_pairs={{0,0},{4,8},{8,4},{12,12},{1,1},{5,9},{9,5},{13,13},{2,2},{6,10},{... | collective-permute-start | bytes 688136 | tf_op jit(solution)/shard_map/ppermute | solution.py:26
  44.6 0.8 %shard_map.104.own_dz = f32[4,8,64,128]{3,2,1,0:T(8,128)S(1)} custom-call(f32[4,8,64,128]{3,2,1,0:T(8,128)S(1)} %get-tuple-element.65.late.cols), custom_call_target="tpu_custom_call" | custom-call | flops 880000000 | bytes 100000 | tf_op jit(solution)/shard_map/pallas_call | solution.py:46
  45.4 1.0 %shard_map.103.total = f32[4,8,64,128]{3,2,1,0:T(8,128)S(1)} custom-call(f32[4,8,64,128]{3,2,1,0:T(8,128)S(1)} %get-tuple-element.69.early, f32[4,8,64,128]{3,2,1,0:T(8,128)S(1)} %get-tuple-element.65.late.cols, f32[8,8,64,128]{3,2,1,0:T(8,128)S(1)} %get-tuple-element.49.early.columns, f32[8,8,64,128]{3,2,1,0:T(8,128)S(1)} %get-tuple-element.70.slopes, ...), custom_call_target="tpu_custom_call" | custom-call | flops 2529999872 | bytes 100000 | tf_op jit(solution)/shard_map/pallas_call | solution.py:46
  46.4 2.3 %collective-permute-done.13.refs_7_ = bf16[14,64,128]{2,1,0:T(8,128)(2,1)S(1)} collective-permute-done((bf16[14,64,128]{2,1,0:T(8,128)(2,1)S(1)}, bf16[14,64,128]{2,1,0:T(8,128)(2,1)S(1)}, u32[]{:S(2)}, u32[]{:S(2)}) %collective-permute-start.13) | collective-permute-done | bytes 229408 | tf_op jit(solution)/shard_map/ppermute | solution.py:26
  48.7 0.1 shard_map.106
  48.8 0.1 collective-permute-start.15
  48.9 3.2 %collective-permute-start.16 = (bf16[6,64,128]{2,1,0:T(8,128)(2,1)S(1)}, bf16[6,64,128]{2,1,0:T(8,128)(2,1)S(1)}, u32[]{:S(2)}, u32[]{:S(2)}) collective-permute-start(bf16[6,64,128]{2,1,0:T(8,128)(2,1)S(1)} %get-tuple-element.81), channel_id=1, source_target_pairs={{0,0},{4,8},{8,4},{12,12},{1,1},{5,9},{9,5},{13,13},{2,2},{6,10},{... | collective-permute-start | bytes 294920 | tf_op jit(solution)/shard_map/ppermute | solution.py:26
  52.1 0.8 %shard_map.105.face_dz = f32[2,4,8,3,8,128]{5,4,3,2,1,0:T(8,128)S(1)} custom-call(bf16[112,8,128]{2,1,0:T(8,128)(2,1)S(1)} %collective-permute-done.11.z_even.refs_5_, bf16[112,8,128]{2,1,0:T(8,128)(2,1)S(1)} %collective-permute-done.12.z_odd.refs_6_), custom_call_target="tpu_custom_call" | custom-call | flops 660000000 | bytes 100000 | tf_op jit(solution)/shard_map/pallas_call | solution.py:46
  52.9 1.9 %collective-permute-done.16.refs_9_ = bf16[6,64,128]{2,1,0:T(8,128)(2,1)S(1)} collective-permute-done((bf16[6,64,128]{2,1,0:T(8,128)(2,1)S(1)}, bf16[6,64,128]{2,1,0:T(8,128)(2,1)S(1)}, u32[]{:S(2)}, u32[]{:S(2)}) %collective-permute-start.16) | collective-permute-done | bytes 98336 | tf_op jit(solution)/shard_map/ppermute | solution.py:26
  54.8 5.4 %shard_map.107 = (f32[4,8,64,128]{3,2,1,0:T(8,128)S(1)}, f32[4,8,64,128]{3,2,1,0:T(8,128)S(1)}, s16[4,4,16,512]{3,2,1,0:T(8,128)(2,1)S(1)}, f32[4,512]{1,0:T(4,128)S(1)}) custom-call(f32[3,1024]{1,0:T(4,128)S(1)} %copy-done.4, f32[4,2048,128]{2,1,0:T(8,128)S(1)} %shard_map.99.inject, f32[4,8,64,128]{3,2,1,0:T(8,128)S(1)} %get-tuple-element.65.late.cols, ...), custom_call_target="tpu_custom_call" | custom-call | flops 9900000256 | bytes 100000 | tf_op jit(solution)/shard_map/pallas_call | solution.py:46
  60.2 1.3 %collective-permute-start.17 = (s16[4,4,16,512]{3,2,1,0:T(8,128)(2,1)S(1)}, s16[4,4,16,512]{3,2,1,0:T(8,128)(2,1)S(1)}, u32[]{:S(2)}, u32[]{:S(2)}) collective-permute-start(s16[4,4,16,512]{3,2,1,0:T(8,128)(2,1)S(1)} %get-tuple-element.85), channel_id=1, source_target_pairs={{0,16},{16,0},{1,17},{17,1},{2,18},{18,2},{3,19},{19,3},{4,20},{20... | collective-permute-start | bytes 786440 | tf_op jit(solution)/shard_map/ppermute | solution.py:796
  61.5 0.3 collective-permute-start.18
  61.8 1.3 %shard_map.108 = (f32[1,4,8,8,1024]{4,3,2,1,0:T(8,128)}, f32[4,8,8,512]{3,2,1,0:T(8,128)S(1)}) custom-call(f32[4,8,64,128]{3,2,1,0:T(8,128)S(1)} %get-tuple-element.82.last, f32[4,8,64,128]{3,2,1,0:T(8,128)S(1)} %get-tuple-element.83.sums), custom_call_target="tpu_custom_call" | custom-call | flops 1100000000 | bytes 100000 | tf_op jit(solution)/shard_map/pallas_call | solution.py:46
  63.0 2.6 %collective-permute-done.18.scales = f32[4,512]{1,0:T(4,128)S(1)} collective-permute-done((f32[4,512]{1,0:T(4,128)S(1)}, f32[4,512]{1,0:T(4,128)S(1)}, u32[]{:S(2)}, u32[]{:S(2)}) %collective-permute-start.18) | collective-permute-done | bytes 8224 | tf_op jit(solution)/shard_map/ppermute | solution.py:796
  65.6 0.9 %shard_map.109 = f32[4,8,8,512]{3,2,1,0:T(8,128)} custom-call(f32[4,8,8,512]{3,2,1,0:T(8,128)S(1)} %get-tuple-element.84.mine, s16[4,4,16,512]{3,2,1,0:T(8,128)(2,1)S(1)} %collective-permute-done.17.other, f32[4,512]{1,0:T(4,128)S(1)} %collective-permute-done.18.scales), custom_call_target="tpu_custom_call" | custom-call | flops 880000000 | bytes 100000 | tf_op jit(solution)/shard_map/pallas_call | solution.py:46
  (23 shorter events, 0.1 us)
Async XLA Ops:
  0.6 1.6 %copy-start = (bf16[4,4,8,8,1024]{4,3,2,1,0:T(8,128)(2,1)S(1)}, bf16[4,4,8,8,1024]{4,3,2,1,0:T(8,128)(2,1)}, u32[]{:S(2)}) copy-start(bf16[4,4,8,8,1024]{4,3,2,1,0:T(8,128)(2,1)} %forward.3) | copy-start | bytes 6291460
  2.2 0.7 %copy-start.5 = (s32[256,3]{0,1:T(4,128)S(1)}, s32[256,3]{0,1:T(4,128)}, u32[]{:S(2)}) copy-start(s32[256,3]{0,1:T(4,128)} %param.13) | copy-start | bytes 9220
  2.9 5.1 %copy-start.1 = (bf16[4,4,8,8,1024]{4,3,2,1,0:T(8,128)(2,1)S(1)}, bf16[4,4,8,8,1024]{4,3,2,1,0:T(8,128)(2,1)}, u32[]{:S(2)}) copy-start(bf16[4,4,8,8,1024]{4,3,2,1,0:T(8,128)(2,1)} %forward.3) | copy-start | bytes 6291460
  2.9 5.1 %copy-start.2 = (f32[1,4,8,8,1024]{4,3,2,1,0:T(8,128)S(1)}, f32[1,4,8,8,1024]{4,3,2,1,0:T(8,128)}, u32[]{:S(2)}) copy-start(f32[1,4,8,8,1024]{4,3,2,1,0:T(8,128)} %state) | copy-start | bytes 3145732
  2.9 5.1 %copy-start.3 = (f32[8,8,1024]{2,1,0:T(8,128)S(1)}, f32[8,8,1024]{2,1,0:T(8,128)}, u32[]{:S(2)}) copy-start(f32[8,8,1024]{2,1,0:T(8,128)} %speed.1) | copy-start | bytes 786436
  3.9 7.5 %collective-permute-start.5 = (f32[8,256]{1,0:T(8,128)S(1)}, f32[8,256]{1,0:T(8,128)S(1)}, u32[]{:S(2)}, u32[]{:S(2)}) collective-permute-start(f32[8,256]{1,0:T(8,128)S(1)} %shard_map.95), channel_id=1, source_target_pairs={{0,12},{4,0},{8,4},{12,8},{1,13},{5,1},{9,5},{13,9},{2,14},{6,2},{... | collective-permute-start | bytes 24584 | tf_op jit(solution)/shard_map/ppermute | solution.py:31
  4.0 9.6 %collective-permute-start.4 = (f32[8,256]{1,0:T(8,128)S(1)}, f32[8,256]{1,0:T(8,128)S(1)}, u32[]{:S(2)}, u32[]{:S(2)}) collective-permute-start(f32[8,256]{1,0:T(8,128)S(1)} %shard_map.95), channel_id=1, source_target_pairs={{0,8},{4,12},{8,0},{12,4},{1,9},{5,13},{9,1},{13,5},{2,10},{6,14},... | collective-permute-start | bytes 24584 | tf_op jit(solution)/shard_map/ppermute | solution.py:31
  6.7 6.9 %collective-permute-start.3 = (f32[8,256]{1,0:T(8,128)S(1)}, f32[8,256]{1,0:T(8,128)S(1)}, u32[]{:S(2)}, u32[]{:S(2)}) collective-permute-start(f32[8,256]{1,0:T(8,128)S(1)} %shard_map.95), channel_id=1, source_target_pairs={{0,4},{4,8},{8,12},{12,0},{1,5},{5,9},{9,13},{13,1},{2,6},{6,10},{... | collective-permute-start | bytes 24584 | tf_op jit(solution)/shard_map/ppermute | solution.py:31
  9.3 16.7 %collective-permute-start = (bf16[200,8,128]{2,1,0:T(8,128)(2,1)S(1)}, bf16[200,8,128]{2,1,0:T(8,128)(2,1)S(1)}, u32[]{:S(2)}, u32[]{:S(2)}) collective-permute-start(bf16[200,8,128]{2,1,0:T(8,128)(2,1)S(1)} %get-tuple-element.46), channel_id=1, source_target_pairs={{0,1},{1,0},{2,3},{3,2},{4,5},{5,4},{6,7},{7,6},{8,9},{9,8},{10,11... | collective-permute-start | bytes 1228808 | tf_op jit(solution)/shard_map/ppermute | solution.py:26
  10.6 15.3 %collective-permute-start.1 = (bf16[200,8,128]{2,1,0:T(8,128)(2,1)S(1)}, bf16[200,8,128]{2,1,0:T(8,128)(2,1)S(1)}, u32[]{:S(2)}, u32[]{:S(2)}) collective-permute-start(bf16[200,8,128]{2,1,0:T(8,128)(2,1)S(1)} %get-tuple-element.47), channel_id=1, source_target_pairs={{0,0},{1,2},{2,1},{3,3},{4,4},{5,6},{6,5},{7,7},{8,8},{9,10},{10,9... | collective-permute-start | bytes 1228808 | tf_op jit(solution)/shard_map/ppermute | solution.py:26
  11.3 14.6 %collective-permute-start.2 = (bf16[33,64,128]{2,1,0:T(8,128)(2,1)S(1)}, bf16[33,64,128]{2,1,0:T(8,128)(2,1)S(1)}, u32[]{:S(2)}, u32[]{:S(2)}) collective-permute-start(bf16[33,64,128]{2,1,0:T(8,128)(2,1)S(1)} %get-tuple-element.48), channel_id=1, source_target_pairs={{0,0},{4,8},{8,4},{12,12},{1,1},{5,9},{9,5},{13,13},{2,2},{6,10},{... | collective-permute-start | bytes 1622024 | tf_op jit(solution)/shard_map/ppermute | solution.py:26
  16.3 5.3 %collective-permute-start.8 = (f32[8,256]{1,0:T(8,128)S(1)}, f32[8,256]{1,0:T(8,128)S(1)}, u32[]{:S(2)}, u32[]{:S(2)}) collective-permute-start(f32[8,256]{1,0:T(8,128)S(1)} %get-tuple-element.52), channel_id=1, source_target_pairs={{0,3},{1,0},{2,1},{3,2},{4,7},{5,4},{6,5},{7,6},{8,11},{9,8},{10,9... | collective-permute-start | bytes 24584 | tf_op jit(solution)/shard_map/ppermute | solution.py:31
  18.6 7.2 %collective-permute-start.7 = (f32[8,256]{1,0:T(8,128)S(1)}, f32[8,256]{1,0:T(8,128)S(1)}, u32[]{:S(2)}, u32[]{:S(2)}) collective-permute-start(f32[8,256]{1,0:T(8,128)S(1)} %get-tuple-element.52), channel_id=1, source_target_pairs={{0,2},{1,3},{2,0},{3,1},{4,6},{5,7},{6,4},{7,5},{8,10},{9,11},{10,... | collective-permute-start | bytes 24584 | tf_op jit(solution)/shard_map/ppermute | solution.py:31
  21.7 4.3 %collective-permute-start.6 = (f32[8,256]{1,0:T(8,128)S(1)}, f32[8,256]{1,0:T(8,128)S(1)}, u32[]{:S(2)}, u32[]{:S(2)}) collective-permute-start(f32[8,256]{1,0:T(8,128)S(1)} %get-tuple-element.52), channel_id=1, source_target_pairs={{0,1},{1,2},{2,3},{3,0},{4,5},{5,6},{6,7},{7,4},{8,9},{9,10},{10,1... | collective-permute-start | bytes 24584 | tf_op jit(solution)/shard_map/ppermute | solution.py:31
  25.8 8.1 %copy-start.6 = (s32[256,3]{0,1:T(4,128)S(1)}, s32[256,3]{0,1:T(4,128)}, u32[]{:S(2)}) copy-start(s32[256,3]{0,1:T(4,128)} %param.14) | copy-start | bytes 9220
  25.8 8.1 %copy-start.7 = (f32[256,4]{0,1:T(4,128)S(1)}, f32[256,4]{0,1:T(4,128)}, u32[]{:S(2)}) copy-start(f32[256,4]{0,1:T(4,128)} %param.15) | copy-start | bytes 12292
  26.1 9.3 %collective-permute-start.9 = (bf16[41,64,128]{2,1,0:T(8,128)(2,1)S(1)}, bf16[41,64,128]{2,1,0:T(8,128)(2,1)S(1)}, u32[]{:S(2)}, u32[]{:S(2)}) collective-permute-start(bf16[41,64,128]{2,1,0:T(8,128)(2,1)S(1)} %get-tuple-element.63), channel_id=1, source_target_pairs={{0,4},{4,0},{8,12},{12,8},{1,5},{5,1},{9,13},{13,9},{2,6},{6,2},{1... | collective-permute-start | bytes 2015240 | tf_op jit(solution)/shard_map/ppermute | solution.py:26
  27.8 7.6 %collective-permute-start.10 = (bf16[8,64,128]{2,1,0:T(8,128)(2,1)S(1)}, bf16[8,64,128]{2,1,0:T(8,128)(2,1)S(1)}, u32[]{:S(2)}, u32[]{:S(2)}) collective-permute-start(bf16[8,64,128]{2,1,0:T(8,128)(2,1)S(1)} %get-tuple-element.64), channel_id=1, source_target_pairs={{0,0},{4,8},{8,4},{12,12},{1,1},{5,9},{9,5},{13,13},{2,2},{6,10},{... | collective-permute-start | bytes 393224 | tf_op jit(solution)/shard_map/ppermute | solution.py:26
  31.8 13.6 %collective-permute-start.14 = (bf16[16,64,128]{2,1,0:T(8,128)(2,1)S(1)}, bf16[16,64,128]{2,1,0:T(8,128)(2,1)S(1)}, u32[]{:S(2)}, u32[]{:S(2)}) collective-permute-start(bf16[16,64,128]{2,1,0:T(8,128)(2,1)S(1)} %get-tuple-element.71), channel_id=1, source_target_pairs={{0,16},{16,0},{1,17},{17,1},{2,18},{18,2},{3,19},{19,3},{4,20},{20... | collective-permute-start | bytes 786440 | tf_op jit(solution)/shard_map/ppermute | solution.py:375
  33.9 1.6 %copy-start.4 = (f32[3,1024]{1,0:T(4,128)S(1)}, f32[3,1024]{1,0:T(4,128)}, u32[]{:S(2)}) copy-start(f32[3,1024]{1,0:T(4,128)} %wind.3) | copy-start | bytes 36868
  39.7 6.7 %collective-permute-start.11 = (bf16[112,8,128]{2,1,0:T(8,128)(2,1)S(1)}, bf16[112,8,128]{2,1,0:T(8,128)(2,1)S(1)}, u32[]{:S(2)}, u32[]{:S(2)}) collective-permute-start(bf16[112,8,128]{2,1,0:T(8,128)(2,1)S(1)} %get-tuple-element.66), channel_id=1, source_target_pairs={{0,1},{1,0},{2,3},{3,2},{4,5},{5,4},{6,7},{7,6},{8,9},{9,8},{10,11... | collective-permute-start | bytes 688136 | tf_op jit(solution)/shard_map/ppermute | solution.py:26
  40.7 5.7 %collective-permute-start.12 = (bf16[112,8,128]{2,1,0:T(8,128)(2,1)S(1)}, bf16[112,8,128]{2,1,0:T(8,128)(2,1)S(1)}, u32[]{:S(2)}, u32[]{:S(2)}) collective-permute-start(bf16[112,8,128]{2,1,0:T(8,128)(2,1)S(1)} %get-tuple-element.67), channel_id=1, source_target_pairs={{0,0},{1,2},{2,1},{3,3},{4,4},{5,6},{6,5},{7,7},{8,8},{9,10},{10,9... | collective-permute-start | bytes 688136 | tf_op jit(solution)/shard_map/ppermute | solution.py:26
  41.4 7.3 %collective-permute-start.13 = (bf16[14,64,128]{2,1,0:T(8,128)(2,1)S(1)}, bf16[14,64,128]{2,1,0:T(8,128)(2,1)S(1)}, u32[]{:S(2)}, u32[]{:S(2)}) collective-permute-start(bf16[14,64,128]{2,1,0:T(8,128)(2,1)S(1)} %get-tuple-element.68), channel_id=1, source_target_pairs={{0,0},{4,8},{8,4},{12,12},{1,1},{5,9},{9,5},{13,13},{2,2},{6,10},{... | collective-permute-start | bytes 688136 | tf_op jit(solution)/shard_map/ppermute | solution.py:26
  48.8 6.0 %collective-permute-start.15 = (bf16[20,64,128]{2,1,0:T(8,128)(2,1)S(1)}, bf16[20,64,128]{2,1,0:T(8,128)(2,1)S(1)}, u32[]{:S(2)}, u32[]{:S(2)}) collective-permute-start(bf16[20,64,128]{2,1,0:T(8,128)(2,1)S(1)} %get-tuple-element.80), channel_id=1, source_target_pairs={{0,4},{4,0},{8,12},{12,8},{1,5},{5,1},{9,13},{13,9},{2,6},{6,2},{1... | collective-permute-start | bytes 983048 | tf_op jit(solution)/shard_map/ppermute | solution.py:26
  48.9 5.9 %collective-permute-start.16 = (bf16[6,64,128]{2,1,0:T(8,128)(2,1)S(1)}, bf16[6,64,128]{2,1,0:T(8,128)(2,1)S(1)}, u32[]{:S(2)}, u32[]{:S(2)}) collective-permute-start(bf16[6,64,128]{2,1,0:T(8,128)(2,1)S(1)} %get-tuple-element.81), channel_id=1, source_target_pairs={{0,0},{4,8},{8,4},{12,12},{1,1},{5,9},{9,5},{13,13},{2,2},{6,10},{... | collective-permute-start | bytes 294920 | tf_op jit(solution)/shard_map/ppermute | solution.py:26
  60.2 5.4 %collective-permute-start.17 = (s16[4,4,16,512]{3,2,1,0:T(8,128)(2,1)S(1)}, s16[4,4,16,512]{3,2,1,0:T(8,128)(2,1)S(1)}, u32[]{:S(2)}, u32[]{:S(2)}) collective-permute-start(s16[4,4,16,512]{3,2,1,0:T(8,128)(2,1)S(1)} %get-tuple-element.85), channel_id=1, source_target_pairs={{0,16},{16,0},{1,17},{17,1},{2,18},{18,2},{3,19},{19,3},{4,20},{20... | collective-permute-start | bytes 786440 | tf_op jit(solution)/shard_map/ppermute | solution.py:796
  61.5 4.1 %collective-permute-start.18 = (f32[4,512]{1,0:T(4,128)S(1)}, f32[4,512]{1,0:T(4,128)S(1)}, u32[]{:S(2)}, u32[]{:S(2)}) collective-permute-start(f32[4,512]{1,0:T(4,128)S(1)} %get-tuple-element.86), channel_id=1, source_target_pairs={{0,16},{16,0},{1,17},{17,1},{2,18},{18,2},{3,19},{19,3},{4,20},{20... | collective-permute-start | bytes 24584 | tf_op jit(solution)/shard_map/ppermute | solution.py:796

commit v7 on v6

--- a/solution.py
+++ b/solution.py
@@ -372,7 +372,6 @@
         if first:
             outs.append(struct((8 * PER_ROUND,) + block, BF))
         even, odd, *rim = call(corner_kernel, outs, micros=0.3, limit=8)(*z, faces)
-        rim = [lax.ppermute(r, "pair", [(0, 1), (1, 0)]) for r in rim]
         return [swapped(even, "gx", 0), swapped(odd, "gx", 1), *rim]
 
     whole = pl.BlockSpec(memory_space=VMEM)
@@ -685,6 +684,9 @@
     early, late, speed_ext = first[:3]
     z_second, x_second = first_hop(first[3:])
 
+    late_dz = own_slopes(late)
+    rim_z, late_dz = lax.optimization_barrier((rim_z, late_dz))
+    rim_z = lax.ppermute(rim_z, "pair", [(0, 1), (1, 0)])
     rim = (*z_first, rim_z, hop, x_first)
 
     def early_kernel(early, late, columns, slopes, z0, z1, zp, c0, x1, total, rim_y, rim_x):
@@ -706,10 +708,7 @@
     total = call(early_kernel, struct((4,) + tile, F32), scratch=rim_scratch, micros=2.3, limit=16)(
         early, late, forward_early, slopes_early, *rim
     )
-    late_dz = own_slopes(late)
-    z_second, x_second, total, late_dz = lax.optimization_barrier(
-        (z_second, x_second, total, late_dz)
-    )
+    z_second, x_second, late_dz = lax.optimization_barrier((z_second, x_second, late_dz))
     again, again_odd = second_hop(4, z_second, first[5], False)
 
     half = depth // 2

time: 67.2 us -> 67.2 us (level)
    ppermute x10, waiting for transfers between devices: 4.28 us -> 3.57 us  [swapped(): return lax.ppermute(x, axis, swap_pairs(lax.axis_size(axis), odd))]
  transfers between devices with their start and end apart: 19 -> 19, of which waited for: 4 -> 5; matrix products, arithmetic and copies ran while one was open for 0% -> 0% of each run, Pallas kernels for 23% -> 17%
where the time goes in v7:
time: 67.2 us; the launch traced here: 66.6 us
  starting transfers between devices  33.4 us (50%)
  Pallas kernels  22.6 us (34%)
  waiting for transfers between devices  6.68 us (10%)
  local copies, waits for them, and re-layouts  2.3 us (3%)
  between operations  1.56 us (2%)
    pallas_call x15, Pallas kernels, run(): pl.pallas_call(kernel, out_shape=outs, in_specs=specs or [pl.BlockSpec(me...  22.6 us
    ppermute x10, starting transfers between devices, swapped(): return lax.ppermute(x, axis, swap_pairs(lax.axis_size(axis), odd))  17.9 us
    ppermute x6, starting transfers between devices, total_of(): lax.ppermute(x, axis, [(i, (i + k) % size) for i in range(size)])  12.8 us
    ppermute x10, waiting for transfers between devices, swapped(): return lax.ppermute(x, axis, swap_pairs(lax.axis_size(axis), odd))  3.57 us
    ppermute x1, waiting for transfers between devices, shards(): lax.ppermute(scales, 'pair', across)  2.95 us
    unnamed x16, local copies, waits for them, and re-layouts  2.3 us
  transfers between devices with their start and end apart: 19, of which 5 were waited for; matrix products, arithmetic and copies ran while one was open for 0% of the time, Pallas kernels for 17%

profile of v7, /device:TPU:1, one launch (start us, length us, event | category | flops | bytes accessed | tf_op | source)
XLA Modules:
  0.0 66.6 jit_solution(10123281786239699389)
XLA Ops:
  0.6 1.6 %copy-done = bf16[4,4,8,8,1024]{4,3,2,1,0:T(8,128)(2,1)S(1)} copy-done((bf16[4,4,8,8,1024]{4,3,2,1,0:T(8,128)(2,1)S(1)}, bf16[4,4,8,8,1024]{4,3,2,1,0:T(8,128)(2,1)}, u32[]{:S(2)}) %copy-start) | copy-done | bytes 2097176
  2.2 0.7 %copy-done.5 = s32[256,3]{0,1:T(4,128)S(1)} copy-done((s32[256,3]{0,1:T(4,128)S(1)}, s32[256,3]{0,1:T(4,128)}, u32[]{:S(2)}) %copy-start.5) | copy-done | bytes 3096
  2.9 0.9 %shard_map.95 = f32[8,256]{1,0:T(8,128)S(1)} custom-call(s32[3,256]{1,0:T(4,128)S(1)} %bitcast.3, bf16[4,4,8,8,1024]{4,3,2,1,0:T(8,128)(2,1)S(1)} %copy-done), custom_call_target="tpu_custom_call" | custom-call | flops 1650000000 | bytes 100000 | tf_op jit(solution)/shard_map/pallas_call | solution.py:46
  3.9 0.1 collective-permute-start.5
  4.0 2.7 %collective-permute-start.4 = (f32[8,256]{1,0:T(8,128)S(1)}, f32[8,256]{1,0:T(8,128)S(1)}, u32[]{:S(2)}, u32[]{:S(2)}) collective-permute-start(f32[8,256]{1,0:T(8,128)S(1)} %shard_map.95), channel_id=1, source_target_pairs={{0,8},{4,12},{8,0},{12,4},{1,9},{5,13},{9,1},{13,5},{2,10},{6,14},... | collective-permute-start | bytes 24584 | tf_op jit(solution)/shard_map/ppermute | solution.py:31
  6.7 1.3 %collective-permute-start.3 = (f32[8,256]{1,0:T(8,128)S(1)}, f32[8,256]{1,0:T(8,128)S(1)}, u32[]{:S(2)}, u32[]{:S(2)}) collective-permute-start(f32[8,256]{1,0:T(8,128)S(1)} %shard_map.95), channel_id=1, source_target_pairs={{0,4},{4,8},{8,12},{12,0},{1,5},{5,9},{9,13},{13,1},{2,6},{6,10},{... | collective-permute-start | bytes 24584 | tf_op jit(solution)/shard_map/ppermute | solution.py:31
  8.0 1.3 %shard_map.96 = (f32[4,8,64,128]{3,2,1,0:T(8,128)S(1)}, f32[8,64,128]{2,1,0:T(8,128)S(1)}, f32[8,8,64,128]{3,2,1,0:T(8,128)S(1)}, f32[8,8,64,128]{3,2,1,0:T(8,12...) custom-call(f32[1,4,8,8,1024]{4,3,2,1,0:T(8,128)S(1)} %copy-done.2, ...), custom_call_target="tpu_custom_call" | custom-call | flops 1430000000 | bytes 100000 | tf_op jit(solution)/shard_map/pallas_call | solution.py:46
  9.3 1.4 %collective-permute-start = (bf16[200,8,128]{2,1,0:T(8,128)(2,1)S(1)}, bf16[200,8,128]{2,1,0:T(8,128)(2,1)S(1)}, u32[]{:S(2)}, u32[]{:S(2)}) collective-permute-start(bf16[200,8,128]{2,1,0:T(8,128)(2,1)S(1)} %get-tuple-element.47), channel_id=1, source_target_pairs={{0,1},{1,0},{2,3},{3,2},{4,5},{5,4},{6,7},{7,6},{8,9},{9,8},{10,11... | collective-permute-start | bytes 1228808 | tf_op jit(solution)/shard_map/ppermute | solution.py:26
  10.6 0.7 %collective-permute-start.1 = (bf16[200,8,128]{2,1,0:T(8,128)(2,1)S(1)}, bf16[200,8,128]{2,1,0:T(8,128)(2,1)S(1)}, u32[]{:S(2)}, u32[]{:S(2)}) collective-permute-start(bf16[200,8,128]{2,1,0:T(8,128)(2,1)S(1)} %get-tuple-element.48), channel_id=1, source_target_pairs={{0,0},{1,2},{2,1},{3,3},{4,4},{5,6},{6,5},{7,7},{8,8},{9,10},{10,9... | collective-permute-start | bytes 1228808 | tf_op jit(solution)/shard_map/ppermute | solution.py:26
  11.3 2.2 %collective-permute-start.2 = (bf16[33,64,128]{2,1,0:T(8,128)(2,1)S(1)}, bf16[33,64,128]{2,1,0:T(8,128)(2,1)S(1)}, u32[]{:S(2)}, u32[]{:S(2)}) collective-permute-start(bf16[33,64,128]{2,1,0:T(8,128)(2,1)S(1)} %get-tuple-element.49), channel_id=1, source_target_pairs={{0,0},{4,8},{8,4},{12,12},{1,1},{5,9},{9,5},{13,13},{2,2},{6,10},{... | collective-permute-start | bytes 1622024 | tf_op jit(solution)/shard_map/ppermute | solution.py:26
  13.6 0.0 collective-permute-done.4
  13.6 0.0 collective-permute-done.3
  13.6 2.7 %shard_map.97 = (f32[8,8,64,128]{3,2,1,0:T(8,128)S(1)}, f32[8,8,64,128]{3,2,1,0:T(8,128)S(1)}, f32[8,256]{1,0:T(8,128)S(1)}) custom-call(f32[8,8,64,128]{3,2,1,0:T(8,128)S(1)} %get-tuple-element.50.early.columns, f32[8,8,64,128]{3,2,1,0:T(8,128)S(1)} %get-tuple-element.51.late.columns, f32[8,256]{1,0:T(8,128)S(1)} %add_add_fusion.1.sample), custom_call_target="tpu_custom_call" | custom-call | flops 2969999872 | bytes 100000 | tf_op jit(solution)/shard_map/pallas_call | solution.py:46
  16.3 2.2 %collective-permute-start.8 = (f32[8,256]{1,0:T(8,128)S(1)}, f32[8,256]{1,0:T(8,128)S(1)}, u32[]{:S(2)}, u32[]{:S(2)}) collective-permute-start(f32[8,256]{1,0:T(8,128)S(1)} %get-tuple-element.53), channel_id=1, source_target_pairs={{0,3},{1,0},{2,1},{3,2},{4,7},{5,4},{6,5},{7,6},{8,11},{9,8},{10,9... | collective-permute-start | bytes 24584 | tf_op jit(solution)/shard_map/ppermute | solution.py:31
  18.6 3.1 %collective-permute-start.7 = (f32[8,256]{1,0:T(8,128)S(1)}, f32[8,256]{1,0:T(8,128)S(1)}, u32[]{:S(2)}, u32[]{:S(2)}) collective-permute-start(f32[8,256]{1,0:T(8,128)S(1)} %get-tuple-element.53), channel_id=1, source_target_pairs={{0,2},{1,3},{2,0},{3,1},{4,6},{5,7},{6,4},{7,5},{8,10},{9,11},{10,... | collective-permute-start | bytes 24584 | tf_op jit(solution)/shard_map/ppermute | solution.py:31
  21.7 3.3 %collective-permute-start.6 = (f32[8,256]{1,0:T(8,128)S(1)}, f32[8,256]{1,0:T(8,128)S(1)}, u32[]{:S(2)}, u32[]{:S(2)}) collective-permute-start(f32[8,256]{1,0:T(8,128)S(1)} %get-tuple-element.53), channel_id=1, source_target_pairs={{0,1},{1,2},{2,3},{3,0},{4,5},{5,6},{6,7},{7,4},{8,9},{9,10},{10,1... | collective-permute-start | bytes 24584 | tf_op jit(solution)/shard_map/ppermute | solution.py:31
  24.9 0.8 %shard_map.98.own_dz = f32[4,8,64,128]{3,2,1,0:T(8,128)S(1)} custom-call(f32[4,8,64,128]{3,2,1,0:T(8,128)S(1)} %get-tuple-element.56.cols), custom_call_target="tpu_custom_call" | custom-call | flops 880000000 | bytes 100000 | tf_op jit(solution)/shard_map/pallas_call | solution.py:46
  25.8 0.0 copy-start.6
  25.8 0.0 copy-start.7
  25.8 0.0 collective-permute-done.7
  25.8 0.1 collective-permute-done.6
  26.0 0.0 collective-permute-done.z_even.z0.refs_0_
  26.0 0.1 shard_map.101
  26.1 1.0 %collective-permute-start.9 = (bf16[41,64,128]{2,1,0:T(8,128)(2,1)S(1)}, bf16[41,64,128]{2,1,0:T(8,128)(2,1)S(1)}, u32[]{:S(2)}, u32[]{:S(2)}) collective-permute-start(bf16[41,64,128]{2,1,0:T(8,128)(2,1)S(1)} %get-tuple-element.64), channel_id=1, source_target_pairs={{0,4},{4,0},{8,12},{12,8},{1,5},{5,1},{9,13},{13,9},{2,6},{6,2},{1... | collective-permute-start | bytes 2015240 | tf_op jit(solution)/shard_map/ppermute | solution.py:26
  27.8 4.0 %collective-permute-start.10 = (bf16[8,64,128]{2,1,0:T(8,128)(2,1)S(1)}, bf16[8,64,128]{2,1,0:T(8,128)(2,1)S(1)}, u32[]{:S(2)}, u32[]{:S(2)}) collective-permute-start(bf16[8,64,128]{2,1,0:T(8,128)(2,1)S(1)} %get-tuple-element.65), channel_id=1, source_target_pairs={{0,0},{4,8},{8,4},{12,12},{1,1},{5,9},{9,5},{13,13},{2,2},{6,10},{... | collective-permute-start | bytes 393224 | tf_op jit(solution)/shard_map/ppermute | solution.py:26
  31.8 0.8 %shard_map.100.face_dz = f32[2,4,8,3,8,128]{5,4,3,2,1,0:T(8,128)S(1)} custom-call(bf16[200,8,128]{2,1,0:T(8,128)(2,1)S(1)} %collective-permute-done.z_even.z0.refs_0_, bf16[200,8,128]{2,1,0:T(8,128)(2,1)S(1)} %collective-permute-done.1.z_odd.z1.refs_1_), custom_call_target="tpu_custom_call" | custom-call | flops 660000000 | bytes 100000 | tf_op jit(solution)/shard_map/pallas_call | solution.py:46
  32.6 0.0 copy-start.4
  32.6 1.5 %shard_map.99.inject = f32[4,2048,128]{2,1,0:T(8,128)S(1)} custom-call(s32[1]{0:T(128)S(6)} %copy.10.counts, s32[3,256]{1,0:T(4,128)S(1)} %bitcast.4, f32[4,256]{1,0:T(4,128)S(1)} %bitcast.5, f32[8,256]{1,0:T(8,128)S(1)} %add_add_fusion.samples), custom_call_target="tpu_custom_call" | custom-call | flops 1760000000 | bytes 100000 | tf_op jit(solution)/shard_map/pallas_call | solution.py:46
  34.1 0.3 collective-permute-done.10.c1
  34.4 4.2 %shard_map.102 = (f32[4,8,64,128]{3,2,1,0:T(8,128)S(1)}, f32[4,8,64,128]{3,2,1,0:T(8,128)S(1)}, f32[16,128,128]{2,1,0:T(8,128)S(1)}, bf16[112,8,128]{2,1,0:T(8,1...) custom-call(f32[3,1024]{1,0:T(4,128)S(1)} %copy-done.4, ...), custom_call_target="tpu_custom_call" | custom-call | flops 6600000000 | bytes 100000 | tf_op jit(solution)/shard_map/pallas_call | solution.py:46
  38.7 1.8 %collective-permute-start.11 = (bf16[112,8,128]{2,1,0:T(8,128)(2,1)S(1)}, bf16[112,8,128]{2,1,0:T(8,128)(2,1)S(1)}, u32[]{:S(2)}, u32[]{:S(2)}) collective-permute-start(bf16[112,8,128]{2,1,0:T(8,128)(2,1)S(1)} %get-tuple-element.67), channel_id=1, source_target_pairs={{0,1},{1,0},{2,3},{3,2},{4,5},{5,4},{6,7},{7,6},{8,9},{9,8},{10,11... | collective-permute-start | bytes 688136 | tf_op jit(solution)/shard_map/ppermute | solution.py:26
  40.4 0.7 collective-permute-start.12
  41.1 3.0 %collective-permute-start.13 = (bf16[14,64,128]{2,1,0:T(8,128)(2,1)S(1)}, bf16[14,64,128]{2,1,0:T(8,128)(2,1)S(1)}, u32[]{:S(2)}, u32[]{:S(2)}) collective-permute-start(bf16[14,64,128]{2,1,0:T(8,128)(2,1)S(1)} %get-tuple-element.69), channel_id=1, source_target_pairs={{0,0},{4,8},{8,4},{12,12},{1,1},{5,9},{9,5},{13,13},{2,2},{6,10},{... | collective-permute-start | bytes 688136 | tf_op jit(solution)/shard_map/ppermute | solution.py:26
  44.1 0.8 %shard_map.103.own_dz = f32[4,8,64,128]{3,2,1,0:T(8,128)S(1)} custom-call(f32[4,8,64,128]{3,2,1,0:T(8,128)S(1)} %get-tuple-element.66.cols.late), custom_call_target="tpu_custom_call" | custom-call | flops 880000000 | bytes 100000 | tf_op jit(solution)/shard_map/pallas_call | solution.py:46
  45.0 1.3 %collective-permute-start.14 = (bf16[16,64,128]{2,1,0:T(8,128)(2,1)S(1)}, bf16[16,64,128]{2,1,0:T(8,128)(2,1)S(1)}, u32[]{:S(2)}, u32[]{:S(2)}) collective-permute-start(bf16[16,64,128]{2,1,0:T(8,128)(2,1)S(1)} %get-tuple-element.78), channel_id=1, source_target_pairs={{0,16},{16,0},{1,17},{17,1},{2,18},{18,2},{3,19},{19,3},{4,20},{20... | collective-permute-start | bytes 786440 | tf_op jit(solution)/shard_map/ppermute | solution.py:689
  46.2 2.2 %collective-permute-done.13.refs_7_ = bf16[14,64,128]{2,1,0:T(8,128)(2,1)S(1)} collective-permute-done((bf16[14,64,128]{2,1,0:T(8,128)(2,1)S(1)}, bf16[14,64,128]{2,1,0:T(8,128)(2,1)S(1)}, u32[]{:S(2)}, u32[]{:S(2)}) %collective-permute-start.13) | collective-permute-done | bytes 229408 | tf_op jit(solution)/shard_map/ppermute | solution.py:26
  48.4 0.1 shard_map.106
  48.5 0.1 collective-permute-start.15
  48.6 3.0 %collective-permute-start.16 = (bf16[6,64,128]{2,1,0:T(8,128)(2,1)S(1)}, bf16[6,64,128]{2,1,0:T(8,128)(2,1)S(1)}, u32[]{:S(2)}, u32[]{:S(2)}) collective-permute-start(bf16[6,64,128]{2,1,0:T(8,128)(2,1)S(1)} %get-tuple-element.83), channel_id=1, source_target_pairs={{0,0},{4,8},{8,4},{12,12},{1,1},{5,9},{9,5},{13,13},{2,2},{6,10},{... | collective-permute-start | bytes 294920 | tf_op jit(solution)/shard_map/ppermute | solution.py:26
  51.6 0.8 %shard_map.104.face_dz = f32[2,4,8,3,8,128]{5,4,3,2,1,0:T(8,128)S(1)} custom-call(bf16[112,8,128]{2,1,0:T(8,128)(2,1)S(1)} %collective-permute-done.11.z_even.refs_5_, bf16[112,8,128]{2,1,0:T(8,128)(2,1)S(1)} %collective-permute-done.12.z_odd.refs_6_), custom_call_target="tpu_custom_call" | custom-call | flops 660000000 | bytes 100000 | tf_op jit(solution)/shard_map/pallas_call | solution.py:46
  52.4 1.0 %shard_map.105.total = f32[4,8,64,128]{3,2,1,0:T(8,128)S(1)} custom-call(f32[4,8,64,128]{3,2,1,0:T(8,128)S(1)} %get-tuple-element.76.early, f32[4,8,64,128]{3,2,1,0:T(8,128)S(1)} %get-tuple-element.66.cols.late, f32[8,8,64,128]{3,2,1,0:T(8,128)S(1)} %get-tuple-element.50.early.columns, f32[8,8,64,128]{3,2,1,0:T(8,128)S(1)} %get-tuple-element.77.slopes, ...), custom_call_target="tpu_custom_call" | custom-call | flops 2529999872 | bytes 100000 | tf_op jit(solution)/shard_map/pallas_call | solution.py:46
  53.4 1.1 %collective-permute-done.16.refs_9_ = bf16[6,64,128]{2,1,0:T(8,128)(2,1)S(1)} collective-permute-done((bf16[6,64,128]{2,1,0:T(8,128)(2,1)S(1)}, bf16[6,64,128]{2,1,0:T(8,128)(2,1)S(1)}, u32[]{:S(2)}, u32[]{:S(2)}) %collective-permute-start.16) | collective-permute-done | bytes 98336 | tf_op jit(solution)/shard_map/ppermute | solution.py:26
  54.5 5.4 %shard_map.107 = (f32[4,8,64,128]{3,2,1,0:T(8,128)S(1)}, f32[4,8,64,128]{3,2,1,0:T(8,128)S(1)}, s16[4,4,16,512]{3,2,1,0:T(8,128)(2,1)S(1)}, f32[4,512]{1,0:T(4,128)S(1)}) custom-call(f32[3,1024]{1,0:T(4,128)S(1)} %copy-done.4, f32[4,2048,128]{2,1,0:T(8,128)S(1)} %shard_map.99.inject, f32[4,8,64,128]{3,2,1,0:T(8,128)S(1)} %get-tuple-element.66.cols.late, ...), custom_call_target="tpu_custom_call" | custom-call | flops 9900000256 | bytes 100000 | tf_op jit(solution)/shard_map/pallas_call | solution.py:46
  59.9 1.3 %collective-permute-start.17 = (s16[4,4,16,512]{3,2,1,0:T(8,128)(2,1)S(1)}, s16[4,4,16,512]{3,2,1,0:T(8,128)(2,1)S(1)}, u32[]{:S(2)}, u32[]{:S(2)}) collective-permute-start(s16[4,4,16,512]{3,2,1,0:T(8,128)(2,1)S(1)} %get-tuple-element.87), channel_id=1, source_target_pairs={{0,16},{16,0},{1,17},{17,1},{2,18},{18,2},{3,19},{19,3},{4,20},{20... | collective-permute-start | bytes 786440 | tf_op jit(solution)/shard_map/ppermute | solution.py:795
  61.2 0.3 collective-permute-start.18
  61.5 1.3 %shard_map.108 = (f32[1,4,8,8,1024]{4,3,2,1,0:T(8,128)}, f32[4,8,8,512]{3,2,1,0:T(8,128)S(1)}) custom-call(f32[4,8,64,128]{3,2,1,0:T(8,128)S(1)} %get-tuple-element.84.last, f32[4,8,64,128]{3,2,1,0:T(8,128)S(1)} %get-tuple-element.85.sums), custom_call_target="tpu_custom_call" | custom-call | flops 1100000000 | bytes 100000 | tf_op jit(solution)/shard_map/pallas_call | solution.py:46
  62.7 2.9 %collective-permute-done.18.scales = f32[4,512]{1,0:T(4,128)S(1)} collective-permute-done((f32[4,512]{1,0:T(4,128)S(1)}, f32[4,512]{1,0:T(4,128)S(1)}, u32[]{:S(2)}, u32[]{:S(2)}) %collective-permute-start.18) | collective-permute-done | bytes 8224 | tf_op jit(solution)/shard_map/ppermute | solution.py:795
  65.7 0.9 %shard_map.109 = f32[4,8,8,512]{3,2,1,0:T(8,128)} custom-call(f32[4,8,8,512]{3,2,1,0:T(8,128)S(1)} %get-tuple-element.86.mine, s16[4,4,16,512]{3,2,1,0:T(8,128)(2,1)S(1)} %collective-permute-done.17.other, f32[4,512]{1,0:T(4,128)S(1)} %collective-permute-done.18.scales), custom_call_target="tpu_custom_call" | custom-call | flops 880000000 | bytes 100000 | tf_op jit(solution)/shard_map/pallas_call | solution.py:46
  (23 shorter events, 0.1 us)
Async XLA Ops:
  0.6 1.6 %copy-start = (bf16[4,4,8,8,1024]{4,3,2,1,0:T(8,128)(2,1)S(1)}, bf16[4,4,8,8,1024]{4,3,2,1,0:T(8,128)(2,1)}, u32[]{:S(2)}) copy-start(bf16[4,4,8,8,1024]{4,3,2,1,0:T(8,128)(2,1)} %forward.3) | copy-start | bytes 6291460
  2.2 0.7 %copy-start.5 = (s32[256,3]{0,1:T(4,128)S(1)}, s32[256,3]{0,1:T(4,128)}, u32[]{:S(2)}) copy-start(s32[256,3]{0,1:T(4,128)} %param.13) | copy-start | bytes 9220
  2.9 5.1 %copy-start.1 = (bf16[4,4,8,8,1024]{4,3,2,1,0:T(8,128)(2,1)S(1)}, bf16[4,4,8,8,1024]{4,3,2,1,0:T(8,128)(2,1)}, u32[]{:S(2)}) copy-start(bf16[4,4,8,8,1024]{4,3,2,1,0:T(8,128)(2,1)} %forward.3) | copy-start | bytes 6291460
  2.9 5.1 %copy-start.2 = (f32[1,4,8,8,1024]{4,3,2,1,0:T(8,128)S(1)}, f32[1,4,8,8,1024]{4,3,2,1,0:T(8,128)}, u32[]{:S(2)}) copy-start(f32[1,4,8,8,1024]{4,3,2,1,0:T(8,128)} %state) | copy-start | bytes 3145732
  2.9 5.1 %copy-start.3 = (f32[8,8,1024]{2,1,0:T(8,128)S(1)}, f32[8,8,1024]{2,1,0:T(8,128)}, u32[]{:S(2)}) copy-start(f32[8,8,1024]{2,1,0:T(8,128)} %speed.1) | copy-start | bytes 786436
  3.9 7.5 %collective-permute-start.5 = (f32[8,256]{1,0:T(8,128)S(1)}, f32[8,256]{1,0:T(8,128)S(1)}, u32[]{:S(2)}, u32[]{:S(2)}) collective-permute-start(f32[8,256]{1,0:T(8,128)S(1)} %shard_map.95), channel_id=1, source_target_pairs={{0,12},{4,0},{8,4},{12,8},{1,13},{5,1},{9,5},{13,9},{2,14},{6,2},{... | collective-permute-start | bytes 24584 | tf_op jit(solution)/shard_map/ppermute | solution.py:31
  4.0 9.6 %collective-permute-start.4 = (f32[8,256]{1,0:T(8,128)S(1)}, f32[8,256]{1,0:T(8,128)S(1)}, u32[]{:S(2)}, u32[]{:S(2)}) collective-permute-start(f32[8,256]{1,0:T(8,128)S(1)} %shard_map.95), channel_id=1, source_target_pairs={{0,8},{4,12},{8,0},{12,4},{1,9},{5,13},{9,1},{13,5},{2,10},{6,14},... | collective-permute-start | bytes 24584 | tf_op jit(solution)/shard_map/ppermute | solution.py:31
  6.7 6.9 %collective-permute-start.3 = (f32[8,256]{1,0:T(8,128)S(1)}, f32[8,256]{1,0:T(8,128)S(1)}, u32[]{:S(2)}, u32[]{:S(2)}) collective-permute-start(f32[8,256]{1,0:T(8,128)S(1)} %shard_map.95), channel_id=1, source_target_pairs={{0,4},{4,8},{8,12},{12,0},{1,5},{5,9},{9,13},{13,1},{2,6},{6,10},{... | collective-permute-start | bytes 24584 | tf_op jit(solution)/shard_map/ppermute | solution.py:31
  9.3 16.7 %collective-permute-start = (bf16[200,8,128]{2,1,0:T(8,128)(2,1)S(1)}, bf16[200,8,128]{2,1,0:T(8,128)(2,1)S(1)}, u32[]{:S(2)}, u32[]{:S(2)}) collective-permute-start(bf16[200,8,128]{2,1,0:T(8,128)(2,1)S(1)} %get-tuple-element.47), channel_id=1, source_target_pairs={{0,1},{1,0},{2,3},{3,2},{4,5},{5,4},{6,7},{7,6},{8,9},{9,8},{10,11... | collective-permute-start | bytes 1228808 | tf_op jit(solution)/shard_map/ppermute | solution.py:26
  10.6 15.3 %collective-permute-start.1 = (bf16[200,8,128]{2,1,0:T(8,128)(2,1)S(1)}, bf16[200,8,128]{2,1,0:T(8,128)(2,1)S(1)}, u32[]{:S(2)}, u32[]{:S(2)}) collective-permute-start(bf16[200,8,128]{2,1,0:T(8,128)(2,1)S(1)} %get-tuple-element.48), channel_id=1, source_target_pairs={{0,0},{1,2},{2,1},{3,3},{4,4},{5,6},{6,5},{7,7},{8,8},{9,10},{10,9... | collective-permute-start | bytes 1228808 | tf_op jit(solution)/shard_map/ppermute | solution.py:26
  11.3 14.6 %collective-permute-start.2 = (bf16[33,64,128]{2,1,0:T(8,128)(2,1)S(1)}, bf16[33,64,128]{2,1,0:T(8,128)(2,1)S(1)}, u32[]{:S(2)}, u32[]{:S(2)}) collective-permute-start(bf16[33,64,128]{2,1,0:T(8,128)(2,1)S(1)} %get-tuple-element.49), channel_id=1, source_target_pairs={{0,0},{4,8},{8,4},{12,12},{1,1},{5,9},{9,5},{13,13},{2,2},{6,10},{... | collective-permute-start | bytes 1622024 | tf_op jit(solution)/shard_map/ppermute | solution.py:26
  16.3 5.3 %collective-permute-start.8 = (f32[8,256]{1,0:T(8,128)S(1)}, f32[8,256]{1,0:T(8,128)S(1)}, u32[]{:S(2)}, u32[]{:S(2)}) collective-permute-start(f32[8,256]{1,0:T(8,128)S(1)} %get-tuple-element.53), channel_id=1, source_target_pairs={{0,3},{1,0},{2,1},{3,2},{4,7},{5,4},{6,5},{7,6},{8,11},{9,8},{10,9... | collective-permute-start | bytes 24584 | tf_op jit(solution)/shard_map/ppermute | solution.py:31
  18.6 7.2 %collective-permute-start.7 = (f32[8,256]{1,0:T(8,128)S(1)}, f32[8,256]{1,0:T(8,128)S(1)}, u32[]{:S(2)}, u32[]{:S(2)}) collective-permute-start(f32[8,256]{1,0:T(8,128)S(1)} %get-tuple-element.53), channel_id=1, source_target_pairs={{0,2},{1,3},{2,0},{3,1},{4,6},{5,7},{6,4},{7,5},{8,10},{9,11},{10,... | collective-permute-start | bytes 24584 | tf_op jit(solution)/shard_map/ppermute | solution.py:31
  21.7 4.3 %collective-permute-start.6 = (f32[8,256]{1,0:T(8,128)S(1)}, f32[8,256]{1,0:T(8,128)S(1)}, u32[]{:S(2)}, u32[]{:S(2)}) collective-permute-start(f32[8,256]{1,0:T(8,128)S(1)} %get-tuple-element.53), channel_id=1, source_target_pairs={{0,1},{1,2},{2,3},{3,0},{4,5},{5,6},{6,7},{7,4},{8,9},{9,10},{10,1... | collective-permute-start | bytes 24584 | tf_op jit(solution)/shard_map/ppermute | solution.py:31
  25.8 6.8 %copy-start.6 = (s32[256,3]{0,1:T(4,128)S(1)}, s32[256,3]{0,1:T(4,128)}, u32[]{:S(2)}) copy-start(s32[256,3]{0,1:T(4,128)} %param.14) | copy-start | bytes 9220
  25.8 6.8 %copy-start.7 = (f32[256,4]{0,1:T(4,128)S(1)}, f32[256,4]{0,1:T(4,128)}, u32[]{:S(2)}) copy-start(f32[256,4]{0,1:T(4,128)} %param.15) | copy-start | bytes 12292
  26.1 8.3 %collective-permute-start.9 = (bf16[41,64,128]{2,1,0:T(8,128)(2,1)S(1)}, bf16[41,64,128]{2,1,0:T(8,128)(2,1)S(1)}, u32[]{:S(2)}, u32[]{:S(2)}) collective-permute-start(bf16[41,64,128]{2,1,0:T(8,128)(2,1)S(1)} %get-tuple-element.64), channel_id=1, source_target_pairs={{0,4},{4,0},{8,12},{12,8},{1,5},{5,1},{9,13},{13,9},{2,6},{6,2},{1... | collective-permute-start | bytes 2015240 | tf_op jit(solution)/shard_map/ppermute | solution.py:26
  27.8 6.6 %collective-permute-start.10 = (bf16[8,64,128]{2,1,0:T(8,128)(2,1)S(1)}, bf16[8,64,128]{2,1,0:T(8,128)(2,1)S(1)}, u32[]{:S(2)}, u32[]{:S(2)}) collective-permute-start(bf16[8,64,128]{2,1,0:T(8,128)(2,1)S(1)} %get-tuple-element.65), channel_id=1, source_target_pairs={{0,0},{4,8},{8,4},{12,12},{1,1},{5,9},{9,5},{13,13},{2,2},{6,10},{... | collective-permute-start | bytes 393224 | tf_op jit(solution)/shard_map/ppermute | solution.py:26
  32.6 1.8 %copy-start.4 = (f32[3,1024]{1,0:T(4,128)S(1)}, f32[3,1024]{1,0:T(4,128)}, u32[]{:S(2)}) copy-start(f32[3,1024]{1,0:T(4,128)} %wind.3) | copy-start | bytes 36868
  38.7 7.6 %collective-permute-start.11 = (bf16[112,8,128]{2,1,0:T(8,128)(2,1)S(1)}, bf16[112,8,128]{2,1,0:T(8,128)(2,1)S(1)}, u32[]{:S(2)}, u32[]{:S(2)}) collective-permute-start(bf16[112,8,128]{2,1,0:T(8,128)(2,1)S(1)} %get-tuple-element.67), channel_id=1, source_target_pairs={{0,1},{1,0},{2,3},{3,2},{4,5},{5,4},{6,7},{7,6},{8,9},{9,8},{10,11... | collective-permute-start | bytes 688136 | tf_op jit(solution)/shard_map/ppermute | solution.py:26
  40.4 5.8 %collective-permute-start.12 = (bf16[112,8,128]{2,1,0:T(8,128)(2,1)S(1)}, bf16[112,8,128]{2,1,0:T(8,128)(2,1)S(1)}, u32[]{:S(2)}, u32[]{:S(2)}) collective-permute-start(bf16[112,8,128]{2,1,0:T(8,128)(2,1)S(1)} %get-tuple-element.68), channel_id=1, source_target_pairs={{0,0},{1,2},{2,1},{3,3},{4,4},{5,6},{6,5},{7,7},{8,8},{9,10},{10,9... | collective-permute-start | bytes 688136 | tf_op jit(solution)/shard_map/ppermute | solution.py:26
  41.1 7.3 %collective-permute-start.13 = (bf16[14,64,128]{2,1,0:T(8,128)(2,1)S(1)}, bf16[14,64,128]{2,1,0:T(8,128)(2,1)S(1)}, u32[]{:S(2)}, u32[]{:S(2)}) collective-permute-start(bf16[14,64,128]{2,1,0:T(8,128)(2,1)S(1)} %get-tuple-element.69), channel_id=1, source_target_pairs={{0,0},{4,8},{8,4},{12,12},{1,1},{5,9},{9,5},{13,13},{2,2},{6,10},{... | collective-permute-start | bytes 688136 | tf_op jit(solution)/shard_map/ppermute | solution.py:26
  45.0 7.5 %collective-permute-start.14 = (bf16[16,64,128]{2,1,0:T(8,128)(2,1)S(1)}, bf16[16,64,128]{2,1,0:T(8,128)(2,1)S(1)}, u32[]{:S(2)}, u32[]{:S(2)}) collective-permute-start(bf16[16,64,128]{2,1,0:T(8,128)(2,1)S(1)} %get-tuple-element.78), channel_id=1, source_target_pairs={{0,16},{16,0},{1,17},{17,1},{2,18},{18,2},{3,19},{19,3},{4,20},{20... | collective-permute-start | bytes 786440 | tf_op jit(solution)/shard_map/ppermute | solution.py:689
  48.5 6.0 %collective-permute-start.15 = (bf16[20,64,128]{2,1,0:T(8,128)(2,1)S(1)}, bf16[20,64,128]{2,1,0:T(8,128)(2,1)S(1)}, u32[]{:S(2)}, u32[]{:S(2)}) collective-permute-start(bf16[20,64,128]{2,1,0:T(8,128)(2,1)S(1)} %get-tuple-element.82), channel_id=1, source_target_pairs={{0,4},{4,0},{8,12},{12,8},{1,5},{5,1},{9,13},{13,9},{2,6},{6,2},{1... | collective-permute-start | bytes 983048 | tf_op jit(solution)/shard_map/ppermute | solution.py:26
  48.6 5.9 %collective-permute-start.16 = (bf16[6,64,128]{2,1,0:T(8,128)(2,1)S(1)}, bf16[6,64,128]{2,1,0:T(8,128)(2,1)S(1)}, u32[]{:S(2)}, u32[]{:S(2)}) collective-permute-start(bf16[6,64,128]{2,1,0:T(8,128)(2,1)S(1)} %get-tuple-element.83), channel_id=1, source_target_pairs={{0,0},{4,8},{8,4},{12,12},{1,1},{5,9},{9,5},{13,13},{2,2},{6,10},{... | collective-permute-start | bytes 294920 | tf_op jit(solution)/shard_map/ppermute | solution.py:26
  59.9 5.8 %collective-permute-start.17 = (s16[4,4,16,512]{3,2,1,0:T(8,128)(2,1)S(1)}, s16[4,4,16,512]{3,2,1,0:T(8,128)(2,1)S(1)}, u32[]{:S(2)}, u32[]{:S(2)}) collective-permute-start(s16[4,4,16,512]{3,2,1,0:T(8,128)(2,1)S(1)} %get-tuple-element.87), channel_id=1, source_target_pairs={{0,16},{16,0},{1,17},{17,1},{2,18},{18,2},{3,19},{19,3},{4,20},{20... | collective-permute-start | bytes 786440 | tf_op jit(solution)/shard_map/ppermute | solution.py:795
  61.2 4.5 %collective-permute-start.18 = (f32[4,512]{1,0:T(4,128)S(1)}, f32[4,512]{1,0:T(4,128)S(1)}, u32[]{:S(2)}, u32[]{:S(2)}) collective-permute-start(f32[4,512]{1,0:T(4,128)S(1)} %get-tuple-element.88), channel_id=1, source_target_pairs={{0,16},{16,0},{1,17},{17,1},{2,18},{18,2},{3,19},{19,3},{4,20},{20... | collective-permute-start | bytes 24584 | tf_op jit(solution)/shard_map/ppermute | solution.py:795

commit v8 on v6

--- a/solution.py
+++ b/solution.py
@@ -707,9 +707,7 @@
         early, late, forward_early, slopes_early, *rim
     )
     late_dz = own_slopes(late)
-    z_second, x_second, total, late_dz = lax.optimization_barrier(
-        (z_second, x_second, total, late_dz)
-    )
+    z_second, x_second, late_dz = lax.optimization_barrier((z_second, x_second, late_dz))
     again, again_odd = second_hop(4, z_second, first[5], False)
 
     half = depth // 2

time: 67.2 us -> 67.2 us (level)
    ppermute x10, waiting for transfers between devices: 4.28 us -> 3.55 us  [swapped(): return lax.ppermute(x, axis, swap_pairs(lax.axis_size(axis), odd))]
  transfers between devices with their start and end apart: 19 -> 19, of which waited for: 4 -> 5; matrix products, arithmetic and copies ran while one was open for 0% -> 0% of each run, Pallas kernels for 23% -> 17%
where the time goes in v8:
time: 67.2 us; the launch traced here: 66.6 us
  starting transfers between devices  33.4 us (50%)
  Pallas kernels  22.6 us (34%)
  waiting for transfers between devices  6.67 us (10%)
  local copies, waits for them, and re-layouts  2.3 us (3%)
  between operations  1.57 us (2%)
    pallas_call x15, Pallas kernels, run(): pl.pallas_call(kernel, out_shape=outs, in_specs=specs or [pl.BlockSpec(me...  22.6 us
    ppermute x10, starting transfers between devices, swapped(): return lax.ppermute(x, axis, swap_pairs(lax.axis_size(axis), odd))  17.9 us
    ppermute x6, starting transfers between devices, total_of(): lax.ppermute(x, axis, [(i, (i + k) % size) for i in range(size)])  12.8 us
    ppermute x10, waiting for transfers between devices, swapped(): return lax.ppermute(x, axis, swap_pairs(lax.axis_size(axis), odd))  3.55 us
    ppermute x1, waiting for transfers between devices, shards(): lax.ppermute(scales, 'pair', across)  2.95 us
    unnamed x16, local copies, waits for them, and re-layouts  2.3 us
  transfers between devices with their start and end apart: 19, of which 5 were waited for; matrix products, arithmetic and copies ran while one was open for 0% of the time, Pallas kernels for 17%

profile of v8, /device:TPU:1, one launch (start us, length us, event | category | flops | bytes accessed | tf_op | source)
XLA Modules:
  0.0 66.6 jit_solution(7717138673272453737)
XLA Ops:
  0.6 1.6 %copy-done = bf16[4,4,8,8,1024]{4,3,2,1,0:T(8,128)(2,1)S(1)} copy-done((bf16[4,4,8,8,1024]{4,3,2,1,0:T(8,128)(2,1)S(1)}, bf16[4,4,8,8,1024]{4,3,2,1,0:T(8,128)(2,1)}, u32[]{:S(2)}) %copy-start) | copy-done | bytes 2097176
  2.2 0.7 %copy-done.5 = s32[256,3]{0,1:T(4,128)S(1)} copy-done((s32[256,3]{0,1:T(4,128)S(1)}, s32[256,3]{0,1:T(4,128)}, u32[]{:S(2)}) %copy-start.5) | copy-done | bytes 3096
  2.9 0.9 %shard_map.95 = f32[8,256]{1,0:T(8,128)S(1)} custom-call(s32[3,256]{1,0:T(4,128)S(1)} %bitcast.3, bf16[4,4,8,8,1024]{4,3,2,1,0:T(8,128)(2,1)S(1)} %copy-done), custom_call_target="tpu_custom_call" | custom-call | flops 1650000000 | bytes 100000 | tf_op jit(solution)/shard_map/pallas_call | solution.py:46
  3.9 0.1 collective-permute-start.5
  4.0 2.7 %collective-permute-start.4 = (f32[8,256]{1,0:T(8,128)S(1)}, f32[8,256]{1,0:T(8,128)S(1)}, u32[]{:S(2)}, u32[]{:S(2)}) collective-permute-start(f32[8,256]{1,0:T(8,128)S(1)} %shard_map.95), channel_id=1, source_target_pairs={{0,8},{4,12},{8,0},{12,4},{1,9},{5,13},{9,1},{13,5},{2,10},{6,14},... | collective-permute-start | bytes 24584 | tf_op jit(solution)/shard_map/ppermute | solution.py:31
  6.7 1.3 %collective-permute-start.3 = (f32[8,256]{1,0:T(8,128)S(1)}, f32[8,256]{1,0:T(8,128)S(1)}, u32[]{:S(2)}, u32[]{:S(2)}) collective-permute-start(f32[8,256]{1,0:T(8,128)S(1)} %shard_map.95), channel_id=1, source_target_pairs={{0,4},{4,8},{8,12},{12,0},{1,5},{5,9},{9,13},{13,1},{2,6},{6,10},{... | collective-permute-start | bytes 24584 | tf_op jit(solution)/shard_map/ppermute | solution.py:31
  8.0 1.3 %shard_map.96 = (f32[4,8,64,128]{3,2,1,0:T(8,128)S(1)}, f32[8,64,128]{2,1,0:T(8,128)S(1)}, f32[8,8,64,128]{3,2,1,0:T(8,128)S(1)}, f32[8,8,64,128]{3,2,1,0:T(8,12...) custom-call(f32[1,4,8,8,1024]{4,3,2,1,0:T(8,128)S(1)} %copy-done.2, ...), custom_call_target="tpu_custom_call" | custom-call | flops 1430000000 | bytes 100000 | tf_op jit(solution)/shard_map/pallas_call | solution.py:46
  9.3 1.4 %collective-permute-start = (bf16[200,8,128]{2,1,0:T(8,128)(2,1)S(1)}, bf16[200,8,128]{2,1,0:T(8,128)(2,1)S(1)}, u32[]{:S(2)}, u32[]{:S(2)}) collective-permute-start(bf16[200,8,128]{2,1,0:T(8,128)(2,1)S(1)} %get-tuple-element.45), channel_id=1, source_target_pairs={{0,1},{1,0},{2,3},{3,2},{4,5},{5,4},{6,7},{7,6},{8,9},{9,8},{10,11... | collective-permute-start | bytes 1228808 | tf_op jit(solution)/shard_map/ppermute | solution.py:26
  10.6 0.7 %collective-permute-start.1 = (bf16[200,8,128]{2,1,0:T(8,128)(2,1)S(1)}, bf16[200,8,128]{2,1,0:T(8,128)(2,1)S(1)}, u32[]{:S(2)}, u32[]{:S(2)}) collective-permute-start(bf16[200,8,128]{2,1,0:T(8,128)(2,1)S(1)} %get-tuple-element.46), channel_id=1, source_target_pairs={{0,0},{1,2},{2,1},{3,3},{4,4},{5,6},{6,5},{7,7},{8,8},{9,10},{10,9... | collective-permute-start | bytes 1228808 | tf_op jit(solution)/shard_map/ppermute | solution.py:26
  11.3 2.2 %collective-permute-start.2 = (bf16[33,64,128]{2,1,0:T(8,128)(2,1)S(1)}, bf16[33,64,128]{2,1,0:T(8,128)(2,1)S(1)}, u32[]{:S(2)}, u32[]{:S(2)}) collective-permute-start(bf16[33,64,128]{2,1,0:T(8,128)(2,1)S(1)} %get-tuple-element.47), channel_id=1, source_target_pairs={{0,0},{4,8},{8,4},{12,12},{1,1},{5,9},{9,5},{13,13},{2,2},{6,10},{... | collective-permute-start | bytes 1622024 | tf_op jit(solution)/shard_map/ppermute | solution.py:26
  13.6 0.0 collective-permute-done.4
  13.6 0.0 collective-permute-done.3
  13.6 2.7 %shard_map.97 = (f32[8,8,64,128]{3,2,1,0:T(8,128)S(1)}, f32[8,8,64,128]{3,2,1,0:T(8,128)S(1)}, f32[8,256]{1,0:T(8,128)S(1)}) custom-call(f32[8,8,64,128]{3,2,1,0:T(8,128)S(1)} %get-tuple-element.48.early.columns, f32[8,8,64,128]{3,2,1,0:T(8,128)S(1)} %get-tuple-element.49.late.columns, f32[8,256]{1,0:T(8,128)S(1)} %add_add_fusion.1.sample), custom_call_target="tpu_custom_call" | custom-call | flops 2969999872 | bytes 100000 | tf_op jit(solution)/shard_map/pallas_call | solution.py:46
  16.3 2.2 %collective-permute-start.8 = (f32[8,256]{1,0:T(8,128)S(1)}, f32[8,256]{1,0:T(8,128)S(1)}, u32[]{:S(2)}, u32[]{:S(2)}) collective-permute-start(f32[8,256]{1,0:T(8,128)S(1)} %get-tuple-element.51), channel_id=1, source_target_pairs={{0,3},{1,0},{2,1},{3,2},{4,7},{5,4},{6,5},{7,6},{8,11},{9,8},{10,9... | collective-permute-start | bytes 24584 | tf_op jit(solution)/shard_map/ppermute | solution.py:31
  18.6 3.1 %collective-permute-start.7 = (f32[8,256]{1,0:T(8,128)S(1)}, f32[8,256]{1,0:T(8,128)S(1)}, u32[]{:S(2)}, u32[]{:S(2)}) collective-permute-start(f32[8,256]{1,0:T(8,128)S(1)} %get-tuple-element.51), channel_id=1, source_target_pairs={{0,2},{1,3},{2,0},{3,1},{4,6},{5,7},{6,4},{7,5},{8,10},{9,11},{10,... | collective-permute-start | bytes 24584 | tf_op jit(solution)/shard_map/ppermute | solution.py:31
  21.7 3.3 %collective-permute-start.6 = (f32[8,256]{1,0:T(8,128)S(1)}, f32[8,256]{1,0:T(8,128)S(1)}, u32[]{:S(2)}, u32[]{:S(2)}) collective-permute-start(f32[8,256]{1,0:T(8,128)S(1)} %get-tuple-element.51), channel_id=1, source_target_pairs={{0,1},{1,2},{2,3},{3,0},{4,5},{5,6},{6,7},{7,4},{8,9},{9,10},{10,1... | collective-permute-start | bytes 24584 | tf_op jit(solution)/shard_map/ppermute | solution.py:31
  24.9 0.8 %shard_map.98.own_dz = f32[4,8,64,128]{3,2,1,0:T(8,128)S(1)} custom-call(f32[4,8,64,128]{3,2,1,0:T(8,128)S(1)} %get-tuple-element.54.cols), custom_call_target="tpu_custom_call" | custom-call | flops 880000000 | bytes 100000 | tf_op jit(solution)/shard_map/pallas_call | solution.py:46
  25.8 0.0 copy-start.6
  25.8 0.0 copy-start.7
  25.8 0.0 collective-permute-done.7
  25.8 0.1 collective-permute-done.6
  26.0 0.0 collective-permute-done.z_even.z0.refs_0_
  26.0 0.1 shard_map.101
  26.1 1.0 %collective-permute-start.9 = (bf16[41,64,128]{2,1,0:T(8,128)(2,1)S(1)}, bf16[41,64,128]{2,1,0:T(8,128)(2,1)S(1)}, u32[]{:S(2)}, u32[]{:S(2)}) collective-permute-start(bf16[41,64,128]{2,1,0:T(8,128)(2,1)S(1)} %get-tuple-element.62), channel_id=1, source_target_pairs={{0,4},{4,0},{8,12},{12,8},{1,5},{5,1},{9,13},{13,9},{2,6},{6,2},{1... | collective-permute-start | bytes 2015240 | tf_op jit(solution)/shard_map/ppermute | solution.py:26
  27.8 4.0 %collective-permute-start.10 = (bf16[8,64,128]{2,1,0:T(8,128)(2,1)S(1)}, bf16[8,64,128]{2,1,0:T(8,128)(2,1)S(1)}, u32[]{:S(2)}, u32[]{:S(2)}) collective-permute-start(bf16[8,64,128]{2,1,0:T(8,128)(2,1)S(1)} %get-tuple-element.63), channel_id=1, source_target_pairs={{0,0},{4,8},{8,4},{12,12},{1,1},{5,9},{9,5},{13,13},{2,2},{6,10},{... | collective-permute-start | bytes 393224 | tf_op jit(solution)/shard_map/ppermute | solution.py:26
  31.8 0.8 %shard_map.100.face_dz = f32[2,4,8,3,8,128]{5,4,3,2,1,0:T(8,128)S(1)} custom-call(bf16[200,8,128]{2,1,0:T(8,128)(2,1)S(1)} %collective-permute-done.z_even.z0.refs_0_, bf16[200,8,128]{2,1,0:T(8,128)(2,1)S(1)} %collective-permute-done.1.z_odd.z1.refs_1_), custom_call_target="tpu_custom_call" | custom-call | flops 660000000 | bytes 100000 | tf_op jit(solution)/shard_map/pallas_call | solution.py:46
  32.6 0.0 copy-start.4
  32.6 1.5 %shard_map.99.inject = f32[4,2048,128]{2,1,0:T(8,128)S(1)} custom-call(s32[1]{0:T(128)S(6)} %copy.10.counts, s32[3,256]{1,0:T(4,128)S(1)} %bitcast.4, f32[4,256]{1,0:T(4,128)S(1)} %bitcast.5, f32[8,256]{1,0:T(8,128)S(1)} %add_add_fusion.samples), custom_call_target="tpu_custom_call" | custom-call | flops 1760000000 | bytes 100000 | tf_op jit(solution)/shard_map/pallas_call | solution.py:46
  34.1 0.3 collective-permute-done.10.c1
  34.4 4.2 %shard_map.102 = (f32[4,8,64,128]{3,2,1,0:T(8,128)S(1)}, f32[4,8,64,128]{3,2,1,0:T(8,128)S(1)}, f32[16,128,128]{2,1,0:T(8,128)S(1)}, bf16[112,8,128]{2,1,0:T(8,1...) custom-call(f32[3,1024]{1,0:T(4,128)S(1)} %copy-done.4, ...), custom_call_target="tpu_custom_call" | custom-call | flops 6600000000 | bytes 100000 | tf_op jit(solution)/shard_map/pallas_call | solution.py:46
  38.7 1.8 %collective-permute-start.11 = (bf16[112,8,128]{2,1,0:T(8,128)(2,1)S(1)}, bf16[112,8,128]{2,1,0:T(8,128)(2,1)S(1)}, u32[]{:S(2)}, u32[]{:S(2)}) collective-permute-start(bf16[112,8,128]{2,1,0:T(8,128)(2,1)S(1)} %get-tuple-element.65), channel_id=1, source_target_pairs={{0,1},{1,0},{2,3},{3,2},{4,5},{5,4},{6,7},{7,6},{8,9},{9,8},{10,11... | collective-permute-start | bytes 688136 | tf_op jit(solution)/shard_map/ppermute | solution.py:26
  40.4 0.7 collective-permute-start.12
  41.1 3.0 %collective-permute-start.13 = (bf16[14,64,128]{2,1,0:T(8,128)(2,1)S(1)}, bf16[14,64,128]{2,1,0:T(8,128)(2,1)S(1)}, u32[]{:S(2)}, u32[]{:S(2)}) collective-permute-start(bf16[14,64,128]{2,1,0:T(8,128)(2,1)S(1)} %get-tuple-element.67), channel_id=1, source_target_pairs={{0,0},{4,8},{8,4},{12,12},{1,1},{5,9},{9,5},{13,13},{2,2},{6,10},{... | collective-permute-start | bytes 688136 | tf_op jit(solution)/shard_map/ppermute | solution.py:26
  44.1 1.3 %collective-permute-start.14 = (bf16[16,64,128]{2,1,0:T(8,128)(2,1)S(1)}, bf16[16,64,128]{2,1,0:T(8,128)(2,1)S(1)}, u32[]{:S(2)}, u32[]{:S(2)}) collective-permute-start(bf16[16,64,128]{2,1,0:T(8,128)(2,1)S(1)} %get-tuple-element.74), channel_id=1, source_target_pairs={{0,16},{16,0},{1,17},{17,1},{2,18},{18,2},{3,19},{19,3},{4,20},{20... | collective-permute-start | bytes 786440 | tf_op jit(solution)/shard_map/ppermute | solution.py:375
  45.4 0.8 %shard_map.103.own_dz = f32[4,8,64,128]{3,2,1,0:T(8,128)S(1)} custom-call(f32[4,8,64,128]{3,2,1,0:T(8,128)S(1)} %get-tuple-element.64.cols.late), custom_call_target="tpu_custom_call" | custom-call | flops 880000000 | bytes 100000 | tf_op jit(solution)/shard_map/pallas_call | solution.py:46
  46.3 2.2 %collective-permute-done.13.refs_7_ = bf16[14,64,128]{2,1,0:T(8,128)(2,1)S(1)} collective-permute-done((bf16[14,64,128]{2,1,0:T(8,128)(2,1)S(1)}, bf16[14,64,128]{2,1,0:T(8,128)(2,1)S(1)}, u32[]{:S(2)}, u32[]{:S(2)}) %collective-permute-start.13) | collective-permute-done | bytes 229408 | tf_op jit(solution)/shard_map/ppermute | solution.py:26
  48.4 0.1 shard_map.106
  48.5 0.1 collective-permute-start.15
  48.6 3.0 %collective-permute-start.16 = (bf16[6,64,128]{2,1,0:T(8,128)(2,1)S(1)}, bf16[6,64,128]{2,1,0:T(8,128)(2,1)S(1)}, u32[]{:S(2)}, u32[]{:S(2)}) collective-permute-start(bf16[6,64,128]{2,1,0:T(8,128)(2,1)S(1)} %get-tuple-element.79), channel_id=1, source_target_pairs={{0,0},{4,8},{8,4},{12,12},{1,1},{5,9},{9,5},{13,13},{2,2},{6,10},{... | collective-permute-start | bytes 294920 | tf_op jit(solution)/shard_map/ppermute | solution.py:26
  51.6 1.0 %shard_map.105.total = f32[4,8,64,128]{3,2,1,0:T(8,128)S(1)} custom-call(f32[4,8,64,128]{3,2,1,0:T(8,128)S(1)} %get-tuple-element.72.early, f32[4,8,64,128]{3,2,1,0:T(8,128)S(1)} %get-tuple-element.64.cols.late, f32[8,8,64,128]{3,2,1,0:T(8,128)S(1)} %get-tuple-element.48.early.columns, f32[8,8,64,128]{3,2,1,0:T(8,128)S(1)} %get-tuple-element.73.slopes, ...), custom_call_target="tpu_custom_call" | custom-call | flops 2529999872 | bytes 100000 | tf_op jit(solution)/shard_map/pallas_call | solution.py:46
  52.6 0.8 %shard_map.104.face_dz = f32[2,4,8,3,8,128]{5,4,3,2,1,0:T(8,128)S(1)} custom-call(bf16[112,8,128]{2,1,0:T(8,128)(2,1)S(1)} %collective-permute-done.11.z_even.refs_5_, bf16[112,8,128]{2,1,0:T(8,128)(2,1)S(1)} %collective-permute-done.12.z_odd.refs_6_), custom_call_target="tpu_custom_call" | custom-call | flops 660000000 | bytes 100000 | tf_op jit(solution)/shard_map/pallas_call | solution.py:46
  53.4 1.1 %collective-permute-done.16.refs_9_ = bf16[6,64,128]{2,1,0:T(8,128)(2,1)S(1)} collective-permute-done((bf16[6,64,128]{2,1,0:T(8,128)(2,1)S(1)}, bf16[6,64,128]{2,1,0:T(8,128)(2,1)S(1)}, u32[]{:S(2)}, u32[]{:S(2)}) %collective-permute-start.16) | collective-permute-done | bytes 98336 | tf_op jit(solution)/shard_map/ppermute | solution.py:26
  54.5 5.4 %shard_map.107 = (f32[4,8,64,128]{3,2,1,0:T(8,128)S(1)}, f32[4,8,64,128]{3,2,1,0:T(8,128)S(1)}, s16[4,4,16,512]{3,2,1,0:T(8,128)(2,1)S(1)}, f32[4,512]{1,0:T(4,128)S(1)}) custom-call(f32[3,1024]{1,0:T(4,128)S(1)} %copy-done.4, f32[4,2048,128]{2,1,0:T(8,128)S(1)} %shard_map.99.inject, f32[4,8,64,128]{3,2,1,0:T(8,128)S(1)} %get-tuple-element.64.cols.late, ...), custom_call_target="tpu_custom_call" | custom-call | flops 9900000256 | bytes 100000 | tf_op jit(solution)/shard_map/pallas_call | solution.py:46
  59.9 1.3 %collective-permute-start.17 = (s16[4,4,16,512]{3,2,1,0:T(8,128)(2,1)S(1)}, s16[4,4,16,512]{3,2,1,0:T(8,128)(2,1)S(1)}, u32[]{:S(2)}, u32[]{:S(2)}) collective-permute-start(s16[4,4,16,512]{3,2,1,0:T(8,128)(2,1)S(1)} %get-tuple-element.83), channel_id=1, source_target_pairs={{0,16},{16,0},{1,17},{17,1},{2,18},{18,2},{3,19},{19,3},{4,20},{20... | collective-permute-start | bytes 786440 | tf_op jit(solution)/shard_map/ppermute | solution.py:794
  61.2 0.3 collective-permute-start.18
  61.5 1.3 %shard_map.108 = (f32[1,4,8,8,1024]{4,3,2,1,0:T(8,128)}, f32[4,8,8,512]{3,2,1,0:T(8,128)S(1)}) custom-call(f32[4,8,64,128]{3,2,1,0:T(8,128)S(1)} %get-tuple-element.80.last, f32[4,8,64,128]{3,2,1,0:T(8,128)S(1)} %get-tuple-element.81.sums), custom_call_target="tpu_custom_call" | custom-call | flops 1100000000 | bytes 100000 | tf_op jit(solution)/shard_map/pallas_call | solution.py:46
  62.7 2.9 %collective-permute-done.18.scales = f32[4,512]{1,0:T(4,128)S(1)} collective-permute-done((f32[4,512]{1,0:T(4,128)S(1)}, f32[4,512]{1,0:T(4,128)S(1)}, u32[]{:S(2)}, u32[]{:S(2)}) %collective-permute-start.18) | collective-permute-done | bytes 8224 | tf_op jit(solution)/shard_map/ppermute | solution.py:794
  65.7 0.9 %shard_map.109 = f32[4,8,8,512]{3,2,1,0:T(8,128)} custom-call(f32[4,8,8,512]{3,2,1,0:T(8,128)S(1)} %get-tuple-element.82.mine, s16[4,4,16,512]{3,2,1,0:T(8,128)(2,1)S(1)} %collective-permute-done.17.other, f32[4,512]{1,0:T(4,128)S(1)} %collective-permute-done.18.scales), custom_call_target="tpu_custom_call" | custom-call | flops 880000000 | bytes 100000 | tf_op jit(solution)/shard_map/pallas_call | solution.py:46
  (23 shorter events, 0.1 us)
Async XLA Ops:
  0.6 1.6 %copy-start = (bf16[4,4,8,8,1024]{4,3,2,1,0:T(8,128)(2,1)S(1)}, bf16[4,4,8,8,1024]{4,3,2,1,0:T(8,128)(2,1)}, u32[]{:S(2)}) copy-start(bf16[4,4,8,8,1024]{4,3,2,1,0:T(8,128)(2,1)} %forward.3) | copy-start | bytes 6291460
  2.2 0.7 %copy-start.5 = (s32[256,3]{0,1:T(4,128)S(1)}, s32[256,3]{0,1:T(4,128)}, u32[]{:S(2)}) copy-start(s32[256,3]{0,1:T(4,128)} %param.13) | copy-start | bytes 9220
  2.9 5.1 %copy-start.1 = (bf16[4,4,8,8,1024]{4,3,2,1,0:T(8,128)(2,1)S(1)}, bf16[4,4,8,8,1024]{4,3,2,1,0:T(8,128)(2,1)}, u32[]{:S(2)}) copy-start(bf16[4,4,8,8,1024]{4,3,2,1,0:T(8,128)(2,1)} %forward.3) | copy-start | bytes 6291460
  2.9 5.1 %copy-start.2 = (f32[1,4,8,8,1024]{4,3,2,1,0:T(8,128)S(1)}, f32[1,4,8,8,1024]{4,3,2,1,0:T(8,128)}, u32[]{:S(2)}) copy-start(f32[1,4,8,8,1024]{4,3,2,1,0:T(8,128)} %state) | copy-start | bytes 3145732
  2.9 5.1 %copy-start.3 = (f32[8,8,1024]{2,1,0:T(8,128)S(1)}, f32[8,8,1024]{2,1,0:T(8,128)}, u32[]{:S(2)}) copy-start(f32[8,8,1024]{2,1,0:T(8,128)} %speed.1) | copy-start | bytes 786436
  3.9 7.5 %collective-permute-start.5 = (f32[8,256]{1,0:T(8,128)S(1)}, f32[8,256]{1,0:T(8,128)S(1)}, u32[]{:S(2)}, u32[]{:S(2)}) collective-permute-start(f32[8,256]{1,0:T(8,128)S(1)} %shard_map.95), channel_id=1, source_target_pairs={{0,12},{4,0},{8,4},{12,8},{1,13},{5,1},{9,5},{13,9},{2,14},{6,2},{... | collective-permute-start | bytes 24584 | tf_op jit(solution)/shard_map/ppermute | solution.py:31
  4.0 9.6 %collective-permute-start.4 = (f32[8,256]{1,0:T(8,128)S(1)}, f32[8,256]{1,0:T(8,128)S(1)}, u32[]{:S(2)}, u32[]{:S(2)}) collective-permute-start(f32[8,256]{1,0:T(8,128)S(1)} %shard_map.95), channel_id=1, source_target_pairs={{0,8},{4,12},{8,0},{12,4},{1,9},{5,13},{9,1},{13,5},{2,10},{6,14},... | collective-permute-start | bytes 24584 | tf_op jit(solution)/shard_map/ppermute | solution.py:31
  6.7 6.9 %collective-permute-start.3 = (f32[8,256]{1,0:T(8,128)S(1)}, f32[8,256]{1,0:T(8,128)S(1)}, u32[]{:S(2)}, u32[]{:S(2)}) collective-permute-start(f32[8,256]{1,0:T(8,128)S(1)} %shard_map.95), channel_id=1, source_target_pairs={{0,4},{4,8},{8,12},{12,0},{1,5},{5,9},{9,13},{13,1},{2,6},{6,10},{... | collective-permute-start | bytes 24584 | tf_op jit(solution)/shard_map/ppermute | solution.py:31
  9.3 16.7 %collective-permute-start = (bf16[200,8,128]{2,1,0:T(8,128)(2,1)S(1)}, bf16[200,8,128]{2,1,0:T(8,128)(2,1)S(1)}, u32[]{:S(2)}, u32[]{:S(2)}) collective-permute-start(bf16[200,8,128]{2,1,0:T(8,128)(2,1)S(1)} %get-tuple-element.45), channel_id=1, source_target_pairs={{0,1},{1,0},{2,3},{3,2},{4,5},{5,4},{6,7},{7,6},{8,9},{9,8},{10,11... | collective-permute-start | bytes 1228808 | tf_op jit(solution)/shard_map/ppermute | solution.py:26
  10.6 15.3 %collective-permute-start.1 = (bf16[200,8,128]{2,1,0:T(8,128)(2,1)S(1)}, bf16[200,8,128]{2,1,0:T(8,128)(2,1)S(1)}, u32[]{:S(2)}, u32[]{:S(2)}) collective-permute-start(bf16[200,8,128]{2,1,0:T(8,128)(2,1)S(1)} %get-tuple-element.46), channel_id=1, source_target_pairs={{0,0},{1,2},{2,1},{3,3},{4,4},{5,6},{6,5},{7,7},{8,8},{9,10},{10,9... | collective-permute-start | bytes 1228808 | tf_op jit(solution)/shard_map/ppermute | solution.py:26
  11.3 14.6 %collective-permute-start.2 = (bf16[33,64,128]{2,1,0:T(8,128)(2,1)S(1)}, bf16[33,64,128]{2,1,0:T(8,128)(2,1)S(1)}, u32[]{:S(2)}, u32[]{:S(2)}) collective-permute-start(bf16[33,64,128]{2,1,0:T(8,128)(2,1)S(1)} %get-tuple-element.47), channel_id=1, source_target_pairs={{0,0},{4,8},{8,4},{12,12},{1,1},{5,9},{9,5},{13,13},{2,2},{6,10},{... | collective-permute-start | bytes 1622024 | tf_op jit(solution)/shard_map/ppermute | solution.py:26
  16.3 5.3 %collective-permute-start.8 = (f32[8,256]{1,0:T(8,128)S(1)}, f32[8,256]{1,0:T(8,128)S(1)}, u32[]{:S(2)}, u32[]{:S(2)}) collective-permute-start(f32[8,256]{1,0:T(8,128)S(1)} %get-tuple-element.51), channel_id=1, source_target_pairs={{0,3},{1,0},{2,1},{3,2},{4,7},{5,4},{6,5},{7,6},{8,11},{9,8},{10,9... | collective-permute-start | bytes 24584 | tf_op jit(solution)/shard_map/ppermute | solution.py:31
  18.6 7.2 %collective-permute-start.7 = (f32[8,256]{1,0:T(8,128)S(1)}, f32[8,256]{1,0:T(8,128)S(1)}, u32[]{:S(2)}, u32[]{:S(2)}) collective-permute-start(f32[8,256]{1,0:T(8,128)S(1)} %get-tuple-element.51), channel_id=1, source_target_pairs={{0,2},{1,3},{2,0},{3,1},{4,6},{5,7},{6,4},{7,5},{8,10},{9,11},{10,... | collective-permute-start | bytes 24584 | tf_op jit(solution)/shard_map/ppermute | solution.py:31
  21.7 4.3 %collective-permute-start.6 = (f32[8,256]{1,0:T(8,128)S(1)}, f32[8,256]{1,0:T(8,128)S(1)}, u32[]{:S(2)}, u32[]{:S(2)}) collective-permute-start(f32[8,256]{1,0:T(8,128)S(1)} %get-tuple-element.51), channel_id=1, source_target_pairs={{0,1},{1,2},{2,3},{3,0},{4,5},{5,6},{6,7},{7,4},{8,9},{9,10},{10,1... | collective-permute-start | bytes 24584 | tf_op jit(solution)/shard_map/ppermute | solution.py:31
  25.8 6.8 %copy-start.6 = (s32[256,3]{0,1:T(4,128)S(1)}, s32[256,3]{0,1:T(4,128)}, u32[]{:S(2)}) copy-start(s32[256,3]{0,1:T(4,128)} %param.14) | copy-start | bytes 9220
  25.8 6.8 %copy-start.7 = (f32[256,4]{0,1:T(4,128)S(1)}, f32[256,4]{0,1:T(4,128)}, u32[]{:S(2)}) copy-start(f32[256,4]{0,1:T(4,128)} %param.15) | copy-start | bytes 12292
  26.1 8.3 %collective-permute-start.9 = (bf16[41,64,128]{2,1,0:T(8,128)(2,1)S(1)}, bf16[41,64,128]{2,1,0:T(8,128)(2,1)S(1)}, u32[]{:S(2)}, u32[]{:S(2)}) collective-permute-start(bf16[41,64,128]{2,1,0:T(8,128)(2,1)S(1)} %get-tuple-element.62), channel_id=1, source_target_pairs={{0,4},{4,0},{8,12},{12,8},{1,5},{5,1},{9,13},{13,9},{2,6},{6,2},{1... | collective-permute-start | bytes 2015240 | tf_op jit(solution)/shard_map/ppermute | solution.py:26
  27.8 6.6 %collective-permute-start.10 = (bf16[8,64,128]{2,1,0:T(8,128)(2,1)S(1)}, bf16[8,64,128]{2,1,0:T(8,128)(2,1)S(1)}, u32[]{:S(2)}, u32[]{:S(2)}) collective-permute-start(bf16[8,64,128]{2,1,0:T(8,128)(2,1)S(1)} %get-tuple-element.63), channel_id=1, source_target_pairs={{0,0},{4,8},{8,4},{12,12},{1,1},{5,9},{9,5},{13,13},{2,2},{6,10},{... | collective-permute-start | bytes 393224 | tf_op jit(solution)/shard_map/ppermute | solution.py:26
  32.6 1.8 %copy-start.4 = (f32[3,1024]{1,0:T(4,128)S(1)}, f32[3,1024]{1,0:T(4,128)}, u32[]{:S(2)}) copy-start(f32[3,1024]{1,0:T(4,128)} %wind.3) | copy-start | bytes 36868
  38.7 7.6 %collective-permute-start.11 = (bf16[112,8,128]{2,1,0:T(8,128)(2,1)S(1)}, bf16[112,8,128]{2,1,0:T(8,128)(2,1)S(1)}, u32[]{:S(2)}, u32[]{:S(2)}) collective-permute-start(bf16[112,8,128]{2,1,0:T(8,128)(2,1)S(1)} %get-tuple-element.65), channel_id=1, source_target_pairs={{0,1},{1,0},{2,3},{3,2},{4,5},{5,4},{6,7},{7,6},{8,9},{9,8},{10,11... | collective-permute-start | bytes 688136 | tf_op jit(solution)/shard_map/ppermute | solution.py:26
  40.4 5.8 %collective-permute-start.12 = (bf16[112,8,128]{2,1,0:T(8,128)(2,1)S(1)}, bf16[112,8,128]{2,1,0:T(8,128)(2,1)S(1)}, u32[]{:S(2)}, u32[]{:S(2)}) collective-permute-start(bf16[112,8,128]{2,1,0:T(8,128)(2,1)S(1)} %get-tuple-element.66), channel_id=1, source_target_pairs={{0,0},{1,2},{2,1},{3,3},{4,4},{5,6},{6,5},{7,7},{8,8},{9,10},{10,9... | collective-permute-start | bytes 688136 | tf_op jit(solution)/shard_map/ppermute | solution.py:26
  41.1 7.3 %collective-permute-start.13 = (bf16[14,64,128]{2,1,0:T(8,128)(2,1)S(1)}, bf16[14,64,128]{2,1,0:T(8,128)(2,1)S(1)}, u32[]{:S(2)}, u32[]{:S(2)}) collective-permute-start(bf16[14,64,128]{2,1,0:T(8,128)(2,1)S(1)} %get-tuple-element.67), channel_id=1, source_target_pairs={{0,0},{4,8},{8,4},{12,12},{1,1},{5,9},{9,5},{13,13},{2,2},{6,10},{... | collective-permute-start | bytes 688136 | tf_op jit(solution)/shard_map/ppermute | solution.py:26
  44.1 7.5 %collective-permute-start.14 = (bf16[16,64,128]{2,1,0:T(8,128)(2,1)S(1)}, bf16[16,64,128]{2,1,0:T(8,128)(2,1)S(1)}, u32[]{:S(2)}, u32[]{:S(2)}) collective-permute-start(bf16[16,64,128]{2,1,0:T(8,128)(2,1)S(1)} %get-tuple-element.74), channel_id=1, source_target_pairs={{0,16},{16,0},{1,17},{17,1},{2,18},{18,2},{3,19},{19,3},{4,20},{20... | collective-permute-start | bytes 786440 | tf_op jit(solution)/shard_map/ppermute | solution.py:375
  48.5 6.0 %collective-permute-start.15 = (bf16[20,64,128]{2,1,0:T(8,128)(2,1)S(1)}, bf16[20,64,128]{2,1,0:T(8,128)(2,1)S(1)}, u32[]{:S(2)}, u32[]{:S(2)}) collective-permute-start(bf16[20,64,128]{2,1,0:T(8,128)(2,1)S(1)} %get-tuple-element.78), channel_id=1, source_target_pairs={{0,4},{4,0},{8,12},{12,8},{1,5},{5,1},{9,13},{13,9},{2,6},{6,2},{1... | collective-permute-start | bytes 983048 | tf_op jit(solution)/shard_map/ppermute | solution.py:26
  48.6 5.9 %collective-permute-start.16 = (bf16[6,64,128]{2,1,0:T(8,128)(2,1)S(1)}, bf16[6,64,128]{2,1,0:T(8,128)(2,1)S(1)}, u32[]{:S(2)}, u32[]{:S(2)}) collective-permute-start(bf16[6,64,128]{2,1,0:T(8,128)(2,1)S(1)} %get-tuple-element.79), channel_id=1, source_target_pairs={{0,0},{4,8},{8,4},{12,12},{1,1},{5,9},{9,5},{13,13},{2,2},{6,10},{... | collective-permute-start | bytes 294920 | tf_op jit(solution)/shard_map/ppermute | solution.py:26
  59.9 5.8 %collective-permute-start.17 = (s16[4,4,16,512]{3,2,1,0:T(8,128)(2,1)S(1)}, s16[4,4,16,512]{3,2,1,0:T(8,128)(2,1)S(1)}, u32[]{:S(2)}, u32[]{:S(2)}) collective-permute-start(s16[4,4,16,512]{3,2,1,0:T(8,128)(2,1)S(1)} %get-tuple-element.83), channel_id=1, source_target_pairs={{0,16},{16,0},{1,17},{17,1},{2,18},{18,2},{3,19},{19,3},{4,20},{20... | collective-permute-start | bytes 786440 | tf_op jit(solution)/shard_map/ppermute | solution.py:794
  61.2 4.5 %collective-permute-start.18 = (f32[4,512]{1,0:T(4,128)S(1)}, f32[4,512]{1,0:T(4,128)S(1)}, u32[]{:S(2)}, u32[]{:S(2)}) collective-permute-start(f32[4,512]{1,0:T(4,128)S(1)} %get-tuple-element.84), channel_id=1, source_target_pairs={{0,16},{16,0},{1,17},{17,1},{2,18},{18,2},{3,19},{19,3},{4,20},{20... | collective-permute-start | bytes 24584 | tf_op jit(solution)/shard_map/ppermute | solution.py:794
